TPU v7x, 256 devices: a whole 4x4x8 slice. The times are simulated.
256 devices in a mesh: dp: 8 (over z), shard: 32 (over y, x, core).
Axes of the slice: x: 4, y: 4, z: 8, core: 2. Of those that a mesh axis runs over, the one named last changes fastest.
Arguments:
- latent: bfloat16 [65536, 512], P(('dp', 'shard')), may hold values from -24 to 24
- latent_grad: bfloat16 [65536, 8192], P(('dp', 'shard')), may hold values from -0.029907227 to 0.029907227
- row_counts: int32 [256], P(('dp', 'shard')), may hold values from 64 to 256, as said below
- momentum: float32 [512, 8192], P('shard'), may hold values from -1.8 to 1.8
Outputs:
- new_momentum: float32 [512, 8192], P('shard')
- update: bfloat16 [512, 8192], P('shard')
Inputs may be any that keep to these rules, and one draw needn't show every extreme that they name: Live rows of one device are its first row_counts rows; some device has all 256 rows live.
All inputs are finite; a program needn't handle non-finite values.
Results may differ from a plain program's by a relative error of at most 0.0055.
Values may be sent and summed in bfloat16 or wider, within the bound.
No kernel may reach another device: no remote copies, remote signals or barrier semaphores. Data moves between devices by JAX's collectives and lax.ppermute only.
A program may use at most 128 MiB of HBM per device.

v0:
```python
import math

import jax
import jax.numpy as jnp
from jax import lax
from jax.sharding import PartitionSpec as P

KNOPE = 128
VDIM = 128
NS_STEPS = 5


coef_a = 3.4445
coef_b = -4.775
coef_c = 2.0315
decay_rate = 0.95
highest = lax.Precision.HIGHEST


def orthogonal(matrices):
    frobenius = jnp.sqrt(jnp.sum(matrices * matrices, axis=(1, 2), keepdims=True))
    matrix = matrices / (frobenius + 1e-07)
    for iteration in range(NS_STEPS):
        gram_matrix = jnp.einsum("krc,krd->kcd", matrix, matrix, precision=highest)
        square = jnp.einsum("kcd,kde->kce", gram_matrix, gram_matrix, precision=highest)
        polynomial = coef_b * gram_matrix + coef_c * square
        matrix = coef_a * matrix + jnp.einsum("krc,kcd->krd", matrix, polynomial, precision=highest)
    return matrix


def regroup(columns, owners, step_scale):
    local_rows, head_count, head_dim = columns.shape
    per_owner = -(-head_count // owners)
    outgoing = columns.reshape(local_rows, per_owner, owners, head_dim).transpose(2, 1, 0, 3)
    outgoing = outgoing.reshape(owners, per_owner, local_rows * head_dim)
    slot_items = lax.all_to_all(outgoing, "shard", split_axis=0, concat_axis=2, tiled=True)
    number = slot_items.shape[1]
    result = orthogonal(slot_items.reshape(number, owners * local_rows, head_dim))
    scaled = (
        (step_scale * result).astype(jnp.bfloat16).reshape(1, number, owners, local_rows * head_dim)
    )
    returned = lax.all_to_all(scaled, "shard", split_axis=2, concat_axis=0, tiled=True)
    returned = returned.reshape(owners, per_owner, local_rows, head_dim).transpose(2, 1, 0, 3)
    returned = returned.reshape(local_rows, per_owner * owners, head_dim)
    return returned


def body(latent, latent_grad, row_counts, momentum):
    owners = lax.axis_size("shard")
    slot_count, latent_width = latent.shape
    local_rows, full_width = momentum.shape
    head_dim = KNOPE + VDIM
    head_count = full_width // head_dim
    step_scale = 0.2 * math.sqrt(max(latent_width, head_dim))
    live_rows = lax.broadcasted_iota(jnp.int32, (slot_count, 1), 0) < row_counts[0]
    masked = jnp.where(live_rows, latent, jnp.zeros_like(latent))
    product = lax.dot_general(
        masked, latent_grad, (((0,), (0,)), ((), ())), preferred_element_type=jnp.float32
    )
    product = lax.optimization_barrier(product.astype(jnp.bfloat16))
    shard_sum = lax.psum_scatter(
        product.astype(jnp.float32), "shard", scatter_dimension=0, tiled=True
    )
    gradient = lax.psum(shard_sum, "dp")
    renewed = decay_rate * momentum + gradient
    update = regroup(renewed.reshape(local_rows, head_count, head_dim), owners, step_scale)
    update = update.reshape(local_rows, full_width)
    return (renewed, update)


def solution(mesh):
    in_specs = (
        P(("dp", "shard"), None),
        P(("dp", "shard"), None),
        P(("dp", "shard")),
        P("shard", None),
    )
    out_specs = (P("shard", None), P("shard", None))
    return jax.shard_map(body, mesh=mesh, in_specs=in_specs, out_specs=out_specs, check_vma=False)
```

profile of v0, /device:TPU:1, one launch (start us, length us, event | category | flops | bytes accessed | tf_op | source)
XLA Modules:
  0.0 290.8 jit_solution(5713920888081296443)
XLA Ops:
  7.2 0.0 reduce-scatter.2.cloned.1.call-start
  7.9 8.0 %convolution_convert_fusion = bf16[512,8192]{1,0:T(8,128)(2,1)} fusion(bf16[256,8192]{1,0:T(8,128)(2,1)} %param.5, bf16[256,512]{1,0:T(8,128)(2,1)} %param.4, pred[256]{0:T(512)(128)(4,1)S(1)} %iota_compare_fusion), kind=kOutput, calls=%fused_computation | convolution fusion | flops 2151809024 | bytes 12845312 | tf_op jit(solution)/shard_map/dot_general | solution.py:57
  15.8 11.3 %convert_element_type.11 = f32[512,8192]{1,0:T(8,128)} convert(bf16[512,8192]{1,0:T(8,128)(2,1)} %convolution_convert_fusion) | non-fusion elementwise | flops 4194304 | bytes 25165824 | tf_op jit(solution)/shard_map/convert_element_type | solution.py:62
  27.1 0.0 copy-start.1
  27.1 0.0 reduce-scatter.2.cloned.1.call-update
  27.2 0.0 all-reduce.2.cloned.1.call-start
  27.2 125.6 %reduce-scatter.2.cloned.1.call-done = f32[16,8192]{1,0:T(8,128)} async-done(((f32[512,8192]{1,0:T(8,128)}), f32[16,8192]{1,0:T(8,128)}) %reduce-scatter.2.cloned.1.call-update) | async-done | bytes 524304 | tf_op jit(solution)/shard_map/reduce_scatter | solution.py:61
  152.8 0.0 all-reduce.2.cloned.1.call-update
  152.8 71.8 %all-reduce.2.cloned.1.call-done = f32[16,8192]{1,0:T(8,128)} async-done(((f32[16,8192]{1,0:T(8,128)}), f32[16,8192]{1,0:T(8,128)}) %all-reduce.2.cloned.1.call-update) | async-done | bytes 524304 | tf_op jit(solution)/shard_map/psum | solution.py:64
  224.6 0.0 copy-done.1
  224.6 1.1 multiply_add_fusion
  225.7 0.0 copy-start
  225.7 0.2 copy.20
  225.9 0.3 copy.25
  226.2 0.5 reshape.154
  226.7 23.4 %all_to_all.8 = f32[32,1,4096]{2,1,0:T(1,128)S(1)} all-to-all(f32[32,1,4096]{2,1,0:T(1,128)S(1)} %reshape.154), channel_id=1, replica_groups=mesh['dp'=8,'shard'=32] {'shard'}, dimensions={0} | all-to-all | bytes 1048576 | tf_op jit(solution)/shard_map/all_to_all | solution.py:36
  250.2 1.7 multiply_reduce_fusion.1
  252.5 2.7 fusion.11
  255.3 0.1 div.21
  255.4 1.0 fusion.12
  256.4 0.4 fusion.6
  256.8 0.1 mul.86
  256.9 0.6 convolution_add_fusion.4
  257.5 1.0 fusion.13
  258.5 0.4 fusion.5
  258.9 0.6 convolution_add_fusion.3
  259.5 1.0 fusion.14
  260.5 0.0 copy-done
  260.5 0.4 fusion.4
  260.9 0.6 convolution_add_fusion.2
  261.5 1.0 fusion.15
  262.6 0.4 fusion.3
  263.0 0.6 convolution_add_fusion.1
  263.6 1.3 fusion.16
  264.8 0.4 fusion.2
  265.2 0.6 fusion.1
  265.8 0.1 reshape.155
  265.9 0.5 broadcast.68
  266.5 2.2 reduce.7
  268.6 0.2 reshape.159
  268.8 12.6 %all_to_all.9 = bf16[32,2,2048]{2,1,0:T(2,128)(2,1)S(1)} all-to-all(bf16[32,2,2048]{2,1,0:T(2,128)(2,1)S(1)} %reshape.159), channel_id=1, replica_groups=mesh['dp'=8,'shard'=32] {'shard'}, dimensions={0} | all-to-all | bytes 524288 | tf_op jit(solution)/shard_map/all_to_all | solution.py:42
  281.4 0.3 reshape.160
  281.7 1.5 bitcast_reduce_fusion
  283.2 0.7 copy.22
  (2 shorter events, 0.1 us)
Async XLA Ops:
  7.2 145.6 %reduce-scatter.2.cloned.1.call-start = ((), (), s32[]{:S(2)}) async-start(), calls=%async_computation.3 | async-start | bytes 17301504 | tf_op jit(solution)/shard_map/reduce_scatter | solution.py:61
  27.1 197.5 %copy-start.1 = (f32[16,8192]{1,0:T(8,128)S(1)}, f32[16,8192]{1,0:T(8,128)}, u32[]{:S(2)}) copy-start(f32[16,8192]{1,0:T(8,128)} %param.7) | copy-start | bytes 1572868
  27.2 197.4 %all-reduce.2.cloned.1.call-start = ((), (), s32[]{:S(2)}) async-start(), calls=%async_computation.4 | async-start | bytes 1048576 | tf_op jit(solution)/shard_map/psum | solution.py:64
  225.7 34.8 %copy-start = (f32[16,8192]{1,0:T(8,128)}, f32[16,8192]{1,0:T(8,128)S(1)}, u32[]{:S(2)}) copy-start(f32[16,8192]{1,0:T(8,128)S(1)} %multiply_add_fusion) | copy-start | bytes 1572868
Sparse Core Ops, SparseCore 0:
  27.3 125.4 reduce-scatter.1
  155.1 69.4 all-reduce.1
where the time goes:
time: 291 us
  waiting for transfers between devices  197 us (68%)
  blocking collectives  36 us (12%)
  other arithmetic  19 us (7%)
  matrix products  18.2 us (6%)
  between operations  15.6 us (5%)
  local copies, waits for them, and re-layouts  4.56 us (2%)
    reduce_scatter x1, waiting for transfers between devices, body(): lax.psum_scatter(product.astype(jnp.float32), 'shard', scatter_dimension=...  126 us
    psum x1, waiting for transfers between devices, body(): gradient = lax.psum(shard_sum, 'dp')  71.8 us
    all_to_all x1, blocking collectives, regroup(): lax.all_to_all(outgoing, 'shard', split_axis=0, concat_axis=2, tiled=True)  23.4 us
    all_to_all x1, blocking collectives, regroup(): lax.all_to_all(scaled, 'shard', split_axis=2, concat_axis=0, tiled=True)  12.6 us
    convert_element_type x1, other arithmetic, body(): product.astype(jnp.float32)  11.3 us
    dot_general x1, matrix products, body(): lax.dot_general(masked, latent_grad, (((0,), (0,)), ((), ())), preferred_...  7.97 us
  transfers between devices with their start and end apart: 2, of which 2 were waited for; matrix products, arithmetic and copies ran while one was open for 0% of the time, Pallas kernels for 0%

commit v1 on v0

v1 whole, which is shorter than its diff:
```python
import functools
import math

import jax
import jax.numpy as jnp
import numpy as np
from jax import lax
from jax.experimental import pallas as pl
from jax.experimental.pallas import tpu as pltpu
from jax.sharding import Mesh
from jax.sharding import PartitionSpec as P

HD = 256
NS_STEPS = 5
NZ, NY, NX, NC = 8, 4, 4, 2
AXES = ("z", "y", "x", "c")
PLANE = ("c", "y", "x")
COEF_A, COEF_B, COEF_C = 3.4445, -4.775, 2.0315
DECAY = 0.95
VMEM = 48 * 1024 * 1024
bf16, f32 = jnp.bfloat16, jnp.float32


SLOT_XOR = (0, 3, 1, 2)


def ring_place(coordinate, core):
    return (coordinate - core) % 4


def ring_coordinate(place, core):
    return (place + core) % 4


def pair_perm(axis, flip):
    pairs = []
    for z in range(NZ):
        for y in range(NY):
            for x in range(NX):
                for c in range(NC):
                    at = {"y": y, "x": x}
                    to = dict(at)
                    if axis == "c":
                        to_c = 1 - c
                    else:
                        to_c = c
                        to[axis] = ring_coordinate(ring_place(at[axis], c) ^ flip, c)
                    here = ((z * NY + y) * NX + x) * NC + c
                    there = ((z * NY + to["y"]) * NX + to["x"]) * NC + to_c
                    pairs.append((here, there))
    return pairs


def send(value, axis, flip=0):
    return lax.ppermute(value, AXES, pair_perm(axis, flip))


def partial_kernel(heads_x, heads_y, place, lat, mom, gx0, gx1, gy0, gy1, out_x, out_y, acc):
    half = acc.shape[0]
    row = place[1]
    for part, (g0, g1, out) in enumerate(((gx0, gx1, out_x), (gy0, gy1, out_y))):
        rows = slice(part * half, (part + 1) * half)
        p0 = jnp.dot(lat[0, rows, :], g0[...], preferred_element_type=f32)
        p1 = jnp.dot(lat[1, rows, :], g1[...], preferred_element_type=f32)
        acc[...] = p0.astype(bf16).astype(f32) + p1.astype(bf16).astype(f32)
        heads = heads_x if part == 0 else heads_y
        column = pl.multiple_of(heads[pl.program_id(0)] * HD, HD)

        @pl.when(row // half == part)
        def _():
            at = pl.ds(pl.multiple_of(row - part * half, 32), 32)
            acc[at, :] += (DECAY / NZ) * mom[:, pl.ds(column, HD)]

        out[0] = acc[...].astype(out.dtype)


def partial_tiles(heads_x, heads_y, place, lat, mom, grad_own, grad_other, dtype):
    tiles = heads_x.shape[0]
    tokens, features = lat.shape[2], lat.shape[1]
    half = features // 2

    def own(which):
        return lambda t, hx, hy, p: (0, p[0] * 16 + (hx if which == 0 else hy)[t])

    def other(which):
        return lambda t, hx, hy, p: (0, (hx if which == 0 else hy)[t])

    whole = lambda rank: lambda t, hx, hy, p: (0,) * rank
    block = pl.BlockSpec((1, half, HD), lambda t, hx, hy, p: (t, 0, 0))
    return pl.pallas_call(
        partial_kernel,
        out_shape=[jax.ShapeDtypeStruct((tiles, half, HD), dtype)] * 2,
        grid_spec=pltpu.PrefetchScalarGridSpec(
            num_scalar_prefetch=3,
            grid=(tiles,),
            in_specs=[
                pl.BlockSpec(lat.shape, whole(3)),
                pl.BlockSpec(mom.shape, whole(2)),
                pl.BlockSpec((tokens, HD), own(0)),
                pl.BlockSpec((tokens, HD), other(0)),
                pl.BlockSpec((tokens, HD), own(1)),
                pl.BlockSpec((tokens, HD), other(1)),
            ],
            out_specs=[block, block],
            scratch_shapes=[pltpu.VMEM((half, HD), f32)],
        ),
        compiler_params=pltpu.CompilerParams(vmem_limit_bytes=VMEM),
        cost_estimate=pl.CostEstimate(
            flops=2 * tiles * 2 * half * HD * 2 * tokens,
            bytes_accessed=tiles * 2 * (2 * tokens * HD * 2 + half * HD * 4),
            transcendentals=0,
        ),
    )(heads_x, heads_y, place, lat, mom, grad_own, grad_other, grad_own, grad_other)


def split(value):
    high = value.astype(bf16)
    return high, (value - high.astype(f32)).astype(bf16)


def product(a, b, dims):
    dot = functools.partial(
        lax.dot_general, dimension_numbers=(dims, ((), ())), preferred_element_type=f32
    )
    return dot(a[0], b[0]) + (dot(a[0], b[1]) + dot(a[1], b[0]))


def newton_schulz_kernel(moment_ref, out_ref):
    moment = moment_ref[...]
    rows, columns = moment.shape
    scale = 0.2 * math.sqrt(max(rows, columns))
    wide = moment.astype(f32).T
    norm = jnp.sqrt(jnp.sum(wide * wide))
    x = wide / (norm + 1e-7)
    for _ in range(NS_STEPS):
        pair = split(x)
        gram = product(pair, pair, ((1,), (1,)))
        gram_pair = split(gram)
        poly = COEF_B * gram + COEF_C * product(gram_pair, gram_pair, ((1,), (0,)))
        x = COEF_A * x + product(split(poly), pair, ((1,), (0,)))
    update = (scale * x).T.astype(bf16)
    moment = moment.astype(bf16)
    owners = out_ref.shape[0]
    depth = rows // owners
    for c in range(NC):
        for chip in range(owners // NC):
            at = slice((chip * NC + c) * depth, (chip * NC + c + 1) * depth)
            out_ref[c * (owners // NC) + chip, 0] = update[at, :]
            out_ref[c * (owners // NC) + chip, 1] = moment[at, :]


def newton_schulz(moment, owners):
    rows, columns = moment.shape
    return pl.pallas_call(
        newton_schulz_kernel,
        out_shape=jax.ShapeDtypeStruct((owners, 2, rows // owners, columns), bf16),
        compiler_params=pltpu.CompilerParams(vmem_limit_bytes=VMEM),
    )(moment)


def spread_kernel(returned, moment, update):
    for head in range(returned.shape[0]):
        at = slice(head * HD, (head + 1) * HD)
        update[:, at] = returned[head, 0]
        moment[:, at] = returned[head, 1].astype(f32)


def spread(returned):
    heads, _, rows, columns = returned.shape
    return pl.pallas_call(
        spread_kernel,
        out_shape=(
            jax.ShapeDtypeStruct((rows, heads * columns), f32),
            jax.ShapeDtypeStruct((rows, heads * columns), bf16),
        ),
        compiler_params=pltpu.CompilerParams(vmem_limit_bytes=VMEM),
    )(returned)


def body(latent, latent_grad, row_counts, momentum):
    z, y, x, c = (lax.axis_index(a) for a in AXES)
    slots, features = latent.shape
    columns = latent_grad.shape[1] // NC

    grad_other = send(lax.dynamic_slice_in_dim(latent_grad, (1 - c) * columns, columns, 1), "c")
    live = lax.broadcasted_iota(jnp.int32, (slots, 1), 0) < row_counts[0]
    masked = jnp.where(live, latent, jnp.zeros_like(latent)).T
    masked_other = send(masked, "c")
    lat = jnp.stack([masked, masked_other])
    mom_own = lax.dynamic_slice_in_dim(momentum, c * columns, columns, 1)
    mom_other = send(lax.dynamic_slice_in_dim(momentum, (1 - c) * columns, columns, 1), "c")
    mom = jnp.where(
        c == 0,
        jnp.concatenate([mom_own, mom_other], 0),
        jnp.concatenate([mom_other, mom_own], 0),
    )

    flips = jnp.array(SLOT_XOR, jnp.int32)
    x_at = ring_coordinate(ring_place(x, c) ^ flips, c)
    y_at = ring_coordinate(ring_place(y, c) ^ flips, c)
    heads_x = (x_at[:, None] + 4 * y_at[None, :]).reshape(-1).astype(jnp.int32)
    heads_y = (4 * y_at[:, None] + x_at[None, :]).reshape(-1).astype(jnp.int32)
    place = jnp.stack([c, (4 * y + x) * 32]).astype(jnp.int32)

    tiles = functools.partial(
        partial_tiles, place=place, lat=lat, mom=mom, grad_own=latent_grad, grad_other=grad_other
    )
    going = tiles(heads_x[8:], heads_y[8:], dtype=bf16)
    kept = tiles(heads_x[:8], heads_y[:8], dtype=f32)

    parts = []
    for first, second, out, keep in (("x", "y", going[0], kept[0]), ("y", "x", going[1], kept[1])):
        for axis in (first, second):
            width = keep.shape[0] // 2
            got = send(out, axis, 1)
            out = (keep[width:] + got[width:].astype(f32)).astype(bf16)
            keep = keep[:width] + got[:width].astype(f32)
            keep = keep + send(out, axis, 3).astype(f32)
            if axis == first:
                out = keep[2:].astype(bf16)
                keep = keep[:2]
        parts.append(keep[0])
    head = jnp.concatenate(parts, 0)

    pieces = head.astype(bf16).reshape(NZ, -1, HD)
    pieces = lax.all_to_all(pieces, "z", 0, 0, tiled=True)
    piece = jnp.sum(pieces.astype(f32), axis=0).astype(bf16)
    moment = lax.all_to_all(jnp.broadcast_to(piece, (NZ,) + piece.shape), "z", 0, 0, tiled=True)
    moment = moment.reshape(features, HD)

    outgoing = newton_schulz(moment, NC * NY * NX)
    returned = lax.all_to_all(outgoing, PLANE, 0, 0, tiled=True)
    return tuple(spread(returned))


def solution(mesh):
    fine = Mesh(mesh.devices.reshape(NZ, NY, NX, NC), AXES)
    shard = ("y", "x", "c")
    in_specs = (P(AXES, None), P(AXES, None), P(AXES), P(shard, None))
    out_specs = (P(shard, None), P(shard, None))
    return jax.shard_map(body, mesh=fine, in_specs=in_specs, out_specs=out_specs, check_vma=False)
```

time: 291 us -> 118 us (0.41)
  waiting for transfers between devices: 197 us -> 20.7 us
  Pallas kernels: 0 us -> 23.2 us
  matrix products: 18.2 us -> 0 us
  blocking collectives: 36 us -> 52.6 us
  other arithmetic: 19 us -> 3.05 us
  between operations: 15.6 us -> 1.48 us
  starting transfers between devices: 0.08 us -> 11.6 us
    reduce_scatter x1 -> x0, waiting for transfers between devices: 126 us -> none  [body(): lax.psum_scatter(product.astype(jnp.float32), 'shard', scatter_dimension=...]
    psum x1 -> x0, waiting for transfers between devices: 71.8 us -> none  [body(): gradient = lax.psum(shard_sum, 'dp')]
    pallas_call x0 -> x4, Pallas kernels: none -> 23.2 us  [the longest x2 15.8 us: partial_tiles(): pl.pallas_call(partial_kernel, out_shape=[jax.ShapeDtypeStruct((tiles, ha...]
    ppermute x0 -> x11, waiting for transfers between devices: none -> 20.7 us  [send(): return lax.ppermute(value, AXES, pair_perm(axis, flip))]
    dot_general x16 -> x0, matrix products: 18.2 us -> none  [the longest x1 7.97 us: body(): lax.dot_general(masked, latent_grad, (((0,), (0,)), ((), ())), preferred_...]
    all_to_all x2 -> x3, blocking collectives: 36 us -> 52.6 us  [the longest x1 23.3 us: body(): returned = lax.all_to_all(outgoing, PLANE, 0, 0, tiled=True)]
    ppermute x0 -> x11, starting transfers between devices: none -> 11.6 us  [send(): return lax.ppermute(value, AXES, pair_perm(axis, flip))]
    convert_element_type x1 -> x4, other arithmetic: 11.3 us -> 0.3 us  [body(): out = (keep[width:] + got[width:].astype(f32)).astype(bf16)]
  transfers between devices with their start and end apart: 2 -> 11, of which waited for: 2 -> 8; matrix products, arithmetic and copies ran while one was open for 0% -> 4% of each run, Pallas kernels for 0% -> 6%
where the time goes in v1:
time: 118 us; the launch traced here: 117 us
  blocking collectives  52.6 us (45%)
  Pallas kernels  23.2 us (20%)
  waiting for transfers between devices  20.7 us (18%)
  starting transfers between devices  11.6 us (10%)
  local copies, waits for them, and re-layouts  4.82 us (4%)
  other arithmetic  3.05 us (3%)
  between operations  1.48 us (1%)
    all_to_all x1, blocking collectives, body(): returned = lax.all_to_all(outgoing, PLANE, 0, 0, tiled=True)  23.3 us
    ppermute x11, waiting for transfers between devices, send(): return lax.ppermute(value, AXES, pair_perm(axis, flip))  20.7 us
    all_to_all x1, blocking collectives, body(): pieces = lax.all_to_all(pieces, 'z', 0, 0, tiled=True)  17.6 us
    pallas_call x2, Pallas kernels, partial_tiles(): pl.pallas_call(partial_kernel, out_shape=[jax.ShapeDtypeStruct((tiles, ha...  15.8 us
    all_to_all x1, blocking collectives, body(): lax.all_to_all(jnp.broadcast_to(piece, (NZ,) + piece.shape), 'z', 0, 0, t...  11.7 us
    ppermute x11, starting transfers between devices, send(): return lax.ppermute(value, AXES, pair_perm(axis, flip))  11.6 us
    pallas_call x1, Pallas kernels, newton_schulz(): pl.pallas_call(newton_schulz_kernel, out_shape=jax.ShapeDtypeStruct((owne...  6.52 us
    dynamic_slice x1, local copies, waits for them, and re-layouts, body(): lax.dynamic_slice_in_dim(latent_grad, (1 - c) * columns, columns, 1)  3.2 us
  transfers between devices with their start and end apart: 11, of which 8 were waited for; matrix products, arithmetic and copies ran while one was open for 4% of the time, Pallas kernels for 6%

profile of v1, /device:TPU:1, one launch (start us, length us, event | category | flops | bytes accessed | tf_op | source)
XLA Modules:
  0.0 117.5 jit_solution(16286025670158708140)
XLA Ops:
  0.6 0.0 copy-start.1
  0.6 3.2 %constant_dynamic-slice_fusion = bf16[256,4096]{1,0:T(8,128)(2,1)} fusion(bf16[256,8192]{1,0:T(8,128)(2,1)} %gy0.3, s32[]{:T(128)S(6)} %select_n.47), kind=kLoop, calls=%fused_computation.33 | loop fusion | bytes 4194308 | tf_op jit(solution)/shard_map/dynamic_slice | solution.py:185
  3.8 3.2 %collective-permute-start.2 = (bf16[256,4096]{1,0:T(8,128)(2,1)}, bf16[256,4096]{1,0:T(8,128)(2,1)S(1)}, u32[]{:S(2)}, u32[]{:S(2)}) collective-permute-start(bf16[256,4096]{1,0:T(8,128)(2,1)} %constant_dynamic-slice_fusion), channel_id=1, source_target_pairs={{0,1},{1,0},{2,3},{3,2},{4,5},{5,4},{6,7},{7,6},{8,9},{9,8},{10,11... | collective-permute-start | bytes 6291464 | tf_op jit(solution)/shard_map/ppermute | solution.py:55
  7.8 0.1 copy.7
  7.9 0.1 collective-permute-start
  8.1 1.1 constant_dynamic-slice_fusion.2
  9.1 0.6 collective-permute-start.1
  9.7 0.0 copy-done.2
  9.7 0.1 broadcast_add_fusion
  9.8 0.1 slice.94.heads_y
  9.9 0.1 slice.92.heads_x
  10.0 0.1 pad_add_fusion.place
  10.0 1.3 %collective-permute-done = bf16[512,256]{1,0:T(8,128)(2,1)} collective-permute-done((bf16[512,256]{1,0:T(8,128)(2,1)S(1)}, bf16[512,256]{1,0:T(8,128)(2,1)}, u32[]{:S(2)}, u32[]{:S(2)}) %collective-permute-start) | collective-permute-done | bytes 262176 | tf_op jit(solution)/shard_map/ppermute | solution.py:55
  11.4 1.0 pad_maximum_fusion.lat
  12.4 0.0 collective-permute-done.1
  12.4 1.1 maximum_select_fusion.mom
  13.5 0.0 collective-permute-done.2.gx1.gy1
  13.5 8.2 %shard_map.69 = (bf16[8,256,256]{2,1,0:T(8,128)(2,1)}, bf16[8,256,256]{2,1,0:T(8,128)(2,1)}) custom-call(s32[8]{0:T(128)S(1)} %slice.92.heads_x, s32[8]{0:T(128)S(1)} %slice.94.heads_y, s32[2]{0:T(128)S(1)} %pad_add_fusion.place, bf16[2,512,256]{2,1,0:T(8,128)(2,1)S(1)} %pad_maximum_fusion.lat, f32[32,4096]{1,0:T(8,128)S(1)} %maximum_select_fusion.mom, ...), custom_call_target="tpu_custom_call" | custom-call | flops 1073741824 | bytes 8388608 | tf_op jit(solution)/shard_map/pallas_call | solution.py:90
  21.7 0.7 collective-permute-start.3
  22.5 2.8 %collective-permute-start.7 = (bf16[8,256,256]{2,1,0:T(8,128)(2,1)}, bf16[8,256,256]{2,1,0:T(8,128)(2,1)S(1)}, u32[]{:S(2)}, u32[]{:S(2)}) collective-permute-start(bf16[8,256,256]{2,1,0:T(8,128)(2,1)} %get-tuple-element.9), channel_id=1, source_target_pairs={{0,8},{1,25},{2,10},{3,27},{4,12},{5,29},{6,14},{7,31},{8,0},{9,17... | collective-permute-start | bytes 3145736 | tf_op jit(solution)/shard_map/ppermute | solution.py:55
  25.2 0.1 slice.89.heads_y
  25.3 0.1 slice.87.heads_x
  25.4 7.6 %shard_map.68 = (f32[8,256,256]{2,1,0:T(8,128)S(1)}, f32[8,256,256]{2,1,0:T(8,128)S(1)}) custom-call(s32[8]{0:T(128)S(1)} %slice.87.heads_x, s32[8]{0:T(128)S(1)} %slice.89.heads_y, s32[2]{0:T(128)S(1)} %pad_add_fusion.place, bf16[2,512,256]{2,1,0:T(8,128)(2,1)S(1)} %pad_maximum_fusion.lat, f32[32,4096]{1,0:T(8,128)S(1)} %maximum_select_fusion.mom, ...), custom_call_target="tpu_custom_call" | custom-call | flops 1073741824 | bytes 8388608 | tf_op jit(solution)/shard_map/pallas_call | solution.py:90
  33.0 3.8 %collective-permute-done.3 = bf16[8,256,256]{2,1,0:T(8,128)(2,1)S(1)} collective-permute-done((bf16[8,256,256]{2,1,0:T(8,128)(2,1)}, bf16[8,256,256]{2,1,0:T(8,128)(2,1)S(1)}, u32[]{:S(2)}, u32[]{:S(2)}) %collective-permute-start.3) | collective-permute-done | bytes 1048608 | tf_op jit(solution)/shard_map/ppermute | solution.py:55
  36.8 0.1 add_convert_fusion.1
  36.9 0.1 collective-permute-start.4
  37.0 0.6 collective-permute-done.7
  37.6 0.1 add_convert_fusion
  37.7 0.2 collective-permute-start.8
  38.0 7.4 %collective-permute-done.4 = bf16[4,256,256]{2,1,0:T(8,128)(2,1)S(1)} collective-permute-done((bf16[4,256,256]{2,1,0:T(8,128)(2,1)S(1)}, bf16[4,256,256]{2,1,0:T(8,128)(2,1)S(1)}, u32[]{:S(2)}, u32[]{:S(2)}) %collective-permute-start.4) | collective-permute-done | bytes 524320 | tf_op jit(solution)/shard_map/ppermute | solution.py:55
  45.3 0.1 convert_add_fusion.1
  45.5 1.1 collective-permute-start.5
  46.6 0.0 collective-permute-done.8
  46.6 0.1 convert_add_fusion
  46.8 2.6 %collective-permute-start.9 = (bf16[2,256,256]{2,1,0:T(8,128)(2,1)S(1)}, bf16[2,256,256]{2,1,0:T(8,128)(2,1)S(1)}, u32[]{:S(2)}, u32[]{:S(2)}) collective-permute-start(bf16[2,256,256]{2,1,0:T(8,128)(2,1)S(1)} %slice.160), channel_id=1, source_target_pairs={{0,2},{1,7},{2,0},{3,5},{4,6},{5,3},{6,4},{7,1},{8,10},{9,15},{10,... | collective-permute-start | bytes 786440 | tf_op jit(solution)/shard_map/ppermute | solution.py:55
  49.4 2.7 %collective-permute-done.5 = bf16[2,256,256]{2,1,0:T(8,128)(2,1)S(1)} collective-permute-done((bf16[2,256,256]{2,1,0:T(8,128)(2,1)S(1)}, bf16[2,256,256]{2,1,0:T(8,128)(2,1)S(1)}, u32[]{:S(2)}, u32[]{:S(2)}) %collective-permute-start.5) | collective-permute-done | bytes 262176 | tf_op jit(solution)/shard_map/ppermute | solution.py:55
  52.1 0.1 collective-permute-start.6
  52.2 1.1 collective-permute-done.9
  53.3 0.1 collective-permute-start.10
  53.4 2.5 %collective-permute-done.6 = bf16[1,256,256]{2,1,0:T(8,128)(2,1)S(1)} collective-permute-done((bf16[1,256,256]{2,1,0:T(8,128)(2,1)S(1)}, bf16[1,256,256]{2,1,0:T(8,128)(2,1)S(1)}, u32[]{:S(2)}, u32[]{:S(2)}) %collective-permute-start.6) | collective-permute-done | bytes 131104 | tf_op jit(solution)/shard_map/ppermute | solution.py:55
  56.0 0.1 fusion.8
  56.0 1.2 %collective-permute-done.10 = bf16[1,256,256]{2,1,0:T(8,128)(2,1)S(1)} collective-permute-done((bf16[1,256,256]{2,1,0:T(8,128)(2,1)S(1)}, bf16[1,256,256]{2,1,0:T(8,128)(2,1)S(1)}, u32[]{:S(2)}, u32[]{:S(2)}) %collective-permute-start.10) | collective-permute-done | bytes 131104 | tf_op jit(solution)/shard_map/ppermute | solution.py:55
  57.3 0.1 fusion.9
  57.3 17.6 %all_to_all.15 = bf16[8,64,256]{2,1,0:T(8,128)(2,1)S(1)} all-to-all(bf16[8,64,256]{2,1,0:T(8,128)(2,1)S(1)} %bitcast.17), channel_id=1, replica_groups=mesh['z'=8,'y'=4,'x'=4,'c'=2] {'z'}, dimensions={0} | all-to-all | bytes 524288 | tf_op jit(solution)/shard_map/all_to_all | solution.py:226
  75.0 11.7 %all_to_all.16 = bf16[8,64,256]{2,1,0:T(8,128)(2,1)S(1)} all-to-all(bf16[8,64,256]{2,1,0:T(8,128)(2,1)S(1)} %broadcast_in_dim.20), channel_id=1, replica_groups=mesh['z'=8,'y'=4,'x'=4,'c'=2] {'z'}, dimensions={0} | all-to-all | bytes 524288 | tf_op jit(solution)/shard_map/all_to_all | solution.py:228
  86.8 6.5 %shard_map.70 = bf16[32,2,16,256]{3,2,1,0:T(8,128)(2,1)S(1)} custom-call(bf16[512,256]{1,0:T(8,128)(2,1)S(1)} %bitcast.16), custom_call_target="tpu_custom_call" | custom-call | tf_op jit(solution)/shard_map/pallas_call | solution.py:154
  93.3 23.3 %all_to_all.17.returned = bf16[32,2,16,256]{3,2,1,0:T(8,128)(2,1)S(1)} all-to-all(bf16[32,2,16,256]{3,2,1,0:T(8,128)(2,1)S(1)} %shard_map.70), channel_id=1, replica_groups=mesh['z'=8,'y'=4,'x'=4,'c'=2] {'c','y','x'}, dimensions={0} | all-to-all | bytes 1048576 | tf_op jit(solution)/shard_map/all_to_all | solution.py:232
  116.5 0.9 shard_map.71
  (15 shorter events, 0.3 us)
Async XLA Ops:
  0.6 7.1 %copy-start.1 = (bf16[256,512]{1,0:T(8,128)(2,1)S(1)}, bf16[256,512]{1,0:T(8,128)(2,1)}, u32[]{:S(2)}) copy-start(bf16[256,512]{1,0:T(8,128)(2,1)} %param.5) | copy-start | bytes 786436
  3.8 5.9 %copy-start.2 = (s32[4]{0:T(128)S(1)}, s32[4]{0:T(128)}, u32[]{:S(2)}) copy-start(s32[4]{0:T(128)} %constant.58.clone) | copy-start | bytes 52
  3.8 9.7 %collective-permute-start.2 = (bf16[256,4096]{1,0:T(8,128)(2,1)}, bf16[256,4096]{1,0:T(8,128)(2,1)S(1)}, u32[]{:S(2)}, u32[]{:S(2)}) collective-permute-start(bf16[256,4096]{1,0:T(8,128)(2,1)} %constant_dynamic-slice_fusion), channel_id=1, source_target_pairs={{0,1},{1,0},{2,3},{3,2},{4,5},{5,4},{6,7},{7,6},{8,9},{9,8},{10,11... | collective-permute-start | bytes 6291464 | tf_op jit(solution)/shard_map/ppermute | solution.py:55
  7.9 3.4 %collective-permute-start = (bf16[512,256]{1,0:T(8,128)(2,1)S(1)}, bf16[512,256]{1,0:T(8,128)(2,1)}, u32[]{:S(2)}, u32[]{:S(2)}) collective-permute-start(bf16[512,256]{1,0:T(8,128)(2,1)S(1)} %get-tuple-element.13), channel_id=1, source_target_pairs={{0,1},{1,0},{2,3},{3,2},{4,5},{5,4},{6,7},{7,6},{8,9},{9,8},{10,11... | collective-permute-start | bytes 786440 | tf_op jit(solution)/shard_map/ppermute | solution.py:55
  9.1 3.3 %collective-permute-start.1 = (f32[16,4096]{1,0:T(8,128)S(1)}, f32[16,4096]{1,0:T(8,128)}, u32[]{:S(2)}, u32[]{:S(2)}) collective-permute-start(f32[16,4096]{1,0:T(8,128)S(1)} %get-tuple-element.11), channel_id=1, source_target_pairs={{0,1},{1,0},{2,3},{3,2},{4,5},{5,4},{6,7},{7,6},{8,9},{9,8},{10,11... | collective-permute-start | bytes 786440 | tf_op jit(solution)/shard_map/ppermute | solution.py:55
  13.5 8.2 %copy-start = (bf16[256,4096]{1,0:T(8,128)(2,1)}, bf16[256,4096]{1,0:T(8,128)(2,1)S(1)}, u32[]{:S(2)}) copy-start(bf16[256,4096]{1,0:T(8,128)(2,1)S(1)} %collective-permute-done.2.gx1.gy1) | copy-start | bytes 6291460
  21.7 15.1 %collective-permute-start.3 = (bf16[8,256,256]{2,1,0:T(8,128)(2,1)}, bf16[8,256,256]{2,1,0:T(8,128)(2,1)S(1)}, u32[]{:S(2)}, u32[]{:S(2)}) collective-permute-start(bf16[8,256,256]{2,1,0:T(8,128)(2,1)} %get-tuple-element.7), channel_id=1, source_target_pairs={{0,2},{1,7},{2,0},{3,5},{4,6},{5,3},{6,4},{7,1},{8,10},{9,15},{10,... | collective-permute-start | bytes 3145736 | tf_op jit(solution)/shard_map/ppermute | solution.py:55
  22.5 15.2 %collective-permute-start.7 = (bf16[8,256,256]{2,1,0:T(8,128)(2,1)}, bf16[8,256,256]{2,1,0:T(8,128)(2,1)S(1)}, u32[]{:S(2)}, u32[]{:S(2)}) collective-permute-start(bf16[8,256,256]{2,1,0:T(8,128)(2,1)} %get-tuple-element.9), channel_id=1, source_target_pairs={{0,8},{1,25},{2,10},{3,27},{4,12},{5,29},{6,14},{7,31},{8,0},{9,17... | collective-permute-start | bytes 3145736 | tf_op jit(solution)/shard_map/ppermute | solution.py:55
  36.9 8.4 %collective-permute-start.4 = (bf16[4,256,256]{2,1,0:T(8,128)(2,1)S(1)}, bf16[4,256,256]{2,1,0:T(8,128)(2,1)S(1)}, u32[]{:S(2)}, u32[]{:S(2)}) collective-permute-start(bf16[4,256,256]{2,1,0:T(8,128)(2,1)S(1)} %add_convert_fusion.1), channel_id=1, source_target_pairs={{0,6},{1,3},{2,4},{3,1},{4,2},{5,7},{6,0},{7,5},{8,14},{9,11},{10,... | collective-permute-start | bytes 1572872 | tf_op jit(solution)/shard_map/ppermute | solution.py:55
  37.7 8.9 %collective-permute-start.8 = (bf16[4,256,256]{2,1,0:T(8,128)(2,1)S(1)}, bf16[4,256,256]{2,1,0:T(8,128)(2,1)S(1)}, u32[]{:S(2)}, u32[]{:S(2)}) collective-permute-start(bf16[4,256,256]{2,1,0:T(8,128)(2,1)S(1)} %add_convert_fusion), channel_id=1, source_target_pairs={{0,24},{1,9},{2,26},{3,11},{4,28},{5,13},{6,30},{7,15},{8,16},{9,1... | collective-permute-start | bytes 1572872 | tf_op jit(solution)/shard_map/ppermute | solution.py:55
  45.5 6.5 %collective-permute-start.5 = (bf16[2,256,256]{2,1,0:T(8,128)(2,1)S(1)}, bf16[2,256,256]{2,1,0:T(8,128)(2,1)S(1)}, u32[]{:S(2)}, u32[]{:S(2)}) collective-permute-start(bf16[2,256,256]{2,1,0:T(8,128)(2,1)S(1)} %slice.161), channel_id=1, source_target_pairs={{0,8},{1,25},{2,10},{3,27},{4,12},{5,29},{6,14},{7,31},{8,0},{9,17... | collective-permute-start | bytes 786440 | tf_op jit(solution)/shard_map/ppermute | solution.py:55
  46.8 6.5 %collective-permute-start.9 = (bf16[2,256,256]{2,1,0:T(8,128)(2,1)S(1)}, bf16[2,256,256]{2,1,0:T(8,128)(2,1)S(1)}, u32[]{:S(2)}, u32[]{:S(2)}) collective-permute-start(bf16[2,256,256]{2,1,0:T(8,128)(2,1)S(1)} %slice.160), channel_id=1, source_target_pairs={{0,2},{1,7},{2,0},{3,5},{4,6},{5,3},{6,4},{7,1},{8,10},{9,15},{10,... | collective-permute-start | bytes 786440 | tf_op jit(solution)/shard_map/ppermute | solution.py:55
  52.1 3.9 %collective-permute-start.6 = (bf16[1,256,256]{2,1,0:T(8,128)(2,1)S(1)}, bf16[1,256,256]{2,1,0:T(8,128)(2,1)S(1)}, u32[]{:S(2)}, u32[]{:S(2)}) collective-permute-start(bf16[1,256,256]{2,1,0:T(8,128)(2,1)S(1)} %fusion.3), channel_id=1, source_target_pairs={{0,24},{1,9},{2,26},{3,11},{4,28},{5,13},{6,30},{7,15},{8,16},{9,1... | collective-permute-start | bytes 393224 | tf_op jit(solution)/shard_map/ppermute | solution.py:55
  53.3 3.9 %collective-permute-start.10 = (bf16[1,256,256]{2,1,0:T(8,128)(2,1)S(1)}, bf16[1,256,256]{2,1,0:T(8,128)(2,1)S(1)}, u32[]{:S(2)}, u32[]{:S(2)}) collective-permute-start(bf16[1,256,256]{2,1,0:T(8,128)(2,1)S(1)} %fusion), channel_id=1, source_target_pairs={{0,6},{1,3},{2,4},{3,1},{4,2},{5,7},{6,0},{7,5},{8,14},{9,11},{10,... | collective-permute-start | bytes 393224 | tf_op jit(solution)/shard_map/ppermute | solution.py:55

commit v2 on v1

--- a/solution.py
+++ b/solution.py
@@ -17,7 +17,7 @@
 PLANE = ("c", "y", "x")
 COEF_A, COEF_B, COEF_C = 3.4445, -4.775, 2.0315
 DECAY = 0.95
-VMEM = 48 * 1024 * 1024
+VMEM = 16 * 1024 * 1024
 bf16, f32 = jnp.bfloat16, jnp.float32
 
 
@@ -55,62 +55,102 @@
     return lax.ppermute(value, AXES, pair_perm(axis, flip))
 
 
-def partial_kernel(heads_x, heads_y, place, lat, mom, gx0, gx1, gy0, gy1, out_x, out_y, acc):
+def column_copy_kernel(place, grad, out, sems):
+    width = out.shape[1] // sems.shape[0]
+    copies = []
+    for k in range(sems.shape[0]):
+        start = pl.multiple_of((1 - place[0]) * out.shape[1] + k * width, width)
+        copies.append(
+            pltpu.make_async_copy(
+                grad.at[:, pl.ds(start, width)], out.at[:, pl.ds(k * width, width)], sems.at[k]
+            )
+        )
+    for copy in copies:
+        copy.start()
+    for copy in copies:
+        copy.wait()
+
+
+def column_copy(place, grad):
+    rows, columns = grad.shape
+    return pl.pallas_call(
+        column_copy_kernel,
+        out_shape=jax.ShapeDtypeStruct((rows, columns // NC), grad.dtype),
+        in_specs=[pl.BlockSpec(memory_space=pltpu.SMEM), pl.BlockSpec(memory_space=pl.ANY)],
+        out_specs=pl.BlockSpec(memory_space=pl.ANY),
+        scratch_shapes=[pltpu.SemaphoreType.DMA((8,))],
+        compiler_params=pltpu.CompilerParams(vmem_limit_bytes=VMEM),
+    )(place, grad)
+
+
+def partial_kernel(
+    heads, place, lat_own, lat_other, mom_own, mom_other, grad_own, grad_other, out_x, out_y, acc, held, sems
+):
     half = acc.shape[0]
-    row = place[1]
-    for part, (g0, g1, out) in enumerate(((gx0, gx1, out_x), (gy0, gy1, out_y))):
+    tiles = out_x.shape[0]
+    core, row = place[0], place[1]
+
+    def copies(part, tile):
+        head = heads[part * tiles + tile]
+        own = pl.multiple_of((core * 16 + head) * HD, HD)
+        other = pl.multiple_of(head * HD, HD)
+        at = part * tiles + tile
+        return (
+            pltpu.make_async_copy(grad_own.at[:, pl.ds(own, HD)], held.at[at, 0], sems.at[at, 0]),
+            pltpu.make_async_copy(grad_other.at[:, pl.ds(other, HD)], held.at[at, 1], sems.at[at, 1]),
+        )
+
+    order = [(part, tile) for tile in range(tiles) for part in range(2)]
+    for part, tile in order:
+        for copy in copies(part, tile):
+            copy.start()
+    for part, tile in order:
+        for copy in copies(part, tile):
+            copy.wait()
+        at = part * tiles + tile
         rows = slice(part * half, (part + 1) * half)
-        p0 = jnp.dot(lat[0, rows, :], g0[...], preferred_element_type=f32)
-        p1 = jnp.dot(lat[1, rows, :], g1[...], preferred_element_type=f32)
+        p0 = jnp.dot(lat_own[rows, :], held[at, 0], preferred_element_type=f32)
+        p1 = jnp.dot(lat_other[rows, :], held[at, 1], preferred_element_type=f32)
         acc[...] = p0.astype(bf16).astype(f32) + p1.astype(bf16).astype(f32)
-        heads = heads_x if part == 0 else heads_y
-        column = pl.multiple_of(heads[pl.program_id(0)] * HD, HD)
 
         @pl.when(row // half == part)
         def _():
-            at = pl.ds(pl.multiple_of(row - part * half, 32), 32)
-            acc[at, :] += (DECAY / NZ) * mom[:, pl.ds(column, HD)]
-
-        out[0] = acc[...].astype(out.dtype)
-
-
-def partial_tiles(heads_x, heads_y, place, lat, mom, grad_own, grad_other, dtype):
-    tiles = heads_x.shape[0]
-    tokens, features = lat.shape[2], lat.shape[1]
+            column = pl.multiple_of(heads[at] * HD, HD)
+            first = row - part * half
+            depth = mom_own.shape[0]
+            mine = pl.ds(pl.multiple_of(first + core * depth, depth), depth)
+            theirs = pl.ds(pl.multiple_of(first + (1 - core) * depth, depth), depth)
+            acc[mine, :] += (DECAY / NZ) * mom_own[:, pl.ds(column, HD)]
+            acc[theirs, :] += (DECAY / NZ) * mom_other[:, pl.ds(column, HD)]
+
+        out = out_x if part == 0 else out_y
+        out[tile] = acc[...].astype(out.dtype)
+
+
+def partial_tiles(heads, place, lat_own, lat_other, mom_own, mom_other, grad_own, grad_other, dtype):
+    tiles = heads.shape[0] // 2
+    features, tokens = lat_own.shape
     half = features // 2
-
-    def own(which):
-        return lambda t, hx, hy, p: (0, p[0] * 16 + (hx if which == 0 else hy)[t])
-
-    def other(which):
-        return lambda t, hx, hy, p: (0, (hx if which == 0 else hy)[t])
-
-    whole = lambda rank: lambda t, hx, hy, p: (0,) * rank
-    block = pl.BlockSpec((1, half, HD), lambda t, hx, hy, p: (t, 0, 0))
+    smem = pl.BlockSpec(memory_space=pltpu.SMEM)
+    vmem = pl.BlockSpec(memory_space=pltpu.VMEM)
+    hbm = pl.BlockSpec(memory_space=pl.ANY)
     return pl.pallas_call(
         partial_kernel,
         out_shape=[jax.ShapeDtypeStruct((tiles, half, HD), dtype)] * 2,
-        grid_spec=pltpu.PrefetchScalarGridSpec(
-            num_scalar_prefetch=3,
-            grid=(tiles,),
-            in_specs=[
-                pl.BlockSpec(lat.shape, whole(3)),
-                pl.BlockSpec(mom.shape, whole(2)),
-                pl.BlockSpec((tokens, HD), own(0)),
-                pl.BlockSpec((tokens, HD), other(0)),
-                pl.BlockSpec((tokens, HD), own(1)),
-                pl.BlockSpec((tokens, HD), other(1)),
-            ],
-            out_specs=[block, block],
-            scratch_shapes=[pltpu.VMEM((half, HD), f32)],
-        ),
+        in_specs=[smem, smem, vmem, vmem, vmem, vmem, hbm, hbm],
+        out_specs=[vmem, vmem],
+        scratch_shapes=[
+            pltpu.VMEM((half, HD), f32),
+            pltpu.VMEM((2 * tiles, 2, tokens, HD), bf16),
+            pltpu.SemaphoreType.DMA((2 * tiles, 2)),
+        ],
         compiler_params=pltpu.CompilerParams(vmem_limit_bytes=VMEM),
         cost_estimate=pl.CostEstimate(
             flops=2 * tiles * 2 * half * HD * 2 * tokens,
             bytes_accessed=tiles * 2 * (2 * tokens * HD * 2 + half * HD * 4),
             transcendentals=0,
         ),
-    )(heads_x, heads_y, place, lat, mom, grad_own, grad_other, grad_own, grad_other)
+    )(heads, place, lat_own, lat_other, mom_own, mom_other, grad_own, grad_other)
 
 
 def split(value):
@@ -181,45 +221,47 @@
     z, y, x, c = (lax.axis_index(a) for a in AXES)
     slots, features = latent.shape
     columns = latent_grad.shape[1] // NC
-
-    grad_other = send(lax.dynamic_slice_in_dim(latent_grad, (1 - c) * columns, columns, 1), "c")
+    place = jnp.stack([c, (4 * y + x) * 32]).astype(jnp.int32)
+
+    grad_other = send(column_copy(place, latent_grad), "c")
     live = lax.broadcasted_iota(jnp.int32, (slots, 1), 0) < row_counts[0]
-    masked = jnp.where(live, latent, jnp.zeros_like(latent)).T
-    masked_other = send(masked, "c")
-    lat = jnp.stack([masked, masked_other])
+    lat_own = jnp.where(live, latent, jnp.zeros_like(latent)).T
+    lat_other = send(lat_own, "c")
     mom_own = lax.dynamic_slice_in_dim(momentum, c * columns, columns, 1)
     mom_other = send(lax.dynamic_slice_in_dim(momentum, (1 - c) * columns, columns, 1), "c")
-    mom = jnp.where(
-        c == 0,
-        jnp.concatenate([mom_own, mom_other], 0),
-        jnp.concatenate([mom_other, mom_own], 0),
-    )
 
     flips = jnp.array(SLOT_XOR, jnp.int32)
     x_at = ring_coordinate(ring_place(x, c) ^ flips, c)
     y_at = ring_coordinate(ring_place(y, c) ^ flips, c)
-    heads_x = (x_at[:, None] + 4 * y_at[None, :]).reshape(-1).astype(jnp.int32)
-    heads_y = (4 * y_at[:, None] + x_at[None, :]).reshape(-1).astype(jnp.int32)
-    place = jnp.stack([c, (4 * y + x) * 32]).astype(jnp.int32)
-
-    tiles = functools.partial(
-        partial_tiles, place=place, lat=lat, mom=mom, grad_own=latent_grad, grad_other=grad_other
-    )
-    going = tiles(heads_x[8:], heads_y[8:], dtype=bf16)
-    kept = tiles(heads_x[:8], heads_y[:8], dtype=f32)
+
+    def tiles(first, second, dtype):
+        heads = jnp.concatenate(
+            [
+                (x_at[first][:, None] + 4 * y_at[second][None, :]).reshape(-1),
+                (4 * y_at[first][:, None] + x_at[second][None, :]).reshape(-1),
+            ]
+        ).astype(jnp.int32)
+        return partial_tiles(
+            heads, place, lat_own, lat_other, mom_own, mom_other, latent_grad, grad_other, dtype
+        )
+
+    near, far = slice(0, 2), slice(2, 4)
+    far_going = tiles(far, far, bf16)
+    near_going = tiles(far, near, bf16)
+    far_kept = tiles(near, far, f32)
+    near_kept = tiles(near, near, f32)
+
+    def reduce_first(axis, going, kept):
+        got = send(going, axis, 1).astype(f32)
+        out = (kept[2:] + got[2:]).astype(bf16)
+        return kept[:2] + got[:2] + send(out, axis, 3).astype(f32)
 
     parts = []
-    for first, second, out, keep in (("x", "y", going[0], kept[0]), ("y", "x", going[1], kept[1])):
-        for axis in (first, second):
-            width = keep.shape[0] // 2
-            got = send(out, axis, 1)
-            out = (keep[width:] + got[width:].astype(f32)).astype(bf16)
-            keep = keep[:width] + got[:width].astype(f32)
-            keep = keep + send(out, axis, 3).astype(f32)
-            if axis == first:
-                out = keep[2:].astype(bf16)
-                keep = keep[:2]
-        parts.append(keep[0])
+    for part, (first, second) in enumerate((("x", "y"), ("y", "x"))):
+        out = reduce_first(first, far_going[part], far_kept[part]).astype(bf16)
+        keep = reduce_first(first, near_going[part], near_kept[part])
+        keep = keep + send(out, second, 1).astype(f32)
+        parts.append(keep[0] + send(keep[1].astype(bf16), second, 3).astype(f32))
     head = jnp.concatenate(parts, 0)
 
     pieces = head.astype(bf16).reshape(NZ, -1, HD)

time: 118 us -> 130 us (1.10)
  local copies, waits for them, and re-layouts: 4.82 us -> 12.2 us
  starting transfers between devices: 11.6 us -> 15.4 us
  waiting for transfers between devices: 20.7 us -> 18 us
  blocking collectives: 52.6 us -> 54.8 us
    unnamed x7 -> x17, local copies, waits for them, and re-layouts: 0.14 us -> 11.5 us
    dynamic_slice x2 -> x1, local copies, waits for them, and re-layouts: 4.27 us -> 0.03 us  [body(): lax.dynamic_slice_in_dim(momentum, (1 - c) * columns, columns, 1)]
    all_to_all x1, blocking collectives: 23.3 us -> 27.1 us  [body(): returned = lax.all_to_all(outgoing, PLANE, 0, 0, tiled=True)]
    ppermute x11 -> x15, starting transfers between devices: 11.6 us -> 15.4 us  [send(): return lax.ppermute(value, AXES, pair_perm(axis, flip))]
    ppermute x11 -> x15, waiting for transfers between devices: 20.7 us -> 18 us  [send(): return lax.ppermute(value, AXES, pair_perm(axis, flip))]
    convert_element_type x4 -> x10, other arithmetic: 0.3 us -> 2.91 us  [the longest x4 2.42 us: reduce_first(): got = send(going, axis, 1).astype(f32)]
    pallas_call x0 -> x1, Pallas kernels: none -> 1.97 us  [column_copy(): pl.pallas_call(column_copy_kernel, out_shape=jax.ShapeDtypeStruct((rows,...]
    pallas_call x2 -> x4, Pallas kernels: 15.8 us -> 13.8 us  [partial_tiles(): pl.pallas_call(partial_kernel, out_shape=[jax.ShapeDtypeStruct((tiles, ha...]
  transfers between devices with their start and end apart: 11 -> 15, of which waited for: 8 -> 7; matrix products, arithmetic and copies ran while one was open for 4% -> 4% of each run, Pallas kernels for 6% -> 8%
where the time goes in v2:
time: 130 us; the launch traced here: 129 us
  blocking collectives  54.8 us (42%)
  Pallas kernels  23.3 us (18%)
  waiting for transfers between devices  18 us (14%)
  starting transfers between devices  15.4 us (12%)
  local copies, waits for them, and re-layouts  12.2 us (9%)
  other arithmetic  3.84 us (3%)
  between operations  1.58 us (1%)
    all_to_all x1, blocking collectives, body(): returned = lax.all_to_all(outgoing, PLANE, 0, 0, tiled=True)  27.1 us
    ppermute x15, waiting for transfers between devices, send(): return lax.ppermute(value, AXES, pair_perm(axis, flip))  18 us
    all_to_all x1, blocking collectives, body(): pieces = lax.all_to_all(pieces, 'z', 0, 0, tiled=True)  15.9 us
    ppermute x15, starting transfers between devices, send(): return lax.ppermute(value, AXES, pair_perm(axis, flip))  15.4 us
    pallas_call x4, Pallas kernels, partial_tiles(): pl.pallas_call(partial_kernel, out_shape=[jax.ShapeDtypeStruct((tiles, ha...  13.8 us
    all_to_all x1, blocking collectives, body(): lax.all_to_all(jnp.broadcast_to(piece, (NZ,) + piece.shape), 'z', 0, 0, t...  11.7 us
    unnamed x17, local copies, waits for them, and re-layouts  11.5 us
    pallas_call x1, Pallas kernels, newton_schulz(): pl.pallas_call(newton_schulz_kernel, out_shape=jax.ShapeDtypeStruct((owne...  6.52 us
  transfers between devices with their start and end apart: 15, of which 7 were waited for; matrix products, arithmetic and copies ran while one was open for 4% of the time, Pallas kernels for 8%

profile of v2, /device:TPU:1, one launch (start us, length us, event | category | flops | bytes accessed | tf_op | source)
XLA Modules:
  0.0 129.1 jit_solution(14119935345212859800)
XLA Ops:
  0.7 2.2 %copy-done = bf16[256,8192]{1,0:T(8,128)(2,1)S(1)} copy-done((bf16[256,8192]{1,0:T(8,128)(2,1)S(1)}, bf16[256,8192]{1,0:T(8,128)(2,1)}, u32[]{:S(2)}) %copy-start) | copy-done | bytes 4194328
  2.9 2.0 %shard_map.68 = bf16[256,4096]{1,0:T(8,128)(2,1)} custom-call(s32[2]{0:T(128)S(1)} %pad_add_fusion.1.place, bf16[256,8192]{1,0:T(8,128)(2,1)S(1)} %copy-done), custom_call_target="tpu_custom_call" | custom-call | tf_op jit(solution)/shard_map/pallas_call | solution.py:76
  4.9 3.3 %collective-permute-start.2 = (bf16[256,4096]{1,0:T(8,128)(2,1)}, bf16[256,4096]{1,0:T(8,128)(2,1)S(1)}, u32[]{:S(2)}, u32[]{:S(2)}) collective-permute-start(bf16[256,4096]{1,0:T(8,128)(2,1)} %shard_map.68), channel_id=1, source_target_pairs={{0,1},{1,0},{2,3},{3,2},{4,5},{5,4},{6,7},{7,6},{8,9},{9,8},{10,11... | collective-permute-start | bytes 6291464 | tf_op jit(solution)/shard_map/ppermute | solution.py:55
  8.3 0.1 collective-permute-start.1
  8.4 1.1 copy.7
  10.2 0.6 collective-permute-start
  10.9 0.1 add.238
  11.1 1.1 collective-permute-done.1.mom_other
  12.2 0.5 collective-permute-done.lat_other
  12.8 2.2 %copy-done.1 = bf16[256,8192]{1,0:T(8,128)(2,1)S(1)} copy-done((bf16[256,8192]{1,0:T(8,128)(2,1)S(1)}, bf16[256,8192]{1,0:T(8,128)(2,1)}, u32[]{:S(2)}) %copy-start.1) | copy-done | bytes 4194328
  14.9 3.8 %shard_map.72 = (bf16[4,256,256]{2,1,0:T(8,128)(2,1)}, bf16[4,256,256]{2,1,0:T(8,128)(2,1)S(1)}) custom-call(s32[8]{0:T(128)S(1)} %pad_add_fusion.4.heads, s32[2]{0:T(128)S(1)} %pad_add_fusion.1.place, bf16[512,256]{1,0:T(8,128)(2,1)S(1)} %select_bitcast_fusion.lat_own, bf16[512,256]{1,0:T(8,128)(2,1)S(1)} %collective-permute-done.lat_other, ...), custom_call_target="tpu_custom_call" | custom-call | flops 536870912 | bytes 4194304 | tf_op jit(solution)/shard_map/pallas_call | solution.py:137
  18.8 0.8 copy-done.4
  19.6 0.7 collective-permute-start.5
  20.7 2.2 %copy-done.2 = bf16[256,8192]{1,0:T(8,128)(2,1)S(1)} copy-done((bf16[256,8192]{1,0:T(8,128)(2,1)S(1)}, bf16[256,8192]{1,0:T(8,128)(2,1)}, u32[]{:S(2)}) %copy-start.2) | copy-done | bytes 4194328
  22.9 3.8 %shard_map.70 = (bf16[4,256,256]{2,1,0:T(8,128)(2,1)}, bf16[4,256,256]{2,1,0:T(8,128)(2,1)S(1)}) custom-call(s32[8]{0:T(128)S(1)} %pad_add_fusion.2.heads, s32[2]{0:T(128)S(1)} %pad_add_fusion.1.place, bf16[512,256]{1,0:T(8,128)(2,1)S(1)} %select_bitcast_fusion.lat_own, bf16[512,256]{1,0:T(8,128)(2,1)S(1)} %collective-permute-done.lat_other, ...), custom_call_target="tpu_custom_call" | custom-call | flops 536870912 | bytes 4194304 | tf_op jit(solution)/shard_map/pallas_call | solution.py:137
  26.8 0.8 copy-done.5
  27.6 1.9 %collective-permute-start.3 = (bf16[4,256,256]{2,1,0:T(8,128)(2,1)}, bf16[4,256,256]{2,1,0:T(8,128)(2,1)}, u32[]{:S(2)}, u32[]{:S(2)}) collective-permute-start(bf16[4,256,256]{2,1,0:T(8,128)(2,1)} %get-tuple-element.11), channel_id=1, source_target_pairs={{0,2},{1,7},{2,0},{3,5},{4,6},{5,3},{6,4},{7,1},{8,10},{9,15},{10,... | collective-permute-start | bytes 1572872 | tf_op jit(solution)/shard_map/ppermute | solution.py:55
  29.8 1.0 collective-permute-start.9
  30.8 1.7 %collective-permute-start.11 = (bf16[4,256,256]{2,1,0:T(8,128)(2,1)}, bf16[4,256,256]{2,1,0:T(8,128)(2,1)S(1)}, u32[]{:S(2)}, u32[]{:S(2)}) collective-permute-start(bf16[4,256,256]{2,1,0:T(8,128)(2,1)} %copy-done.4), channel_id=1, source_target_pairs={{0,8},{1,25},{2,10},{3,27},{4,12},{5,29},{6,14},{7,31},{8,0},{9,17... | collective-permute-start | bytes 1572872 | tf_op jit(solution)/shard_map/ppermute | solution.py:55
  32.5 2.2 %copy-done.3 = bf16[256,8192]{1,0:T(8,128)(2,1)S(1)} copy-done((bf16[256,8192]{1,0:T(8,128)(2,1)S(1)}, bf16[256,8192]{1,0:T(8,128)(2,1)}, u32[]{:S(2)}) %copy-start.3) | copy-done | bytes 4194328
  34.7 3.1 %shard_map.71 = (f32[4,256,256]{2,1,0:T(8,128)S(1)}, f32[4,256,256]{2,1,0:T(8,128)S(1)}) custom-call(s32[8]{0:T(128)S(1)} %pad_add_fusion.3.heads, s32[2]{0:T(128)S(1)} %pad_add_fusion.1.place, bf16[512,256]{1,0:T(8,128)(2,1)S(1)} %select_bitcast_fusion.lat_own, bf16[512,256]{1,0:T(8,128)(2,1)S(1)} %collective-permute-done.lat_other, ...), custom_call_target="tpu_custom_call" | custom-call | flops 536870912 | bytes 4194304 | tf_op jit(solution)/shard_map/pallas_call | solution.py:137
  37.8 3.1 %shard_map.69 = (f32[4,256,256]{2,1,0:T(8,128)S(1)}, f32[4,256,256]{2,1,0:T(8,128)S(1)}) custom-call(s32[8]{0:T(128)S(1)} %pad_add_fusion.heads, s32[2]{0:T(128)S(1)} %pad_add_fusion.1.place, bf16[512,256]{1,0:T(8,128)(2,1)S(1)} %select_bitcast_fusion.lat_own, bf16[512,256]{1,0:T(8,128)(2,1)S(1)} %collective-permute-done.lat_other, ...), custom_call_target="tpu_custom_call" | custom-call | flops 536870912 | bytes 4194304 | tf_op jit(solution)/shard_map/pallas_call | solution.py:137
  40.9 1.1 convert_element_type.72
  42.1 0.1 collective-permute-start.6
  42.2 1.1 convert_element_type.69
  43.5 1.7 %collective-permute-start.4 = (bf16[2,256,256]{2,1,0:T(8,128)(2,1)S(1)}, bf16[2,256,256]{2,1,0:T(8,128)(2,1)S(1)}, u32[]{:S(2)}, u32[]{:S(2)}) collective-permute-start(bf16[2,256,256]{2,1,0:T(8,128)(2,1)S(1)} %fusion.9), channel_id=1, source_target_pairs={{0,6},{1,3},{2,4},{3,1},{4,2},{5,7},{6,0},{7,5},{8,14},{9,11},{10,... | collective-permute-start | bytes 786440 | tf_op jit(solution)/shard_map/ppermute | solution.py:55
  45.2 0.1 convert_element_type.79
  45.4 0.1 collective-permute-start.10
  45.5 0.1 convert_element_type.82
  45.6 1.5 %collective-permute-start.12 = (bf16[2,256,256]{2,1,0:T(8,128)(2,1)S(1)}, bf16[2,256,256]{2,1,0:T(8,128)(2,1)S(1)}, u32[]{:S(2)}, u32[]{:S(2)}) collective-permute-start(bf16[2,256,256]{2,1,0:T(8,128)(2,1)S(1)} %fusion), channel_id=1, source_target_pairs={{0,24},{1,9},{2,26},{3,11},{4,28},{5,13},{6,30},{7,15},{8,16},{9,1... | collective-permute-start | bytes 786440 | tf_op jit(solution)/shard_map/ppermute | solution.py:55
  47.2 0.6 collective-permute-done.6
  47.7 0.1 fusion.8
  47.8 1.0 collective-permute-start.7
  48.9 5.5 %collective-permute-done.12 = bf16[2,256,256]{2,1,0:T(8,128)(2,1)S(1)} collective-permute-done((bf16[2,256,256]{2,1,0:T(8,128)(2,1)S(1)}, bf16[2,256,256]{2,1,0:T(8,128)(2,1)S(1)}, u32[]{:S(2)}, u32[]{:S(2)}) %collective-permute-start.12) | collective-permute-done | bytes 262176 | tf_op jit(solution)/shard_map/ppermute | solution.py:55
  54.4 0.1 fusion.2
  54.5 1.1 collective-permute-start.13
  55.6 1.9 %collective-permute-done.7 = bf16[2,256,256]{2,1,0:T(8,128)(2,1)S(1)} collective-permute-done((bf16[2,256,256]{2,1,0:T(8,128)(2,1)S(1)}, bf16[2,256,256]{2,1,0:T(8,128)(2,1)S(1)}, u32[]{:S(2)}, u32[]{:S(2)}) %collective-permute-start.7) | collective-permute-done | bytes 262176 | tf_op jit(solution)/shard_map/ppermute | solution.py:55
  57.5 0.1 fusion.11
  57.6 0.1 collective-permute-start.8
  57.7 3.2 %collective-permute-done.13 = bf16[2,256,256]{2,1,0:T(8,128)(2,1)S(1)} collective-permute-done((bf16[2,256,256]{2,1,0:T(8,128)(2,1)S(1)}, bf16[2,256,256]{2,1,0:T(8,128)(2,1)S(1)}, u32[]{:S(2)}, u32[]{:S(2)}) %collective-permute-start.13) | collective-permute-done | bytes 262176 | tf_op jit(solution)/shard_map/ppermute | solution.py:55
  61.0 0.1 fusion.5
  61.1 0.4 collective-permute-start.14
  61.6 5.2 %collective-permute-done.14 = bf16[256,256]{1,0:T(8,128)(2,1)S(1)} collective-permute-done((bf16[256,256]{1,0:T(8,128)(2,1)S(1)}, bf16[256,256]{1,0:T(8,128)(2,1)S(1)}, u32[]{:S(2)}, u32[]{:S(2)}) %collective-permute-start.14) | collective-permute-done | bytes 131104 | tf_op jit(solution)/shard_map/ppermute | solution.py:55
  66.8 15.9 %all_to_all.15 = bf16[8,64,256]{2,1,0:T(8,128)(2,1)S(1)} all-to-all(bf16[8,64,256]{2,1,0:T(8,128)(2,1)S(1)} %bitcast.25), channel_id=1, replica_groups=mesh['z'=8,'y'=4,'x'=4,'c'=2] {'z'}, dimensions={0} | all-to-all | bytes 524288 | tf_op jit(solution)/shard_map/all_to_all | solution.py:268
  82.7 11.7 %all_to_all.16 = bf16[8,64,256]{2,1,0:T(8,128)(2,1)S(1)} all-to-all(bf16[8,64,256]{2,1,0:T(8,128)(2,1)S(1)} %broadcast_in_dim.14), channel_id=1, replica_groups=mesh['z'=8,'y'=4,'x'=4,'c'=2] {'z'}, dimensions={0} | all-to-all | bytes 524288 | tf_op jit(solution)/shard_map/all_to_all | solution.py:270
  94.5 6.5 %shard_map.73 = bf16[32,2,16,256]{3,2,1,0:T(8,128)(2,1)S(1)} custom-call(bf16[512,256]{1,0:T(8,128)(2,1)S(1)} %bitcast.24), custom_call_target="tpu_custom_call" | custom-call | tf_op jit(solution)/shard_map/pallas_call | solution.py:194
  101.0 27.1 %all_to_all.17.returned = bf16[32,2,16,256]{3,2,1,0:T(8,128)(2,1)S(1)} all-to-all(bf16[32,2,16,256]{3,2,1,0:T(8,128)(2,1)S(1)} %shard_map.73), channel_id=1, replica_groups=mesh['z'=8,'y'=4,'x'=4,'c'=2] {'c','y','x'}, dimensions={0} | all-to-all | bytes 1048576 | tf_op jit(solution)/shard_map/all_to_all | solution.py:274
  128.2 0.9 shard_map.74
  (47 shorter events, 1.7 us)
Async XLA Ops:
  0.7 2.2 %copy-start = (bf16[256,8192]{1,0:T(8,128)(2,1)S(1)}, bf16[256,8192]{1,0:T(8,128)(2,1)}, u32[]{:S(2)}) copy-start(bf16[256,8192]{1,0:T(8,128)(2,1)} %grad_own.7) | copy-start | bytes 12582916
  2.9 5.3 %copy-start.6 = (f32[16,8192]{1,0:T(8,128)S(1)}, f32[16,8192]{1,0:T(8,128)}, u32[]{:S(2)}) copy-start(f32[16,8192]{1,0:T(8,128)} %param.8) | copy-start | bytes 1572868
  4.9 5.9 %copy-start.7 = (s32[4]{0:T(128)S(1)}, s32[4]{0:T(128)}, u32[]{:S(2)}) copy-start(s32[4]{0:T(128)} %constant.58.clone) | copy-start | bytes 52
  4.9 7.9 %collective-permute-start.2 = (bf16[256,4096]{1,0:T(8,128)(2,1)}, bf16[256,4096]{1,0:T(8,128)(2,1)S(1)}, u32[]{:S(2)}, u32[]{:S(2)}) collective-permute-start(bf16[256,4096]{1,0:T(8,128)(2,1)} %shard_map.68), channel_id=1, source_target_pairs={{0,1},{1,0},{2,3},{3,2},{4,5},{5,4},{6,7},{7,6},{8,9},{9,8},{10,11... | collective-permute-start | bytes 6291464 | tf_op jit(solution)/shard_map/ppermute | solution.py:55
  8.3 4.0 %collective-permute-start.1 = (f32[16,4096]{1,0:T(8,128)S(1)}, f32[16,4096]{1,0:T(8,128)S(1)}, u32[]{:S(2)}, u32[]{:S(2)}) collective-permute-start(f32[16,4096]{1,0:T(8,128)S(1)} %get-tuple-element.18), channel_id=1, source_target_pairs={{0,1},{1,0},{2,3},{3,2},{4,5},{5,4},{6,7},{7,6},{8,9},{9,8},{10,11... | collective-permute-start | bytes 786440 | tf_op jit(solution)/shard_map/ppermute | solution.py:55
  10.2 2.6 %collective-permute-start = (bf16[512,256]{1,0:T(8,128)(2,1)S(1)}, bf16[512,256]{1,0:T(8,128)(2,1)S(1)}, u32[]{:S(2)}, u32[]{:S(2)}) collective-permute-start(bf16[512,256]{1,0:T(8,128)(2,1)S(1)} %select_bitcast_fusion.lat_own), channel_id=1, source_target_pairs={{0,1},{1,0},{2,3},{3,2},{4,5},{5,4},{6,7},{7,6},{8,9},{9,8},{10,11... | collective-permute-start | bytes 786440 | tf_op jit(solution)/shard_map/ppermute | solution.py:55
  12.8 2.2 %copy-start.1 = (bf16[256,8192]{1,0:T(8,128)(2,1)S(1)}, bf16[256,8192]{1,0:T(8,128)(2,1)}, u32[]{:S(2)}) copy-start(bf16[256,8192]{1,0:T(8,128)(2,1)} %grad_own.7) | copy-start | bytes 12582916
  18.8 0.8 copy-start.4
  19.6 21.3 %collective-permute-start.5 = (bf16[4,256,256]{2,1,0:T(8,128)(2,1)}, bf16[4,256,256]{2,1,0:T(8,128)(2,1)}, u32[]{:S(2)}, u32[]{:S(2)}) collective-permute-start(bf16[4,256,256]{2,1,0:T(8,128)(2,1)} %get-tuple-element.13), channel_id=1, source_target_pairs={{0,2},{1,7},{2,0},{3,5},{4,6},{5,3},{6,4},{7,1},{8,10},{9,15},{10,... | collective-permute-start | bytes 1572872 | tf_op jit(solution)/shard_map/ppermute | solution.py:55
  20.7 2.2 %copy-start.2 = (bf16[256,8192]{1,0:T(8,128)(2,1)S(1)}, bf16[256,8192]{1,0:T(8,128)(2,1)}, u32[]{:S(2)}) copy-start(bf16[256,8192]{1,0:T(8,128)(2,1)} %grad_own.7) | copy-start | bytes 12582916
  26.8 0.8 copy-start.5
  27.6 14.7 %collective-permute-start.3 = (bf16[4,256,256]{2,1,0:T(8,128)(2,1)}, bf16[4,256,256]{2,1,0:T(8,128)(2,1)}, u32[]{:S(2)}, u32[]{:S(2)}) collective-permute-start(bf16[4,256,256]{2,1,0:T(8,128)(2,1)} %get-tuple-element.11), channel_id=1, source_target_pairs={{0,2},{1,7},{2,0},{3,5},{4,6},{5,3},{6,4},{7,1},{8,10},{9,15},{10,... | collective-permute-start | bytes 1572872 | tf_op jit(solution)/shard_map/ppermute | solution.py:55
  29.8 15.3 %collective-permute-start.9 = (bf16[4,256,256]{2,1,0:T(8,128)(2,1)}, bf16[4,256,256]{2,1,0:T(8,128)(2,1)S(1)}, u32[]{:S(2)}, u32[]{:S(2)}) collective-permute-start(bf16[4,256,256]{2,1,0:T(8,128)(2,1)} %copy-done.5), channel_id=1, source_target_pairs={{0,8},{1,25},{2,10},{3,27},{4,12},{5,29},{6,14},{7,31},{8,0},{9,17... | collective-permute-start | bytes 1572872 | tf_op jit(solution)/shard_map/ppermute | solution.py:55
  30.8 14.6 %collective-permute-start.11 = (bf16[4,256,256]{2,1,0:T(8,128)(2,1)}, bf16[4,256,256]{2,1,0:T(8,128)(2,1)S(1)}, u32[]{:S(2)}, u32[]{:S(2)}) collective-permute-start(bf16[4,256,256]{2,1,0:T(8,128)(2,1)} %copy-done.4), channel_id=1, source_target_pairs={{0,8},{1,25},{2,10},{3,27},{4,12},{5,29},{6,14},{7,31},{8,0},{9,17... | collective-permute-start | bytes 1572872 | tf_op jit(solution)/shard_map/ppermute | solution.py:55
  32.5 2.2 %copy-start.3 = (bf16[256,8192]{1,0:T(8,128)(2,1)S(1)}, bf16[256,8192]{1,0:T(8,128)(2,1)}, u32[]{:S(2)}) copy-start(bf16[256,8192]{1,0:T(8,128)(2,1)} %grad_own.7) | copy-start | bytes 12582916
  42.1 5.6 %collective-permute-start.6 = (bf16[2,256,256]{2,1,0:T(8,128)(2,1)S(1)}, bf16[2,256,256]{2,1,0:T(8,128)(2,1)S(1)}, u32[]{:S(2)}, u32[]{:S(2)}) collective-permute-start(bf16[2,256,256]{2,1,0:T(8,128)(2,1)S(1)} %fusion.6), channel_id=1, source_target_pairs={{0,6},{1,3},{2,4},{3,1},{4,2},{5,7},{6,0},{7,5},{8,14},{9,11},{10,... | collective-permute-start | bytes 786440 | tf_op jit(solution)/shard_map/ppermute | solution.py:55
  43.5 12.1 %collective-permute-start.4 = (bf16[2,256,256]{2,1,0:T(8,128)(2,1)S(1)}, bf16[2,256,256]{2,1,0:T(8,128)(2,1)S(1)}, u32[]{:S(2)}, u32[]{:S(2)}) collective-permute-start(bf16[2,256,256]{2,1,0:T(8,128)(2,1)S(1)} %fusion.9), channel_id=1, source_target_pairs={{0,6},{1,3},{2,4},{3,1},{4,2},{5,7},{6,0},{7,5},{8,14},{9,11},{10,... | collective-permute-start | bytes 786440 | tf_op jit(solution)/shard_map/ppermute | solution.py:55
  45.4 12.4 %collective-permute-start.10 = (bf16[2,256,256]{2,1,0:T(8,128)(2,1)S(1)}, bf16[2,256,256]{2,1,0:T(8,128)(2,1)S(1)}, u32[]{:S(2)}, u32[]{:S(2)}) collective-permute-start(bf16[2,256,256]{2,1,0:T(8,128)(2,1)S(1)} %fusion.3), channel_id=1, source_target_pairs={{0,24},{1,9},{2,26},{3,11},{4,28},{5,13},{6,30},{7,15},{8,16},{9,1... | collective-permute-start | bytes 786440 | tf_op jit(solution)/shard_map/ppermute | solution.py:55
  45.6 8.7 %collective-permute-start.12 = (bf16[2,256,256]{2,1,0:T(8,128)(2,1)S(1)}, bf16[2,256,256]{2,1,0:T(8,128)(2,1)S(1)}, u32[]{:S(2)}, u32[]{:S(2)}) collective-permute-start(bf16[2,256,256]{2,1,0:T(8,128)(2,1)S(1)} %fusion), channel_id=1, source_target_pairs={{0,24},{1,9},{2,26},{3,11},{4,28},{5,13},{6,30},{7,15},{8,16},{9,1... | collective-permute-start | bytes 786440 | tf_op jit(solution)/shard_map/ppermute | solution.py:55
  47.8 9.6 %collective-permute-start.7 = (bf16[2,256,256]{2,1,0:T(8,128)(2,1)S(1)}, bf16[2,256,256]{2,1,0:T(8,128)(2,1)S(1)}, u32[]{:S(2)}, u32[]{:S(2)}) collective-permute-start(bf16[2,256,256]{2,1,0:T(8,128)(2,1)S(1)} %fusion.8), channel_id=1, source_target_pairs={{0,8},{1,25},{2,10},{3,27},{4,12},{5,29},{6,14},{7,31},{8,0},{9,17... | collective-permute-start | bytes 786440 | tf_op jit(solution)/shard_map/ppermute | solution.py:55
  54.5 6.5 %collective-permute-start.13 = (bf16[2,256,256]{2,1,0:T(8,128)(2,1)S(1)}, bf16[2,256,256]{2,1,0:T(8,128)(2,1)S(1)}, u32[]{:S(2)}, u32[]{:S(2)}) collective-permute-start(bf16[2,256,256]{2,1,0:T(8,128)(2,1)S(1)} %fusion.2), channel_id=1, source_target_pairs={{0,2},{1,7},{2,0},{3,5},{4,6},{5,3},{6,4},{7,1},{8,10},{9,15},{10,... | collective-permute-start | bytes 786440 | tf_op jit(solution)/shard_map/ppermute | solution.py:55
  57.6 3.9 %collective-permute-start.8 = (bf16[256,256]{1,0:T(8,128)(2,1)S(1)}, bf16[256,256]{1,0:T(8,128)(2,1)S(1)}, u32[]{:S(2)}, u32[]{:S(2)}) collective-permute-start(bf16[256,256]{1,0:T(8,128)(2,1)S(1)} %fusion.16), channel_id=1, source_target_pairs={{0,24},{1,9},{2,26},{3,11},{4,28},{5,13},{6,30},{7,15},{8,16},{9,1... | collective-permute-start | bytes 393224 | tf_op jit(solution)/shard_map/ppermute | solution.py:55
  61.1 5.6 %collective-permute-start.14 = (bf16[256,256]{1,0:T(8,128)(2,1)S(1)}, bf16[256,256]{1,0:T(8,128)(2,1)S(1)}, u32[]{:S(2)}, u32[]{:S(2)}) collective-permute-start(bf16[256,256]{1,0:T(8,128)(2,1)S(1)} %fusion.17), channel_id=1, source_target_pairs={{0,6},{1,3},{2,4},{3,1},{4,2},{5,7},{6,0},{7,5},{8,14},{9,11},{10,... | collective-permute-start | bytes 393224 | tf_op jit(solution)/shard_map/ppermute | solution.py:55

commit v3 on v2

v3 whole, which is shorter than its diff:
```python
import functools
import math

import jax
import jax.numpy as jnp
from jax import lax
from jax.experimental import pallas as pl
from jax.experimental.pallas import tpu as pltpu
from jax.sharding import Mesh
from jax.sharding import PartitionSpec as P

HD = 256
NS_STEPS = 5
NZ, NY, NX, NC = 8, 4, 4, 2
RING = 4
AXES = ("z", "y", "x", "c")
PLANE = ("c", "y", "x")
COEF_A, COEF_B, COEF_C = 3.4445, -4.775, 2.0315
DECAY = 0.95
VMEM = 16 * 1024 * 1024
bf16, f32 = jnp.bfloat16, jnp.float32


def device_at(z, y, x, c):
    return ((z * NY + y) * NX + x) * NC + c


def every_device():
    return [(z, y, x, c) for z in range(NZ) for y in range(NY) for x in range(NX) for c in range(NC)]


def partner(place, part, flip):
    return (((place - part) % RING) ^ flip) + part & (RING - 1)


def send(value, part, flip):
    pairs = []
    for z, y, x, c in every_device():
        to = (y, partner(x, part, flip)) if c == 0 else (partner(y, part, flip), x)
        pairs.append((device_at(z, y, x, c), device_at(z, *to, c)))
    return lax.ppermute(value, AXES, pairs)


def swap_cores(value):
    return lax.ppermute(
        value, AXES, [(device_at(z, y, x, c), device_at(z, y, x, 1 - c)) for z, y, x, c in every_device()]
    )


def second_axis_groups():
    groups = []
    for z in range(NZ):
        for place in range(RING):
            groups.append([device_at(z, other, place, 0) for other in range(RING)])
            groups.append([device_at(z, place, other, 1) for other in range(RING)])
    return groups


def first_place():
    core = lax.axis_index("c")
    return jnp.where(core == 0, lax.axis_index("x"), lax.axis_index("y"))


def column_copy_kernel(grad, out, sems):
    width = out.shape[1] // sems.shape[0]
    copies = []
    for k in range(sems.shape[0]):
        start = pl.multiple_of((1 - lax.axis_index("c")) * out.shape[1] + k * width, width)
        copies.append(
            pltpu.make_async_copy(
                grad.at[:, pl.ds(start, width)], out.at[:, pl.ds(k * width, width)], sems.at[k]
            )
        )
    for copy in copies:
        copy.start()
    for copy in copies:
        copy.wait()


def column_copy(grad):
    rows, columns = grad.shape
    return pl.pallas_call(
        column_copy_kernel,
        out_shape=jax.ShapeDtypeStruct((rows, columns // NC), grad.dtype),
        in_specs=[pl.BlockSpec(memory_space=pltpu.HBM)],
        out_specs=pl.BlockSpec(memory_space=pl.ANY),
        scratch_shapes=[pltpu.SemaphoreType.DMA((8,))],
        compiler_params=pltpu.CompilerParams(vmem_limit_bytes=VMEM),
    )(grad)


def partial_kernel(
    going, lat_own, lat_other, mom_own, mom_other, grad_own, grad_other, out_0, out_1, held, unit, sems
):
    features, tokens = lat_own.shape
    half = features // 2
    depth = mom_own.shape[0]
    width = RING * HD
    core, place = lax.axis_index("c"), first_place()
    here = lax.axis_index("y") * NX + lax.axis_index("x")

    def turned(part, flip):
        return lax.rem(lax.rem(place + RING - part, RING) ^ flip, RING) + part

    one = lax.rem(turned(0, 1), RING)
    two = lax.rem(turned(1, 1), RING)
    shared = lax.rem(place + (2 if going else 0), RING)
    blocks = (one, two, shared) if going else (two, one, shared)
    columns = grad_other.shape[1]

    def copies(k):
        other = pl.multiple_of(blocks[k] * width, width)
        own = pl.multiple_of(core * columns + blocks[k] * width, width)
        return (
            pltpu.make_async_copy(grad_own.at[:, pl.ds(own, width)], held.at[k, 0], sems.at[k, 0]),
            pltpu.make_async_copy(grad_other.at[:, pl.ds(other, width)], held.at[k, 1], sems.at[k, 1]),
        )

    for k in range(3):
        for copy in copies(k):
            copy.start()

    row = lax.broadcasted_iota(jnp.int32, (features, 4 * depth), 0)
    at = lax.broadcasted_iota(jnp.int32, (features, 4 * depth), 1)
    core_of = jnp.where((at // depth) % 2 == 0, core, 1 - core)
    unit[...] = (row == (here * NC + core_of) * depth + at % depth).astype(f32).astype(bf16)

    for k in range(3):
        for copy in copies(k):
            copy.wait()
        start = pl.multiple_of(blocks[k] * width, width)
        mom = []
        for ref in (mom_own, mom_other):
            value = (DECAY / NZ) * ref[:, pl.ds(start, width)]
            high = value.astype(bf16)
            mom.append((high, (value - high.astype(f32)).astype(bf16)))
        mom = jnp.concatenate([mom[0][0], mom[1][0], mom[0][1], mom[1][1]], axis=0)
        for part, out in ((0, out_0), (1, out_1)):
            if part == 1 - k:
                continue
            rows = slice(part * half, (part + 1) * half)
            slot = int(going) if k == 2 else 1 - int(going)
            for t in range(RING):
                at = slice(t * HD, (t + 1) * HD)
                p0 = jnp.dot(lat_own[rows, :], held[k, 0, :, at], preferred_element_type=f32)
                p1 = jnp.dot(lat_other[rows, :], held[k, 1, :, at], preferred_element_type=f32)
                p2 = jnp.dot(unit[rows, :], mom[:, at], preferred_element_type=f32)
                total = p0.astype(bf16).astype(f32) + p1.astype(bf16).astype(f32) + p2
                out[slot * RING + t] = total.astype(out.dtype)


def partial_tiles(going, lat_own, lat_other, mom_own, mom_other, grad_own, grad_other):
    features, tokens = lat_own.shape
    half = features // 2
    tiles = 2 * RING
    vmem = pl.BlockSpec(memory_space=pltpu.VMEM)
    hbm = pl.BlockSpec(memory_space=pl.ANY)
    return pl.pallas_call(
        functools.partial(partial_kernel, going),
        out_shape=[jax.ShapeDtypeStruct((tiles, half, HD), bf16 if going else f32)] * 2,
        in_specs=[vmem, vmem, vmem, vmem, hbm, hbm],
        out_specs=[vmem, vmem],
        scratch_shapes=[
            pltpu.VMEM((3, 2, tokens, RING * HD), bf16),
            pltpu.VMEM((features, 4 * mom_own.shape[0]), bf16),
            pltpu.SemaphoreType.DMA((3, 2)),
        ],
        compiler_params=pltpu.CompilerParams(vmem_limit_bytes=VMEM),
        cost_estimate=pl.CostEstimate(
            flops=2 * tiles * 2 * half * HD * 3 * tokens,
            bytes_accessed=tiles * 2 * (2 * tokens * HD * 2 + half * HD * 4),
            transcendentals=0,
        ),
    )(lat_own, lat_other, mom_own, mom_other, grad_own, grad_other)


def split(value):
    high = value.astype(bf16)
    return high, (value - high.astype(f32)).astype(bf16)


def product(a, b, dims):
    dot = functools.partial(
        lax.dot_general, dimension_numbers=(dims, ((), ())), preferred_element_type=f32
    )
    return dot(a[0], b[0]) + (dot(a[0], b[1]) + dot(a[1], b[0]))


def newton_schulz_kernel(moment_ref, out_ref):
    moment = moment_ref[...]
    rows, columns = moment.shape
    scale = 0.2 * math.sqrt(max(rows, columns))
    wide = moment.T
    gram = lax.dot_general(wide, wide, (((1,), (1,)), ((), ())), preferred_element_type=f32)
    wide = wide.astype(f32)
    inverse = 1.0 / (jnp.sqrt(jnp.sum(wide * wide)) + 1e-7)
    gram = (gram * inverse) * inverse
    x = wide * inverse
    for step in range(NS_STEPS):
        pair = split(x)
        if step > 0:
            gram = product(pair, pair, ((1,), (1,)))
        gram_pair = split(gram)
        poly = COEF_B * gram + COEF_C * product(gram_pair, gram_pair, ((1,), (0,)))
        x = COEF_A * x + product(split(poly), pair, ((1,), (0,)))
    update = (scale * x).T.astype(bf16)
    owners = out_ref.shape[0]
    depth = rows // owners
    for c in range(NC):
        for chip in range(owners // NC):
            at = slice((chip * NC + c) * depth, (chip * NC + c + 1) * depth)
            out_ref[c * (owners // NC) + chip, 0] = update[at, :]
            out_ref[c * (owners // NC) + chip, 1] = moment[at, :]


def newton_schulz(moment, owners):
    rows, columns = moment.shape
    return pl.pallas_call(
        newton_schulz_kernel,
        out_shape=jax.ShapeDtypeStruct((owners, 2, rows // owners, columns), bf16),
        compiler_params=pltpu.CompilerParams(vmem_limit_bytes=VMEM),
    )(moment)


def spread_kernel(returned, moment, update):
    for c in range(NC):
        for y in range(NY):
            for x in range(NX):
                source = (c * NY + y) * NX + x
                head = c * NY * NX + (RING * x + y if c == 0 else RING * y + x)
                at = slice(head * HD, (head + 1) * HD)
                update[:, at] = returned[source, 0]
                moment[:, at] = returned[source, 1].astype(f32)


def spread(returned):
    heads, _, rows, columns = returned.shape
    return pl.pallas_call(
        spread_kernel,
        out_shape=(
            jax.ShapeDtypeStruct((rows, heads * columns), f32),
            jax.ShapeDtypeStruct((rows, heads * columns), bf16),
        ),
        compiler_params=pltpu.CompilerParams(vmem_limit_bytes=VMEM),
    )(returned)


def body(latent, latent_grad, row_counts, momentum):
    c = lax.axis_index("c")
    slots, features = latent.shape
    columns = latent_grad.shape[1] // NC

    grad_other = swap_cores(column_copy(latent_grad))
    live = lax.broadcasted_iota(jnp.int32, (slots, 1), 0) < row_counts[0]
    lat_own = jnp.where(live, latent, jnp.zeros_like(latent)).T
    lat_other = swap_cores(lat_own)
    mom_own = lax.dynamic_slice_in_dim(momentum, c * columns, columns, 1)
    mom_other = swap_cores(lax.dynamic_slice_in_dim(momentum, (1 - c) * columns, columns, 1))

    operands = (lat_own, lat_other, mom_own, mom_other, latent_grad, grad_other)
    going = partial_tiles(True, *operands)
    kept = partial_tiles(False, *operands)

    parts = []
    for part in range(2):
        got = send(going[part], part, 1)
        out = (kept[part][RING:] + got[RING:].astype(f32)).astype(bf16)
        keep = kept[part][:RING] + got[:RING].astype(f32)
        parts.append((keep + send(out, part, 3).astype(f32)).astype(bf16))

    stack = jnp.concatenate(parts, axis=1)
    stack = lax.all_to_all(stack, AXES, 0, 0, axis_index_groups=second_axis_groups(), tiled=True)
    head = jnp.sum(stack.astype(f32), axis=0).astype(bf16)

    pieces = lax.all_to_all(head.reshape(NZ, -1, HD), "z", 0, 0, tiled=True)
    piece = jnp.sum(pieces.astype(f32), axis=0).astype(bf16)
    moment = lax.all_to_all(jnp.broadcast_to(piece, (NZ,) + piece.shape), "z", 0, 0, tiled=True)
    moment = moment.reshape(features, HD)

    outgoing = newton_schulz(moment, NC * NY * NX)
    returned = lax.all_to_all(outgoing, PLANE, 0, 0, tiled=True)
    return tuple(spread(returned))


def solution(mesh):
    fine = Mesh(mesh.devices.reshape(NZ, NY, NX, NC), AXES)
    shard = ("y", "x", "c")
    in_specs = (P(AXES, None), P(AXES, None), P(AXES), P(shard, None))
    out_specs = (P(shard, None), P(shard, None))
    return jax.shard_map(body, mesh=fine, in_specs=in_specs, out_specs=out_specs, check_vma=False)
```

time: 130 us -> 112 us (0.86)
  Pallas kernels: 23.3 us -> 13.4 us
  blocking collectives: 54.8 us -> 63.5 us
  starting transfers between devices: 15.4 us -> 6.85 us
  local copies, waits for them, and re-layouts: 12.2 us -> 4.57 us
  waiting for transfers between devices: 18 us -> 21.1 us
  other arithmetic: 3.84 us -> 0.98 us
    all_to_all x1 -> x2, blocking collectives: 15.9 us -> 31.1 us  [the longest x1 17.4 us: body(): pieces = lax.all_to_all(head.reshape(NZ, -1, HD), 'z', 0, 0, tiled=True)]
    pallas_call x4 -> x2, Pallas kernels: 13.8 us -> 5.11 us  [partial_tiles(): pl.pallas_call(functools.partial(partial_kernel, going), out_shape=[jax.S...]
    ppermute x15 -> x7, starting transfers between devices: 15.4 us -> 6.85 us  [the longest x3 3.98 us: swap_cores(): lax.ppermute(value, AXES, [(device_at(z, y, x, c), device_at(z, y, x, 1 -...]
    unnamed x17 -> x9, local copies, waits for them, and re-layouts: 11.5 us -> 4.51 us
    all_to_all x1, blocking collectives: 27.1 us -> 20.6 us  [body(): returned = lax.all_to_all(outgoing, PLANE, 0, 0, tiled=True)]
    ppermute x15 -> x7, waiting for transfers between devices: 18 us -> 21.1 us  [the longest x4 18.1 us: send(): return lax.ppermute(value, AXES, pairs)]
    convert_element_type x10 -> x4, other arithmetic: 2.91 us -> 0.58 us  [the longest x2 0.34 us: body(): parts.append((keep + send(out, part, 3).astype(f32)).astype(bf16))]
  transfers between devices with their start and end apart: 15 -> 7, of which waited for: 7 -> 5; matrix products, arithmetic and copies ran while one was open for 4% -> 1% of each run, Pallas kernels for 8% -> 2%
where the time goes in v3:
time: 112 us
  blocking collectives  63.5 us (57%)
  waiting for transfers between devices  21.1 us (19%)
  Pallas kernels  13.4 us (12%)
  starting transfers between devices  6.85 us (6%)
  local copies, waits for them, and re-layouts  4.57 us (4%)
  between operations  1.44 us (1%)
    all_to_all x1, blocking collectives, body(): returned = lax.all_to_all(outgoing, PLANE, 0, 0, tiled=True)  20.6 us
    ppermute x4, waiting for transfers between devices, send(): return lax.ppermute(value, AXES, pairs)  18.1 us
    all_to_all x1, blocking collectives, body(): pieces = lax.all_to_all(head.reshape(NZ, -1, HD), 'z', 0, 0, tiled=True)  17.4 us
    all_to_all x1, blocking collectives, body(): lax.all_to_all(stack, AXES, 0, 0, axis_index_groups=second_axis_groups(),...  13.7 us
    all_to_all x1, blocking collectives, body(): lax.all_to_all(jnp.broadcast_to(piece, (NZ,) + piece.shape), 'z', 0, 0, t...  11.8 us
    pallas_call x1, Pallas kernels, newton_schulz(): pl.pallas_call(newton_schulz_kernel, out_shape=jax.ShapeDtypeStruct((owne...  5.97 us
    pallas_call x2, Pallas kernels, partial_tiles(): pl.pallas_call(functools.partial(partial_kernel, going), out_shape=[jax.S...  5.11 us
    unnamed x9, local copies, waits for them, and re-layouts  4.51 us
  transfers between devices with their start and end apart: 7, of which 5 were waited for; matrix products, arithmetic and copies ran while one was open for 1% of the time, Pallas kernels for 2%

profile of v3, /device:TPU:1, one launch (start us, length us, event | category | flops | bytes accessed | tf_op | source)
XLA Modules:
  0.0 111.8 jit_solution(6492713135160585132)
XLA Ops:
  0.6 0.0 copy-start
  0.6 2.2 %copy-done = bf16[256,8192]{1,0:T(8,128)(2,1)S(1)} copy-done((bf16[256,8192]{1,0:T(8,128)(2,1)S(1)}, bf16[256,8192]{1,0:T(8,128)(2,1)}, u32[]{:S(2)}) %copy-start) | copy-done | bytes 4194328
  2.8 0.0 copy-start.3
  2.8 0.0 copy-start.2
  2.8 1.4 %shard_map.59 = bf16[256,4096]{1,0:T(8,128)(2,1)} custom-call(bf16[256,8192]{1,0:T(8,128)(2,1)S(1)} %copy-done), custom_call_target="tpu_custom_call" | custom-call | tf_op jit(solution)/shard_map/pallas_call | solution.py:82
  4.2 3.3 %collective-permute-start.2 = (bf16[256,4096]{1,0:T(8,128)(2,1)}, bf16[256,4096]{1,0:T(8,128)(2,1)S(1)}, u32[]{:S(2)}, u32[]{:S(2)}) collective-permute-start(bf16[256,4096]{1,0:T(8,128)(2,1)} %shard_map.59), channel_id=1, source_target_pairs={{0,1},{1,0},{2,3},{3,2},{4,5},{5,4},{6,7},{7,6},{8,9},{9,8},{10,11... | collective-permute-start | bytes 6291464 | tf_op jit(solution)/shard_map/ppermute | solution.py:45
  8.2 0.0 copy-done.3
  8.2 0.1 copy.7
  8.4 0.1 collective-permute-start
  8.5 0.0 copy-done.2
  8.6 0.6 collective-permute-start.1
  9.1 2.6 %collective-permute-done.lat_other = bf16[512,256]{1,0:T(8,128)(2,1)S(1)} collective-permute-done((bf16[512,256]{1,0:T(8,128)(2,1)S(1)}, bf16[512,256]{1,0:T(8,128)(2,1)S(1)}, u32[]{:S(2)}, u32[]{:S(2)}) %collective-permute-start) | collective-permute-done | bytes 262176 | tf_op jit(solution)/shard_map/ppermute | solution.py:45
  11.7 0.4 collective-permute-done.1.mom_other
  12.1 0.0 collective-permute-done.2.grad_other
  12.1 0.0 copy-start.1
  12.1 2.2 %copy-done.1 = bf16[256,8192]{1,0:T(8,128)(2,1)S(1)} copy-done((bf16[256,8192]{1,0:T(8,128)(2,1)S(1)}, bf16[256,8192]{1,0:T(8,128)(2,1)}, u32[]{:S(2)}) %copy-start.1) | copy-done | bytes 4194328
  14.3 2.6 %shard_map.61 = (bf16[8,256,256]{2,1,0:T(8,128)(2,1)S(1)}, bf16[8,256,256]{2,1,0:T(8,128)(2,1)S(1)}) custom-call(bf16[512,256]{1,0:T(8,128)(2,1)S(1)} %select_bitcast_fusion.lat_own, bf16[512,256]{1,0:T(8,128)(2,1)S(1)} %collective-permute-done.lat_other, f32[16,4096]{1,0:T(8,128)S(1)} %get-tuple-element.11.mom_own, ...), custom_call_target="tpu_custom_call" | custom-call | flops 1610612736 | bytes 8388608 | tf_op jit(solution)/shard_map/pallas_call | solution.py:158
  16.8 0.1 collective-permute-start.3
  16.9 1.4 %collective-permute-start.5 = (bf16[8,256,256]{2,1,0:T(8,128)(2,1)S(1)}, bf16[8,256,256]{2,1,0:T(8,128)(2,1)S(1)}, u32[]{:S(2)}, u32[]{:S(2)}) collective-permute-start(bf16[8,256,256]{2,1,0:T(8,128)(2,1)S(1)} %get-tuple-element.9), channel_id=1, source_target_pairs={{0,6},{1,25},{2,4},{3,27},{4,2},{5,29},{6,0},{7,31},{8,14},{9,17},... | collective-permute-start | bytes 3145736 | tf_op jit(solution)/shard_map/ppermute | solution.py:41
  18.4 2.6 %shard_map.60 = (f32[8,256,256]{2,1,0:T(8,128)S(1)}, f32[8,256,256]{2,1,0:T(8,128)S(1)}) custom-call(bf16[512,256]{1,0:T(8,128)(2,1)S(1)} %select_bitcast_fusion.lat_own, bf16[512,256]{1,0:T(8,128)(2,1)S(1)} %collective-permute-done.lat_other, f32[16,4096]{1,0:T(8,128)S(1)} %get-tuple-element.11.mom_own, f32[16,4096]{1,0:T(8,128)S(1)} %collective-permute-done.1.mom_other, ...), custom_call_target="tpu_custom_call" | custom-call | flops 1610612736 | bytes 8388608 | tf_op jit(solution)/shard_map/pallas_call | solution.py:158
  21.0 9.9 %collective-permute-done.3 = bf16[8,256,256]{2,1,0:T(8,128)(2,1)S(1)} collective-permute-done((bf16[8,256,256]{2,1,0:T(8,128)(2,1)S(1)}, bf16[8,256,256]{2,1,0:T(8,128)(2,1)S(1)}, u32[]{:S(2)}, u32[]{:S(2)}) %collective-permute-start.3) | collective-permute-done | bytes 1048608 | tf_op jit(solution)/shard_map/ppermute | solution.py:41
  30.9 0.1 add_convert_fusion.3
  31.0 1.1 collective-permute-start.4
  32.1 0.1 collective-permute-done.5
  32.2 0.1 add_convert_fusion.1
  32.3 0.2 collective-permute-start.6
  32.6 8.1 %collective-permute-done.4 = bf16[4,256,256]{2,1,0:T(8,128)(2,1)S(1)} collective-permute-done((bf16[4,256,256]{2,1,0:T(8,128)(2,1)S(1)}, bf16[4,256,256]{2,1,0:T(8,128)(2,1)S(1)}, u32[]{:S(2)}, u32[]{:S(2)}) %collective-permute-start.4) | collective-permute-done | bytes 524320 | tf_op jit(solution)/shard_map/ppermute | solution.py:41
  40.6 0.2 add_convert_fusion.2
  40.8 0.0 collective-permute-done.6
  40.8 0.2 add_convert_fusion
  41.0 0.1 pad_maximum_fusion
  41.1 13.7 %all_to_all.20 = bf16[4,512,256]{2,1,0:T(8,128)(2,1)S(1)} all-to-all(bf16[4,512,256]{2,1,0:T(8,128)(2,1)S(1)} %pad_maximum_fusion), channel_id=1, replica_groups={{0,8,16,24},{1,3,5,7},{2,10,18,26},{9,11,13,15},{4,12,20,28},{17,19,21,..., dimensions={0} | all-to-all | bytes 2097152 | tf_op jit(solution)/shard_map/all_to_all | solution.py:272
  54.7 0.3 reduce_sum.24
  55.0 17.4 %all_to_all.21 = bf16[8,64,256]{2,1,0:T(8,128)(2,1)S(1)} all-to-all(bf16[8,64,256]{2,1,0:T(8,128)(2,1)S(1)} %bitcast.7), channel_id=1, replica_groups=mesh['z'=8,'y'=4,'x'=4,'c'=2] {'z'}, dimensions={0} | all-to-all | bytes 524288 | tf_op jit(solution)/shard_map/all_to_all | solution.py:275
  72.5 11.8 %all_to_all.22 = bf16[8,64,256]{2,1,0:T(8,128)(2,1)S(1)} all-to-all(bf16[8,64,256]{2,1,0:T(8,128)(2,1)S(1)} %broadcast_in_dim.16), channel_id=1, replica_groups=mesh['z'=8,'y'=4,'x'=4,'c'=2] {'z'}, dimensions={0} | all-to-all | bytes 524288 | tf_op jit(solution)/shard_map/all_to_all | solution.py:277
  84.3 6.0 %shard_map.62 = bf16[32,2,16,256]{3,2,1,0:T(8,128)(2,1)S(1)} custom-call(bf16[512,256]{1,0:T(8,128)(2,1)S(1)} %bitcast.6), custom_call_target="tpu_custom_call" | custom-call | tf_op jit(solution)/shard_map/pallas_call | solution.py:218
  90.3 20.6 %all_to_all.23.returned = bf16[32,2,16,256]{3,2,1,0:T(8,128)(2,1)S(1)} all-to-all(bf16[32,2,16,256]{3,2,1,0:T(8,128)(2,1)S(1)} %shard_map.62), channel_id=1, replica_groups=mesh['z'=8,'y'=4,'x'=4,'c'=2] {'c','y','x'}, dimensions={0} | all-to-all | bytes 1048576 | tf_op jit(solution)/shard_map/all_to_all | solution.py:281
  110.9 0.9 shard_map.63
  (5 shorter events, 0.1 us)
Async XLA Ops:
  0.6 2.2 %copy-start = (bf16[256,8192]{1,0:T(8,128)(2,1)S(1)}, bf16[256,8192]{1,0:T(8,128)(2,1)}, u32[]{:S(2)}) copy-start(bf16[256,8192]{1,0:T(8,128)(2,1)} %grad_own.3) | copy-start | bytes 12582916
  2.8 5.4 %copy-start.3 = (bf16[256,512]{1,0:T(8,128)(2,1)S(1)}, bf16[256,512]{1,0:T(8,128)(2,1)}, u32[]{:S(2)}) copy-start(bf16[256,512]{1,0:T(8,128)(2,1)} %param.4) | copy-start | bytes 786436
  2.8 5.7 %copy-start.2 = (f32[16,8192]{1,0:T(8,128)S(1)}, f32[16,8192]{1,0:T(8,128)}, u32[]{:S(2)}) copy-start(f32[16,8192]{1,0:T(8,128)} %param.7) | copy-start | bytes 1572868
  4.2 7.9 %collective-permute-start.2 = (bf16[256,4096]{1,0:T(8,128)(2,1)}, bf16[256,4096]{1,0:T(8,128)(2,1)S(1)}, u32[]{:S(2)}, u32[]{:S(2)}) collective-permute-start(bf16[256,4096]{1,0:T(8,128)(2,1)} %shard_map.59), channel_id=1, source_target_pairs={{0,1},{1,0},{2,3},{3,2},{4,5},{5,4},{6,7},{7,6},{8,9},{9,8},{10,11... | collective-permute-start | bytes 6291464 | tf_op jit(solution)/shard_map/ppermute | solution.py:45
  8.4 3.3 %collective-permute-start = (bf16[512,256]{1,0:T(8,128)(2,1)S(1)}, bf16[512,256]{1,0:T(8,128)(2,1)S(1)}, u32[]{:S(2)}, u32[]{:S(2)}) collective-permute-start(bf16[512,256]{1,0:T(8,128)(2,1)S(1)} %select_bitcast_fusion.lat_own), channel_id=1, source_target_pairs={{0,1},{1,0},{2,3},{3,2},{4,5},{5,4},{6,7},{7,6},{8,9},{9,8},{10,11... | collective-permute-start | bytes 786440 | tf_op jit(solution)/shard_map/ppermute | solution.py:45
  8.6 3.5 %collective-permute-start.1 = (f32[16,4096]{1,0:T(8,128)S(1)}, f32[16,4096]{1,0:T(8,128)S(1)}, u32[]{:S(2)}, u32[]{:S(2)}) collective-permute-start(f32[16,4096]{1,0:T(8,128)S(1)} %get-tuple-element.10), channel_id=1, source_target_pairs={{0,1},{1,0},{2,3},{3,2},{4,5},{5,4},{6,7},{7,6},{8,9},{9,8},{10,11... | collective-permute-start | bytes 786440 | tf_op jit(solution)/shard_map/ppermute | solution.py:45
  12.1 2.2 %copy-start.1 = (bf16[256,8192]{1,0:T(8,128)(2,1)S(1)}, bf16[256,8192]{1,0:T(8,128)(2,1)}, u32[]{:S(2)}) copy-start(bf16[256,8192]{1,0:T(8,128)(2,1)} %grad_own.3) | copy-start | bytes 12582916
  16.8 14.0 %collective-permute-start.3 = (bf16[8,256,256]{2,1,0:T(8,128)(2,1)S(1)}, bf16[8,256,256]{2,1,0:T(8,128)(2,1)S(1)}, u32[]{:S(2)}, u32[]{:S(2)}) collective-permute-start(bf16[8,256,256]{2,1,0:T(8,128)(2,1)S(1)} %get-tuple-element.7), channel_id=1, source_target_pairs={{0,2},{1,9},{2,0},{3,11},{4,6},{5,13},{6,4},{7,15},{8,10},{9,1},{1... | collective-permute-start | bytes 3145736 | tf_op jit(solution)/shard_map/ppermute | solution.py:41
  16.9 15.2 %collective-permute-start.5 = (bf16[8,256,256]{2,1,0:T(8,128)(2,1)S(1)}, bf16[8,256,256]{2,1,0:T(8,128)(2,1)S(1)}, u32[]{:S(2)}, u32[]{:S(2)}) collective-permute-start(bf16[8,256,256]{2,1,0:T(8,128)(2,1)S(1)} %get-tuple-element.9), channel_id=1, source_target_pairs={{0,6},{1,25},{2,4},{3,27},{4,2},{5,29},{6,0},{7,31},{8,14},{9,17},... | collective-permute-start | bytes 3145736 | tf_op jit(solution)/shard_map/ppermute | solution.py:41
  31.0 9.6 %collective-permute-start.4 = (bf16[4,256,256]{2,1,0:T(8,128)(2,1)S(1)}, bf16[4,256,256]{2,1,0:T(8,128)(2,1)S(1)}, u32[]{:S(2)}, u32[]{:S(2)}) collective-permute-start(bf16[4,256,256]{2,1,0:T(8,128)(2,1)S(1)} %add_convert_fusion.3), channel_id=1, source_target_pairs={{0,6},{1,25},{2,4},{3,27},{4,2},{5,29},{6,0},{7,31},{8,14},{9,17},... | collective-permute-start | bytes 1572872 | tf_op jit(solution)/shard_map/ppermute | solution.py:41
  32.3 8.5 %collective-permute-start.6 = (bf16[4,256,256]{2,1,0:T(8,128)(2,1)S(1)}, bf16[4,256,256]{2,1,0:T(8,128)(2,1)S(1)}, u32[]{:S(2)}, u32[]{:S(2)}) collective-permute-start(bf16[4,256,256]{2,1,0:T(8,128)(2,1)S(1)} %add_convert_fusion.1), channel_id=1, source_target_pairs={{0,2},{1,9},{2,0},{3,11},{4,6},{5,13},{6,4},{7,15},{8,10},{9,1},{1... | collective-permute-start | bytes 1572872 | tf_op jit(solution)/shard_map/ppermute | solution.py:41

commit v4 on v3

v4 whole, which is shorter than its diff:
```python
import functools
import math

import jax
import jax.numpy as jnp
from jax import lax
from jax.experimental import pallas as pl
from jax.experimental.pallas import tpu as pltpu
from jax.sharding import Mesh
from jax.sharding import PartitionSpec as P

HD = 256
NS_STEPS = 5
NZ, NY, NX, NC = 8, 4, 4, 2
RING = 4
AXES = ("z", "y", "x", "c")
PLANE = ("c", "y", "x")
COEF_A, COEF_B, COEF_C = 3.4445, -4.775, 2.0315
DECAY = 0.95
VMEM = 16 * 1024 * 1024
bf16, f32 = jnp.bfloat16, jnp.float32


def device_at(z, y, x, c):
    return ((z * NY + y) * NX + x) * NC + c


def every_device():
    return [(z, y, x, c) for z in range(NZ) for y in range(NY) for x in range(NX) for c in range(NC)]


def shift(value, axis, distance):
    pairs = []
    for z, y, x, c in every_device():
        if axis == c:
            to = (y, (x + distance) % NX)
        else:
            to = ((y + distance) % NY, x)
        pairs.append((device_at(z, y, x, c), device_at(z, *to, c)))
    return lax.ppermute(value, AXES, pairs)


def swap_cores(value):
    return lax.ppermute(
        value, AXES, [(device_at(z, y, x, c), device_at(z, y, x, 1 - c)) for z, y, x, c in every_device()]
    )


def places():
    core, y, x = lax.axis_index("c"), lax.axis_index("y"), lax.axis_index("x")
    return jnp.where(core == 0, x, y), jnp.where(core == 0, y, x)


def column_copy_kernel(grad, out, sems):
    width = out.shape[1] // sems.shape[0]
    copies = []
    for k in range(sems.shape[0]):
        start = pl.multiple_of((1 - lax.axis_index("c")) * out.shape[1] + k * width, width)
        copies.append(
            pltpu.make_async_copy(
                grad.at[:, pl.ds(start, width)], out.at[:, pl.ds(k * width, width)], sems.at[k]
            )
        )
    for copy in copies:
        copy.start()
    for copy in copies:
        copy.wait()


def column_copy(grad):
    rows, columns = grad.shape
    return pl.pallas_call(
        column_copy_kernel,
        out_shape=jax.ShapeDtypeStruct((rows, columns // NC), grad.dtype),
        in_specs=[pl.BlockSpec(memory_space=pl.ANY)],
        out_specs=pl.BlockSpec(memory_space=pl.ANY),
        scratch_shapes=[pltpu.SemaphoreType.DMA((8,))],
        compiler_params=pltpu.CompilerParams(vmem_limit_bytes=62 * 1024 * 1024),
    )(grad)


def head_columns(near, far):
    first, second = places()
    head = lax.rem(first + near, RING) * RING + lax.rem(second + far, RING)
    return pl.multiple_of(head * HD, HD)


def own_kernel(depth, lat, grad, *refs):
    outs, (unit, held, sems) = refs[:RING], refs[RING:]
    core = lax.axis_index("c")
    half = grad.shape[1] // NC
    copies = []
    for near in range(RING):
        for far in range(RING):
            start = pl.multiple_of(core * half + head_columns(near, far), HD)
            at = near * RING + far
            copies.append(
                pltpu.make_async_copy(grad.at[:, pl.ds(start, HD)], held.at[at], sems.at[at])
            )
    for copy in copies:
        copy.start()

    features = lat.shape[0]
    here = lax.axis_index("y") * NX + lax.axis_index("x")
    row = lax.broadcasted_iota(jnp.int32, (features, 4 * depth), 0)
    at = lax.broadcasted_iota(jnp.int32, (features, 4 * depth), 1)
    core_of = jnp.where((at // depth) % 2 == 0, core, 1 - core)
    unit[...] = (row == (here * NC + core_of) * depth + at % depth).astype(f32).astype(bf16)

    for copy in copies:
        copy.wait()
    for near in range(RING):
        for far in range(RING):
            product = jnp.dot(lat[...], held[near * RING + far], preferred_element_type=f32)
            outs[near][far] = product.astype(bf16)


def own_products(lat, grad, depth):
    features, tokens = lat.shape
    out = jax.ShapeDtypeStruct((RING, features, HD), bf16)
    vmem = pl.BlockSpec(memory_space=pltpu.VMEM)
    return pl.pallas_call(
        functools.partial(own_kernel, depth),
        out_shape=[out] * RING + [jax.ShapeDtypeStruct((features, 4 * depth), bf16)],
        in_specs=[vmem, pl.BlockSpec(memory_space=pl.ANY)],
        out_specs=[vmem] * (RING + 1),
        scratch_shapes=[
            pltpu.VMEM((RING * RING, tokens, HD), bf16),
            pltpu.SemaphoreType.DMA((RING * RING,)),
        ],
        compiler_params=pltpu.CompilerParams(vmem_limit_bytes=VMEM),
        cost_estimate=pl.CostEstimate(
            flops=2 * RING * RING * features * HD * tokens,
            bytes_accessed=RING * RING * (tokens + features) * HD * 2,
            transcendentals=0,
        ),
    )(lat, grad)


def block_kernel(near, own, unit, lat, mom_own, mom_other, grad, out):
    for far in range(RING):
        at = pl.ds(head_columns(near, far), HD)
        high, low = [], []
        for ref in (mom_own, mom_other):
            value = (DECAY / NZ) * ref[:, at]
            high.append(value.astype(bf16))
            low.append((value - high[-1].astype(f32)).astype(bf16))
        mom = jnp.concatenate(high + low, axis=0)
        other = jnp.dot(lat[...], grad[:, at], preferred_element_type=f32)
        added = jnp.dot(unit[...], mom, preferred_element_type=f32)
        total = own[far].astype(f32) + other.astype(bf16).astype(f32) + added
        out[far] = total.astype(out.dtype)


def block(near, own, unit, lat, mom_own, mom_other, grad):
    features, tokens = lat.shape
    dtype = f32 if near == 0 else bf16
    return pl.pallas_call(
        functools.partial(block_kernel, near),
        out_shape=jax.ShapeDtypeStruct(own.shape, dtype),
        compiler_params=pltpu.CompilerParams(vmem_limit_bytes=VMEM),
        cost_estimate=pl.CostEstimate(
            flops=2 * RING * features * HD * (tokens + unit.shape[1]),
            bytes_accessed=RING * (tokens + 2 * features) * HD * 2,
            transcendentals=0,
        ),
    )(own, unit, lat, mom_own, mom_other, grad)


def split(value):
    high = value.astype(bf16)
    return high, (value - high.astype(f32)).astype(bf16)


def product(a, b, dims):
    dot = functools.partial(
        lax.dot_general, dimension_numbers=(dims, ((), ())), preferred_element_type=f32
    )
    return dot(a[0], b[0]) + (dot(a[0], b[1]) + dot(a[1], b[0]))


def newton_schulz_kernel(moment_ref, out_ref):
    moment = moment_ref[...]
    rows, columns = moment.shape
    scale = 0.2 * math.sqrt(max(rows, columns))
    wide = moment.T
    gram = lax.dot_general(wide, wide, (((1,), (1,)), ((), ())), preferred_element_type=f32)
    wide = wide.astype(f32)
    inverse = 1.0 / (jnp.sqrt(jnp.sum(wide * wide)) + 1e-7)
    gram = (gram * inverse) * inverse
    x = wide * inverse
    for step in range(NS_STEPS):
        pair = split(x)
        if step > 0:
            gram = product(pair, pair, ((1,), (1,)))
        gram_pair = split(gram)
        poly = COEF_B * gram + COEF_C * product(gram_pair, gram_pair, ((1,), (0,)))
        x = COEF_A * x + product(split(poly), pair, ((1,), (0,)))
    update = (scale * x).T.astype(bf16)
    owners = out_ref.shape[0]
    depth = rows // owners
    for c in range(NC):
        for chip in range(owners // NC):
            at = slice((chip * NC + c) * depth, (chip * NC + c + 1) * depth)
            out_ref[c * (owners // NC) + chip, 0] = update[at, :]
            out_ref[c * (owners // NC) + chip, 1] = moment[at, :]


def newton_schulz(moment, owners):
    rows, columns = moment.shape
    return pl.pallas_call(
        newton_schulz_kernel,
        out_shape=jax.ShapeDtypeStruct((owners, 2, rows // owners, columns), bf16),
        compiler_params=pltpu.CompilerParams(vmem_limit_bytes=VMEM),
    )(moment)


def spread_kernel(returned, moment, update):
    for c in range(NC):
        for y in range(NY):
            for x in range(NX):
                source = (c * NY + y) * NX + x
                head = c * NY * NX + (RING * x + y if c == 0 else RING * y + x)
                at = slice(head * HD, (head + 1) * HD)
                update[:, at] = returned[source, 0]
                moment[:, at] = returned[source, 1].astype(f32)


def spread(returned):
    heads, _, rows, columns = returned.shape
    return pl.pallas_call(
        spread_kernel,
        out_shape=(
            jax.ShapeDtypeStruct((rows, heads * columns), f32),
            jax.ShapeDtypeStruct((rows, heads * columns), bf16),
        ),
        compiler_params=pltpu.CompilerParams(vmem_limit_bytes=VMEM),
    )(returned)


def body(latent, latent_grad, row_counts, momentum):
    c = lax.axis_index("c")
    slots, features = latent.shape
    columns = latent_grad.shape[1] // NC

    grad_other = swap_cores(column_copy(latent_grad))
    live = lax.broadcasted_iota(jnp.int32, (slots, 1), 0) < row_counts[0]
    lat_own = jnp.where(live, latent, jnp.zeros_like(latent)).T
    lat_other = swap_cores(lat_own)
    mom_own = lax.dynamic_slice_in_dim(momentum, c * columns, columns, 1)
    mom_other = swap_cores(lax.dynamic_slice_in_dim(momentum, (1 - c) * columns, columns, 1))

    *own, unit = own_products(lat_own, latent_grad, momentum.shape[0])
    blocks = [block(k, own[k], unit, lat_other, mom_own, mom_other, grad_other) for k in range(RING)]
    got = [shift(blocks[k], 0, k) for k in (2, 1, 3)]
    total = blocks[0] + sum(g.astype(f32) for g in got)

    got = [shift(total[k].astype(bf16), 1, k) for k in (2, 1, 3)]
    head = (total[0] + sum(g.astype(f32) for g in got)).astype(bf16)

    pieces = lax.all_to_all(head.reshape(NZ, -1, HD), "z", 0, 0, tiled=True)
    piece = jnp.sum(pieces.astype(f32), axis=0).astype(bf16)
    moment = lax.all_to_all(jnp.broadcast_to(piece, (NZ,) + piece.shape), "z", 0, 0, tiled=True)
    moment = moment.reshape(features, HD)

    outgoing = newton_schulz(moment, NC * NY * NX)
    returned = lax.all_to_all(outgoing, PLANE, 0, 0, tiled=True)
    return tuple(spread(returned))


def solution(mesh):
    fine = Mesh(mesh.devices.reshape(NZ, NY, NX, NC), AXES)
    shard = ("y", "x", "c")
    in_specs = (P(AXES, None), P(AXES, None), P(AXES), P(shard, None))
    out_specs = (P(shard, None), P(shard, None))
    return jax.shard_map(body, mesh=fine, in_specs=in_specs, out_specs=out_specs, check_vma=False)
```

time: 112 us -> 170 us (1.52)
  Pallas kernels: 13.4 us -> 76.2 us
  blocking collectives: 63.5 us -> 49.2 us
  waiting for transfers between devices: 21.1 us -> 29.4 us
  starting transfers between devices: 6.85 us -> 10.9 us
  local copies, waits for them, and re-layouts: 4.57 us -> 2.44 us
    pallas_call x1, Pallas kernels: 1.4 us -> 64.7 us  [column_copy(): pl.pallas_call(column_copy_kernel, out_shape=jax.ShapeDtypeStruct((rows,...]
    all_to_all x1 -> x0, blocking collectives: 13.7 us -> none  [body(): lax.all_to_all(stack, AXES, 0, 0, axis_index_groups=second_axis_groups(),...]
    ppermute x4 -> x6, waiting for transfers between devices: 18.1 us -> 29.4 us  [shift(): return lax.ppermute(value, AXES, pairs)]
    ppermute x4 -> x6, starting transfers between devices: 2.87 us -> 6.9 us  [shift(): return lax.ppermute(value, AXES, pairs)]
    ppermute x3, waiting for transfers between devices: 2.97 us -> 0.01 us  [swap_cores(): lax.ppermute(value, AXES, [(device_at(z, y, x, c), device_at(z, y, x, 1 -...]
    unnamed x9 -> x7, local copies, waits for them, and re-layouts: 4.51 us -> 2.33 us
    pallas_call x2 -> x5, Pallas kernels: 5.11 us -> 4.59 us  [the longest x4 2.8 us: block(): pl.pallas_call(functools.partial(block_kernel, near), out_shape=jax.Shape...]
  transfers between devices with their start and end apart: 7 -> 9, of which waited for: 5 -> 5; matrix products, arithmetic and copies ran while one was open for 1% -> 0% of each run, Pallas kernels for 2% -> 2%
where the time goes in v4:
time: 170 us
  Pallas kernels  76.2 us (45%)
  blocking collectives  49.2 us (29%)
  waiting for transfers between devices  29.4 us (17%)
  starting transfers between devices  10.9 us (6%)
  local copies, waits for them, and re-layouts  2.44 us (1%)
    pallas_call x1, Pallas kernels, column_copy(): pl.pallas_call(column_copy_kernel, out_shape=jax.ShapeDtypeStruct((rows,...  64.7 us
    ppermute x6, waiting for transfers between devices, shift(): return lax.ppermute(value, AXES, pairs)  29.4 us
    all_to_all x1, blocking collectives, body(): returned = lax.all_to_all(outgoing, PLANE, 0, 0, tiled=True)  20 us
    all_to_all x1, blocking collectives, body(): pieces = lax.all_to_all(head.reshape(NZ, -1, HD), 'z', 0, 0, tiled=True)  17.4 us
    all_to_all x1, blocking collectives, body(): lax.all_to_all(jnp.broadcast_to(piece, (NZ,) + piece.shape), 'z', 0, 0, t...  11.8 us
    ppermute x6, starting transfers between devices, shift(): return lax.ppermute(value, AXES, pairs)  6.9 us
    pallas_call x1, Pallas kernels, newton_schulz(): pl.pallas_call(newton_schulz_kernel, out_shape=jax.ShapeDtypeStruct((owne...  5.97 us
    ppermute x3, starting transfers between devices, swap_cores(): lax.ppermute(value, AXES, [(device_at(z, y, x, c), device_at(z, y, x, 1 -...  3.98 us
  transfers between devices with their start and end apart: 9, of which 5 were waited for; matrix products, arithmetic and copies ran while one was open for 0% of the time, Pallas kernels for 2%

profile of v4, /device:TPU:1, one launch (start us, length us, event | category | flops | bytes accessed | tf_op | source)
XLA Modules:
  0.0 170.2 jit_solution(812337502982375402)
XLA Ops:
  0.6 0.0 copy-start.2
  0.6 0.0 copy-start.1
  0.6 64.7 %shard_map.60 = bf16[256,4096]{1,0:T(8,128)(2,1)} custom-call(bf16[256,8192]{1,0:T(8,128)(2,1)} %grad.3), custom_call_target="tpu_custom_call" | custom-call | tf_op jit(solution)/shard_map/pallas_call | solution.py:72
  65.4 3.3 %collective-permute-start.2 = (bf16[256,4096]{1,0:T(8,128)(2,1)}, bf16[256,4096]{1,0:T(8,128)(2,1)S(1)}, u32[]{:S(2)}, u32[]{:S(2)}) collective-permute-start(bf16[256,4096]{1,0:T(8,128)(2,1)} %shard_map.60), channel_id=1, source_target_pairs={{0,1},{1,0},{2,3},{3,2},{4,5},{5,4},{6,7},{7,6},{8,9},{9,8},{10,11... | collective-permute-start | bytes 6291464 | tf_op jit(solution)/shard_map/ppermute | solution.py:44
  69.3 0.0 copy-done.2
  69.4 0.1 copy.6
  69.5 0.1 collective-permute-start
  69.6 0.0 copy-done.1
  69.7 0.6 collective-permute-start.1
  70.3 0.0 copy-start
  70.3 2.2 %copy-done = bf16[256,8192]{1,0:T(8,128)(2,1)S(1)} copy-done((bf16[256,8192]{1,0:T(8,128)(2,1)S(1)}, bf16[256,8192]{1,0:T(8,128)(2,1)}, u32[]{:S(2)}) %copy-start) | copy-done | bytes 4194328
  72.5 1.8 %shard_map.59 = (bf16[4,512,256]{2,1,0:T(8,128)(2,1)S(1)}, bf16[4,512,256]{2,1,0:T(8,128)(2,1)S(1)}, bf16[4,512,256]{2,1,0:T(8,128)(2,1)S(1)}, bf16[4,512,256]{2,1,0:T(8,128)(2,1)S(1)}, bf16[512,64]{1,0:T(8,128)(2,1)S(1)}) custom-call(bf16[512,256]{1,0:T(8,128)(2,1)S(1)} %select_bitcast_fusion.lat, bf16[256,8192]{1,0:T(8,128)(2,1)S(1)} %copy-done), custom_call_target="tpu_custom_call" | custom-call | flops 1073741824 | bytes 6291456 | tf_op jit(solution)/shard_map/pallas_call | solution.py:122
  74.3 0.0 collective-permute-done.lat
  74.3 0.0 collective-permute-done.1.mom_other
  74.3 0.0 collective-permute-done.2.grad
  74.3 0.7 shard_map.64
  75.0 1.1 collective-permute-start.5
  76.1 0.7 shard_map.63
  76.8 0.5 collective-permute-start.4
  77.3 0.7 shard_map.62
  78.0 1.3 collective-permute-start.3
  79.3 0.7 shard_map.61
  80.0 9.0 %collective-permute-done.5 = bf16[4,512,256]{2,1,0:T(8,128)(2,1)S(1)} collective-permute-done((bf16[4,512,256]{2,1,0:T(8,128)(2,1)S(1)}, bf16[4,512,256]{2,1,0:T(8,128)(2,1)S(1)}, u32[]{:S(2)}, u32[]{:S(2)}) %collective-permute-start.5) | collective-permute-done | bytes 1048608 | tf_op jit(solution)/shard_map/ppermute | solution.py:40
  89.0 14.2 %collective-permute-done.4 = bf16[4,512,256]{2,1,0:T(8,128)(2,1)S(1)} collective-permute-done((bf16[4,512,256]{2,1,0:T(8,128)(2,1)S(1)}, bf16[4,512,256]{2,1,0:T(8,128)(2,1)S(1)}, u32[]{:S(2)}, u32[]{:S(2)}) %collective-permute-start.4) | collective-permute-done | bytes 1048608 | tf_op jit(solution)/shard_map/ppermute | solution.py:40
  103.3 0.0 collective-permute-done.3
  103.3 0.4 fusion.2
  103.7 0.1 slice_bitcast_fusion.3
  103.8 2.5 %collective-permute-start.6 = (bf16[512,256]{1,0:T(8,128)(2,1)S(1)}, bf16[512,256]{1,0:T(8,128)(2,1)S(1)}, u32[]{:S(2)}, u32[]{:S(2)}) collective-permute-start(bf16[512,256]{1,0:T(8,128)(2,1)S(1)} %get-tuple-element.14), channel_id=1, source_target_pairs={{0,16},{1,5},{2,18},{3,7},{4,20},{5,1},{6,22},{7,3},{8,24},{9,13},... | collective-permute-start | bytes 786440 | tf_op jit(solution)/shard_map/ppermute | solution.py:40
  106.3 0.8 collective-permute-start.8
  107.2 0.6 collective-permute-start.7
  107.8 3.1 %collective-permute-done.6 = bf16[512,256]{1,0:T(8,128)(2,1)S(1)} collective-permute-done((bf16[512,256]{1,0:T(8,128)(2,1)S(1)}, bf16[512,256]{1,0:T(8,128)(2,1)S(1)}, u32[]{:S(2)}, u32[]{:S(2)}) %collective-permute-start.6) | collective-permute-done | bytes 262176 | tf_op jit(solution)/shard_map/ppermute | solution.py:40
  110.9 2.6 %collective-permute-done.8 = bf16[512,256]{1,0:T(8,128)(2,1)S(1)} collective-permute-done((bf16[512,256]{1,0:T(8,128)(2,1)S(1)}, bf16[512,256]{1,0:T(8,128)(2,1)S(1)}, u32[]{:S(2)}, u32[]{:S(2)}) %collective-permute-start.8) | collective-permute-done | bytes 262176 | tf_op jit(solution)/shard_map/ppermute | solution.py:40
  113.5 0.4 collective-permute-done.7
  113.9 0.1 fusion.1
  114.0 17.4 %all_to_all.15 = bf16[8,64,256]{2,1,0:T(8,128)(2,1)S(1)} all-to-all(bf16[8,64,256]{2,1,0:T(8,128)(2,1)S(1)} %bitcast.19), channel_id=1, replica_groups=mesh['z'=8,'y'=4,'x'=4,'c'=2] {'z'}, dimensions={0} | all-to-all | bytes 524288 | tf_op jit(solution)/shard_map/all_to_all | solution.py:261
  131.4 11.8 %all_to_all.16 = bf16[8,64,256]{2,1,0:T(8,128)(2,1)S(1)} all-to-all(bf16[8,64,256]{2,1,0:T(8,128)(2,1)S(1)} %broadcast_in_dim.16), channel_id=1, replica_groups=mesh['z'=8,'y'=4,'x'=4,'c'=2] {'z'}, dimensions={0} | all-to-all | bytes 524288 | tf_op jit(solution)/shard_map/all_to_all | solution.py:263
  143.3 6.0 %shard_map.65 = bf16[32,2,16,256]{3,2,1,0:T(8,128)(2,1)S(1)} custom-call(bf16[512,256]{1,0:T(8,128)(2,1)S(1)} %bitcast.18), custom_call_target="tpu_custom_call" | custom-call | tf_op jit(solution)/shard_map/pallas_call | solution.py:211
  149.3 20.0 %all_to_all.17.returned = bf16[32,2,16,256]{3,2,1,0:T(8,128)(2,1)S(1)} all-to-all(bf16[32,2,16,256]{3,2,1,0:T(8,128)(2,1)S(1)} %shard_map.65), channel_id=1, replica_groups=mesh['z'=8,'y'=4,'x'=4,'c'=2] {'c','y','x'}, dimensions={0} | all-to-all | bytes 1048576 | tf_op jit(solution)/shard_map/all_to_all | solution.py:267
  169.3 0.9 shard_map.66
  (5 shorter events, 0.1 us)
Async XLA Ops:
  0.6 68.7 %copy-start.2 = (bf16[256,512]{1,0:T(8,128)(2,1)S(1)}, bf16[256,512]{1,0:T(8,128)(2,1)}, u32[]{:S(2)}) copy-start(bf16[256,512]{1,0:T(8,128)(2,1)} %param.4) | copy-start | bytes 786436
  0.6 69.0 %copy-start.1 = (f32[16,8192]{1,0:T(8,128)S(1)}, f32[16,8192]{1,0:T(8,128)}, u32[]{:S(2)}) copy-start(f32[16,8192]{1,0:T(8,128)} %param.7) | copy-start | bytes 1572868
  65.4 8.9 %collective-permute-start.2 = (bf16[256,4096]{1,0:T(8,128)(2,1)}, bf16[256,4096]{1,0:T(8,128)(2,1)S(1)}, u32[]{:S(2)}, u32[]{:S(2)}) collective-permute-start(bf16[256,4096]{1,0:T(8,128)(2,1)} %shard_map.60), channel_id=1, source_target_pairs={{0,1},{1,0},{2,3},{3,2},{4,5},{5,4},{6,7},{7,6},{8,9},{9,8},{10,11... | collective-permute-start | bytes 6291464 | tf_op jit(solution)/shard_map/ppermute | solution.py:44
  69.5 4.7 %collective-permute-start = (bf16[512,256]{1,0:T(8,128)(2,1)S(1)}, bf16[512,256]{1,0:T(8,128)(2,1)S(1)}, u32[]{:S(2)}, u32[]{:S(2)}) collective-permute-start(bf16[512,256]{1,0:T(8,128)(2,1)S(1)} %select_bitcast_fusion.lat), channel_id=1, source_target_pairs={{0,1},{1,0},{2,3},{3,2},{4,5},{5,4},{6,7},{7,6},{8,9},{9,8},{10,11... | collective-permute-start | bytes 786440 | tf_op jit(solution)/shard_map/ppermute | solution.py:44
  69.7 4.6 %collective-permute-start.1 = (f32[16,4096]{1,0:T(8,128)S(1)}, f32[16,4096]{1,0:T(8,128)S(1)}, u32[]{:S(2)}, u32[]{:S(2)}) collective-permute-start(f32[16,4096]{1,0:T(8,128)S(1)} %get-tuple-element.17), channel_id=1, source_target_pairs={{0,1},{1,0},{2,3},{3,2},{4,5},{5,4},{6,7},{7,6},{8,9},{9,8},{10,11... | collective-permute-start | bytes 786440 | tf_op jit(solution)/shard_map/ppermute | solution.py:44
  70.3 2.2 %copy-start = (bf16[256,8192]{1,0:T(8,128)(2,1)S(1)}, bf16[256,8192]{1,0:T(8,128)(2,1)}, u32[]{:S(2)}) copy-start(bf16[256,8192]{1,0:T(8,128)(2,1)} %grad.3) | copy-start | bytes 12582916
  75.0 14.0 %collective-permute-start.5 = (bf16[4,512,256]{2,1,0:T(8,128)(2,1)S(1)}, bf16[4,512,256]{2,1,0:T(8,128)(2,1)S(1)}, u32[]{:S(2)}, u32[]{:S(2)}) collective-permute-start(bf16[4,512,256]{2,1,0:T(8,128)(2,1)S(1)} %shard_map.64), channel_id=1, source_target_pairs={{0,6},{1,25},{2,0},{3,27},{4,2},{5,29},{6,4},{7,31},{8,14},{9,1},{... | collective-permute-start | bytes 3145736 | tf_op jit(solution)/shard_map/ppermute | solution.py:40
  76.8 26.5 %collective-permute-start.4 = (bf16[4,512,256]{2,1,0:T(8,128)(2,1)S(1)}, bf16[4,512,256]{2,1,0:T(8,128)(2,1)S(1)}, u32[]{:S(2)}, u32[]{:S(2)}) collective-permute-start(bf16[4,512,256]{2,1,0:T(8,128)(2,1)S(1)} %shard_map.63), channel_id=1, source_target_pairs={{0,2},{1,9},{2,4},{3,11},{4,6},{5,13},{6,0},{7,15},{8,10},{9,17},{... | collective-permute-start | bytes 3145736 | tf_op jit(solution)/shard_map/ppermute | solution.py:40
  78.0 25.2 %collective-permute-start.3 = (bf16[4,512,256]{2,1,0:T(8,128)(2,1)S(1)}, bf16[4,512,256]{2,1,0:T(8,128)(2,1)S(1)}, u32[]{:S(2)}, u32[]{:S(2)}) collective-permute-start(bf16[4,512,256]{2,1,0:T(8,128)(2,1)S(1)} %shard_map.62), channel_id=1, source_target_pairs={{0,4},{1,17},{2,6},{3,19},{4,0},{5,21},{6,2},{7,23},{8,12},{9,25},... | collective-permute-start | bytes 3145736 | tf_op jit(solution)/shard_map/ppermute | solution.py:40
  103.8 7.1 %collective-permute-start.6 = (bf16[512,256]{1,0:T(8,128)(2,1)S(1)}, bf16[512,256]{1,0:T(8,128)(2,1)S(1)}, u32[]{:S(2)}, u32[]{:S(2)}) collective-permute-start(bf16[512,256]{1,0:T(8,128)(2,1)S(1)} %get-tuple-element.14), channel_id=1, source_target_pairs={{0,16},{1,5},{2,18},{3,7},{4,20},{5,1},{6,22},{7,3},{8,24},{9,13},... | collective-permute-start | bytes 786440 | tf_op jit(solution)/shard_map/ppermute | solution.py:40
  106.3 7.2 %collective-permute-start.8 = (bf16[512,256]{1,0:T(8,128)(2,1)S(1)}, bf16[512,256]{1,0:T(8,128)(2,1)S(1)}, u32[]{:S(2)}, u32[]{:S(2)}) collective-permute-start(bf16[512,256]{1,0:T(8,128)(2,1)S(1)} %get-tuple-element.15), channel_id=1, source_target_pairs={{0,24},{1,7},{2,26},{3,1},{4,28},{5,3},{6,30},{7,5},{8,0},{9,15},{... | collective-permute-start | bytes 786440 | tf_op jit(solution)/shard_map/ppermute | solution.py:40
  107.2 6.7 %collective-permute-start.7 = (bf16[512,256]{1,0:T(8,128)(2,1)S(1)}, bf16[512,256]{1,0:T(8,128)(2,1)S(1)}, u32[]{:S(2)}, u32[]{:S(2)}) collective-permute-start(bf16[512,256]{1,0:T(8,128)(2,1)S(1)} %get-tuple-element.16), channel_id=1, source_target_pairs={{0,8},{1,3},{2,10},{3,5},{4,12},{5,7},{6,14},{7,1},{8,16},{9,11},{... | collective-permute-start | bytes 786440 | tf_op jit(solution)/shard_map/ppermute | solution.py:40

commit v5 on v4

--- a/solution.py
+++ b/solution.py
@@ -18,6 +18,7 @@
 COEF_A, COEF_B, COEF_C = 3.4445, -4.775, 2.0315
 DECAY = 0.95
 VMEM = 16 * 1024 * 1024
+LARGE = 48 * 1024 * 1024
 bf16, f32 = jnp.bfloat16, jnp.float32
 
 
@@ -73,9 +74,9 @@
         column_copy_kernel,
         out_shape=jax.ShapeDtypeStruct((rows, columns // NC), grad.dtype),
         in_specs=[pl.BlockSpec(memory_space=pl.ANY)],
-        out_specs=pl.BlockSpec(memory_space=pl.ANY),
+        out_specs=pl.BlockSpec(memory_space=pltpu.VMEM),
         scratch_shapes=[pltpu.SemaphoreType.DMA((8,))],
-        compiler_params=pltpu.CompilerParams(vmem_limit_bytes=62 * 1024 * 1024),
+        compiler_params=pltpu.CompilerParams(vmem_limit_bytes=LARGE),
     )(grad)
 
 
@@ -128,7 +129,7 @@
             pltpu.VMEM((RING * RING, tokens, HD), bf16),
             pltpu.SemaphoreType.DMA((RING * RING,)),
         ],
-        compiler_params=pltpu.CompilerParams(vmem_limit_bytes=VMEM),
+        compiler_params=pltpu.CompilerParams(vmem_limit_bytes=LARGE),
         cost_estimate=pl.CostEstimate(
             flops=2 * RING * RING * features * HD * tokens,
             bytes_accessed=RING * RING * (tokens + features) * HD * 2,
@@ -137,34 +138,41 @@
     )(lat, grad)
 
 
-def block_kernel(near, own, unit, lat, mom_own, mom_other, grad, out):
-    for far in range(RING):
-        at = pl.ds(head_columns(near, far), HD)
-        high, low = [], []
-        for ref in (mom_own, mom_other):
-            value = (DECAY / NZ) * ref[:, at]
-            high.append(value.astype(bf16))
-            low.append((value - high[-1].astype(f32)).astype(bf16))
-        mom = jnp.concatenate(high + low, axis=0)
-        other = jnp.dot(lat[...], grad[:, at], preferred_element_type=f32)
-        added = jnp.dot(unit[...], mom, preferred_element_type=f32)
-        total = own[far].astype(f32) + other.astype(bf16).astype(f32) + added
-        out[far] = total.astype(out.dtype)
-
-
-def block(near, own, unit, lat, mom_own, mom_other, grad):
+def block_kernel(tiles, unit, lat, mom_own, mom_other, grad, *refs):
+    operands, outs = refs[: 1 + max(t[0] for t in tiles)], refs[1 + max(t[0] for t in tiles) :]
+    for operand, result, near, fars in tiles:
+        for place, far in enumerate(fars):
+            at = pl.ds(head_columns(near, far), HD)
+            high, low = [], []
+            for ref in (mom_own, mom_other):
+                value = (DECAY / NZ) * ref[:, at]
+                high.append(value.astype(bf16))
+                low.append((value - high[-1].astype(f32)).astype(bf16))
+            mom = jnp.concatenate(high + low, axis=0)
+            other = jnp.dot(lat[...], grad[:, at], preferred_element_type=f32)
+            added = jnp.dot(unit[...], mom, preferred_element_type=f32)
+            total = operands[operand][far].astype(f32) + other.astype(bf16).astype(f32) + added
+            outs[result][place] = total.astype(outs[result].dtype)
+
+
+def block(own, which, unit, lat, mom_own, mom_other, grad):
     features, tokens = lat.shape
-    dtype = f32 if near == 0 else bf16
-    return pl.pallas_call(
-        functools.partial(block_kernel, near),
-        out_shape=jax.ShapeDtypeStruct(own.shape, dtype),
+    nears = sorted({near for near, _ in which})
+    tiles = [(nears.index(near), k, near, fars) for k, (near, fars) in enumerate(which)]
+    heads = sum(len(fars) for _, fars in which)
+    return pl.pallas_call(
+        functools.partial(block_kernel, tiles),
+        out_shape=[
+            jax.ShapeDtypeStruct((len(fars), features, HD), f32 if near == 0 else bf16)
+            for near, fars in which
+        ],
         compiler_params=pltpu.CompilerParams(vmem_limit_bytes=VMEM),
         cost_estimate=pl.CostEstimate(
-            flops=2 * RING * features * HD * (tokens + unit.shape[1]),
-            bytes_accessed=RING * (tokens + 2 * features) * HD * 2,
+            flops=2 * heads * features * HD * (tokens + unit.shape[1]),
+            bytes_accessed=heads * (tokens + 2 * features) * HD * 2,
             transcendentals=0,
         ),
-    )(own, unit, lat, mom_own, mom_other, grad)
+    )(unit, lat, mom_own, mom_other, grad, *[own[near] for near in nears])
 
 
 def split(value):
@@ -251,12 +259,18 @@
     mom_other = swap_cores(lax.dynamic_slice_in_dim(momentum, (1 - c) * columns, columns, 1))
 
     *own, unit = own_products(lat_own, latent_grad, momentum.shape[0])
-    blocks = [block(k, own[k], unit, lat_other, mom_own, mom_other, grad_other) for k in range(RING)]
-    got = [shift(blocks[k], 0, k) for k in (2, 1, 3)]
-    total = blocks[0] + sum(g.astype(f32) for g in got)
-
-    got = [shift(total[k].astype(bf16), 1, k) for k in (2, 1, 3)]
-    head = (total[0] + sum(g.astype(f32) for g in got)).astype(bf16)
+    operands = (unit, lat_other, mom_own, mom_other, grad_other)
+    order, rest = (2, 1, 3), (1, 2, 3)
+    on = [shift(block(own, [(k, rest)], *operands)[0], 0, k) for k in order]
+    *stay, kept_stay, kept_on = block(
+        own, [(k, (0,)) for k in order] + [(0, (0,)), (0, rest)], *operands
+    )
+    stay = [shift(value, 0, k) for value, k in zip(stay, order)]
+
+    total = kept_on + sum(value.astype(f32) for value in on)
+    got = [shift(total[k - 1].astype(bf16), 1, k) for k in order]
+    head = kept_stay[0] + sum(value[0].astype(f32) for value in stay)
+    head = (head + sum(value.astype(f32) for value in got)).astype(bf16)
 
     pieces = lax.all_to_all(head.reshape(NZ, -1, HD), "z", 0, 0, tiled=True)
     piece = jnp.sum(pieces.astype(f32), axis=0).astype(bf16)

time: 170 us -> 104 us (0.61)
  Pallas kernels: 76.2 us -> 15.7 us
  waiting for transfers between devices: 29.4 us -> 21.7 us
  local copies, waits for them, and re-layouts: 2.44 us -> 0.25 us
  starting transfers between devices: 10.9 us -> 12.9 us
  blocking collectives: 49.2 us -> 51.1 us
    pallas_call x1, Pallas kernels: 64.7 us -> 3 us  [column_copy(): pl.pallas_call(column_copy_kernel, out_shape=jax.ShapeDtypeStruct((rows,...]
    ppermute x6 -> x9, waiting for transfers between devices: 29.4 us -> 21.6 us  [shift(): return lax.ppermute(value, AXES, pairs)]
    all_to_all x1, blocking collectives: 20 us -> 23 us  [body(): returned = lax.all_to_all(outgoing, PLANE, 0, 0, tiled=True)]
    unnamed x7 -> x5, local copies, waits for them, and re-layouts: 2.33 us -> 0.14 us
    ppermute x6 -> x9, starting transfers between devices: 6.9 us -> 8.91 us  [shift(): return lax.ppermute(value, AXES, pairs)]
  transfers between devices with their start and end apart: 9 -> 12, of which waited for: 5 -> 6; matrix products, arithmetic and copies ran while one was open for 0% -> 1% of each run, Pallas kernels for 2% -> 5%
where the time goes in v5:
time: 104 us
  blocking collectives  51.1 us (49%)
  waiting for transfers between devices  21.7 us (21%)
  Pallas kernels  15.7 us (15%)
  starting transfers between devices  12.9 us (12%)
  between operations  1.44 us (1%)
    all_to_all x1, blocking collectives, body(): returned = lax.all_to_all(outgoing, PLANE, 0, 0, tiled=True)  23 us
    ppermute x9, waiting for transfers between devices, shift(): return lax.ppermute(value, AXES, pairs)  21.6 us
    all_to_all x1, blocking collectives, body(): pieces = lax.all_to_all(head.reshape(NZ, -1, HD), 'z', 0, 0, tiled=True)  15.9 us
    all_to_all x1, blocking collectives, body(): lax.all_to_all(jnp.broadcast_to(piece, (NZ,) + piece.shape), 'z', 0, 0, t...  12.2 us
    ppermute x9, starting transfers between devices, shift(): return lax.ppermute(value, AXES, pairs)  8.91 us
    pallas_call x1, Pallas kernels, newton_schulz(): pl.pallas_call(newton_schulz_kernel, out_shape=jax.ShapeDtypeStruct((owne...  5.96 us
    ppermute x3, starting transfers between devices, swap_cores(): lax.ppermute(value, AXES, [(device_at(z, y, x, c), device_at(z, y, x, 1 -...  4.01 us
    pallas_call x1, Pallas kernels, own_products(): pl.pallas_call(functools.partial(own_kernel, depth), out_shape=[out] * RI...  3.05 us
  transfers between devices with their start and end apart: 12, of which 6 were waited for; matrix products, arithmetic and copies ran while one was open for 1% of the time, Pallas kernels for 5%

profile of v5, /device:TPU:1, one launch (start us, length us, event | category | flops | bytes accessed | tf_op | source)
XLA Modules:
  0.0 104.0 jit_solution(3114431029606491130)
XLA Ops:
  0.6 0.0 copy-start
  0.6 0.0 copy-start.1
  0.6 3.0 %shard_map.60 = bf16[256,4096]{1,0:T(8,128)(2,1)} custom-call(bf16[256,8192]{1,0:T(8,128)(2,1)} %grad.3), custom_call_target="tpu_custom_call" | custom-call | tf_op jit(solution)/shard_map/pallas_call | solution.py:73
  3.7 3.3 %collective-permute-start.2 = (bf16[256,4096]{1,0:T(8,128)(2,1)}, bf16[256,4096]{1,0:T(8,128)(2,1)S(1)}, u32[]{:S(2)}, u32[]{:S(2)}) collective-permute-start(bf16[256,4096]{1,0:T(8,128)(2,1)} %shard_map.60), channel_id=1, source_target_pairs={{0,1},{1,0},{2,3},{3,2},{4,5},{5,4},{6,7},{7,6},{8,9},{9,8},{10,11... | collective-permute-start | bytes 6291464 | tf_op jit(solution)/shard_map/ppermute | solution.py:45
  7.0 0.0 copy-done
  7.0 0.1 collective-permute-start.1
  7.1 0.0 copy-done.1
  7.1 0.1 copy.6
  8.0 0.6 collective-permute-start
  8.5 3.1 %shard_map.59 = (bf16[4,512,256]{2,1,0:T(8,128)(2,1)S(1)}, bf16[4,512,256]{2,1,0:T(8,128)(2,1)S(1)}, bf16[4,512,256]{2,1,0:T(8,128)(2,1)S(1)}, bf16[4,512,256]{2,1,0:T(8,128)(2,1)S(1)}, bf16[512,64]{1,0:T(8,128)(2,1)S(1)}) custom-call(bf16[512,256]{1,0:T(8,128)(2,1)S(1)} %select_bitcast_fusion.lat, bf16[256,8192]{1,0:T(8,128)(2,1)} %grad.3), custom_call_target="tpu_custom_call" | custom-call | flops 1073741824 | bytes 6291456 | tf_op jit(solution)/shard_map/pallas_call | solution.py:123
  11.6 0.0 collective-permute-done.1.mom_other
  11.6 0.0 collective-permute-done.lat
  11.6 0.1 collective-permute-done.2.grad
  11.7 0.6 shard_map.62
  12.3 1.3 %collective-permute-start.6 = (bf16[3,512,256]{2,1,0:T(8,128)(2,1)S(1)}, bf16[3,512,256]{2,1,0:T(8,128)(2,1)S(1)}, u32[]{:S(2)}, u32[]{:S(2)}) collective-permute-start(bf16[3,512,256]{2,1,0:T(8,128)(2,1)S(1)} %shard_map.62), channel_id=1, source_target_pairs={{0,4},{1,17},{2,6},{3,19},{4,0},{5,21},{6,2},{7,23},{8,12},{9,25},... | collective-permute-start | bytes 2359304 | tf_op jit(solution)/shard_map/ppermute | solution.py:41
  13.6 0.6 shard_map.63
  14.1 0.5 collective-permute-start.7
  14.6 0.6 shard_map.64
  15.2 2.4 %collective-permute-start.8 = (bf16[3,512,256]{2,1,0:T(8,128)(2,1)S(1)}, bf16[3,512,256]{2,1,0:T(8,128)(2,1)S(1)}, u32[]{:S(2)}, u32[]{:S(2)}) collective-permute-start(bf16[3,512,256]{2,1,0:T(8,128)(2,1)S(1)} %shard_map.64), channel_id=1, source_target_pairs={{0,6},{1,25},{2,0},{3,27},{4,2},{5,29},{6,4},{7,31},{8,14},{9,1},{... | collective-permute-start | bytes 2359304 | tf_op jit(solution)/shard_map/ppermute | solution.py:41
  17.5 1.1 %shard_map.61 = (bf16[1,512,256]{2,1,0:T(8,128)(2,1)S(1)}, bf16[1,512,256]{2,1,0:T(8,128)(2,1)S(1)}, bf16[1,512,256]{2,1,0:T(8,128)(2,1)S(1)}, f32[1,512,256]{2,1,0:T(8,128)S(1)}, f32[3,512,256]{2,1,0:T(8,128)S(1)}) custom-call(bf16[512,64]{1,0:T(8,128)(2,1)S(1)} %get-tuple-element.12.unit, bf16[512,256]{1,0:T(8,128)(2,1)S(1)} %collective-permute-done.lat, ...), custom_call_target="tpu_custom_call" | custom-call | flops 587202560 | bytes 4587520 | tf_op jit(solution)/shard_map/pallas_call | solution.py:163
  18.6 0.7 collective-permute-start.3
  19.3 0.0 collective-permute-start.4
  19.3 5.7 %collective-permute-done.6 = bf16[3,512,256]{2,1,0:T(8,128)(2,1)S(1)} collective-permute-done((bf16[3,512,256]{2,1,0:T(8,128)(2,1)S(1)}, bf16[3,512,256]{2,1,0:T(8,128)(2,1)S(1)}, u32[]{:S(2)}, u32[]{:S(2)}) %collective-permute-start.6) | collective-permute-done | bytes 786464 | tf_op jit(solution)/shard_map/ppermute | solution.py:41
  25.1 1.0 collective-permute-start.5
  26.1 7.4 %collective-permute-done.7 = bf16[3,512,256]{2,1,0:T(8,128)(2,1)S(1)} collective-permute-done((bf16[3,512,256]{2,1,0:T(8,128)(2,1)S(1)}, bf16[3,512,256]{2,1,0:T(8,128)(2,1)S(1)}, u32[]{:S(2)}, u32[]{:S(2)}) %collective-permute-start.7) | collective-permute-done | bytes 786464 | tf_op jit(solution)/shard_map/ppermute | solution.py:41
  33.4 0.0 collective-permute-done.8
  33.4 0.5 add_convert_fusion
  33.9 0.1 slice_bitcast_fusion.2
  34.0 0.1 collective-permute-start.10
  34.1 2.7 %collective-permute-start.11 = (bf16[512,256]{1,0:T(8,128)(2,1)S(1)}, bf16[512,256]{1,0:T(8,128)(2,1)S(1)}, u32[]{:S(2)}, u32[]{:S(2)}) collective-permute-start(bf16[512,256]{1,0:T(8,128)(2,1)S(1)} %get-tuple-element.23), channel_id=1, source_target_pairs={{0,24},{1,7},{2,26},{3,1},{4,28},{5,3},{6,30},{7,5},{8,0},{9,15},{... | collective-permute-start | bytes 786440 | tf_op jit(solution)/shard_map/ppermute | solution.py:41
  36.7 0.0 collective-permute-done.3
  36.7 0.4 collective-permute-start.9
  37.1 1.9 %collective-permute-done.4 = bf16[1,512,256]{2,1,0:T(8,128)(2,1)S(1)} collective-permute-done((bf16[1,512,256]{2,1,0:T(8,128)(2,1)S(1)}, bf16[1,512,256]{2,1,0:T(8,128)(2,1)S(1)}, u32[]{:S(2)}, u32[]{:S(2)}) %collective-permute-start.4) | collective-permute-done | bytes 262176 | tf_op jit(solution)/shard_map/ppermute | solution.py:41
  39.1 0.0 collective-permute-done.5
  39.1 3.4 %collective-permute-done.10 = bf16[512,256]{1,0:T(8,128)(2,1)S(1)} collective-permute-done((bf16[512,256]{1,0:T(8,128)(2,1)S(1)}, bf16[512,256]{1,0:T(8,128)(2,1)S(1)}, u32[]{:S(2)}, u32[]{:S(2)}) %collective-permute-start.10) | collective-permute-done | bytes 262176 | tf_op jit(solution)/shard_map/ppermute | solution.py:41
  42.5 0.0 collective-permute-done.11
  42.5 3.1 %collective-permute-done.9 = bf16[512,256]{1,0:T(8,128)(2,1)S(1)} collective-permute-done((bf16[512,256]{1,0:T(8,128)(2,1)S(1)}, bf16[512,256]{1,0:T(8,128)(2,1)S(1)}, u32[]{:S(2)}, u32[]{:S(2)}) %collective-permute-start.9) | collective-permute-done | bytes 262176 | tf_op jit(solution)/shard_map/ppermute | solution.py:41
  45.6 0.3 fusion
  45.9 15.9 %all_to_all.15 = bf16[8,64,256]{2,1,0:T(8,128)(2,1)S(1)} all-to-all(bf16[8,64,256]{2,1,0:T(8,128)(2,1)S(1)} %bitcast.17), channel_id=1, replica_groups=mesh['z'=8,'y'=4,'x'=4,'c'=2] {'z'}, dimensions={0} | all-to-all | bytes 524288 | tf_op jit(solution)/shard_map/all_to_all | solution.py:275
  61.8 12.2 %all_to_all.16 = bf16[8,64,256]{2,1,0:T(8,128)(2,1)S(1)} all-to-all(bf16[8,64,256]{2,1,0:T(8,128)(2,1)S(1)} %broadcast_in_dim.16), channel_id=1, replica_groups=mesh['z'=8,'y'=4,'x'=4,'c'=2] {'z'}, dimensions={0} | all-to-all | bytes 524288 | tf_op jit(solution)/shard_map/all_to_all | solution.py:277
  74.1 6.0 %shard_map.65 = bf16[32,2,16,256]{3,2,1,0:T(8,128)(2,1)S(1)} custom-call(bf16[512,256]{1,0:T(8,128)(2,1)S(1)} %bitcast.16), custom_call_target="tpu_custom_call" | custom-call | tf_op jit(solution)/shard_map/pallas_call | solution.py:219
  80.0 23.0 %all_to_all.17.returned = bf16[32,2,16,256]{3,2,1,0:T(8,128)(2,1)S(1)} all-to-all(bf16[32,2,16,256]{3,2,1,0:T(8,128)(2,1)S(1)} %shard_map.65), channel_id=1, replica_groups=mesh['z'=8,'y'=4,'x'=4,'c'=2] {'c','y','x'}, dimensions={0} | all-to-all | bytes 1048576 | tf_op jit(solution)/shard_map/all_to_all | solution.py:281
  103.0 0.9 shard_map.66
  (5 shorter events, 0.1 us)
Async XLA Ops:
  0.6 6.4 %copy-start = (f32[16,8192]{1,0:T(8,128)S(1)}, f32[16,8192]{1,0:T(8,128)}, u32[]{:S(2)}) copy-start(f32[16,8192]{1,0:T(8,128)} %param.7) | copy-start | bytes 1572868
  0.6 6.5 %copy-start.1 = (bf16[256,512]{1,0:T(8,128)(2,1)S(1)}, bf16[256,512]{1,0:T(8,128)(2,1)}, u32[]{:S(2)}) copy-start(bf16[256,512]{1,0:T(8,128)(2,1)} %param.4) | copy-start | bytes 786436
  3.7 8.1 %collective-permute-start.2 = (bf16[256,4096]{1,0:T(8,128)(2,1)}, bf16[256,4096]{1,0:T(8,128)(2,1)S(1)}, u32[]{:S(2)}, u32[]{:S(2)}) collective-permute-start(bf16[256,4096]{1,0:T(8,128)(2,1)} %shard_map.60), channel_id=1, source_target_pairs={{0,1},{1,0},{2,3},{3,2},{4,5},{5,4},{6,7},{7,6},{8,9},{9,8},{10,11... | collective-permute-start | bytes 6291464 | tf_op jit(solution)/shard_map/ppermute | solution.py:45
  7.0 4.6 %collective-permute-start.1 = (f32[16,4096]{1,0:T(8,128)S(1)}, f32[16,4096]{1,0:T(8,128)S(1)}, u32[]{:S(2)}, u32[]{:S(2)}) collective-permute-start(f32[16,4096]{1,0:T(8,128)S(1)} %get-tuple-element.25), channel_id=1, source_target_pairs={{0,1},{1,0},{2,3},{3,2},{4,5},{5,4},{6,7},{7,6},{8,9},{9,8},{10,11... | collective-permute-start | bytes 786440 | tf_op jit(solution)/shard_map/ppermute | solution.py:45
  8.0 3.6 %collective-permute-start = (bf16[512,256]{1,0:T(8,128)(2,1)S(1)}, bf16[512,256]{1,0:T(8,128)(2,1)S(1)}, u32[]{:S(2)}, u32[]{:S(2)}) collective-permute-start(bf16[512,256]{1,0:T(8,128)(2,1)S(1)} %select_bitcast_fusion.lat), channel_id=1, source_target_pairs={{0,1},{1,0},{2,3},{3,2},{4,5},{5,4},{6,7},{7,6},{8,9},{9,8},{10,11... | collective-permute-start | bytes 786440 | tf_op jit(solution)/shard_map/ppermute | solution.py:45
  12.3 12.8 %collective-permute-start.6 = (bf16[3,512,256]{2,1,0:T(8,128)(2,1)S(1)}, bf16[3,512,256]{2,1,0:T(8,128)(2,1)S(1)}, u32[]{:S(2)}, u32[]{:S(2)}) collective-permute-start(bf16[3,512,256]{2,1,0:T(8,128)(2,1)S(1)} %shard_map.62), channel_id=1, source_target_pairs={{0,4},{1,17},{2,6},{3,19},{4,0},{5,21},{6,2},{7,23},{8,12},{9,25},... | collective-permute-start | bytes 2359304 | tf_op jit(solution)/shard_map/ppermute | solution.py:41
  14.1 19.3 %collective-permute-start.7 = (bf16[3,512,256]{2,1,0:T(8,128)(2,1)S(1)}, bf16[3,512,256]{2,1,0:T(8,128)(2,1)S(1)}, u32[]{:S(2)}, u32[]{:S(2)}) collective-permute-start(bf16[3,512,256]{2,1,0:T(8,128)(2,1)S(1)} %shard_map.63), channel_id=1, source_target_pairs={{0,2},{1,9},{2,4},{3,11},{4,6},{5,13},{6,0},{7,15},{8,10},{9,17},{... | collective-permute-start | bytes 2359304 | tf_op jit(solution)/shard_map/ppermute | solution.py:41
  15.2 18.3 %collective-permute-start.8 = (bf16[3,512,256]{2,1,0:T(8,128)(2,1)S(1)}, bf16[3,512,256]{2,1,0:T(8,128)(2,1)S(1)}, u32[]{:S(2)}, u32[]{:S(2)}) collective-permute-start(bf16[3,512,256]{2,1,0:T(8,128)(2,1)S(1)} %shard_map.64), channel_id=1, source_target_pairs={{0,6},{1,25},{2,0},{3,27},{4,2},{5,29},{6,4},{7,31},{8,14},{9,1},{... | collective-permute-start | bytes 2359304 | tf_op jit(solution)/shard_map/ppermute | solution.py:41
  18.6 18.1 %collective-permute-start.3 = (bf16[1,512,256]{2,1,0:T(8,128)(2,1)S(1)}, bf16[1,512,256]{2,1,0:T(8,128)(2,1)S(1)}, u32[]{:S(2)}, u32[]{:S(2)}) collective-permute-start(bf16[1,512,256]{2,1,0:T(8,128)(2,1)S(1)} %get-tuple-element.18), channel_id=1, source_target_pairs={{0,4},{1,17},{2,6},{3,19},{4,0},{5,21},{6,2},{7,23},{8,12},{9,25},... | collective-permute-start | bytes 786440 | tf_op jit(solution)/shard_map/ppermute | solution.py:41
  19.3 19.8 %collective-permute-start.4 = (bf16[1,512,256]{2,1,0:T(8,128)(2,1)S(1)}, bf16[1,512,256]{2,1,0:T(8,128)(2,1)S(1)}, u32[]{:S(2)}, u32[]{:S(2)}) collective-permute-start(bf16[1,512,256]{2,1,0:T(8,128)(2,1)S(1)} %get-tuple-element.19), channel_id=1, source_target_pairs={{0,2},{1,9},{2,4},{3,11},{4,6},{5,13},{6,0},{7,15},{8,10},{9,17},{... | collective-permute-start | bytes 786440 | tf_op jit(solution)/shard_map/ppermute | solution.py:41
  25.1 14.0 %collective-permute-start.5 = (bf16[1,512,256]{2,1,0:T(8,128)(2,1)S(1)}, bf16[1,512,256]{2,1,0:T(8,128)(2,1)S(1)}, u32[]{:S(2)}, u32[]{:S(2)}) collective-permute-start(bf16[1,512,256]{2,1,0:T(8,128)(2,1)S(1)} %get-tuple-element.20), channel_id=1, source_target_pairs={{0,6},{1,25},{2,0},{3,27},{4,2},{5,29},{6,4},{7,31},{8,14},{9,1},{... | collective-permute-start | bytes 786440 | tf_op jit(solution)/shard_map/ppermute | solution.py:41
  34.0 8.5 %collective-permute-start.10 = (bf16[512,256]{1,0:T(8,128)(2,1)S(1)}, bf16[512,256]{1,0:T(8,128)(2,1)S(1)}, u32[]{:S(2)}, u32[]{:S(2)}) collective-permute-start(bf16[512,256]{1,0:T(8,128)(2,1)S(1)} %get-tuple-element.24), channel_id=1, source_target_pairs={{0,8},{1,3},{2,10},{3,5},{4,12},{5,7},{6,14},{7,1},{8,16},{9,11},{... | collective-permute-start | bytes 786440 | tf_op jit(solution)/shard_map/ppermute | solution.py:41
  34.1 8.4 %collective-permute-start.11 = (bf16[512,256]{1,0:T(8,128)(2,1)S(1)}, bf16[512,256]{1,0:T(8,128)(2,1)S(1)}, u32[]{:S(2)}, u32[]{:S(2)}) collective-permute-start(bf16[512,256]{1,0:T(8,128)(2,1)S(1)} %get-tuple-element.23), channel_id=1, source_target_pairs={{0,24},{1,7},{2,26},{3,1},{4,28},{5,3},{6,30},{7,5},{8,0},{9,15},{... | collective-permute-start | bytes 786440 | tf_op jit(solution)/shard_map/ppermute | solution.py:41
  36.7 8.9 %collective-permute-start.9 = (bf16[512,256]{1,0:T(8,128)(2,1)S(1)}, bf16[512,256]{1,0:T(8,128)(2,1)S(1)}, u32[]{:S(2)}, u32[]{:S(2)}) collective-permute-start(bf16[512,256]{1,0:T(8,128)(2,1)S(1)} %get-tuple-element.22), channel_id=1, source_target_pairs={{0,16},{1,5},{2,18},{3,7},{4,20},{5,1},{6,22},{7,3},{8,24},{9,13},... | collective-permute-start | bytes 786440 | tf_op jit(solution)/shard_map/ppermute | solution.py:41

commit v6 on v5

v6 whole, which is shorter than its diff:
```python
import functools
import math

import jax
import jax.numpy as jnp
from jax import lax
from jax.experimental import pallas as pl
from jax.experimental.pallas import tpu as pltpu
from jax.sharding import Mesh
from jax.sharding import PartitionSpec as P

HD = 256
NS_STEPS = 5
NZ, NY, NX, NC = 8, 4, 4, 2
RING = 4
AXES = ("z", "y", "x", "c")
PLANE = ("c", "y", "x")
COEF_A, COEF_B, COEF_C = 3.4445, -4.775, 2.0315
DECAY = 0.95
VMEM = 16 * 1024 * 1024
LARGE = 48 * 1024 * 1024
bf16, f32 = jnp.bfloat16, jnp.float32


def device_at(z, y, x, c):
    return ((z * NY + y) * NX + x) * NC + c


def every_device():
    return [(z, y, x, c) for z in range(NZ) for y in range(NY) for x in range(NX) for c in range(NC)]


def shift(value, axis, distance):
    pairs = []
    for z, y, x, c in every_device():
        if axis == c:
            to = (y, (x + distance) % NX)
        else:
            to = ((y + distance) % NY, x)
        pairs.append((device_at(z, y, x, c), device_at(z, *to, c)))
    return lax.ppermute(value, AXES, pairs)


def swap_cores(value):
    return lax.ppermute(
        value, AXES, [(device_at(z, y, x, c), device_at(z, y, x, 1 - c)) for z, y, x, c in every_device()]
    )


def places():
    core, y, x = lax.axis_index("c"), lax.axis_index("y"), lax.axis_index("x")
    return jnp.where(core == 0, x, y), jnp.where(core == 0, y, x)


def head_columns(near, far, other=False):
    first, second = places()
    if other:
        first, second = second, first
    head = lax.rem(first + near, RING) * RING + lax.rem(second + far, RING)
    return pl.multiple_of(head * HD, HD)


def gather(grad, held, sems, nears, other):
    core = lax.axis_index("c")
    half = grad.shape[1] // NC
    base = (1 - core if other else core) * half
    copies = []
    for near in nears:
        for far in range(RING):
            k = len(copies)
            start = pl.multiple_of(base + head_columns(near, far, other), HD)
            copies.append(
                pltpu.make_async_copy(
                    grad.at[:, pl.ds(start, HD)], held.at[:, pl.ds(k * HD, HD)], sems.at[k]
                )
            )
            copies[-1].start()
    return copies


def first_kernel(nears, counts, latent, momentum, grad, lat, mom_own, mom_other, unit, piece, sems):
    copies = gather(grad, piece, sems, nears, True)
    core = lax.axis_index("c")
    slots, features = latent.shape
    live = lax.broadcasted_iota(jnp.int32, (slots, features), 0) < counts[0]
    lat[...] = jnp.where(live, latent[...], jnp.zeros_like(latent)).T
    depth, half = momentum.shape[0], momentum.shape[1] // NC
    for out, which in ((mom_own, core), (mom_other, 1 - core)):
        value = (DECAY / NZ) * momentum[:, pl.ds(pl.multiple_of(which * half, half), half)]
        high = value.astype(bf16)
        out[:depth, :] = high
        out[depth:, :] = (value - high.astype(f32)).astype(bf16)
    here = lax.axis_index("y") * NX + lax.axis_index("x")
    row = lax.broadcasted_iota(jnp.int32, unit.shape, 0)
    at = lax.broadcasted_iota(jnp.int32, unit.shape, 1)
    core_of = jnp.where(at < 2 * depth, core, 1 - core)
    unit[...] = (row == (here * NC + core_of) * depth + at % depth).astype(f32).astype(bf16)
    for copy in copies:
        copy.wait()


def first(counts, latent, momentum, grad, nears):
    slots, features = latent.shape
    depth, columns = momentum.shape
    heads = RING * len(nears)
    vmem = pl.BlockSpec(memory_space=pltpu.VMEM)
    mom = jax.ShapeDtypeStruct((2 * depth, columns // NC), bf16)
    return pl.pallas_call(
        functools.partial(first_kernel, nears),
        out_shape=[
            jax.ShapeDtypeStruct((features, slots), bf16),
            mom,
            mom,
            jax.ShapeDtypeStruct((features, 4 * depth), bf16),
            jax.ShapeDtypeStruct((slots, heads * HD), bf16),
        ],
        in_specs=[pl.BlockSpec(memory_space=pltpu.SMEM), vmem, vmem, pl.BlockSpec(memory_space=pl.ANY)],
        out_specs=[vmem] * 5,
        scratch_shapes=[pltpu.SemaphoreType.DMA((heads,))],
        compiler_params=pltpu.CompilerParams(vmem_limit_bytes=LARGE),
    )(counts, latent, momentum, grad)


def piece_kernel(nears, grad, piece, sems):
    for copy in gather(grad, piece, sems, nears, True):
        copy.wait()


def later_piece(grad, nears):
    heads = RING * len(nears)
    return pl.pallas_call(
        functools.partial(piece_kernel, nears),
        out_shape=jax.ShapeDtypeStruct((grad.shape[0], heads * HD), bf16),
        in_specs=[pl.BlockSpec(memory_space=pl.ANY)],
        out_specs=pl.BlockSpec(memory_space=pltpu.VMEM),
        scratch_shapes=[pltpu.SemaphoreType.DMA((heads,))],
        compiler_params=pltpu.CompilerParams(vmem_limit_bytes=LARGE),
    )(grad)


def own_kernel(nears, lat, grad, *refs):
    outs, (held, sems) = refs[: len(nears)], refs[len(nears) :]
    for copy in gather(grad, held, sems, nears, False):
        copy.wait()
    for k in range(RING * len(nears)):
        product = jnp.dot(lat[...], held[:, k * HD : (k + 1) * HD], preferred_element_type=f32)
        outs[k // RING][k % RING] = product.astype(bf16)


def own_products(lat, grad, nears):
    features, tokens = lat.shape
    heads = RING * len(nears)
    vmem = pl.BlockSpec(memory_space=pltpu.VMEM)
    return pl.pallas_call(
        functools.partial(own_kernel, nears),
        out_shape=[jax.ShapeDtypeStruct((RING, features, HD), bf16)] * len(nears),
        in_specs=[vmem, pl.BlockSpec(memory_space=pl.ANY)],
        out_specs=[vmem] * len(nears),
        scratch_shapes=[
            pltpu.VMEM((tokens, heads * HD), bf16),
            pltpu.SemaphoreType.DMA((heads,)),
        ],
        compiler_params=pltpu.CompilerParams(vmem_limit_bytes=LARGE),
        cost_estimate=pl.CostEstimate(
            flops=2 * heads * features * HD * tokens,
            bytes_accessed=heads * (tokens + features) * HD * 2,
            transcendentals=0,
        ),
    )(lat, grad)


def block_kernel(tiles, unit, lat, mom_own, mom_other, grad, *refs):
    count = 1 + max(t[0] for t in tiles)
    operands, outs = refs[:count], refs[count:]
    for operand, at_piece, result, near, fars in tiles:
        for place, far in enumerate(fars):
            at = pl.ds(head_columns(near, far), HD)
            in_piece = (at_piece * RING + far) * HD
            mom = jnp.concatenate([mom_own[:, at], mom_other[:, at]], axis=0)
            other = jnp.dot(lat[...], grad[:, in_piece : in_piece + HD], preferred_element_type=f32)
            added = jnp.dot(unit[...], mom, preferred_element_type=f32)
            total = operands[operand][far].astype(f32) + other.astype(bf16).astype(f32) + added
            outs[result][place] = total.astype(outs[result].dtype)


def block(own, held, which, unit, lat, mom_own, mom_other, grad):
    features, tokens = lat.shape
    nears = sorted({near for near, _ in which})
    tiles = [
        (nears.index(near), held.index(near), k, near, fars) for k, (near, fars) in enumerate(which)
    ]
    heads = sum(len(fars) for _, fars in which)
    return pl.pallas_call(
        functools.partial(block_kernel, tiles),
        out_shape=[
            jax.ShapeDtypeStruct((len(fars), features, HD), f32 if near == 0 else bf16)
            for near, fars in which
        ],
        compiler_params=pltpu.CompilerParams(vmem_limit_bytes=VMEM),
        cost_estimate=pl.CostEstimate(
            flops=2 * heads * features * HD * (tokens + unit.shape[1]),
            bytes_accessed=heads * (tokens + 2 * features) * HD * 2,
            transcendentals=0,
        ),
    )(unit, lat, mom_own, mom_other, grad, *[own[near] for near in nears])


def split(value):
    high = value.astype(bf16)
    return high, (value - high.astype(f32)).astype(bf16)


def product(a, b, dims):
    (left,), (right,) = dims
    return lax.dot_general(
        jnp.concatenate([a[0], a[0], a[1]], axis=left),
        jnp.concatenate([b[0], b[1], b[0]], axis=right),
        (dims, ((), ())),
        preferred_element_type=f32,
    )


def newton_schulz_kernel(moment_ref, out_ref):
    moment = moment_ref[...]
    rows, columns = moment.shape
    scale = 0.2 * math.sqrt(max(rows, columns))
    wide = moment.T
    gram = lax.dot_general(wide, wide, (((1,), (1,)), ((), ())), preferred_element_type=f32)
    wide = wide.astype(f32)
    inverse = 1.0 / (jnp.sqrt(jnp.sum(wide * wide)) + 1e-7)
    gram = (gram * inverse) * inverse
    x = wide * inverse
    for step in range(NS_STEPS):
        pair = split(x)
        if step > 0:
            gram = product(pair, pair, ((1,), (1,)))
        gram_pair = split(gram)
        poly = COEF_B * gram + COEF_C * product(gram_pair, gram_pair, ((1,), (0,)))
        x = COEF_A * x + product(split(poly), pair, ((1,), (0,)))
    update = (scale * x).T.astype(bf16)
    owners = out_ref.shape[0]
    depth = rows // owners
    for c in range(NC):
        for chip in range(owners // NC):
            at = slice((chip * NC + c) * depth, (chip * NC + c + 1) * depth)
            out_ref[c * (owners // NC) + chip, 0] = update[at, :]
            out_ref[c * (owners // NC) + chip, 1] = moment[at, :]


def newton_schulz(moment, owners):
    rows, columns = moment.shape
    return pl.pallas_call(
        newton_schulz_kernel,
        out_shape=jax.ShapeDtypeStruct((owners, 2, rows // owners, columns), bf16),
        compiler_params=pltpu.CompilerParams(vmem_limit_bytes=VMEM),
    )(moment)


def spread_kernel(returned, moment, update):
    for c in range(NC):
        for y in range(NY):
            for x in range(NX):
                source = (c * NY + y) * NX + x
                head = c * NY * NX + (RING * x + y if c == 0 else RING * y + x)
                at = slice(head * HD, (head + 1) * HD)
                update[:, at] = returned[source, 0]
                moment[:, at] = returned[source, 1].astype(f32)


def spread(returned):
    heads, _, rows, columns = returned.shape
    return pl.pallas_call(
        spread_kernel,
        out_shape=(
            jax.ShapeDtypeStruct((rows, heads * columns), f32),
            jax.ShapeDtypeStruct((rows, heads * columns), bf16),
        ),
        compiler_params=pltpu.CompilerParams(vmem_limit_bytes=VMEM),
    )(returned)


def body(latent, latent_grad, row_counts, momentum):
    features = latent.shape[1]
    order, rest = (2, 1, 3), (1, 2, 3)

    early, late = (2,), (1, 3, 0)
    lat_own, mom_own, mom_other, unit, piece_early = first(
        row_counts, latent, momentum, latent_grad, early
    )
    grad_late, piece_early = lax.optimization_barrier((latent_grad, piece_early))
    piece_early, lat_other, mom_other = (
        swap_cores(piece_early), swap_cores(lat_own), swap_cores(mom_other)
    )
    piece_late = swap_cores(later_piece(grad_late, late))
    shared = (unit, lat_other, mom_own, mom_other)

    own = dict(zip(early, own_products(lat_own, grad_late, early)))
    on = list(block(own, early, [(early[0], rest)], *shared, piece_early))
    lat_late, on[0] = lax.optimization_barrier((lat_own, on[0]))
    own.update(zip(late, own_products(lat_late, grad_late, late)))
    on += [block(own, late, [(k, rest)], *shared, piece_late)[0] for k in order[1:]]
    on = [shift(value, 0, k) for value, k in zip(on, order)]
    stay_early = block(own, early, [(k, (0,)) for k in early], *shared, piece_early)
    *stay_late, kept_stay, kept_on = block(
        own, late, [(1, (0,)), (3, (0,)), (0, (0,)), (0, rest)], *shared, piece_late
    )
    *stay, on[0] = lax.optimization_barrier((*stay_early, *stay_late, on[0]))
    stay = [shift(value, 0, k) for value, k in zip(stay, order)]

    total = kept_on + sum(value.astype(f32) for value in on)
    got = [shift(total[k - 1].astype(bf16), 1, k) for k in order]
    head = kept_stay[0] + sum(value[0].astype(f32) for value in stay)
    head = (head + sum(value.astype(f32) for value in got)).astype(bf16)

    pieces = lax.all_to_all(head.reshape(NZ, -1, HD), "z", 0, 0, tiled=True)
    eighth = jnp.sum(pieces.astype(f32), axis=0).astype(bf16)
    moment = lax.all_to_all(jnp.broadcast_to(eighth, (NZ,) + eighth.shape), "z", 0, 0, tiled=True)
    moment = moment.reshape(features, HD)

    outgoing = newton_schulz(moment, NC * NY * NX)
    returned = lax.all_to_all(outgoing, PLANE, 0, 0, tiled=True)
    return tuple(spread(returned))


def solution(mesh):
    fine = Mesh(mesh.devices.reshape(NZ, NY, NX, NC), AXES)
    shard = ("y", "x", "c")
    in_specs = (P(AXES, None), P(AXES, None), P(AXES), P(shard, None))
    out_specs = (P(shard, None), P(shard, None))
    return jax.shard_map(body, mesh=fine, in_specs=in_specs, out_specs=out_specs, check_vma=False)
```

time: 104 us -> 105 us (level)
  local copies, waits for them, and re-layouts: 0.25 us -> 3.14 us
  blocking collectives: 51.1 us -> 50 us
  Pallas kernels: 15.7 us -> 14.6 us
    ppermute x9, waiting for transfers between devices: 21.6 us -> 17.8 us  [shift(): return lax.ppermute(value, AXES, pairs)]
    ppermute x3 -> x4, waiting for transfers between devices: 0.11 us -> 3.35 us  [swap_cores(): lax.ppermute(value, AXES, [(device_at(z, y, x, c), device_at(z, y, x, 1 -...]
    unnamed x5 -> x6, local copies, waits for them, and re-layouts: 0.14 us -> 3.07 us
    pallas_call x2 -> x4, Pallas kernels: 6.05 us -> 4.89 us  [the longest x2 3.13 us: own_products(): pl.pallas_call(functools.partial(own_kernel, nears), out_shape=[jax.Shape...]
    pallas_call x4 -> x5, Pallas kernels: 2.77 us -> 3.05 us  [block(): pl.pallas_call(functools.partial(block_kernel, tiles), out_shape=[jax.Sha...]
    ppermute x3 -> x4, starting transfers between devices: 4.01 us -> 3.94 us  [swap_cores(): lax.ppermute(value, AXES, [(device_at(z, y, x, c), device_at(z, y, x, 1 -...]
  transfers between devices with their start and end apart: 12 -> 13, of which waited for: 6 -> 9; matrix products, arithmetic and copies ran while one was open for 1% -> 1% of each run, Pallas kernels for 5% -> 6%
where the time goes in v6:
time: 105 us
  blocking collectives  50 us (48%)
  waiting for transfers between devices  21.1 us (20%)
  Pallas kernels  14.6 us (14%)
  starting transfers between devices  13.8 us (13%)
  local copies, waits for them, and re-layouts  3.14 us (3%)
  between operations  1.4 us (1%)
    all_to_all x1, blocking collectives, body(): returned = lax.all_to_all(outgoing, PLANE, 0, 0, tiled=True)  22.3 us
    ppermute x9, waiting for transfers between devices, shift(): return lax.ppermute(value, AXES, pairs)  17.8 us
    all_to_all x1, blocking collectives, body(): pieces = lax.all_to_all(head.reshape(NZ, -1, HD), 'z', 0, 0, tiled=True)  15.6 us
    all_to_all x1, blocking collectives, body(): lax.all_to_all(jnp.broadcast_to(eighth, (NZ,) + eighth.shape), 'z', 0, 0,...  12.1 us
    ppermute x9, starting transfers between devices, shift(): return lax.ppermute(value, AXES, pairs)  9.84 us
    pallas_call x1, Pallas kernels, newton_schulz(): pl.pallas_call(newton_schulz_kernel, out_shape=jax.ShapeDtypeStruct((owne...  5.75 us
    ppermute x4, starting transfers between devices, swap_cores(): lax.ppermute(value, AXES, [(device_at(z, y, x, c), device_at(z, y, x, 1 -...  3.94 us
    ppermute x4, waiting for transfers between devices, swap_cores(): lax.ppermute(value, AXES, [(device_at(z, y, x, c), device_at(z, y, x, 1 -...  3.35 us
  transfers between devices with their start and end apart: 13, of which 9 were waited for; matrix products, arithmetic and copies ran while one was open for 1% of the time, Pallas kernels for 6%

profile of v6, /device:TPU:1, one launch (start us, length us, event | category | flops | bytes accessed | tf_op | source)
XLA Modules:
  0.0 104.8 jit_solution(909414622871357889)
XLA Ops:
  1.3 0.0 copy-start.1
  1.3 1.0 copy-done.1
  2.3 0.0 copy-start.2
  2.3 0.9 copy-done.2
  3.3 1.4 %shard_map.59 = (bf16[512,256]{1,0:T(8,128)(2,1)S(1)}, bf16[32,4096]{1,0:T(8,128)(2,1)S(1)}, bf16[32,4096]{1,0:T(8,128)(2,1)S(1)}, bf16[512,64]{1,0:T(8,128)(2,1)S(1)}, bf16[256,1024]{1,0:T(8,128)(2,1)S(1)}) custom-call(s32[1]{0:T(128)S(6)} %copy.6.counts, bf16[256,512]{1,0:T(8,128)(2,1)S(1)} %copy-done.2, f32[16,8192]{1,0:T(8,128)S(1)} %copy-done.1, ...), custom_call_target="tpu_custom_call" | custom-call | tf_op jit(solution)/shard_map/pallas_call | solution.py:108
  4.6 1.1 %copy-done = bf16[256,8192]{1,0:T(8,128)(2,1)S(1)} copy-done((bf16[256,8192]{1,0:T(8,128)(2,1)S(1)}, bf16[256,8192]{1,0:T(8,128)(2,1)}, u32[]{:S(2)}) %copy-start) | copy-done | bytes 4194328
  5.7 0.4 shard_map.60
  6.1 3.3 %collective-permute-start.2 = (bf16[256,3072]{1,0:T(8,128)(2,1)S(1)}, bf16[256,3072]{1,0:T(8,128)(2,1)S(1)}, u32[]{:S(2)}, u32[]{:S(2)}) collective-permute-start(bf16[256,3072]{1,0:T(8,128)(2,1)S(1)} %shard_map.60), channel_id=1, source_target_pairs={{0,1},{1,0},{2,3},{3,2},{4,5},{5,4},{6,7},{7,6},{8,9},{9,8},{10,11... | collective-permute-start | bytes 4718600 | tf_op jit(solution)/shard_map/ppermute | solution.py:45
  9.5 0.1 collective-permute-start.3
  9.6 0.4 collective-permute-start.1
  10.0 0.1 collective-permute-start
  10.1 0.6 shard_map.61.refs_0_
  10.7 3.0 %collective-permute-done.1.mom_other = bf16[32,4096]{1,0:T(8,128)(2,1)S(1)} collective-permute-done((bf16[32,4096]{1,0:T(8,128)(2,1)S(1)}, bf16[32,4096]{1,0:T(8,128)(2,1)S(1)}, u32[]{:S(2)}, u32[]{:S(2)}) %collective-permute-start.1) | collective-permute-done | bytes 262176 | tf_op jit(solution)/shard_map/ppermute | solution.py:45
  13.6 0.4 collective-permute-done.lat
  14.0 0.0 collective-permute-done.3.grad
  14.0 0.6 shard_map.62
  14.6 1.3 %collective-permute-start.4 = (bf16[3,512,256]{2,1,0:T(8,128)(2,1)S(1)}, bf16[3,512,256]{2,1,0:T(8,128)(2,1)S(1)}, u32[]{:S(2)}, u32[]{:S(2)}) collective-permute-start(bf16[3,512,256]{2,1,0:T(8,128)(2,1)S(1)} %shard_map.62), channel_id=1, source_target_pairs={{0,4},{1,17},{2,6},{3,19},{4,0},{5,21},{6,2},{7,23},{8,12},{9,25},... | collective-permute-start | bytes 2359304 | tf_op jit(solution)/shard_map/ppermute | solution.py:41
  15.9 2.5 %shard_map.63 = (bf16[4,512,256]{2,1,0:T(8,128)(2,1)S(1)}, bf16[4,512,256]{2,1,0:T(8,128)(2,1)S(1)}, bf16[4,512,256]{2,1,0:T(8,128)(2,1)S(1)}) custom-call(bf16[512,256]{1,0:T(8,128)(2,1)S(1)} %get-tuple-element.29.lat, bf16[256,8192]{1,0:T(8,128)(2,1)} %grad.4), custom_call_target="tpu_custom_call" | custom-call | flops 805306368 | bytes 4718592 | tf_op jit(solution)/shard_map/pallas_call | solution.py:154
  18.4 0.0 collective-permute-done.2.grad
  18.4 0.6 shard_map.67
  19.0 0.9 collective-permute-start.9
  19.9 0.6 shard_map.66
  20.5 0.8 collective-permute-start.8
  21.2 0.3 shard_map.65
  21.5 1.0 shard_map.64
  22.5 4.8 %collective-permute-done.4 = bf16[3,512,256]{2,1,0:T(8,128)(2,1)S(1)} collective-permute-done((bf16[3,512,256]{2,1,0:T(8,128)(2,1)S(1)}, bf16[3,512,256]{2,1,0:T(8,128)(2,1)S(1)}, u32[]{:S(2)}, u32[]{:S(2)}) %collective-permute-start.4) | collective-permute-done | bytes 786464 | tf_op jit(solution)/shard_map/ppermute | solution.py:41
  27.4 1.2 %collective-permute-start.5 = (bf16[1,512,256]{2,1,0:T(8,128)(2,1)S(1)}, bf16[1,512,256]{2,1,0:T(8,128)(2,1)S(1)}, u32[]{:S(2)}, u32[]{:S(2)}) collective-permute-start(bf16[1,512,256]{2,1,0:T(8,128)(2,1)S(1)} %shard_map.65), channel_id=1, source_target_pairs={{0,4},{1,17},{2,6},{3,19},{4,0},{5,21},{6,2},{7,23},{8,12},{9,25},... | collective-permute-start | bytes 786440 | tf_op jit(solution)/shard_map/ppermute | solution.py:41
  28.5 0.4 collective-permute-start.6
  28.9 2.3 %collective-permute-start.7 = (bf16[1,512,256]{2,1,0:T(8,128)(2,1)S(1)}, bf16[1,512,256]{2,1,0:T(8,128)(2,1)S(1)}, u32[]{:S(2)}, u32[]{:S(2)}) collective-permute-start(bf16[1,512,256]{2,1,0:T(8,128)(2,1)S(1)} %get-tuple-element.39), channel_id=1, source_target_pairs={{0,6},{1,25},{2,0},{3,27},{4,2},{5,29},{6,4},{7,31},{8,14},{9,1},{... | collective-permute-start | bytes 786440 | tf_op jit(solution)/shard_map/ppermute | solution.py:41
  31.2 3.2 %collective-permute-done.9 = bf16[3,512,256]{2,1,0:T(8,128)(2,1)S(1)} collective-permute-done((bf16[3,512,256]{2,1,0:T(8,128)(2,1)S(1)}, bf16[3,512,256]{2,1,0:T(8,128)(2,1)S(1)}, u32[]{:S(2)}, u32[]{:S(2)}) %collective-permute-start.9) | collective-permute-done | bytes 786464 | tf_op jit(solution)/shard_map/ppermute | solution.py:41
  34.4 1.4 %collective-permute-done.8 = bf16[3,512,256]{2,1,0:T(8,128)(2,1)S(1)} collective-permute-done((bf16[3,512,256]{2,1,0:T(8,128)(2,1)S(1)}, bf16[3,512,256]{2,1,0:T(8,128)(2,1)S(1)}, u32[]{:S(2)}, u32[]{:S(2)}) %collective-permute-start.8) | collective-permute-done | bytes 786464 | tf_op jit(solution)/shard_map/ppermute | solution.py:41
  35.7 0.5 add_convert_fusion
  36.2 0.1 slice_bitcast_fusion.2
  36.3 1.6 %collective-permute-start.10 = (bf16[512,256]{1,0:T(8,128)(2,1)S(1)}, bf16[512,256]{1,0:T(8,128)(2,1)S(1)}, u32[]{:S(2)}, u32[]{:S(2)}) collective-permute-start(bf16[512,256]{1,0:T(8,128)(2,1)S(1)} %get-tuple-element.42), channel_id=1, source_target_pairs={{0,16},{1,5},{2,18},{3,7},{4,20},{5,1},{6,22},{7,3},{8,24},{9,13},... | collective-permute-start | bytes 786440 | tf_op jit(solution)/shard_map/ppermute | solution.py:41
  37.9 0.9 collective-permute-start.12
  38.8 0.0 collective-permute-done.5
  38.8 0.6 collective-permute-start.11
  39.4 2.0 %collective-permute-done.6 = bf16[1,512,256]{2,1,0:T(8,128)(2,1)S(1)} collective-permute-done((bf16[1,512,256]{2,1,0:T(8,128)(2,1)S(1)}, bf16[1,512,256]{2,1,0:T(8,128)(2,1)S(1)}, u32[]{:S(2)}, u32[]{:S(2)}) %collective-permute-start.6) | collective-permute-done | bytes 262176 | tf_op jit(solution)/shard_map/ppermute | solution.py:41
  41.4 0.0 collective-permute-done.7
  41.4 3.8 %collective-permute-done.10 = bf16[512,256]{1,0:T(8,128)(2,1)S(1)} collective-permute-done((bf16[512,256]{1,0:T(8,128)(2,1)S(1)}, bf16[512,256]{1,0:T(8,128)(2,1)S(1)}, u32[]{:S(2)}, u32[]{:S(2)}) %collective-permute-start.10) | collective-permute-done | bytes 262176 | tf_op jit(solution)/shard_map/ppermute | solution.py:41
  45.1 1.1 %collective-permute-done.12 = bf16[512,256]{1,0:T(8,128)(2,1)S(1)} collective-permute-done((bf16[512,256]{1,0:T(8,128)(2,1)S(1)}, bf16[512,256]{1,0:T(8,128)(2,1)S(1)}, u32[]{:S(2)}, u32[]{:S(2)}) %collective-permute-start.12) | collective-permute-done | bytes 262176 | tf_op jit(solution)/shard_map/ppermute | solution.py:41
  46.3 1.5 %collective-permute-done.11 = bf16[512,256]{1,0:T(8,128)(2,1)S(1)} collective-permute-done((bf16[512,256]{1,0:T(8,128)(2,1)S(1)}, bf16[512,256]{1,0:T(8,128)(2,1)S(1)}, u32[]{:S(2)}, u32[]{:S(2)}) %collective-permute-start.11) | collective-permute-done | bytes 262176 | tf_op jit(solution)/shard_map/ppermute | solution.py:41
  47.8 0.2 fusion
  48.0 15.6 %all_to_all.15 = bf16[8,64,256]{2,1,0:T(8,128)(2,1)S(1)} all-to-all(bf16[8,64,256]{2,1,0:T(8,128)(2,1)S(1)} %bitcast.13), channel_id=1, replica_groups=mesh['z'=8,'y'=4,'x'=4,'c'=2] {'z'}, dimensions={0} | all-to-all | bytes 524288 | tf_op jit(solution)/shard_map/all_to_all | solution.py:315
  63.7 12.1 %all_to_all.16 = bf16[8,64,256]{2,1,0:T(8,128)(2,1)S(1)} all-to-all(bf16[8,64,256]{2,1,0:T(8,128)(2,1)S(1)} %broadcast_in_dim.3), channel_id=1, replica_groups=mesh['z'=8,'y'=4,'x'=4,'c'=2] {'z'}, dimensions={0} | all-to-all | bytes 524288 | tf_op jit(solution)/shard_map/all_to_all | solution.py:317
  75.8 5.7 %shard_map.68 = bf16[32,2,16,256]{3,2,1,0:T(8,128)(2,1)S(1)} custom-call(bf16[512,256]{1,0:T(8,128)(2,1)S(1)} %bitcast.12), custom_call_target="tpu_custom_call" | custom-call | tf_op jit(solution)/shard_map/pallas_call | solution.py:252
  81.6 22.3 %all_to_all.17.returned = bf16[32,2,16,256]{3,2,1,0:T(8,128)(2,1)S(1)} all-to-all(bf16[32,2,16,256]{3,2,1,0:T(8,128)(2,1)S(1)} %shard_map.68), channel_id=1, replica_groups=mesh['z'=8,'y'=4,'x'=4,'c'=2] {'c','y','x'}, dimensions={0} | all-to-all | bytes 1048576 | tf_op jit(solution)/shard_map/all_to_all | solution.py:321
  103.9 0.9 shard_map.69
  (3 shorter events, 0.1 us)
Async XLA Ops:
  1.3 1.0 copy-start.1
  2.3 0.9 copy-start.2
  3.3 2.4 %copy-start = (bf16[256,8192]{1,0:T(8,128)(2,1)S(1)}, bf16[256,8192]{1,0:T(8,128)(2,1)}, u32[]{:S(2)}) copy-start(bf16[256,8192]{1,0:T(8,128)(2,1)} %grad.4) | copy-start | bytes 12582916
  6.1 12.3 %collective-permute-start.2 = (bf16[256,3072]{1,0:T(8,128)(2,1)S(1)}, bf16[256,3072]{1,0:T(8,128)(2,1)S(1)}, u32[]{:S(2)}, u32[]{:S(2)}) collective-permute-start(bf16[256,3072]{1,0:T(8,128)(2,1)S(1)} %shard_map.60), channel_id=1, source_target_pairs={{0,1},{1,0},{2,3},{3,2},{4,5},{5,4},{6,7},{7,6},{8,9},{9,8},{10,11... | collective-permute-start | bytes 4718600 | tf_op jit(solution)/shard_map/ppermute | solution.py:45
  9.5 4.5 %collective-permute-start.3 = (bf16[256,1024]{1,0:T(8,128)(2,1)S(1)}, bf16[256,1024]{1,0:T(8,128)(2,1)S(1)}, u32[]{:S(2)}, u32[]{:S(2)}) collective-permute-start(bf16[256,1024]{1,0:T(8,128)(2,1)S(1)} %get-tuple-element.28), channel_id=1, source_target_pairs={{0,1},{1,0},{2,3},{3,2},{4,5},{5,4},{6,7},{7,6},{8,9},{9,8},{10,11... | collective-permute-start | bytes 1572872 | tf_op jit(solution)/shard_map/ppermute | solution.py:45
  9.6 4.1 %collective-permute-start.1 = (bf16[32,4096]{1,0:T(8,128)(2,1)S(1)}, bf16[32,4096]{1,0:T(8,128)(2,1)S(1)}, u32[]{:S(2)}, u32[]{:S(2)}) collective-permute-start(bf16[32,4096]{1,0:T(8,128)(2,1)S(1)} %get-tuple-element.25), channel_id=1, source_target_pairs={{0,1},{1,0},{2,3},{3,2},{4,5},{5,4},{6,7},{7,6},{8,9},{9,8},{10,11... | collective-permute-start | bytes 786440 | tf_op jit(solution)/shard_map/ppermute | solution.py:45
  10.0 4.0 %collective-permute-start = (bf16[512,256]{1,0:T(8,128)(2,1)S(1)}, bf16[512,256]{1,0:T(8,128)(2,1)S(1)}, u32[]{:S(2)}, u32[]{:S(2)}) collective-permute-start(bf16[512,256]{1,0:T(8,128)(2,1)S(1)} %get-tuple-element.29.lat), channel_id=1, source_target_pairs={{0,1},{1,0},{2,3},{3,2},{4,5},{5,4},{6,7},{7,6},{8,9},{9,8},{10,11... | collective-permute-start | bytes 786440 | tf_op jit(solution)/shard_map/ppermute | solution.py:45
  14.6 12.8 %collective-permute-start.4 = (bf16[3,512,256]{2,1,0:T(8,128)(2,1)S(1)}, bf16[3,512,256]{2,1,0:T(8,128)(2,1)S(1)}, u32[]{:S(2)}, u32[]{:S(2)}) collective-permute-start(bf16[3,512,256]{2,1,0:T(8,128)(2,1)S(1)} %shard_map.62), channel_id=1, source_target_pairs={{0,4},{1,17},{2,6},{3,19},{4,0},{5,21},{6,2},{7,23},{8,12},{9,25},... | collective-permute-start | bytes 2359304 | tf_op jit(solution)/shard_map/ppermute | solution.py:41
  19.0 15.4 %collective-permute-start.9 = (bf16[3,512,256]{2,1,0:T(8,128)(2,1)S(1)}, bf16[3,512,256]{2,1,0:T(8,128)(2,1)S(1)}, u32[]{:S(2)}, u32[]{:S(2)}) collective-permute-start(bf16[3,512,256]{2,1,0:T(8,128)(2,1)S(1)} %shard_map.67), channel_id=1, source_target_pairs={{0,6},{1,25},{2,0},{3,27},{4,2},{5,29},{6,4},{7,31},{8,14},{9,1},{... | collective-permute-start | bytes 2359304 | tf_op jit(solution)/shard_map/ppermute | solution.py:41
  20.5 15.3 %collective-permute-start.8 = (bf16[3,512,256]{2,1,0:T(8,128)(2,1)S(1)}, bf16[3,512,256]{2,1,0:T(8,128)(2,1)S(1)}, u32[]{:S(2)}, u32[]{:S(2)}) collective-permute-start(bf16[3,512,256]{2,1,0:T(8,128)(2,1)S(1)} %shard_map.66), channel_id=1, source_target_pairs={{0,2},{1,9},{2,4},{3,11},{4,6},{5,13},{6,0},{7,15},{8,10},{9,17},{... | collective-permute-start | bytes 2359304 | tf_op jit(solution)/shard_map/ppermute | solution.py:41
  27.4 11.4 %collective-permute-start.5 = (bf16[1,512,256]{2,1,0:T(8,128)(2,1)S(1)}, bf16[1,512,256]{2,1,0:T(8,128)(2,1)S(1)}, u32[]{:S(2)}, u32[]{:S(2)}) collective-permute-start(bf16[1,512,256]{2,1,0:T(8,128)(2,1)S(1)} %shard_map.65), channel_id=1, source_target_pairs={{0,4},{1,17},{2,6},{3,19},{4,0},{5,21},{6,2},{7,23},{8,12},{9,25},... | collective-permute-start | bytes 786440 | tf_op jit(solution)/shard_map/ppermute | solution.py:41
  28.5 12.8 %collective-permute-start.6 = (bf16[1,512,256]{2,1,0:T(8,128)(2,1)S(1)}, bf16[1,512,256]{2,1,0:T(8,128)(2,1)S(1)}, u32[]{:S(2)}, u32[]{:S(2)}) collective-permute-start(bf16[1,512,256]{2,1,0:T(8,128)(2,1)S(1)} %get-tuple-element.38), channel_id=1, source_target_pairs={{0,2},{1,9},{2,4},{3,11},{4,6},{5,13},{6,0},{7,15},{8,10},{9,17},{... | collective-permute-start | bytes 786440 | tf_op jit(solution)/shard_map/ppermute | solution.py:41
  28.9 12.4 %collective-permute-start.7 = (bf16[1,512,256]{2,1,0:T(8,128)(2,1)S(1)}, bf16[1,512,256]{2,1,0:T(8,128)(2,1)S(1)}, u32[]{:S(2)}, u32[]{:S(2)}) collective-permute-start(bf16[1,512,256]{2,1,0:T(8,128)(2,1)S(1)} %get-tuple-element.39), channel_id=1, source_target_pairs={{0,6},{1,25},{2,0},{3,27},{4,2},{5,29},{6,4},{7,31},{8,14},{9,1},{... | collective-permute-start | bytes 786440 | tf_op jit(solution)/shard_map/ppermute | solution.py:41
  36.3 8.9 %collective-permute-start.10 = (bf16[512,256]{1,0:T(8,128)(2,1)S(1)}, bf16[512,256]{1,0:T(8,128)(2,1)S(1)}, u32[]{:S(2)}, u32[]{:S(2)}) collective-permute-start(bf16[512,256]{1,0:T(8,128)(2,1)S(1)} %get-tuple-element.42), channel_id=1, source_target_pairs={{0,16},{1,5},{2,18},{3,7},{4,20},{5,1},{6,22},{7,3},{8,24},{9,13},... | collective-permute-start | bytes 786440 | tf_op jit(solution)/shard_map/ppermute | solution.py:41
  37.9 8.3 %collective-permute-start.12 = (bf16[512,256]{1,0:T(8,128)(2,1)S(1)}, bf16[512,256]{1,0:T(8,128)(2,1)S(1)}, u32[]{:S(2)}, u32[]{:S(2)}) collective-permute-start(bf16[512,256]{1,0:T(8,128)(2,1)S(1)} %get-tuple-element.43), channel_id=1, source_target_pairs={{0,24},{1,7},{2,26},{3,1},{4,28},{5,3},{6,30},{7,5},{8,0},{9,15},{... | collective-permute-start | bytes 786440 | tf_op jit(solution)/shard_map/ppermute | solution.py:41
  38.8 9.0 %collective-permute-start.11 = (bf16[512,256]{1,0:T(8,128)(2,1)S(1)}, bf16[512,256]{1,0:T(8,128)(2,1)S(1)}, u32[]{:S(2)}, u32[]{:S(2)}) collective-permute-start(bf16[512,256]{1,0:T(8,128)(2,1)S(1)} %get-tuple-element.44), channel_id=1, source_target_pairs={{0,8},{1,3},{2,10},{3,5},{4,12},{5,7},{6,14},{7,1},{8,16},{9,11},{... | collective-permute-start | bytes 786440 | tf_op jit(solution)/shard_map/ppermute | solution.py:41

commit v7 on v5

--- a/solution.py
+++ b/solution.py
@@ -52,113 +52,131 @@
     return jnp.where(core == 0, x, y), jnp.where(core == 0, y, x)
 
 
-def column_copy_kernel(grad, out, sems):
-    width = out.shape[1] // sems.shape[0]
+def head_columns(near, far, other=False):
+    first, second = places()
+    if other:
+        first, second = second, first
+    head = lax.rem(first + near, RING) * RING + lax.rem(second + far, RING)
+    return pl.multiple_of(head * HD, HD)
+
+
+def pieces_kernel(groups, grad, *refs):
+    outs, (held, sems) = refs[: len(groups)], refs[len(groups) :]
+    base = (1 - lax.axis_index("c")) * (grad.shape[1] // NC)
+    into, onto = [], []
+    for nears, out in zip(groups, outs):
+        for place, near in enumerate(nears):
+            for far in range(RING):
+                k = len(into)
+                start = pl.multiple_of(base + head_columns(near, far, True), HD)
+                target = (place * RING + far) * HD
+                into.append(
+                    pltpu.make_async_copy(grad.at[:, pl.ds(start, HD)], held.at[k], sems.at[0, k])
+                )
+                onto.append(
+                    pltpu.make_async_copy(held.at[k], out.at[:, pl.ds(target, HD)], sems.at[1, k])
+                )
+    for copy in into:
+        copy.start()
+    for k in range(len(into)):
+        into[k].wait()
+        onto[k].start()
+    for copy in onto:
+        copy.wait()
+
+
+def column_pieces(grad, groups):
+    rows = grad.shape[0]
+    count = RING * RING
+    hbm = pl.BlockSpec(memory_space=pl.ANY)
+    return pl.pallas_call(
+        functools.partial(pieces_kernel, groups),
+        out_shape=[jax.ShapeDtypeStruct((rows, len(g) * RING * HD), grad.dtype) for g in groups],
+        in_specs=[hbm],
+        out_specs=[hbm] * len(groups),
+        scratch_shapes=[
+            pltpu.VMEM((count, rows, HD), grad.dtype),
+            pltpu.SemaphoreType.DMA((2, count)),
+        ],
+        compiler_params=pltpu.CompilerParams(vmem_limit_bytes=LARGE),
+    )(grad)
+
+
+def own_kernel(nears, depth, lat, grad, *refs):
+    outs, (unit, held, sems) = refs[: len(nears)], refs[len(nears) :]
+    base = lax.axis_index("c") * (grad.shape[1] // NC)
     copies = []
-    for k in range(sems.shape[0]):
-        start = pl.multiple_of((1 - lax.axis_index("c")) * out.shape[1] + k * width, width)
-        copies.append(
-            pltpu.make_async_copy(
-                grad.at[:, pl.ds(start, width)], out.at[:, pl.ds(k * width, width)], sems.at[k]
+    for near in nears:
+        for far in range(RING):
+            k = len(copies)
+            start = pl.multiple_of(base + head_columns(near, far), HD)
+            copies.append(
+                pltpu.make_async_copy(grad.at[:, pl.ds(start, HD)], held.at[k], sems.at[k])
             )
-        )
-    for copy in copies:
-        copy.start()
+            copies[k].start()
+
+    core = lax.axis_index("c")
+    here = lax.axis_index("y") * NX + lax.axis_index("x")
+    row = lax.broadcasted_iota(jnp.int32, unit.shape, 0)
+    at = lax.broadcasted_iota(jnp.int32, unit.shape, 1)
+    core_of = jnp.where((at // depth) % 2 == 0, core, 1 - core)
+    unit[...] = (row == (here * NC + core_of) * depth + at % depth).astype(f32).astype(bf16)
+
     for copy in copies:
         copy.wait()
-
-
-def column_copy(grad):
-    rows, columns = grad.shape
-    return pl.pallas_call(
-        column_copy_kernel,
-        out_shape=jax.ShapeDtypeStruct((rows, columns // NC), grad.dtype),
-        in_specs=[pl.BlockSpec(memory_space=pl.ANY)],
-        out_specs=pl.BlockSpec(memory_space=pltpu.VMEM),
-        scratch_shapes=[pltpu.SemaphoreType.DMA((8,))],
-        compiler_params=pltpu.CompilerParams(vmem_limit_bytes=LARGE),
-    )(grad)
-
-
-def head_columns(near, far):
-    first, second = places()
-    head = lax.rem(first + near, RING) * RING + lax.rem(second + far, RING)
-    return pl.multiple_of(head * HD, HD)
-
-
-def own_kernel(depth, lat, grad, *refs):
-    outs, (unit, held, sems) = refs[:RING], refs[RING:]
-    core = lax.axis_index("c")
-    half = grad.shape[1] // NC
-    copies = []
-    for near in range(RING):
-        for far in range(RING):
-            start = pl.multiple_of(core * half + head_columns(near, far), HD)
-            at = near * RING + far
-            copies.append(
-                pltpu.make_async_copy(grad.at[:, pl.ds(start, HD)], held.at[at], sems.at[at])
-            )
-    for copy in copies:
-        copy.start()
-
-    features = lat.shape[0]
-    here = lax.axis_index("y") * NX + lax.axis_index("x")
-    row = lax.broadcasted_iota(jnp.int32, (features, 4 * depth), 0)
-    at = lax.broadcasted_iota(jnp.int32, (features, 4 * depth), 1)
-    core_of = jnp.where((at // depth) % 2 == 0, core, 1 - core)
-    unit[...] = (row == (here * NC + core_of) * depth + at % depth).astype(f32).astype(bf16)
-
-    for copy in copies:
-        copy.wait()
-    for near in range(RING):
-        for far in range(RING):
-            product = jnp.dot(lat[...], held[near * RING + far], preferred_element_type=f32)
-            outs[near][far] = product.astype(bf16)
-
-
-def own_products(lat, grad, depth):
+    for k in range(len(copies)):
+        value = jnp.dot(lat[...], held[k], preferred_element_type=f32)
+        outs[k // RING][k % RING] = value.astype(bf16)
+
+
+def own_products(lat, grad, depth, nears):
     features, tokens = lat.shape
-    out = jax.ShapeDtypeStruct((RING, features, HD), bf16)
+    count = RING * len(nears)
     vmem = pl.BlockSpec(memory_space=pltpu.VMEM)
     return pl.pallas_call(
-        functools.partial(own_kernel, depth),
-        out_shape=[out] * RING + [jax.ShapeDtypeStruct((features, 4 * depth), bf16)],
+        functools.partial(own_kernel, nears, depth),
+        out_shape=[jax.ShapeDtypeStruct((RING, features, HD), bf16)] * len(nears)
+        + [jax.ShapeDtypeStruct((features, 4 * depth), bf16)],
         in_specs=[vmem, pl.BlockSpec(memory_space=pl.ANY)],
-        out_specs=[vmem] * (RING + 1),
+        out_specs=[vmem] * (len(nears) + 1),
         scratch_shapes=[
-            pltpu.VMEM((RING * RING, tokens, HD), bf16),
-            pltpu.SemaphoreType.DMA((RING * RING,)),
+            pltpu.VMEM((count, tokens, HD), bf16),
+            pltpu.SemaphoreType.DMA((count,)),
         ],
         compiler_params=pltpu.CompilerParams(vmem_limit_bytes=LARGE),
         cost_estimate=pl.CostEstimate(
-            flops=2 * RING * RING * features * HD * tokens,
-            bytes_accessed=RING * RING * (tokens + features) * HD * 2,
+            flops=2 * count * features * HD * tokens,
+            bytes_accessed=count * (tokens + features) * HD * 2,
             transcendentals=0,
         ),
     )(lat, grad)
 
 
 def block_kernel(tiles, unit, lat, mom_own, mom_other, grad, *refs):
-    operands, outs = refs[: 1 + max(t[0] for t in tiles)], refs[1 + max(t[0] for t in tiles) :]
-    for operand, result, near, fars in tiles:
+    count = 1 + max(t[0] for t in tiles)
+    operands, outs = refs[:count], refs[count:]
+    for operand, at_piece, result, near, fars in tiles:
         for place, far in enumerate(fars):
             at = pl.ds(head_columns(near, far), HD)
+            in_piece = (at_piece * RING + far) * HD
             high, low = [], []
             for ref in (mom_own, mom_other):
                 value = (DECAY / NZ) * ref[:, at]
                 high.append(value.astype(bf16))
                 low.append((value - high[-1].astype(f32)).astype(bf16))
             mom = jnp.concatenate(high + low, axis=0)
-            other = jnp.dot(lat[...], grad[:, at], preferred_element_type=f32)
+            other = jnp.dot(lat[...], grad[:, in_piece : in_piece + HD], preferred_element_type=f32)
             added = jnp.dot(unit[...], mom, preferred_element_type=f32)
             total = operands[operand][far].astype(f32) + other.astype(bf16).astype(f32) + added
             outs[result][place] = total.astype(outs[result].dtype)
 
 
-def block(own, which, unit, lat, mom_own, mom_other, grad):
+def block(own, held, which, unit, lat, mom_own, mom_other, grad):
     features, tokens = lat.shape
     nears = sorted({near for near, _ in which})
-    tiles = [(nears.index(near), k, near, fars) for k, (near, fars) in enumerate(which)]
+    tiles = [
+        (nears.index(near), held.index(near), k, near, fars) for k, (near, fars) in enumerate(which)
+    ]
     heads = sum(len(fars) for _, fars in which)
     return pl.pallas_call(
         functools.partial(block_kernel, tiles),
@@ -181,10 +199,13 @@
 
 
 def product(a, b, dims):
-    dot = functools.partial(
-        lax.dot_general, dimension_numbers=(dims, ((), ())), preferred_element_type=f32
+    (left,), (right,) = dims
+    return lax.dot_general(
+        jnp.concatenate([a[0], a[0], a[1]], axis=left),
+        jnp.concatenate([b[0], b[1], b[0]], axis=right),
+        (dims, ((), ())),
+        preferred_element_type=f32,
     )
-    return dot(a[0], b[0]) + (dot(a[0], b[1]) + dot(a[1], b[0]))
 
 
 def newton_schulz_kernel(moment_ref, out_ref):
@@ -249,23 +270,36 @@
 def body(latent, latent_grad, row_counts, momentum):
     c = lax.axis_index("c")
     slots, features = latent.shape
-    columns = latent_grad.shape[1] // NC
-
-    grad_other = swap_cores(column_copy(latent_grad))
+    depth, columns = momentum.shape[0], momentum.shape[1] // NC
+    order, rest = (2, 1, 3), (1, 2, 3)
+    tie = lax.optimization_barrier
+
+    early, late = (2,), (1, 3, 0)
+    piece_early, piece_late = column_pieces(latent_grad, (early, late))
+    piece_early = swap_cores(piece_early)
     live = lax.broadcasted_iota(jnp.int32, (slots, 1), 0) < row_counts[0]
     lat_own = jnp.where(live, latent, jnp.zeros_like(latent)).T
     lat_other = swap_cores(lat_own)
     mom_own = lax.dynamic_slice_in_dim(momentum, c * columns, columns, 1)
     mom_other = swap_cores(lax.dynamic_slice_in_dim(momentum, (1 - c) * columns, columns, 1))
-
-    *own, unit = own_products(lat_own, latent_grad, momentum.shape[0])
-    operands = (unit, lat_other, mom_own, mom_other, grad_other)
-    order, rest = (2, 1, 3), (1, 2, 3)
-    on = [shift(block(own, [(k, rest)], *operands)[0], 0, k) for k in order]
-    *stay, kept_stay, kept_on = block(
-        own, [(k, (0,)) for k in order] + [(0, (0,)), (0, rest)], *operands
+    own_early, unit = own_products(lat_own, latent_grad, depth, early)
+    piece_late, piece_early, lat_other, mom_other, own_early = tie(
+        (piece_late, piece_early, lat_other, mom_other, own_early)
     )
-    stay = [shift(value, 0, k) for value, k in zip(stay, order)]
+    piece_late = swap_cores(piece_late)
+    shared = (unit, lat_other, mom_own, mom_other)
+
+    own = {2: own_early}
+    (first_on,) = block(own, early, [(2, rest)], *shared, piece_early)
+    lat_late, first_on = tie((lat_own, first_on))
+    own[1], own[3], own[0], _ = own_products(lat_late, latent_grad, depth, late)
+    on = [first_on] + [block(own, late, [(k, rest)], *shared, piece_late)[0] for k in order[1:]]
+    on = [shift(value, 0, k) for value, k in zip(on, order)]
+    (stay,) = block(own, early, [(2, (0,))], *shared, piece_early)
+    *stays, kept_stay, kept_on = block(
+        own, late, [(1, (0,)), (3, (0,)), (0, (0,)), (0, rest)], *shared, piece_late
+    )
+    stay = [shift(value, 0, k) for value, k in zip([stay] + stays, order)]
 
     total = kept_on + sum(value.astype(f32) for value in on)
     got = [shift(total[k - 1].astype(bf16), 1, k) for k in order]

time: 104 us -> 104 us (level)
  local copies, waits for them, and re-layouts: 0.25 us -> 4.41 us
  waiting for transfers between devices: 21.7 us -> 17.9 us
  blocking collectives: 51.1 us -> 50 us
    ppermute x9, waiting for transfers between devices: 21.6 us -> 17.8 us  [shift(): return lax.ppermute(value, AXES, pairs)]
    unnamed x5 -> x3, local copies, waits for them, and re-layouts: 0.14 us -> 3.27 us
    pallas_call x2 -> x3, Pallas kernels: 6.05 us -> 5.24 us  [the longest x2 3.29 us: own_products(): pl.pallas_call(functools.partial(own_kernel, nears, depth), out_shape=[ja...]
    pallas_call x4 -> x5, Pallas kernels: 2.77 us -> 3.04 us  [block(): pl.pallas_call(functools.partial(block_kernel, tiles), out_shape=[jax.Sha...]
    ppermute x3 -> x4, starting transfers between devices: 4.01 us -> 4.14 us  [swap_cores(): lax.ppermute(value, AXES, [(device_at(z, y, x, c), device_at(z, y, x, 1 -...]
  transfers between devices with their start and end apart: 12 -> 13, of which waited for: 6 -> 7; matrix products, arithmetic and copies ran while one was open for 1% -> 2% of each run, Pallas kernels for 5% -> 8%
where the time goes in v7:
time: 104 us; the launch traced here: 103 us
  blocking collectives  50 us (48%)
  waiting for transfers between devices  17.9 us (17%)
  Pallas kernels  15 us (14%)
  starting transfers between devices  13.9 us (13%)
  local copies, waits for them, and re-layouts  4.41 us (4%)
  between operations  1.43 us (1%)
    all_to_all x1, blocking collectives, body(): returned = lax.all_to_all(outgoing, PLANE, 0, 0, tiled=True)  22.3 us
    ppermute x9, waiting for transfers between devices, shift(): return lax.ppermute(value, AXES, pairs)  17.8 us
    all_to_all x1, blocking collectives, body(): pieces = lax.all_to_all(head.reshape(NZ, -1, HD), 'z', 0, 0, tiled=True)  15.7 us
    all_to_all x1, blocking collectives, body(): lax.all_to_all(jnp.broadcast_to(piece, (NZ,) + piece.shape), 'z', 0, 0, t...  12.1 us
    ppermute x9, starting transfers between devices, shift(): return lax.ppermute(value, AXES, pairs)  9.74 us
    pallas_call x1, Pallas kernels, newton_schulz(): pl.pallas_call(newton_schulz_kernel, out_shape=jax.ShapeDtypeStruct((owne...  5.75 us
    ppermute x4, starting transfers between devices, swap_cores(): lax.ppermute(value, AXES, [(device_at(z, y, x, c), device_at(z, y, x, 1 -...  4.14 us
    pallas_call x2, Pallas kernels, own_products(): pl.pallas_call(functools.partial(own_kernel, nears, depth), out_shape=[ja...  3.29 us
  transfers between devices with their start and end apart: 13, of which 7 were waited for; matrix products, arithmetic and copies ran while one was open for 2% of the time, Pallas kernels for 8%

profile of v7, /device:TPU:1, one launch (start us, length us, event | category | flops | bytes accessed | tf_op | source)
XLA Modules:
  0.0 103.3 jit_solution(8331699123131464362)
XLA Ops:
  1.3 1.1 %copy.6 = bf16[256,512]{0,1:T(8,128)(2,1)S(1)} copy(bf16[256,512]{1,0:T(8,128)(2,1)} %param.4) | data formatting | bytes 524288 | tf_op args[0]
  2.4 3.3 %collective-permute-start.1 = (bf16[512,256]{1,0:T(8,128)(2,1)S(1)}, bf16[512,256]{1,0:T(8,128)(2,1)S(1)}, u32[]{:S(2)}, u32[]{:S(2)}) collective-permute-start(bf16[512,256]{1,0:T(8,128)(2,1)S(1)} %select_bitcast_fusion.lat), channel_id=1, source_target_pairs={{0,1},{1,0},{2,3},{3,2},{4,5},{5,4},{6,7},{7,6},{8,9},{9,8},{10,11... | collective-permute-start | bytes 786440 | tf_op jit(solution)/shard_map/ppermute | solution.py:45
  5.7 1.9 %shard_map.60 = (bf16[256,1024]{1,0:T(8,128)(2,1)S(1)}, bf16[256,3072]{1,0:T(8,128)(2,1)S(1)}) custom-call(bf16[256,8192]{1,0:T(8,128)(2,1)} %grad.5), custom_call_target="tpu_custom_call" | custom-call | tf_op jit(solution)/shard_map/pallas_call | solution.py:92
  7.7 0.1 collective-permute-start
  7.8 1.1 %constant_dynamic-slice_fusion = (f32[16,4096]{1,0:T(8,128)S(1)}, f32[16,4096]{1,0:T(8,128)S(1)}) fusion(f32[16,8192]{1,0:T(8,128)} %param.7, s32[]{:T(128)S(6)} %select_n.12, s32[]{:T(128)S(6)} %select_n.11), kind=kLoop, calls=%fused_computation.8 | loop fusion | bytes 1048584 | tf_op jit(solution)/shard_map/dynamic_slice | solution.py:283
  8.9 0.6 collective-permute-start.2
  9.4 0.0 copy-start
  9.4 2.2 %copy-done = bf16[256,8192]{1,0:T(8,128)(2,1)S(1)} copy-done((bf16[256,8192]{1,0:T(8,128)(2,1)S(1)}, bf16[256,8192]{1,0:T(8,128)(2,1)}, u32[]{:S(2)}) %copy-start) | copy-done | bytes 4194328
  11.6 0.6 shard_map.59
  12.3 0.0 collective-permute-done.1.lat
  12.3 0.0 collective-permute-done.2.mom_other
  12.3 0.0 collective-permute-done.grad
  12.3 0.1 collective-permute-start.3
  12.4 0.6 shard_map.61
  13.0 1.3 %collective-permute-start.7 = (bf16[3,512,256]{2,1,0:T(8,128)(2,1)S(1)}, bf16[3,512,256]{2,1,0:T(8,128)(2,1)S(1)}, u32[]{:S(2)}, u32[]{:S(2)}) collective-permute-start(bf16[3,512,256]{2,1,0:T(8,128)(2,1)S(1)} %shard_map.61), channel_id=1, source_target_pairs={{0,4},{1,17},{2,6},{3,19},{4,0},{5,21},{6,2},{7,23},{8,12},{9,25},... | collective-permute-start | bytes 2359304 | tf_op jit(solution)/shard_map/ppermute | solution.py:41
  14.3 2.7 %shard_map.62 = (bf16[4,512,256]{2,1,0:T(8,128)(2,1)S(1)}, bf16[4,512,256]{2,1,0:T(8,128)(2,1)S(1)}, bf16[4,512,256]{2,1,0:T(8,128)(2,1)S(1)}, bf16[512,64]{1,0:T(8,128)(2,1)}) custom-call(bf16[512,256]{1,0:T(8,128)(2,1)S(1)} %select_bitcast_fusion.lat, bf16[256,8192]{1,0:T(8,128)(2,1)} %grad.5), custom_call_target="tpu_custom_call" | custom-call | flops 805306368 | bytes 4718592 | tf_op jit(solution)/shard_map/pallas_call | solution.py:136
  17.0 0.0 collective-permute-done.3.grad
  17.0 0.6 shard_map.66
  17.6 0.9 collective-permute-start.9
  18.4 0.6 shard_map.65
  19.0 0.8 collective-permute-start.8
  19.8 0.3 shard_map.64
  20.1 1.9 %collective-permute-start.4 = (bf16[1,512,256]{2,1,0:T(8,128)(2,1)S(1)}, bf16[1,512,256]{2,1,0:T(8,128)(2,1)S(1)}, u32[]{:S(2)}, u32[]{:S(2)}) collective-permute-start(bf16[1,512,256]{2,1,0:T(8,128)(2,1)S(1)} %shard_map.64), channel_id=1, source_target_pairs={{0,4},{1,17},{2,6},{3,19},{4,0},{5,21},{6,2},{7,23},{8,12},{9,25},... | collective-permute-start | bytes 786440 | tf_op jit(solution)/shard_map/ppermute | solution.py:41
  22.0 1.0 shard_map.63
  23.0 0.9 collective-permute-start.5
  23.8 2.0 %collective-permute-done.7 = bf16[3,512,256]{2,1,0:T(8,128)(2,1)S(1)} collective-permute-done((bf16[3,512,256]{2,1,0:T(8,128)(2,1)S(1)}, bf16[3,512,256]{2,1,0:T(8,128)(2,1)S(1)}, u32[]{:S(2)}, u32[]{:S(2)}) %collective-permute-start.7) | collective-permute-done | bytes 786464 | tf_op jit(solution)/shard_map/ppermute | solution.py:41
  25.8 1.0 collective-permute-start.6
  26.8 6.0 %collective-permute-done.9 = bf16[3,512,256]{2,1,0:T(8,128)(2,1)S(1)} collective-permute-done((bf16[3,512,256]{2,1,0:T(8,128)(2,1)S(1)}, bf16[3,512,256]{2,1,0:T(8,128)(2,1)S(1)}, u32[]{:S(2)}, u32[]{:S(2)}) %collective-permute-start.9) | collective-permute-done | bytes 786464 | tf_op jit(solution)/shard_map/ppermute | solution.py:41
  32.8 1.4 %collective-permute-done.8 = bf16[3,512,256]{2,1,0:T(8,128)(2,1)S(1)} collective-permute-done((bf16[3,512,256]{2,1,0:T(8,128)(2,1)S(1)}, bf16[3,512,256]{2,1,0:T(8,128)(2,1)S(1)}, u32[]{:S(2)}, u32[]{:S(2)}) %collective-permute-start.8) | collective-permute-done | bytes 786464 | tf_op jit(solution)/shard_map/ppermute | solution.py:41
  34.2 0.5 add_convert_fusion
  34.6 0.1 slice_bitcast_fusion.2
  34.7 1.7 %collective-permute-start.10 = (bf16[512,256]{1,0:T(8,128)(2,1)S(1)}, bf16[512,256]{1,0:T(8,128)(2,1)S(1)}, u32[]{:S(2)}, u32[]{:S(2)}) collective-permute-start(bf16[512,256]{1,0:T(8,128)(2,1)S(1)} %get-tuple-element.38), channel_id=1, source_target_pairs={{0,16},{1,5},{2,18},{3,7},{4,20},{5,1},{6,22},{7,3},{8,24},{9,13},... | collective-permute-start | bytes 786440 | tf_op jit(solution)/shard_map/ppermute | solution.py:41
  36.4 0.9 collective-permute-start.12
  37.2 0.0 collective-permute-done.4
  37.2 0.6 collective-permute-start.11
  37.8 1.9 %collective-permute-done.5 = bf16[1,512,256]{2,1,0:T(8,128)(2,1)S(1)} collective-permute-done((bf16[1,512,256]{2,1,0:T(8,128)(2,1)S(1)}, bf16[1,512,256]{2,1,0:T(8,128)(2,1)S(1)}, u32[]{:S(2)}, u32[]{:S(2)}) %collective-permute-start.5) | collective-permute-done | bytes 262176 | tf_op jit(solution)/shard_map/ppermute | solution.py:41
  39.8 0.0 collective-permute-done.6
  39.8 3.9 %collective-permute-done.10 = bf16[512,256]{1,0:T(8,128)(2,1)S(1)} collective-permute-done((bf16[512,256]{1,0:T(8,128)(2,1)S(1)}, bf16[512,256]{1,0:T(8,128)(2,1)S(1)}, u32[]{:S(2)}, u32[]{:S(2)}) %collective-permute-start.10) | collective-permute-done | bytes 262176 | tf_op jit(solution)/shard_map/ppermute | solution.py:41
  43.6 1.2 %collective-permute-done.12 = bf16[512,256]{1,0:T(8,128)(2,1)S(1)} collective-permute-done((bf16[512,256]{1,0:T(8,128)(2,1)S(1)}, bf16[512,256]{1,0:T(8,128)(2,1)S(1)}, u32[]{:S(2)}, u32[]{:S(2)}) %collective-permute-start.12) | collective-permute-done | bytes 262176 | tf_op jit(solution)/shard_map/ppermute | solution.py:41
  44.8 1.5 %collective-permute-done.11 = bf16[512,256]{1,0:T(8,128)(2,1)S(1)} collective-permute-done((bf16[512,256]{1,0:T(8,128)(2,1)S(1)}, bf16[512,256]{1,0:T(8,128)(2,1)S(1)}, u32[]{:S(2)}, u32[]{:S(2)}) %collective-permute-start.11) | collective-permute-done | bytes 262176 | tf_op jit(solution)/shard_map/ppermute | solution.py:41
  46.3 0.2 fusion
  46.5 15.7 %all_to_all.15 = bf16[8,64,256]{2,1,0:T(8,128)(2,1)S(1)} all-to-all(bf16[8,64,256]{2,1,0:T(8,128)(2,1)S(1)} %bitcast.17), channel_id=1, replica_groups=mesh['z'=8,'y'=4,'x'=4,'c'=2] {'z'}, dimensions={0} | all-to-all | bytes 524288 | tf_op jit(solution)/shard_map/all_to_all | solution.py:309
  62.3 12.1 %all_to_all.16 = bf16[8,64,256]{2,1,0:T(8,128)(2,1)S(1)} all-to-all(bf16[8,64,256]{2,1,0:T(8,128)(2,1)S(1)} %broadcast_in_dim.16), channel_id=1, replica_groups=mesh['z'=8,'y'=4,'x'=4,'c'=2] {'z'}, dimensions={0} | all-to-all | bytes 524288 | tf_op jit(solution)/shard_map/all_to_all | solution.py:311
  74.4 5.7 %shard_map.67 = bf16[32,2,16,256]{3,2,1,0:T(8,128)(2,1)S(1)} custom-call(bf16[512,256]{1,0:T(8,128)(2,1)S(1)} %bitcast.16), custom_call_target="tpu_custom_call" | custom-call | tf_op jit(solution)/shard_map/pallas_call | solution.py:240
  80.1 22.3 %all_to_all.17.returned = bf16[32,2,16,256]{3,2,1,0:T(8,128)(2,1)S(1)} all-to-all(bf16[32,2,16,256]{3,2,1,0:T(8,128)(2,1)S(1)} %shard_map.67), channel_id=1, replica_groups=mesh['z'=8,'y'=4,'x'=4,'c'=2] {'c','y','x'}, dimensions={0} | all-to-all | bytes 1048576 | tf_op jit(solution)/shard_map/all_to_all | solution.py:315
  102.4 0.9 shard_map.68
  (4 shorter events, 0.1 us)
Async XLA Ops:
  2.4 9.8 %collective-permute-start.1 = (bf16[512,256]{1,0:T(8,128)(2,1)S(1)}, bf16[512,256]{1,0:T(8,128)(2,1)S(1)}, u32[]{:S(2)}, u32[]{:S(2)}) collective-permute-start(bf16[512,256]{1,0:T(8,128)(2,1)S(1)} %select_bitcast_fusion.lat), channel_id=1, source_target_pairs={{0,1},{1,0},{2,3},{3,2},{4,5},{5,4},{6,7},{7,6},{8,9},{9,8},{10,11... | collective-permute-start | bytes 786440 | tf_op jit(solution)/shard_map/ppermute | solution.py:45
  7.7 4.6 %collective-permute-start = (bf16[256,1024]{1,0:T(8,128)(2,1)S(1)}, bf16[256,1024]{1,0:T(8,128)(2,1)S(1)}, u32[]{:S(2)}, u32[]{:S(2)}) collective-permute-start(bf16[256,1024]{1,0:T(8,128)(2,1)S(1)} %get-tuple-element.22), channel_id=1, source_target_pairs={{0,1},{1,0},{2,3},{3,2},{4,5},{5,4},{6,7},{7,6},{8,9},{9,8},{10,11... | collective-permute-start | bytes 1572872 | tf_op jit(solution)/shard_map/ppermute | solution.py:45
  8.9 3.4 %collective-permute-start.2 = (f32[16,4096]{1,0:T(8,128)S(1)}, f32[16,4096]{1,0:T(8,128)S(1)}, u32[]{:S(2)}, u32[]{:S(2)}) collective-permute-start(f32[16,4096]{1,0:T(8,128)S(1)} %get-tuple-element.42), channel_id=1, source_target_pairs={{0,1},{1,0},{2,3},{3,2},{4,5},{5,4},{6,7},{7,6},{8,9},{9,8},{10,11... | collective-permute-start | bytes 786440 | tf_op jit(solution)/shard_map/ppermute | solution.py:45
  9.4 2.2 %copy-start = (bf16[256,8192]{1,0:T(8,128)(2,1)S(1)}, bf16[256,8192]{1,0:T(8,128)(2,1)}, u32[]{:S(2)}) copy-start(bf16[256,8192]{1,0:T(8,128)(2,1)} %grad.5) | copy-start | bytes 12582916
  12.3 4.7 %collective-permute-start.3 = (bf16[256,3072]{1,0:T(8,128)(2,1)S(1)}, bf16[256,3072]{1,0:T(8,128)(2,1)S(1)}, u32[]{:S(2)}, u32[]{:S(2)}) collective-permute-start(bf16[256,3072]{1,0:T(8,128)(2,1)S(1)} %get-tuple-element.26), channel_id=1, source_target_pairs={{0,1},{1,0},{2,3},{3,2},{4,5},{5,4},{6,7},{7,6},{8,9},{9,8},{10,11... | collective-permute-start | bytes 4718600 | tf_op jit(solution)/shard_map/ppermute | solution.py:45
  13.0 12.8 %collective-permute-start.7 = (bf16[3,512,256]{2,1,0:T(8,128)(2,1)S(1)}, bf16[3,512,256]{2,1,0:T(8,128)(2,1)S(1)}, u32[]{:S(2)}, u32[]{:S(2)}) collective-permute-start(bf16[3,512,256]{2,1,0:T(8,128)(2,1)S(1)} %shard_map.61), channel_id=1, source_target_pairs={{0,4},{1,17},{2,6},{3,19},{4,0},{5,21},{6,2},{7,23},{8,12},{9,25},... | collective-permute-start | bytes 2359304 | tf_op jit(solution)/shard_map/ppermute | solution.py:41
  17.6 15.2 %collective-permute-start.9 = (bf16[3,512,256]{2,1,0:T(8,128)(2,1)S(1)}, bf16[3,512,256]{2,1,0:T(8,128)(2,1)S(1)}, u32[]{:S(2)}, u32[]{:S(2)}) collective-permute-start(bf16[3,512,256]{2,1,0:T(8,128)(2,1)S(1)} %shard_map.66), channel_id=1, source_target_pairs={{0,6},{1,25},{2,0},{3,27},{4,2},{5,29},{6,4},{7,31},{8,14},{9,1},{... | collective-permute-start | bytes 2359304 | tf_op jit(solution)/shard_map/ppermute | solution.py:41
  19.0 15.2 %collective-permute-start.8 = (bf16[3,512,256]{2,1,0:T(8,128)(2,1)S(1)}, bf16[3,512,256]{2,1,0:T(8,128)(2,1)S(1)}, u32[]{:S(2)}, u32[]{:S(2)}) collective-permute-start(bf16[3,512,256]{2,1,0:T(8,128)(2,1)S(1)} %shard_map.65), channel_id=1, source_target_pairs={{0,2},{1,9},{2,4},{3,11},{4,6},{5,13},{6,0},{7,15},{8,10},{9,17},{... | collective-permute-start | bytes 2359304 | tf_op jit(solution)/shard_map/ppermute | solution.py:41
  20.1 17.2 %collective-permute-start.4 = (bf16[1,512,256]{2,1,0:T(8,128)(2,1)S(1)}, bf16[1,512,256]{2,1,0:T(8,128)(2,1)S(1)}, u32[]{:S(2)}, u32[]{:S(2)}) collective-permute-start(bf16[1,512,256]{2,1,0:T(8,128)(2,1)S(1)} %shard_map.64), channel_id=1, source_target_pairs={{0,4},{1,17},{2,6},{3,19},{4,0},{5,21},{6,2},{7,23},{8,12},{9,25},... | collective-permute-start | bytes 786440 | tf_op jit(solution)/shard_map/ppermute | solution.py:41
  23.0 16.8 %collective-permute-start.5 = (bf16[1,512,256]{2,1,0:T(8,128)(2,1)S(1)}, bf16[1,512,256]{2,1,0:T(8,128)(2,1)S(1)}, u32[]{:S(2)}, u32[]{:S(2)}) collective-permute-start(bf16[1,512,256]{2,1,0:T(8,128)(2,1)S(1)} %get-tuple-element.34), channel_id=1, source_target_pairs={{0,2},{1,9},{2,4},{3,11},{4,6},{5,13},{6,0},{7,15},{8,10},{9,17},{... | collective-permute-start | bytes 786440 | tf_op jit(solution)/shard_map/ppermute | solution.py:41
  25.8 14.0 %collective-permute-start.6 = (bf16[1,512,256]{2,1,0:T(8,128)(2,1)S(1)}, bf16[1,512,256]{2,1,0:T(8,128)(2,1)S(1)}, u32[]{:S(2)}, u32[]{:S(2)}) collective-permute-start(bf16[1,512,256]{2,1,0:T(8,128)(2,1)S(1)} %get-tuple-element.35), channel_id=1, source_target_pairs={{0,6},{1,25},{2,0},{3,27},{4,2},{5,29},{6,4},{7,31},{8,14},{9,1},{... | collective-permute-start | bytes 786440 | tf_op jit(solution)/shard_map/ppermute | solution.py:41
  34.7 8.9 %collective-permute-start.10 = (bf16[512,256]{1,0:T(8,128)(2,1)S(1)}, bf16[512,256]{1,0:T(8,128)(2,1)S(1)}, u32[]{:S(2)}, u32[]{:S(2)}) collective-permute-start(bf16[512,256]{1,0:T(8,128)(2,1)S(1)} %get-tuple-element.38), channel_id=1, source_target_pairs={{0,16},{1,5},{2,18},{3,7},{4,20},{5,1},{6,22},{7,3},{8,24},{9,13},... | collective-permute-start | bytes 786440 | tf_op jit(solution)/shard_map/ppermute | solution.py:41
  36.4 8.4 %collective-permute-start.12 = (bf16[512,256]{1,0:T(8,128)(2,1)S(1)}, bf16[512,256]{1,0:T(8,128)(2,1)S(1)}, u32[]{:S(2)}, u32[]{:S(2)}) collective-permute-start(bf16[512,256]{1,0:T(8,128)(2,1)S(1)} %get-tuple-element.39), channel_id=1, source_target_pairs={{0,24},{1,7},{2,26},{3,1},{4,28},{5,3},{6,30},{7,5},{8,0},{9,15},{... | collective-permute-start | bytes 786440 | tf_op jit(solution)/shard_map/ppermute | solution.py:41
  37.2 9.1 %collective-permute-start.11 = (bf16[512,256]{1,0:T(8,128)(2,1)S(1)}, bf16[512,256]{1,0:T(8,128)(2,1)S(1)}, u32[]{:S(2)}, u32[]{:S(2)}) collective-permute-start(bf16[512,256]{1,0:T(8,128)(2,1)S(1)} %get-tuple-element.40), channel_id=1, source_target_pairs={{0,8},{1,3},{2,10},{3,5},{4,12},{5,7},{6,14},{7,1},{8,16},{9,11},{... | collective-permute-start | bytes 786440 | tf_op jit(solution)/shard_map/ppermute | solution.py:41

commit v8 on v6

--- a/solution.py
+++ b/solution.py
@@ -62,29 +62,64 @@
 
 def gather(grad, held, sems, nears, other):
     core = lax.axis_index("c")
-    half = grad.shape[1] // NC
-    base = (1 - core if other else core) * half
+    base = (1 - core if other else core) * (grad.shape[1] // NC)
     copies = []
     for near in nears:
         for far in range(RING):
             k = len(copies)
             start = pl.multiple_of(base + head_columns(near, far, other), HD)
             copies.append(
+                pltpu.make_async_copy(grad.at[:, pl.ds(start, HD)], held.at[k], sems.at[k])
+            )
+    return copies
+
+
+def pieces_kernel(groups, grad, early, late, mine, held, sems_in, sems_out):
+    lists = [(groups[0], True), (groups[1], True), (groups[0], False)]
+    into, onto = [], []
+    for (nears, other), out in zip(lists, (early, late, mine)):
+        at = len(into)
+        count = RING * len(nears)
+        into += gather(grad, held.at[pl.ds(at, count)], sems_in.at[pl.ds(at, count)], nears, other)
+        for k in range(count):
+            onto.append(
                 pltpu.make_async_copy(
-                    grad.at[:, pl.ds(start, HD)], held.at[:, pl.ds(k * HD, HD)], sems.at[k]
+                    held.at[at + k], out.at[:, k * HD : (k + 1) * HD], sems_out.at[at + k]
                 )
             )
-            copies[-1].start()
-    return copies
-
-
-def first_kernel(nears, counts, latent, momentum, grad, lat, mom_own, mom_other, unit, piece, sems):
-    copies = gather(grad, piece, sems, nears, True)
+    for copy in into:
+        copy.start()
+    for k in range(len(into)):
+        into[k].wait()
+        onto[k].start()
+    for copy in onto:
+        copy.wait()
+
+
+def column_pieces(grad, groups):
+    slots = grad.shape[0]
+    widths = [RING * len(nears) for nears in (groups[0], groups[1], groups[0])]
+    hbm = pl.BlockSpec(memory_space=pl.ANY)
+    return pl.pallas_call(
+        functools.partial(pieces_kernel, groups),
+        out_shape=[jax.ShapeDtypeStruct((slots, width * HD), bf16) for width in widths],
+        in_specs=[hbm],
+        out_specs=[hbm] * 3,
+        scratch_shapes=[
+            pltpu.VMEM((sum(widths), slots, HD), bf16),
+            pltpu.SemaphoreType.DMA((sum(widths),)),
+            pltpu.SemaphoreType.DMA((sum(widths),)),
+        ],
+        compiler_params=pltpu.CompilerParams(vmem_limit_bytes=LARGE),
+    )(grad)
+
+
+def first_kernel(counts, latent, momentum, mine, lat, mom_own, mom_other, unit, own):
     core = lax.axis_index("c")
     slots, features = latent.shape
+    depth, half = momentum.shape[0], momentum.shape[1] // NC
     live = lax.broadcasted_iota(jnp.int32, (slots, features), 0) < counts[0]
     lat[...] = jnp.where(live, latent[...], jnp.zeros_like(latent)).T
-    depth, half = momentum.shape[0], momentum.shape[1] // NC
     for out, which in ((mom_own, core), (mom_other, 1 - core)):
         value = (DECAY / NZ) * momentum[:, pl.ds(pl.multiple_of(which * half, half), half)]
         high = value.astype(bf16)
@@ -95,61 +130,46 @@
     at = lax.broadcasted_iota(jnp.int32, unit.shape, 1)
     core_of = jnp.where(at < 2 * depth, core, 1 - core)
     unit[...] = (row == (here * NC + core_of) * depth + at % depth).astype(f32).astype(bf16)
-    for copy in copies:
-        copy.wait()
-
-
-def first(counts, latent, momentum, grad, nears):
+    for far in range(RING):
+        columns = mine[:, far * HD : (far + 1) * HD]
+        own[far] = jnp.dot(lat[...], columns, preferred_element_type=f32).astype(bf16)
+
+
+def first(counts, latent, momentum, mine):
     slots, features = latent.shape
     depth, columns = momentum.shape
-    heads = RING * len(nears)
     vmem = pl.BlockSpec(memory_space=pltpu.VMEM)
     mom = jax.ShapeDtypeStruct((2 * depth, columns // NC), bf16)
     return pl.pallas_call(
-        functools.partial(first_kernel, nears),
+        first_kernel,
         out_shape=[
             jax.ShapeDtypeStruct((features, slots), bf16),
             mom,
             mom,
             jax.ShapeDtypeStruct((features, 4 * depth), bf16),
-            jax.ShapeDtypeStruct((slots, heads * HD), bf16),
+            jax.ShapeDtypeStruct((RING, features, HD), bf16),
         ],
-        in_specs=[pl.BlockSpec(memory_space=pltpu.SMEM), vmem, vmem, pl.BlockSpec(memory_space=pl.ANY)],
-        out_specs=[vmem] * 5,
-        scratch_shapes=[pltpu.SemaphoreType.DMA((heads,))],
-        compiler_params=pltpu.CompilerParams(vmem_limit_bytes=LARGE),
-    )(counts, latent, momentum, grad)
-
-
-def piece_kernel(nears, grad, piece, sems):
-    for copy in gather(grad, piece, sems, nears, True):
-        copy.wait()
-
-
-def later_piece(grad, nears):
-    heads = RING * len(nears)
-    return pl.pallas_call(
-        functools.partial(piece_kernel, nears),
-        out_shape=jax.ShapeDtypeStruct((grad.shape[0], heads * HD), bf16),
-        in_specs=[pl.BlockSpec(memory_space=pl.ANY)],
-        out_specs=pl.BlockSpec(memory_space=pltpu.VMEM),
-        scratch_shapes=[pltpu.SemaphoreType.DMA((heads,))],
-        compiler_params=pltpu.CompilerParams(vmem_limit_bytes=LARGE),
-    )(grad)
+        in_specs=[pl.BlockSpec(memory_space=pltpu.SMEM), vmem, vmem, vmem],
+        compiler_params=pltpu.CompilerParams(vmem_limit_bytes=VMEM),
+    )(counts, latent, momentum, mine)
 
 
 def own_kernel(nears, lat, grad, *refs):
     outs, (held, sems) = refs[: len(nears)], refs[len(nears) :]
-    for copy in gather(grad, held, sems, nears, False):
-        copy.wait()
-    for k in range(RING * len(nears)):
-        product = jnp.dot(lat[...], held[:, k * HD : (k + 1) * HD], preferred_element_type=f32)
-        outs[k // RING][k % RING] = product.astype(bf16)
+    copies = gather(grad, held, sems, nears, False)
+    for copy in copies:
+        copy.start()
+    for near in range(len(nears)):
+        for far in range(RING):
+            copies[near * RING + far].wait()
+        for far in range(RING):
+            value = jnp.dot(lat[...], held[near * RING + far], preferred_element_type=f32)
+            outs[near][far] = value.astype(bf16)
 
 
 def own_products(lat, grad, nears):
     features, tokens = lat.shape
-    heads = RING * len(nears)
+    count = RING * len(nears)
     vmem = pl.BlockSpec(memory_space=pltpu.VMEM)
     return pl.pallas_call(
         functools.partial(own_kernel, nears),
@@ -157,13 +177,13 @@
         in_specs=[vmem, pl.BlockSpec(memory_space=pl.ANY)],
         out_specs=[vmem] * len(nears),
         scratch_shapes=[
-            pltpu.VMEM((tokens, heads * HD), bf16),
-            pltpu.SemaphoreType.DMA((heads,)),
+            pltpu.VMEM((count, tokens, HD), bf16),
+            pltpu.SemaphoreType.DMA((count,)),
         ],
         compiler_params=pltpu.CompilerParams(vmem_limit_bytes=LARGE),
         cost_estimate=pl.CostEstimate(
-            flops=2 * heads * features * HD * tokens,
-            bytes_accessed=heads * (tokens + features) * HD * 2,
+            flops=2 * count * features * HD * tokens,
+            bytes_accessed=count * (tokens + features) * HD * 2,
             transcendentals=0,
         ),
     )(lat, grad)
@@ -282,30 +302,31 @@
 def body(latent, latent_grad, row_counts, momentum):
     features = latent.shape[1]
     order, rest = (2, 1, 3), (1, 2, 3)
+    tie = lax.optimization_barrier
 
     early, late = (2,), (1, 3, 0)
-    lat_own, mom_own, mom_other, unit, piece_early = first(
-        row_counts, latent, momentum, latent_grad, early
-    )
-    grad_late, piece_early = lax.optimization_barrier((latent_grad, piece_early))
+    piece_early, piece_late, mine = column_pieces(latent_grad, (early, late))
+    lat_own, mom_own, mom_other, unit, own_early = first(row_counts, latent, momentum, mine)
     piece_early, lat_other, mom_other = (
         swap_cores(piece_early), swap_cores(lat_own), swap_cores(mom_other)
     )
-    piece_late = swap_cores(later_piece(grad_late, late))
+    piece_late, piece_early, lat_other, mom_other = tie(
+        (piece_late, piece_early, lat_other, mom_other)
+    )
+    piece_late = swap_cores(piece_late)
     shared = (unit, lat_other, mom_own, mom_other)
 
-    own = dict(zip(early, own_products(lat_own, grad_late, early)))
-    on = list(block(own, early, [(early[0], rest)], *shared, piece_early))
-    lat_late, on[0] = lax.optimization_barrier((lat_own, on[0]))
-    own.update(zip(late, own_products(lat_late, grad_late, late)))
-    on += [block(own, late, [(k, rest)], *shared, piece_late)[0] for k in order[1:]]
+    own = {2: own_early}
+    (first_on,) = block(own, early, [(2, rest)], *shared, piece_early)
+    lat_late, first_on = tie((lat_own, first_on))
+    own[1], own[3], own[0] = own_products(lat_late, latent_grad, late)
+    on = [first_on] + [block(own, late, [(k, rest)], *shared, piece_late)[0] for k in order[1:]]
     on = [shift(value, 0, k) for value, k in zip(on, order)]
-    stay_early = block(own, early, [(k, (0,)) for k in early], *shared, piece_early)
-    *stay_late, kept_stay, kept_on = block(
+    (stay,) = block(own, early, [(2, (0,))], *shared, piece_early)
+    *stays, kept_stay, kept_on = block(
         own, late, [(1, (0,)), (3, (0,)), (0, (0,)), (0, rest)], *shared, piece_late
     )
-    *stay, on[0] = lax.optimization_barrier((*stay_early, *stay_late, on[0]))
-    stay = [shift(value, 0, k) for value, k in zip(stay, order)]
+    stay = [shift(value, 0, k) for value, k in zip([stay] + stays, order)]
 
     total = kept_on + sum(value.astype(f32) for value in on)
     got = [shift(total[k - 1].astype(bf16), 1, k) for k in order]
@@ -313,8 +334,8 @@
     head = (head + sum(value.astype(f32) for value in got)).astype(bf16)
 
     pieces = lax.all_to_all(head.reshape(NZ, -1, HD), "z", 0, 0, tiled=True)
-    eighth = jnp.sum(pieces.astype(f32), axis=0).astype(bf16)
-    moment = lax.all_to_all(jnp.broadcast_to(eighth, (NZ,) + eighth.shape), "z", 0, 0, tiled=True)
+    piece = jnp.sum(pieces.astype(f32), axis=0).astype(bf16)
+    moment = lax.all_to_all(jnp.broadcast_to(piece, (NZ,) + piece.shape), "z", 0, 0, tiled=True)
     moment = moment.reshape(features, HD)
 
     outgoing = newton_schulz(moment, NC * NY * NX)

time: 105 us -> 101 us (0.962)
  local copies, waits for them, and re-layouts: 3.14 us -> 0.08 us
  waiting for transfers between devices: 21.1 us -> 19.5 us
    unnamed x6 -> x4, local copies, waits for them, and re-layouts: 3.07 us -> 0.01 us
    ppermute x4, waiting for transfers between devices: 3.35 us -> 1.4 us  [swap_cores(): lax.ppermute(value, AXES, [(device_at(z, y, x, c), device_at(z, y, x, 1 -...]
    pallas_call x2, Pallas kernels: 1.77 us -> 2.94 us  [the longest x1 2.28 us: column_pieces(): pl.pallas_call(functools.partial(pieces_kernel, groups), out_shape=[jax.S...]
    pallas_call x2 -> x1, Pallas kernels: 3.13 us -> 2.54 us  [own_products(): pl.pallas_call(functools.partial(own_kernel, nears), out_shape=[jax.Shape...]
where the time goes in v8:
time: 101 us
  blocking collectives  50.2 us (50%)
  waiting for transfers between devices  19.5 us (19%)
  Pallas kernels  15.2 us (15%)
  starting transfers between devices  13.6 us (13%)
  between operations  1.42 us (1%)
    all_to_all x1, blocking collectives, body(): returned = lax.all_to_all(outgoing, PLANE, 0, 0, tiled=True)  21.9 us
    ppermute x9, waiting for transfers between devices, shift(): return lax.ppermute(value, AXES, pairs)  18.1 us
    all_to_all x1, blocking collectives, body(): pieces = lax.all_to_all(head.reshape(NZ, -1, HD), 'z', 0, 0, tiled=True)  15.9 us
    all_to_all x1, blocking collectives, body(): lax.all_to_all(jnp.broadcast_to(piece, (NZ,) + piece.shape), 'z', 0, 0, t...  12.4 us
    ppermute x9, starting transfers between devices, shift(): return lax.ppermute(value, AXES, pairs)  9.56 us
    pallas_call x1, Pallas kernels, newton_schulz(): pl.pallas_call(newton_schulz_kernel, out_shape=jax.ShapeDtypeStruct((owne...  5.75 us
    ppermute x4, starting transfers between devices, swap_cores(): lax.ppermute(value, AXES, [(device_at(z, y, x, c), device_at(z, y, x, 1 -...  4.06 us
    pallas_call x5, Pallas kernels, block(): pl.pallas_call(functools.partial(block_kernel, tiles), out_shape=[jax.Sha...  3.05 us
  transfers between devices with their start and end apart: 13, of which 9 were waited for; matrix products, arithmetic and copies ran while one was open for 1% of the time, Pallas kernels for 6%

profile of v8, /device:TPU:1, one launch (start us, length us, event | category | flops | bytes accessed | tf_op | source)
XLA Modules:
  0.0 100.7 jit_solution(1320695168413114463)
XLA Ops:
  0.6 0.0 copy-start
  0.6 0.0 copy-start.1
  0.6 2.3 %shard_map.59 = (bf16[256,1024]{1,0:T(8,128)(2,1)S(1)}, bf16[256,3072]{1,0:T(8,128)(2,1)S(1)}, bf16[256,1024]{1,0:T(8,128)(2,1)S(1)}) custom-call(bf16[256,8192]{1,0:T(8,128)(2,1)} %grad.3), custom_call_target="tpu_custom_call" | custom-call | tf_op jit(solution)/shard_map/pallas_call | solution.py:103
  2.9 3.3 %collective-permute-start = (bf16[256,1024]{1,0:T(8,128)(2,1)S(1)}, bf16[256,1024]{1,0:T(8,128)(2,1)S(1)}, u32[]{:S(2)}, u32[]{:S(2)}) collective-permute-start(bf16[256,1024]{1,0:T(8,128)(2,1)S(1)} %get-tuple-element.26), channel_id=1, source_target_pairs={{0,1},{1,0},{2,3},{3,2},{4,5},{5,4},{6,7},{7,6},{8,9},{9,8},{10,11... | collective-permute-start | bytes 1572872 | tf_op jit(solution)/shard_map/ppermute | solution.py:45
  6.9 0.0 copy-done
  6.9 0.0 copy-done.1
  6.9 0.7 shard_map.60
  7.6 0.1 collective-permute-start.2
  7.7 0.5 collective-permute-start.1
  8.2 1.0 %collective-permute-done.2.mom_other = bf16[32,4096]{1,0:T(8,128)(2,1)S(1)} collective-permute-done((bf16[32,4096]{1,0:T(8,128)(2,1)S(1)}, bf16[32,4096]{1,0:T(8,128)(2,1)S(1)}, u32[]{:S(2)}, u32[]{:S(2)}) %collective-permute-start.2) | collective-permute-done | bytes 262176 | tf_op jit(solution)/shard_map/ppermute | solution.py:45
  9.2 0.4 collective-permute-done.1.lat
  9.6 0.0 collective-permute-done.grad
  9.6 0.1 collective-permute-start.3
  9.7 0.6 shard_map.61
  10.3 1.3 %collective-permute-start.7 = (bf16[3,512,256]{2,1,0:T(8,128)(2,1)S(1)}, bf16[3,512,256]{2,1,0:T(8,128)(2,1)S(1)}, u32[]{:S(2)}, u32[]{:S(2)}) collective-permute-start(bf16[3,512,256]{2,1,0:T(8,128)(2,1)S(1)} %shard_map.61), channel_id=1, source_target_pairs={{0,4},{1,17},{2,6},{3,19},{4,0},{5,21},{6,2},{7,23},{8,12},{9,25},... | collective-permute-start | bytes 2359304 | tf_op jit(solution)/shard_map/ppermute | solution.py:41
  11.6 2.5 %shard_map.62 = (bf16[4,512,256]{2,1,0:T(8,128)(2,1)S(1)}, bf16[4,512,256]{2,1,0:T(8,128)(2,1)S(1)}, bf16[4,512,256]{2,1,0:T(8,128)(2,1)S(1)}) custom-call(bf16[512,256]{1,0:T(8,128)(2,1)S(1)} %get-tuple-element.35.lat, bf16[256,8192]{1,0:T(8,128)(2,1)} %grad.3), custom_call_target="tpu_custom_call" | custom-call | flops 805306368 | bytes 4718592 | tf_op jit(solution)/shard_map/pallas_call | solution.py:174
  14.1 0.0 collective-permute-done.3.grad
  14.2 0.6 shard_map.66
  14.7 0.9 collective-permute-start.9
  15.6 0.6 shard_map.65
  16.2 0.8 collective-permute-start.8
  17.0 0.3 shard_map.64
  17.3 1.9 %collective-permute-start.4 = (bf16[1,512,256]{2,1,0:T(8,128)(2,1)S(1)}, bf16[1,512,256]{2,1,0:T(8,128)(2,1)S(1)}, u32[]{:S(2)}, u32[]{:S(2)}) collective-permute-start(bf16[1,512,256]{2,1,0:T(8,128)(2,1)S(1)} %shard_map.64), channel_id=1, source_target_pairs={{0,4},{1,17},{2,6},{3,19},{4,0},{5,21},{6,2},{7,23},{8,12},{9,25},... | collective-permute-start | bytes 786440 | tf_op jit(solution)/shard_map/ppermute | solution.py:41
  19.1 1.0 shard_map.63
  20.1 0.9 collective-permute-start.5
  21.0 2.1 %collective-permute-done.7 = bf16[3,512,256]{2,1,0:T(8,128)(2,1)S(1)} collective-permute-done((bf16[3,512,256]{2,1,0:T(8,128)(2,1)S(1)}, bf16[3,512,256]{2,1,0:T(8,128)(2,1)S(1)}, u32[]{:S(2)}, u32[]{:S(2)}) %collective-permute-start.7) | collective-permute-done | bytes 786464 | tf_op jit(solution)/shard_map/ppermute | solution.py:41
  23.1 1.0 collective-permute-start.6
  24.1 6.0 %collective-permute-done.9 = bf16[3,512,256]{2,1,0:T(8,128)(2,1)S(1)} collective-permute-done((bf16[3,512,256]{2,1,0:T(8,128)(2,1)S(1)}, bf16[3,512,256]{2,1,0:T(8,128)(2,1)S(1)}, u32[]{:S(2)}, u32[]{:S(2)}) %collective-permute-start.9) | collective-permute-done | bytes 786464 | tf_op jit(solution)/shard_map/ppermute | solution.py:41
  30.1 1.3 %collective-permute-done.8 = bf16[3,512,256]{2,1,0:T(8,128)(2,1)S(1)} collective-permute-done((bf16[3,512,256]{2,1,0:T(8,128)(2,1)S(1)}, bf16[3,512,256]{2,1,0:T(8,128)(2,1)S(1)}, u32[]{:S(2)}, u32[]{:S(2)}) %collective-permute-start.8) | collective-permute-done | bytes 786464 | tf_op jit(solution)/shard_map/ppermute | solution.py:41
  31.5 0.5 add_convert_fusion
  32.0 0.1 slice_bitcast_fusion.2
  32.0 1.5 %collective-permute-start.10 = (bf16[512,256]{1,0:T(8,128)(2,1)S(1)}, bf16[512,256]{1,0:T(8,128)(2,1)S(1)}, u32[]{:S(2)}, u32[]{:S(2)}) collective-permute-start(bf16[512,256]{1,0:T(8,128)(2,1)S(1)} %get-tuple-element.44), channel_id=1, source_target_pairs={{0,16},{1,5},{2,18},{3,7},{4,20},{5,1},{6,22},{7,3},{8,24},{9,13},... | collective-permute-start | bytes 786440 | tf_op jit(solution)/shard_map/ppermute | solution.py:41
  33.5 0.9 collective-permute-start.12
  34.4 0.0 collective-permute-done.4
  34.4 0.6 collective-permute-start.11
  35.0 2.1 %collective-permute-done.5 = bf16[1,512,256]{2,1,0:T(8,128)(2,1)S(1)} collective-permute-done((bf16[1,512,256]{2,1,0:T(8,128)(2,1)S(1)}, bf16[1,512,256]{2,1,0:T(8,128)(2,1)S(1)}, u32[]{:S(2)}, u32[]{:S(2)}) %collective-permute-start.5) | collective-permute-done | bytes 262176 | tf_op jit(solution)/shard_map/ppermute | solution.py:41
  37.1 0.0 collective-permute-done.6
  37.1 3.7 %collective-permute-done.10 = bf16[512,256]{1,0:T(8,128)(2,1)S(1)} collective-permute-done((bf16[512,256]{1,0:T(8,128)(2,1)S(1)}, bf16[512,256]{1,0:T(8,128)(2,1)S(1)}, u32[]{:S(2)}, u32[]{:S(2)}) %collective-permute-start.10) | collective-permute-done | bytes 262176 | tf_op jit(solution)/shard_map/ppermute | solution.py:41
  40.8 1.2 %collective-permute-done.12 = bf16[512,256]{1,0:T(8,128)(2,1)S(1)} collective-permute-done((bf16[512,256]{1,0:T(8,128)(2,1)S(1)}, bf16[512,256]{1,0:T(8,128)(2,1)S(1)}, u32[]{:S(2)}, u32[]{:S(2)}) %collective-permute-start.12) | collective-permute-done | bytes 262176 | tf_op jit(solution)/shard_map/ppermute | solution.py:41
  42.0 1.5 %collective-permute-done.11 = bf16[512,256]{1,0:T(8,128)(2,1)S(1)} collective-permute-done((bf16[512,256]{1,0:T(8,128)(2,1)S(1)}, bf16[512,256]{1,0:T(8,128)(2,1)S(1)}, u32[]{:S(2)}, u32[]{:S(2)}) %collective-permute-start.11) | collective-permute-done | bytes 262176 | tf_op jit(solution)/shard_map/ppermute | solution.py:41
  43.6 0.2 fusion
  43.8 15.9 %all_to_all.15 = bf16[8,64,256]{2,1,0:T(8,128)(2,1)S(1)} all-to-all(bf16[8,64,256]{2,1,0:T(8,128)(2,1)S(1)} %bitcast.13), channel_id=1, replica_groups=mesh['z'=8,'y'=4,'x'=4,'c'=2] {'z'}, dimensions={0} | all-to-all | bytes 524288 | tf_op jit(solution)/shard_map/all_to_all | solution.py:336
  59.7 12.4 %all_to_all.16 = bf16[8,64,256]{2,1,0:T(8,128)(2,1)S(1)} all-to-all(bf16[8,64,256]{2,1,0:T(8,128)(2,1)S(1)} %broadcast_in_dim.3), channel_id=1, replica_groups=mesh['z'=8,'y'=4,'x'=4,'c'=2] {'z'}, dimensions={0} | all-to-all | bytes 524288 | tf_op jit(solution)/shard_map/all_to_all | solution.py:338
  72.1 5.7 %shard_map.67 = bf16[32,2,16,256]{3,2,1,0:T(8,128)(2,1)S(1)} custom-call(bf16[512,256]{1,0:T(8,128)(2,1)S(1)} %bitcast.12), custom_call_target="tpu_custom_call" | custom-call | tf_op jit(solution)/shard_map/pallas_call | solution.py:272
  77.9 21.9 %all_to_all.17.returned = bf16[32,2,16,256]{3,2,1,0:T(8,128)(2,1)S(1)} all-to-all(bf16[32,2,16,256]{3,2,1,0:T(8,128)(2,1)S(1)} %shard_map.67), channel_id=1, replica_groups=mesh['z'=8,'y'=4,'x'=4,'c'=2] {'c','y','x'}, dimensions={0} | all-to-all | bytes 1048576 | tf_op jit(solution)/shard_map/all_to_all | solution.py:342
  99.8 0.9 shard_map.68
  (2 shorter events, 0.1 us)
Async XLA Ops:
  0.6 6.3 %copy-start = (f32[16,8192]{1,0:T(8,128)S(1)}, f32[16,8192]{1,0:T(8,128)}, u32[]{:S(2)}) copy-start(f32[16,8192]{1,0:T(8,128)} %momentum.1) | copy-start | bytes 1572868
  0.6 6.3 %copy-start.1 = (bf16[256,512]{1,0:T(8,128)(2,1)S(1)}, bf16[256,512]{1,0:T(8,128)(2,1)}, u32[]{:S(2)}) copy-start(bf16[256,512]{1,0:T(8,128)(2,1)} %latent.1) | copy-start | bytes 786436
  2.9 6.7 %collective-permute-start = (bf16[256,1024]{1,0:T(8,128)(2,1)S(1)}, bf16[256,1024]{1,0:T(8,128)(2,1)S(1)}, u32[]{:S(2)}, u32[]{:S(2)}) collective-permute-start(bf16[256,1024]{1,0:T(8,128)(2,1)S(1)} %get-tuple-element.26), channel_id=1, source_target_pairs={{0,1},{1,0},{2,3},{3,2},{4,5},{5,4},{6,7},{7,6},{8,9},{9,8},{10,11... | collective-permute-start | bytes 1572872 | tf_op jit(solution)/shard_map/ppermute | solution.py:45
  7.6 1.6 %collective-permute-start.2 = (bf16[32,4096]{1,0:T(8,128)(2,1)S(1)}, bf16[32,4096]{1,0:T(8,128)(2,1)S(1)}, u32[]{:S(2)}, u32[]{:S(2)}) collective-permute-start(bf16[32,4096]{1,0:T(8,128)(2,1)S(1)} %get-tuple-element.28), channel_id=1, source_target_pairs={{0,1},{1,0},{2,3},{3,2},{4,5},{5,4},{6,7},{7,6},{8,9},{9,8},{10,11... | collective-permute-start | bytes 786440 | tf_op jit(solution)/shard_map/ppermute | solution.py:45
  7.7 1.9 %collective-permute-start.1 = (bf16[512,256]{1,0:T(8,128)(2,1)S(1)}, bf16[512,256]{1,0:T(8,128)(2,1)S(1)}, u32[]{:S(2)}, u32[]{:S(2)}) collective-permute-start(bf16[512,256]{1,0:T(8,128)(2,1)S(1)} %get-tuple-element.35.lat), channel_id=1, source_target_pairs={{0,1},{1,0},{2,3},{3,2},{4,5},{5,4},{6,7},{7,6},{8,9},{9,8},{10,11... | collective-permute-start | bytes 786440 | tf_op jit(solution)/shard_map/ppermute | solution.py:45
  9.6 4.5 %collective-permute-start.3 = (bf16[256,3072]{1,0:T(8,128)(2,1)S(1)}, bf16[256,3072]{1,0:T(8,128)(2,1)S(1)}, u32[]{:S(2)}, u32[]{:S(2)}) collective-permute-start(bf16[256,3072]{1,0:T(8,128)(2,1)S(1)} %get-tuple-element.32), channel_id=1, source_target_pairs={{0,1},{1,0},{2,3},{3,2},{4,5},{5,4},{6,7},{7,6},{8,9},{9,8},{10,11... | collective-permute-start | bytes 4718600 | tf_op jit(solution)/shard_map/ppermute | solution.py:45
  10.3 12.8 %collective-permute-start.7 = (bf16[3,512,256]{2,1,0:T(8,128)(2,1)S(1)}, bf16[3,512,256]{2,1,0:T(8,128)(2,1)S(1)}, u32[]{:S(2)}, u32[]{:S(2)}) collective-permute-start(bf16[3,512,256]{2,1,0:T(8,128)(2,1)S(1)} %shard_map.61), channel_id=1, source_target_pairs={{0,4},{1,17},{2,6},{3,19},{4,0},{5,21},{6,2},{7,23},{8,12},{9,25},... | collective-permute-start | bytes 2359304 | tf_op jit(solution)/shard_map/ppermute | solution.py:41
  14.7 15.4 %collective-permute-start.9 = (bf16[3,512,256]{2,1,0:T(8,128)(2,1)S(1)}, bf16[3,512,256]{2,1,0:T(8,128)(2,1)S(1)}, u32[]{:S(2)}, u32[]{:S(2)}) collective-permute-start(bf16[3,512,256]{2,1,0:T(8,128)(2,1)S(1)} %shard_map.66), channel_id=1, source_target_pairs={{0,6},{1,25},{2,0},{3,27},{4,2},{5,29},{6,4},{7,31},{8,14},{9,1},{... | collective-permute-start | bytes 2359304 | tf_op jit(solution)/shard_map/ppermute | solution.py:41
  16.2 15.3 %collective-permute-start.8 = (bf16[3,512,256]{2,1,0:T(8,128)(2,1)S(1)}, bf16[3,512,256]{2,1,0:T(8,128)(2,1)S(1)}, u32[]{:S(2)}, u32[]{:S(2)}) collective-permute-start(bf16[3,512,256]{2,1,0:T(8,128)(2,1)S(1)} %shard_map.65), channel_id=1, source_target_pairs={{0,2},{1,9},{2,4},{3,11},{4,6},{5,13},{6,0},{7,15},{8,10},{9,17},{... | collective-permute-start | bytes 2359304 | tf_op jit(solution)/shard_map/ppermute | solution.py:41
  17.3 17.1 %collective-permute-start.4 = (bf16[1,512,256]{2,1,0:T(8,128)(2,1)S(1)}, bf16[1,512,256]{2,1,0:T(8,128)(2,1)S(1)}, u32[]{:S(2)}, u32[]{:S(2)}) collective-permute-start(bf16[1,512,256]{2,1,0:T(8,128)(2,1)S(1)} %shard_map.64), channel_id=1, source_target_pairs={{0,4},{1,17},{2,6},{3,19},{4,0},{5,21},{6,2},{7,23},{8,12},{9,25},... | collective-permute-start | bytes 786440 | tf_op jit(solution)/shard_map/ppermute | solution.py:41
  20.1 17.0 %collective-permute-start.5 = (bf16[1,512,256]{2,1,0:T(8,128)(2,1)S(1)}, bf16[1,512,256]{2,1,0:T(8,128)(2,1)S(1)}, u32[]{:S(2)}, u32[]{:S(2)}) collective-permute-start(bf16[1,512,256]{2,1,0:T(8,128)(2,1)S(1)} %get-tuple-element.40), channel_id=1, source_target_pairs={{0,2},{1,9},{2,4},{3,11},{4,6},{5,13},{6,0},{7,15},{8,10},{9,17},{... | collective-permute-start | bytes 786440 | tf_op jit(solution)/shard_map/ppermute | solution.py:41
  23.1 14.0 %collective-permute-start.6 = (bf16[1,512,256]{2,1,0:T(8,128)(2,1)S(1)}, bf16[1,512,256]{2,1,0:T(8,128)(2,1)S(1)}, u32[]{:S(2)}, u32[]{:S(2)}) collective-permute-start(bf16[1,512,256]{2,1,0:T(8,128)(2,1)S(1)} %get-tuple-element.41), channel_id=1, source_target_pairs={{0,6},{1,25},{2,0},{3,27},{4,2},{5,29},{6,4},{7,31},{8,14},{9,1},{... | collective-permute-start | bytes 786440 | tf_op jit(solution)/shard_map/ppermute | solution.py:41
  32.0 8.8 %collective-permute-start.10 = (bf16[512,256]{1,0:T(8,128)(2,1)S(1)}, bf16[512,256]{1,0:T(8,128)(2,1)S(1)}, u32[]{:S(2)}, u32[]{:S(2)}) collective-permute-start(bf16[512,256]{1,0:T(8,128)(2,1)S(1)} %get-tuple-element.44), channel_id=1, source_target_pairs={{0,16},{1,5},{2,18},{3,7},{4,20},{5,1},{6,22},{7,3},{8,24},{9,13},... | collective-permute-start | bytes 786440 | tf_op jit(solution)/shard_map/ppermute | solution.py:41
  33.5 8.5 %collective-permute-start.12 = (bf16[512,256]{1,0:T(8,128)(2,1)S(1)}, bf16[512,256]{1,0:T(8,128)(2,1)S(1)}, u32[]{:S(2)}, u32[]{:S(2)}) collective-permute-start(bf16[512,256]{1,0:T(8,128)(2,1)S(1)} %get-tuple-element.45), channel_id=1, source_target_pairs={{0,24},{1,7},{2,26},{3,1},{4,28},{5,3},{6,30},{7,5},{8,0},{9,15},{... | collective-permute-start | bytes 786440 | tf_op jit(solution)/shard_map/ppermute | solution.py:41
  34.4 9.2 %collective-permute-start.11 = (bf16[512,256]{1,0:T(8,128)(2,1)S(1)}, bf16[512,256]{1,0:T(8,128)(2,1)S(1)}, u32[]{:S(2)}, u32[]{:S(2)}) collective-permute-start(bf16[512,256]{1,0:T(8,128)(2,1)S(1)} %get-tuple-element.46), channel_id=1, source_target_pairs={{0,8},{1,3},{2,10},{3,5},{4,12},{5,7},{6,14},{7,1},{8,16},{9,11},{... | collective-permute-start | bytes 786440 | tf_op jit(solution)/shard_map/ppermute | solution.py:41

commit v9 on v8

--- a/solution.py
+++ b/solution.py
@@ -18,6 +18,7 @@
 COEF_A, COEF_B, COEF_C = 3.4445, -4.775, 2.0315
 DECAY = 0.95
 VMEM = 16 * 1024 * 1024
+MIDDLE = 5 * 10**9
 LARGE = 48 * 1024 * 1024
 bf16, f32 = jnp.bfloat16, jnp.float32
 
@@ -192,37 +193,85 @@
 def block_kernel(tiles, unit, lat, mom_own, mom_other, grad, *refs):
     count = 1 + max(t[0] for t in tiles)
     operands, outs = refs[:count], refs[count:]
-    for operand, at_piece, result, near, fars in tiles:
+    for (operand, at_piece, near, fars, row), out in zip(tiles, outs):
+        rows = slice(row, row + out.shape[1])
         for place, far in enumerate(fars):
             at = pl.ds(head_columns(near, far), HD)
             in_piece = (at_piece * RING + far) * HD
             mom = jnp.concatenate([mom_own[:, at], mom_other[:, at]], axis=0)
-            other = jnp.dot(lat[...], grad[:, in_piece : in_piece + HD], preferred_element_type=f32)
-            added = jnp.dot(unit[...], mom, preferred_element_type=f32)
-            total = operands[operand][far].astype(f32) + other.astype(bf16).astype(f32) + added
-            outs[result][place] = total.astype(outs[result].dtype)
+            other = jnp.dot(
+                lat[rows, :], grad[:, in_piece : in_piece + HD], preferred_element_type=f32
+            )
+            added = jnp.dot(unit[rows, :], mom, preferred_element_type=f32)
+            total = operands[operand][far, rows].astype(f32) + other.astype(bf16).astype(f32) + added
+            out[place] = total.astype(out.dtype)
 
 
 def block(own, held, which, unit, lat, mom_own, mom_other, grad):
-    features, tokens = lat.shape
-    nears = sorted({near for near, _ in which})
-    tiles = [
-        (nears.index(near), held.index(near), k, near, fars) for k, (near, fars) in enumerate(which)
-    ]
-    heads = sum(len(fars) for _, fars in which)
+    tokens = lat.shape[1]
+    nears = sorted({w[0] for w in which})
+    tiles = [(nears.index(w[0]), held.index(w[0]), *w[:3]) for w in which]
+    work = sum(len(w[1]) * w[3] for w in which)
     return pl.pallas_call(
         functools.partial(block_kernel, tiles),
-        out_shape=[
-            jax.ShapeDtypeStruct((len(fars), features, HD), f32 if near == 0 else bf16)
-            for near, fars in which
-        ],
+        out_shape=[jax.ShapeDtypeStruct((len(w[1]), w[3], HD), w[4]) for w in which],
         compiler_params=pltpu.CompilerParams(vmem_limit_bytes=VMEM),
         cost_estimate=pl.CostEstimate(
-            flops=2 * heads * features * HD * (tokens + unit.shape[1]),
-            bytes_accessed=heads * (tokens + 2 * features) * HD * 2,
+            flops=2 * work * HD * (tokens + unit.shape[1]),
+            bytes_accessed=work * HD * 4 + len(which) * RING * tokens * HD * 2,
             transcendentals=0,
         ),
     )(unit, lat, mom_own, mom_other, grad, *[own[near] for near in nears])
+
+
+def middle_kernel(kept, upper, lower, one, three, two_a, two_b, kept_out, one_out, three_out):
+    half = upper.shape[1]
+    for k in range(kept.shape[0]):
+        kept_out[k, :half] = kept[k, :half] + upper[k].astype(f32)
+        kept_out[k, half:] = kept[k, half:] + lower[k].astype(f32)
+    one_out[:half, :] = (one[0, :half] + two_a[0].astype(f32)).astype(bf16)
+    one_out[half:, :] = one[0, half:].astype(bf16)
+    three_out[:half, :] = three[0, :half].astype(bf16)
+    three_out[half:, :] = (three[0, half:] + two_b[0].astype(f32)).astype(bf16)
+
+
+def middle(kept, *parts):
+    stay = jax.ShapeDtypeStruct(kept.shape[1:], bf16)
+    return pl.pallas_call(
+        middle_kernel,
+        out_shape=[jax.ShapeDtypeStruct(kept.shape, f32), stay, stay],
+        compiler_params=pltpu.CompilerParams(vmem_limit_bytes=VMEM),
+        cost_estimate=pl.CostEstimate(flops=MIDDLE, bytes_accessed=0, transcendentals=0),
+    )(kept, *parts)
+
+
+def stay_kernel(kept, one, three, out):
+    out[...] = kept[0] + one[...].astype(f32) + three[...].astype(f32)
+
+
+def stay_sum(kept, one, three):
+    return pl.pallas_call(
+        stay_kernel,
+        out_shape=jax.ShapeDtypeStruct(kept.shape[1:], f32),
+        compiler_params=pltpu.CompilerParams(vmem_limit_bytes=VMEM),
+        cost_estimate=pl.CostEstimate(flops=MIDDLE, bytes_accessed=0, transcendentals=0),
+    )(kept, one, three)
+
+
+def add_kernel(kept, upper, lower, *outs):
+    half = upper.shape[1]
+    for k, out in enumerate(outs):
+        out[:half, :] = (kept[k, :half] + upper[k].astype(f32)).astype(out.dtype)
+        out[half:, :] = (kept[k, half:] + lower[k].astype(f32)).astype(out.dtype)
+
+
+def add_up(kept, *parts):
+    heads, rows, columns = kept.shape
+    return pl.pallas_call(
+        add_kernel,
+        out_shape=[jax.ShapeDtypeStruct((rows, columns), bf16)] * heads,
+        compiler_params=pltpu.CompilerParams(vmem_limit_bytes=VMEM),
+    )(kept, *parts)
 
 
 def split(value):
@@ -276,32 +325,47 @@
     )(moment)
 
 
-def spread_kernel(returned, moment, update):
+def spread_kernel(returned, moment, update, moment_held, update_held, sems):
+    half = moment_held.shape[1] // NC
+    copies = []
     for c in range(NC):
         for y in range(NY):
             for x in range(NX):
                 source = (c * NY + y) * NX + x
                 head = c * NY * NX + (RING * x + y if c == 0 else RING * y + x)
                 at = slice(head * HD, (head + 1) * HD)
-                update[:, at] = returned[source, 0]
-                moment[:, at] = returned[source, 1].astype(f32)
+                update_held[:, at] = returned[source, 0]
+                moment_held[:, at] = returned[source, 1].astype(f32)
+        done = pl.ds(c * half, half)
+        for k, (held, out) in enumerate(((moment_held, moment), (update_held, update))):
+            copies.append(pltpu.make_async_copy(held.at[:, done], out.at[:, done], sems.at[c, k]))
+            copies[-1].start()
+    for copy in copies:
+        copy.wait()
 
 
 def spread(returned):
     heads, _, rows, columns = returned.shape
+    moment = jax.ShapeDtypeStruct((rows, heads * columns), f32)
+    update = jax.ShapeDtypeStruct((rows, heads * columns), bf16)
+    hbm = pl.BlockSpec(memory_space=pl.ANY)
     return pl.pallas_call(
         spread_kernel,
-        out_shape=(
-            jax.ShapeDtypeStruct((rows, heads * columns), f32),
-            jax.ShapeDtypeStruct((rows, heads * columns), bf16),
-        ),
+        out_shape=(moment, update),
+        in_specs=[pl.BlockSpec(memory_space=pltpu.VMEM)],
+        out_specs=(hbm, hbm),
+        scratch_shapes=[
+            pltpu.VMEM(moment.shape, f32),
+            pltpu.VMEM(update.shape, bf16),
+            pltpu.SemaphoreType.DMA((NC, 2)),
+        ],
         compiler_params=pltpu.CompilerParams(vmem_limit_bytes=VMEM),
     )(returned)
 
 
 def body(latent, latent_grad, row_counts, momentum):
     features = latent.shape[1]
-    order, rest = (2, 1, 3), (1, 2, 3)
+    order = (2, 1, 3)
     tie = lax.optimization_barrier
 
     early, late = (2,), (1, 3, 0)
@@ -310,27 +374,48 @@
     piece_early, lat_other, mom_other = (
         swap_cores(piece_early), swap_cores(lat_own), swap_cores(mom_other)
     )
-    piece_late, piece_early, lat_other, mom_other = tie(
-        (piece_late, piece_early, lat_other, mom_other)
-    )
+    piece_late, piece_early, lat_other, mom_other = tie((piece_late, piece_early, lat_other, mom_other))
     piece_late = swap_cores(piece_late)
     shared = (unit, lat_other, mom_own, mom_other)
 
+    half = features // 2
+    upper, lower, whole = (0, half), (half, half), (0, features)
+    every, rest, stay = (0, 1, 2, 3), (1, 2, 3), (0,)
     own = {2: own_early}
-    (first_on,) = block(own, early, [(2, rest)], *shared, piece_early)
-    lat_late, first_on = tie((lat_own, first_on))
+    two_a, two_b = block(
+        own, early, [(2, every, *upper, bf16), (2, every, *lower, bf16)], *shared, piece_early
+    )
+    lat_late, two_a, two_b = tie((lat_own, two_a, two_b))
     own[1], own[3], own[0] = own_products(lat_late, latent_grad, late)
-    on = [first_on] + [block(own, late, [(k, rest)], *shared, piece_late)[0] for k in order[1:]]
-    on = [shift(value, 0, k) for value, k in zip(on, order)]
-    (stay,) = block(own, early, [(2, (0,))], *shared, piece_early)
-    *stays, kept_stay, kept_on = block(
-        own, late, [(1, (0,)), (3, (0,)), (0, (0,)), (0, rest)], *shared, piece_late
-    )
-    stay = [shift(value, 0, k) for value, k in zip([stay] + stays, order)]
-
-    total = kept_on + sum(value.astype(f32) for value in on)
-    got = [shift(total[k - 1].astype(bf16), 1, k) for k in order]
-    head = kept_stay[0] + sum(value[0].astype(f32) for value in stay)
+    (one_b,) = block(own, late, [(1, rest, *lower, bf16)], *shared, piece_late)
+    (three_a,) = block(own, late, [(3, rest, *upper, bf16)], *shared, piece_late)
+    own[0], one_b, three_a = tie((own[0], one_b, three_a))
+    one_a, three_b, one_stay, three_stay, kept_on, kept_stay = block(
+        own,
+        late,
+        [
+            (1, rest, *upper, f32),
+            (3, rest, *lower, f32),
+            (1, stay, *whole, f32),
+            (3, stay, *whole, f32),
+            (0, rest, *whole, f32),
+            (0, stay, *whole, f32),
+        ],
+        *shared,
+        piece_late,
+    )
+    two_a, two_b = shift(two_a, 0, 1), shift(two_b, 0, 3)
+    one_b, three_a = shift(one_b, 0, 1), shift(three_a, 0, 3)
+    one_a = shift((one_a + two_a[1:].astype(f32)).astype(bf16), 0, 1)
+    three_b = shift((three_b + two_b[1:].astype(f32)).astype(bf16), 0, 3)
+    kept_on, one_stay, three_stay = middle(
+        kept_on, three_a, one_b, one_stay, three_stay, two_a, two_b
+    )
+    one_stay, three_stay = shift(one_stay, 0, 1), shift(three_stay, 0, 3)
+
+    sums = add_up(kept_on, one_a, three_b)
+    got = [shift(sums[k - 1], 1, k) for k in order]
+    head = stay_sum(kept_stay, one_stay, three_stay)
     head = (head + sum(value.astype(f32) for value in got)).astype(bf16)
 
     pieces = lax.all_to_all(head.reshape(NZ, -1, HD), "z", 0, 0, tiled=True)

time: 101 us -> 102 us (level)
  waiting for transfers between devices: 19.5 us -> 11.6 us
  starting transfers between devices: 13.6 us -> 18.8 us
  blocking collectives: 50.2 us -> 54 us
    ppermute x9 -> x11, waiting for transfers between devices: 18.1 us -> 10.2 us  [shift(): return lax.ppermute(value, AXES, pairs)]
    ppermute x9 -> x11, starting transfers between devices: 9.56 us -> 14.8 us  [shift(): return lax.ppermute(value, AXES, pairs)]
    all_to_all x1, blocking collectives: 21.9 us -> 25.2 us  [body(): returned = lax.all_to_all(outgoing, PLANE, 0, 0, tiled=True)]
    all_to_all x1, blocking collectives: 15.9 us -> 17 us  [body(): pieces = lax.all_to_all(head.reshape(NZ, -1, HD), 'z', 0, 0, tiled=True)]
    pallas_call x5 -> x4, Pallas kernels: 3.05 us -> 2.9 us  [block(): pl.pallas_call(functools.partial(block_kernel, tiles), out_shape=[jax.Sha...]
  transfers between devices with their start and end apart: 13 -> 15, of which waited for: 9 -> 7; matrix products, arithmetic and copies ran while one was open for 1% -> 0% of each run, Pallas kernels for 6% -> 6%
where the time goes in v9:
time: 102 us
  blocking collectives  54 us (53%)
  starting transfers between devices  18.8 us (18%)
  Pallas kernels  15.5 us (15%)
  waiting for transfers between devices  11.6 us (11%)
  between operations  1.61 us (2%)
    all_to_all x1, blocking collectives, body(): returned = lax.all_to_all(outgoing, PLANE, 0, 0, tiled=True)  25.2 us
    all_to_all x1, blocking collectives, body(): pieces = lax.all_to_all(head.reshape(NZ, -1, HD), 'z', 0, 0, tiled=True)  17 us
    ppermute x11, starting transfers between devices, shift(): return lax.ppermute(value, AXES, pairs)  14.8 us
    all_to_all x1, blocking collectives, body(): lax.all_to_all(jnp.broadcast_to(piece, (NZ,) + piece.shape), 'z', 0, 0, t...  11.7 us
    ppermute x11, waiting for transfers between devices, shift(): return lax.ppermute(value, AXES, pairs)  10.2 us
    pallas_call x1, Pallas kernels, newton_schulz(): pl.pallas_call(newton_schulz_kernel, out_shape=jax.ShapeDtypeStruct((owne...  5.75 us
    ppermute x4, starting transfers between devices, swap_cores(): lax.ppermute(value, AXES, [(device_at(z, y, x, c), device_at(z, y, x, 1 -...  4.06 us
    pallas_call x4, Pallas kernels, block(): pl.pallas_call(functools.partial(block_kernel, tiles), out_shape=[jax.Sha...  2.9 us
  transfers between devices with their start and end apart: 15, of which 7 were waited for; matrix products, arithmetic and copies ran while one was open for 0% of the time, Pallas kernels for 6%

profile of v9, /device:TPU:1, one launch (start us, length us, event | category | flops | bytes accessed | tf_op | source)
XLA Modules:
  0.0 101.8 jit_solution(18212543027988433887)
XLA Ops:
  0.6 2.3 %shard_map.59 = (bf16[256,1024]{1,0:T(8,128)(2,1)S(1)}, bf16[256,3072]{1,0:T(8,128)(2,1)S(1)}, bf16[256,1024]{1,0:T(8,128)(2,1)S(1)}) custom-call(bf16[256,8192]{1,0:T(8,128)(2,1)} %grad.3), custom_call_target="tpu_custom_call" | custom-call | tf_op jit(solution)/shard_map/pallas_call | solution.py:104
  2.9 3.3 %collective-permute-start = (bf16[256,1024]{1,0:T(8,128)(2,1)S(1)}, bf16[256,1024]{1,0:T(8,128)(2,1)S(1)}, u32[]{:S(2)}, u32[]{:S(2)}) collective-permute-start(bf16[256,1024]{1,0:T(8,128)(2,1)S(1)} %get-tuple-element.40), channel_id=1, source_target_pairs={{0,1},{1,0},{2,3},{3,2},{4,5},{5,4},{6,7},{7,6},{8,9},{9,8},{10,11... | collective-permute-start | bytes 1572872 | tf_op jit(solution)/shard_map/ppermute | solution.py:46
  6.9 0.7 shard_map.60
  7.6 0.1 collective-permute-start.2
  7.7 0.5 collective-permute-start.1
  8.2 1.0 %collective-permute-done.2.mom_other = bf16[32,4096]{1,0:T(8,128)(2,1)S(1)} collective-permute-done((bf16[32,4096]{1,0:T(8,128)(2,1)S(1)}, bf16[32,4096]{1,0:T(8,128)(2,1)S(1)}, u32[]{:S(2)}, u32[]{:S(2)}) %collective-permute-start.2) | collective-permute-done | bytes 262176 | tf_op jit(solution)/shard_map/ppermute | solution.py:46
  9.2 0.4 collective-permute-done.1.lat
  9.6 0.0 collective-permute-done.grad
  9.6 0.1 collective-permute-start.3
  9.7 0.7 shard_map.61
  10.5 1.1 %collective-permute-start.7 = (bf16[4,256,256]{2,1,0:T(8,128)(2,1)S(1)}, bf16[4,256,256]{2,1,0:T(8,128)(2,1)S(1)}, u32[]{:S(2)}, u32[]{:S(2)}) collective-permute-start(bf16[4,256,256]{2,1,0:T(8,128)(2,1)S(1)} %get-tuple-element.63), channel_id=1, source_target_pairs={{0,6},{1,25},{2,0},{3,27},{4,2},{5,29},{6,4},{7,31},{8,14},{9,1},{... | collective-permute-start | bytes 1572872 | tf_op jit(solution)/shard_map/ppermute | solution.py:42
  11.6 0.5 collective-permute-start.6
  12.0 2.5 %shard_map.62 = (bf16[4,512,256]{2,1,0:T(8,128)(2,1)S(1)}, bf16[4,512,256]{2,1,0:T(8,128)(2,1)S(1)}, bf16[4,512,256]{2,1,0:T(8,128)(2,1)S(1)}) custom-call(bf16[512,256]{1,0:T(8,128)(2,1)S(1)} %get-tuple-element.51.lat, bf16[256,8192]{1,0:T(8,128)(2,1)} %grad.3), custom_call_target="tpu_custom_call" | custom-call | flops 805306368 | bytes 4718592 | tf_op jit(solution)/shard_map/pallas_call | solution.py:175
  14.6 0.0 collective-permute-done.3.grad
  14.6 0.4 shard_map.63
  15.0 0.4 shard_map.64
  15.4 2.3 %collective-permute-start.4 = (bf16[3,256,256]{2,1,0:T(8,128)(2,1)S(1)}, bf16[3,256,256]{2,1,0:T(8,128)(2,1)S(1)}, u32[]{:S(2)}, u32[]{:S(2)}) collective-permute-start(bf16[3,256,256]{2,1,0:T(8,128)(2,1)S(1)} %shard_map.64), channel_id=1, source_target_pairs={{0,6},{1,25},{2,0},{3,27},{4,2},{5,29},{6,4},{7,31},{8,14},{9,1},{... | collective-permute-start | bytes 1179656 | tf_op jit(solution)/shard_map/ppermute | solution.py:42
  17.6 0.0 collective-permute-start.5
  17.6 1.4 %shard_map.65 = (f32[3,256,256]{2,1,0:T(8,128)S(1)}, f32[3,256,256]{2,1,0:T(8,128)S(1)}, f32[1,512,256]{2,1,0:T(8,128)S(1)}, f32[1,512,256]{2,1,0:T(8,128)S(1)},...) custom-call(bf16[512,64]{1,0:T(8,128)(2,1)S(1)} %get-tuple-element.38.unit, ...), custom_call_target="tpu_custom_call" | custom-call | flops 754974720 | bytes 7864320 | tf_op jit(solution)/shard_map/pallas_call | solution.py:215
  19.1 0.0 collective-permute-done.7.two_b
  19.1 0.1 add_convert_fusion
  19.2 2.8 %collective-permute-start.11 = (bf16[3,256,256]{2,1,0:T(8,128)(2,1)S(1)}, bf16[3,256,256]{2,1,0:T(8,128)(2,1)S(1)}, u32[]{:S(2)}, u32[]{:S(2)}) collective-permute-start(bf16[3,256,256]{2,1,0:T(8,128)(2,1)S(1)} %add_convert_fusion), channel_id=1, source_target_pairs={{0,6},{1,25},{2,0},{3,27},{4,2},{5,29},{6,4},{7,31},{8,14},{9,1},{... | collective-permute-start | bytes 1179656 | tf_op jit(solution)/shard_map/ppermute | solution.py:42
  21.9 0.0 collective-permute-done.6.two_a
  21.9 0.1 add_convert_fusion.1
  22.0 0.3 collective-permute-start.10
  22.3 0.8 collective-permute-done.4.upper
  23.1 2.7 %collective-permute-done.5.lower = bf16[3,256,256]{2,1,0:T(8,128)(2,1)S(1)} collective-permute-done((bf16[3,256,256]{2,1,0:T(8,128)(2,1)S(1)}, bf16[3,256,256]{2,1,0:T(8,128)(2,1)S(1)}, u32[]{:S(2)}, u32[]{:S(2)}) %collective-permute-start.5) | collective-permute-done | bytes 393248 | tf_op jit(solution)/shard_map/ppermute | solution.py:42
  25.8 0.2 shard_map.66
  26.0 0.1 collective-permute-start.8
  26.1 2.7 %collective-permute-start.9 = (bf16[512,256]{1,0:T(8,128)(2,1)S(1)}, bf16[512,256]{1,0:T(8,128)(2,1)S(1)}, u32[]{:S(2)}, u32[]{:S(2)}) collective-permute-start(bf16[512,256]{1,0:T(8,128)(2,1)S(1)} %get-tuple-element.65), channel_id=1, source_target_pairs={{0,6},{1,25},{2,0},{3,27},{4,2},{5,29},{6,4},{7,31},{8,14},{9,1},{... | collective-permute-start | bytes 786440 | tf_op jit(solution)/shard_map/ppermute | solution.py:42
  28.7 0.0 collective-permute-done.11.lower
  28.7 1.7 %collective-permute-done.10.upper = bf16[3,256,256]{2,1,0:T(8,128)(2,1)S(1)} collective-permute-done((bf16[3,256,256]{2,1,0:T(8,128)(2,1)S(1)}, bf16[3,256,256]{2,1,0:T(8,128)(2,1)S(1)}, u32[]{:S(2)}, u32[]{:S(2)}) %collective-permute-start.10) | collective-permute-done | bytes 393248 | tf_op jit(solution)/shard_map/ppermute | solution.py:42
  30.4 0.1 shard_map.68
  30.5 2.5 %collective-permute-start.12 = (bf16[512,256]{1,0:T(8,128)(2,1)S(1)}, bf16[512,256]{1,0:T(8,128)(2,1)S(1)}, u32[]{:S(2)}, u32[]{:S(2)}) collective-permute-start(bf16[512,256]{1,0:T(8,128)(2,1)S(1)} %get-tuple-element.69), channel_id=1, source_target_pairs={{0,16},{1,5},{2,18},{3,7},{4,20},{5,1},{6,22},{7,3},{8,24},{9,13},... | collective-permute-start | bytes 786440 | tf_op jit(solution)/shard_map/ppermute | solution.py:42
  33.0 0.3 collective-permute-start.13
  33.4 2.4 %collective-permute-start.14 = (bf16[512,256]{1,0:T(8,128)(2,1)S(1)}, bf16[512,256]{1,0:T(8,128)(2,1)S(1)}, u32[]{:S(2)}, u32[]{:S(2)}) collective-permute-start(bf16[512,256]{1,0:T(8,128)(2,1)S(1)} %get-tuple-element.71), channel_id=1, source_target_pairs={{0,24},{1,7},{2,26},{3,1},{4,28},{5,3},{6,30},{7,5},{8,0},{9,15},{... | collective-permute-start | bytes 786440 | tf_op jit(solution)/shard_map/ppermute | solution.py:42
  35.7 0.0 collective-permute-done.8.one
  35.7 0.0 collective-permute-done.9.three
  35.7 0.1 shard_map.67
  35.8 1.6 %collective-permute-done.12 = bf16[512,256]{1,0:T(8,128)(2,1)S(1)} collective-permute-done((bf16[512,256]{1,0:T(8,128)(2,1)S(1)}, bf16[512,256]{1,0:T(8,128)(2,1)S(1)}, u32[]{:S(2)}, u32[]{:S(2)}) %collective-permute-start.12) | collective-permute-done | bytes 262176 | tf_op jit(solution)/shard_map/ppermute | solution.py:42
  37.5 3.4 %collective-permute-done.13 = bf16[512,256]{1,0:T(8,128)(2,1)S(1)} collective-permute-done((bf16[512,256]{1,0:T(8,128)(2,1)S(1)}, bf16[512,256]{1,0:T(8,128)(2,1)S(1)}, u32[]{:S(2)}, u32[]{:S(2)}) %collective-permute-start.13) | collective-permute-done | bytes 262176 | tf_op jit(solution)/shard_map/ppermute | solution.py:42
  40.8 0.0 collective-permute-done.14
  40.8 0.1 add_convert_fusion.2
  40.9 17.0 %all_to_all.15 = bf16[8,64,256]{2,1,0:T(8,128)(2,1)S(1)} all-to-all(bf16[8,64,256]{2,1,0:T(8,128)(2,1)S(1)} %bitcast.3), channel_id=1, replica_groups=mesh['z'=8,'y'=4,'x'=4,'c'=2] {'z'}, dimensions={0} | all-to-all | bytes 524288 | tf_op jit(solution)/shard_map/all_to_all | solution.py:421
  58.0 11.7 %all_to_all.16 = bf16[8,64,256]{2,1,0:T(8,128)(2,1)S(1)} all-to-all(bf16[8,64,256]{2,1,0:T(8,128)(2,1)S(1)} %broadcast_in_dim.3), channel_id=1, replica_groups=mesh['z'=8,'y'=4,'x'=4,'c'=2] {'z'}, dimensions={0} | all-to-all | bytes 524288 | tf_op jit(solution)/shard_map/all_to_all | solution.py:423
  69.7 5.8 %shard_map.69 = bf16[32,2,16,256]{3,2,1,0:T(8,128)(2,1)S(1)} custom-call(bf16[512,256]{1,0:T(8,128)(2,1)S(1)} %bitcast.2), custom_call_target="tpu_custom_call" | custom-call | tf_op jit(solution)/shard_map/pallas_call | solution.py:321
  75.5 25.2 %all_to_all.17.returned = bf16[32,2,16,256]{3,2,1,0:T(8,128)(2,1)S(1)} all-to-all(bf16[32,2,16,256]{3,2,1,0:T(8,128)(2,1)S(1)} %shard_map.69), channel_id=1, replica_groups=mesh['z'=8,'y'=4,'x'=4,'c'=2] {'c','y','x'}, dimensions={0} | all-to-all | bytes 1048576 | tf_op jit(solution)/shard_map/all_to_all | solution.py:427
  100.7 0.9 shard_map.70
  (6 shorter events, 0.1 us)
Async XLA Ops:
  0.6 6.3 %copy-start = (f32[16,8192]{1,0:T(8,128)S(1)}, f32[16,8192]{1,0:T(8,128)}, u32[]{:S(2)}) copy-start(f32[16,8192]{1,0:T(8,128)} %momentum.1) | copy-start | bytes 1572868
  0.6 6.3 %copy-start.1 = (bf16[256,512]{1,0:T(8,128)(2,1)S(1)}, bf16[256,512]{1,0:T(8,128)(2,1)}, u32[]{:S(2)}) copy-start(bf16[256,512]{1,0:T(8,128)(2,1)} %latent.1) | copy-start | bytes 786436
  2.9 6.7 %collective-permute-start = (bf16[256,1024]{1,0:T(8,128)(2,1)S(1)}, bf16[256,1024]{1,0:T(8,128)(2,1)S(1)}, u32[]{:S(2)}, u32[]{:S(2)}) collective-permute-start(bf16[256,1024]{1,0:T(8,128)(2,1)S(1)} %get-tuple-element.40), channel_id=1, source_target_pairs={{0,1},{1,0},{2,3},{3,2},{4,5},{5,4},{6,7},{7,6},{8,9},{9,8},{10,11... | collective-permute-start | bytes 1572872 | tf_op jit(solution)/shard_map/ppermute | solution.py:46
  7.6 1.6 %collective-permute-start.2 = (bf16[32,4096]{1,0:T(8,128)(2,1)S(1)}, bf16[32,4096]{1,0:T(8,128)(2,1)S(1)}, u32[]{:S(2)}, u32[]{:S(2)}) collective-permute-start(bf16[32,4096]{1,0:T(8,128)(2,1)S(1)} %get-tuple-element.42), channel_id=1, source_target_pairs={{0,1},{1,0},{2,3},{3,2},{4,5},{5,4},{6,7},{7,6},{8,9},{9,8},{10,11... | collective-permute-start | bytes 786440 | tf_op jit(solution)/shard_map/ppermute | solution.py:46
  7.7 1.9 %collective-permute-start.1 = (bf16[512,256]{1,0:T(8,128)(2,1)S(1)}, bf16[512,256]{1,0:T(8,128)(2,1)S(1)}, u32[]{:S(2)}, u32[]{:S(2)}) collective-permute-start(bf16[512,256]{1,0:T(8,128)(2,1)S(1)} %get-tuple-element.51.lat), channel_id=1, source_target_pairs={{0,1},{1,0},{2,3},{3,2},{4,5},{5,4},{6,7},{7,6},{8,9},{9,8},{10,11... | collective-permute-start | bytes 786440 | tf_op jit(solution)/shard_map/ppermute | solution.py:46
  9.6 5.0 %collective-permute-start.3 = (bf16[256,3072]{1,0:T(8,128)(2,1)S(1)}, bf16[256,3072]{1,0:T(8,128)(2,1)S(1)}, u32[]{:S(2)}, u32[]{:S(2)}) collective-permute-start(bf16[256,3072]{1,0:T(8,128)(2,1)S(1)} %get-tuple-element.46), channel_id=1, source_target_pairs={{0,1},{1,0},{2,3},{3,2},{4,5},{5,4},{6,7},{7,6},{8,9},{9,8},{10,11... | collective-permute-start | bytes 4718600 | tf_op jit(solution)/shard_map/ppermute | solution.py:46
  10.5 8.6 %collective-permute-start.7 = (bf16[4,256,256]{2,1,0:T(8,128)(2,1)S(1)}, bf16[4,256,256]{2,1,0:T(8,128)(2,1)S(1)}, u32[]{:S(2)}, u32[]{:S(2)}) collective-permute-start(bf16[4,256,256]{2,1,0:T(8,128)(2,1)S(1)} %get-tuple-element.63), channel_id=1, source_target_pairs={{0,6},{1,25},{2,0},{3,27},{4,2},{5,29},{6,4},{7,31},{8,14},{9,1},{... | collective-permute-start | bytes 1572872 | tf_op jit(solution)/shard_map/ppermute | solution.py:42
  11.6 10.4 %collective-permute-start.6 = (bf16[4,256,256]{2,1,0:T(8,128)(2,1)S(1)}, bf16[4,256,256]{2,1,0:T(8,128)(2,1)S(1)}, u32[]{:S(2)}, u32[]{:S(2)}) collective-permute-start(bf16[4,256,256]{2,1,0:T(8,128)(2,1)S(1)} %get-tuple-element.62), channel_id=1, source_target_pairs={{0,2},{1,9},{2,4},{3,11},{4,6},{5,13},{6,0},{7,15},{8,10},{9,17},{... | collective-permute-start | bytes 1572872 | tf_op jit(solution)/shard_map/ppermute | solution.py:42
  15.4 7.7 %collective-permute-start.4 = (bf16[3,256,256]{2,1,0:T(8,128)(2,1)S(1)}, bf16[3,256,256]{2,1,0:T(8,128)(2,1)S(1)}, u32[]{:S(2)}, u32[]{:S(2)}) collective-permute-start(bf16[3,256,256]{2,1,0:T(8,128)(2,1)S(1)} %shard_map.64), channel_id=1, source_target_pairs={{0,6},{1,25},{2,0},{3,27},{4,2},{5,29},{6,4},{7,31},{8,14},{9,1},{... | collective-permute-start | bytes 1179656 | tf_op jit(solution)/shard_map/ppermute | solution.py:42
  17.6 8.1 %collective-permute-start.5 = (bf16[3,256,256]{2,1,0:T(8,128)(2,1)S(1)}, bf16[3,256,256]{2,1,0:T(8,128)(2,1)S(1)}, u32[]{:S(2)}, u32[]{:S(2)}) collective-permute-start(bf16[3,256,256]{2,1,0:T(8,128)(2,1)S(1)} %shard_map.63), channel_id=1, source_target_pairs={{0,2},{1,9},{2,4},{3,11},{4,6},{5,13},{6,0},{7,15},{8,10},{9,17},{... | collective-permute-start | bytes 1179656 | tf_op jit(solution)/shard_map/ppermute | solution.py:42
  19.2 9.6 %collective-permute-start.11 = (bf16[3,256,256]{2,1,0:T(8,128)(2,1)S(1)}, bf16[3,256,256]{2,1,0:T(8,128)(2,1)S(1)}, u32[]{:S(2)}, u32[]{:S(2)}) collective-permute-start(bf16[3,256,256]{2,1,0:T(8,128)(2,1)S(1)} %add_convert_fusion), channel_id=1, source_target_pairs={{0,6},{1,25},{2,0},{3,27},{4,2},{5,29},{6,4},{7,31},{8,14},{9,1},{... | collective-permute-start | bytes 1179656 | tf_op jit(solution)/shard_map/ppermute | solution.py:42
  22.0 8.4 %collective-permute-start.10 = (bf16[3,256,256]{2,1,0:T(8,128)(2,1)S(1)}, bf16[3,256,256]{2,1,0:T(8,128)(2,1)S(1)}, u32[]{:S(2)}, u32[]{:S(2)}) collective-permute-start(bf16[3,256,256]{2,1,0:T(8,128)(2,1)S(1)} %add_convert_fusion.1), channel_id=1, source_target_pairs={{0,2},{1,9},{2,4},{3,11},{4,6},{5,13},{6,0},{7,15},{8,10},{9,17},{... | collective-permute-start | bytes 1179656 | tf_op jit(solution)/shard_map/ppermute | solution.py:42
  26.0 9.8 %collective-permute-start.8 = (bf16[512,256]{1,0:T(8,128)(2,1)S(1)}, bf16[512,256]{1,0:T(8,128)(2,1)S(1)}, u32[]{:S(2)}, u32[]{:S(2)}) collective-permute-start(bf16[512,256]{1,0:T(8,128)(2,1)S(1)} %get-tuple-element.64), channel_id=1, source_target_pairs={{0,2},{1,9},{2,4},{3,11},{4,6},{5,13},{6,0},{7,15},{8,10},{9,17},{... | collective-permute-start | bytes 786440 | tf_op jit(solution)/shard_map/ppermute | solution.py:42
  26.1 9.7 %collective-permute-start.9 = (bf16[512,256]{1,0:T(8,128)(2,1)S(1)}, bf16[512,256]{1,0:T(8,128)(2,1)S(1)}, u32[]{:S(2)}, u32[]{:S(2)}) collective-permute-start(bf16[512,256]{1,0:T(8,128)(2,1)S(1)} %get-tuple-element.65), channel_id=1, source_target_pairs={{0,6},{1,25},{2,0},{3,27},{4,2},{5,29},{6,4},{7,31},{8,14},{9,1},{... | collective-permute-start | bytes 786440 | tf_op jit(solution)/shard_map/ppermute | solution.py:42
  30.5 6.9 %collective-permute-start.12 = (bf16[512,256]{1,0:T(8,128)(2,1)S(1)}, bf16[512,256]{1,0:T(8,128)(2,1)S(1)}, u32[]{:S(2)}, u32[]{:S(2)}) collective-permute-start(bf16[512,256]{1,0:T(8,128)(2,1)S(1)} %get-tuple-element.69), channel_id=1, source_target_pairs={{0,16},{1,5},{2,18},{3,7},{4,20},{5,1},{6,22},{7,3},{8,24},{9,13},... | collective-permute-start | bytes 786440 | tf_op jit(solution)/shard_map/ppermute | solution.py:42
  33.0 7.8 %collective-permute-start.13 = (bf16[512,256]{1,0:T(8,128)(2,1)S(1)}, bf16[512,256]{1,0:T(8,128)(2,1)S(1)}, u32[]{:S(2)}, u32[]{:S(2)}) collective-permute-start(bf16[512,256]{1,0:T(8,128)(2,1)S(1)} %get-tuple-element.70), channel_id=1, source_target_pairs={{0,8},{1,3},{2,10},{3,5},{4,12},{5,7},{6,14},{7,1},{8,16},{9,11},{... | collective-permute-start | bytes 786440 | tf_op jit(solution)/shard_map/ppermute | solution.py:42
  33.4 7.4 %collective-permute-start.14 = (bf16[512,256]{1,0:T(8,128)(2,1)S(1)}, bf16[512,256]{1,0:T(8,128)(2,1)S(1)}, u32[]{:S(2)}, u32[]{:S(2)}) collective-permute-start(bf16[512,256]{1,0:T(8,128)(2,1)S(1)} %get-tuple-element.71), channel_id=1, source_target_pairs={{0,24},{1,7},{2,26},{3,1},{4,28},{5,3},{6,30},{7,5},{8,0},{9,15},{... | collective-permute-start | bytes 786440 | tf_op jit(solution)/shard_map/ppermute | solution.py:42

commit v10 on v8

--- a/solution.py
+++ b/solution.py
@@ -30,13 +30,13 @@
     return [(z, y, x, c) for z in range(NZ) for y in range(NY) for x in range(NX) for c in range(NC)]
 
 
-def shift(value, axis, distance):
+def exchange(value, axis, distance):
     pairs = []
     for z, y, x, c in every_device():
         if axis == c:
-            to = (y, (x + distance) % NX)
+            to = (y, x ^ distance)
         else:
-            to = ((y + distance) % NY, x)
+            to = (y ^ distance, x)
         pairs.append((device_at(z, y, x, c), device_at(z, *to, c)))
     return lax.ppermute(value, AXES, pairs)
 
@@ -56,7 +56,7 @@
     first, second = places()
     if other:
         first, second = second, first
-    head = lax.rem(first + near, RING) * RING + lax.rem(second + far, RING)
+    head = (first ^ near) * RING + (second ^ far)
     return pl.multiple_of(head * HD, HD)
 
 
@@ -276,25 +276,40 @@
     )(moment)
 
 
-def spread_kernel(returned, moment, update):
+def spread_kernel(returned, moment, update, moment_held, update_held, sems):
+    half = moment_held.shape[1] // NC
+    copies = []
     for c in range(NC):
         for y in range(NY):
             for x in range(NX):
                 source = (c * NY + y) * NX + x
                 head = c * NY * NX + (RING * x + y if c == 0 else RING * y + x)
                 at = slice(head * HD, (head + 1) * HD)
-                update[:, at] = returned[source, 0]
-                moment[:, at] = returned[source, 1].astype(f32)
+                update_held[:, at] = returned[source, 0]
+                moment_held[:, at] = returned[source, 1].astype(f32)
+        done = pl.ds(c * half, half)
+        for k, (held, out) in enumerate(((moment_held, moment), (update_held, update))):
+            copies.append(pltpu.make_async_copy(held.at[:, done], out.at[:, done], sems.at[c, k]))
+            copies[-1].start()
+    for copy in copies:
+        copy.wait()
 
 
 def spread(returned):
     heads, _, rows, columns = returned.shape
+    moment = jax.ShapeDtypeStruct((rows, heads * columns), f32)
+    update = jax.ShapeDtypeStruct((rows, heads * columns), bf16)
+    hbm = pl.BlockSpec(memory_space=pl.ANY)
     return pl.pallas_call(
         spread_kernel,
-        out_shape=(
-            jax.ShapeDtypeStruct((rows, heads * columns), f32),
-            jax.ShapeDtypeStruct((rows, heads * columns), bf16),
-        ),
+        out_shape=(moment, update),
+        in_specs=[pl.BlockSpec(memory_space=pltpu.VMEM)],
+        out_specs=(hbm, hbm),
+        scratch_shapes=[
+            pltpu.VMEM(moment.shape, f32),
+            pltpu.VMEM(update.shape, bf16),
+            pltpu.SemaphoreType.DMA((NC, 2)),
+        ],
         compiler_params=pltpu.CompilerParams(vmem_limit_bytes=VMEM),
     )(returned)
 
@@ -310,9 +325,7 @@
     piece_early, lat_other, mom_other = (
         swap_cores(piece_early), swap_cores(lat_own), swap_cores(mom_other)
     )
-    piece_late, piece_early, lat_other, mom_other = tie(
-        (piece_late, piece_early, lat_other, mom_other)
-    )
+    piece_late, piece_early, lat_other, mom_other = tie((piece_late, piece_early, lat_other, mom_other))
     piece_late = swap_cores(piece_late)
     shared = (unit, lat_other, mom_own, mom_other)
 
@@ -321,15 +334,15 @@
     lat_late, first_on = tie((lat_own, first_on))
     own[1], own[3], own[0] = own_products(lat_late, latent_grad, late)
     on = [first_on] + [block(own, late, [(k, rest)], *shared, piece_late)[0] for k in order[1:]]
-    on = [shift(value, 0, k) for value, k in zip(on, order)]
+    on = [exchange(value, 0, k) for value, k in zip(on, order)]
     (stay,) = block(own, early, [(2, (0,))], *shared, piece_early)
     *stays, kept_stay, kept_on = block(
         own, late, [(1, (0,)), (3, (0,)), (0, (0,)), (0, rest)], *shared, piece_late
     )
-    stay = [shift(value, 0, k) for value, k in zip([stay] + stays, order)]
+    stay = [exchange(value, 0, k) for value, k in zip([stay] + stays, order)]
 
     total = kept_on + sum(value.astype(f32) for value in on)
-    got = [shift(total[k - 1].astype(bf16), 1, k) for k in order]
+    got = [exchange(total[k - 1].astype(bf16), 1, k) for k in order]
     head = kept_stay[0] + sum(value[0].astype(f32) for value in stay)
     head = (head + sum(value.astype(f32) for value in got)).astype(bf16)
 

time: 101 us -> 102 us (level)
  blocking collectives: 50.2 us -> 51.3 us
  transfers between devices with their start and end apart: 13 -> 13, of which waited for: 9 -> 8; matrix products, arithmetic and copies ran while one was open for 1% -> 1% of each run, Pallas kernels for 6% -> 6%
where the time goes in v10:
time: 102 us
  blocking collectives  51.3 us (50%)
  waiting for transfers between devices  19.9 us (20%)
  Pallas kernels  15.2 us (15%)
  starting transfers between devices  13.2 us (13%)
  between operations  1.59 us (2%)
    all_to_all x1, blocking collectives, body(): returned = lax.all_to_all(outgoing, PLANE, 0, 0, tiled=True)  22.6 us
    ppermute x9, waiting for transfers between devices, exchange(): return lax.ppermute(value, AXES, pairs)  18.5 us
    all_to_all x1, blocking collectives, body(): pieces = lax.all_to_all(head.reshape(NZ, -1, HD), 'z', 0, 0, tiled=True)  16.7 us
    all_to_all x1, blocking collectives, body(): lax.all_to_all(jnp.broadcast_to(piece, (NZ,) + piece.shape), 'z', 0, 0, t...  12.1 us
    ppermute x9, starting transfers between devices, exchange(): return lax.ppermute(value, AXES, pairs)  9.19 us
    pallas_call x1, Pallas kernels, newton_schulz(): pl.pallas_call(newton_schulz_kernel, out_shape=jax.ShapeDtypeStruct((owne...  5.75 us
    ppermute x4, starting transfers between devices, swap_cores(): lax.ppermute(value, AXES, [(device_at(z, y, x, c), device_at(z, y, x, 1 -...  4.06 us
    pallas_call x5, Pallas kernels, block(): pl.pallas_call(functools.partial(block_kernel, tiles), out_shape=[jax.Sha...  3.03 us
  transfers between devices with their start and end apart: 13, of which 8 were waited for; matrix products, arithmetic and copies ran while one was open for 1% of the time, Pallas kernels for 6%

profile of v10, /device:TPU:1, one launch (start us, length us, event | category | flops | bytes accessed | tf_op | source)
XLA Modules:
  0.0 102.0 jit_solution(17874860294577178603)
XLA Ops:
  0.6 0.0 copy-start
  0.6 0.0 copy-start.1
  0.6 2.3 %shard_map.59 = (bf16[256,1024]{1,0:T(8,128)(2,1)S(1)}, bf16[256,3072]{1,0:T(8,128)(2,1)S(1)}, bf16[256,1024]{1,0:T(8,128)(2,1)S(1)}) custom-call(bf16[256,8192]{1,0:T(8,128)(2,1)} %grad.3), custom_call_target="tpu_custom_call" | custom-call | tf_op jit(solution)/shard_map/pallas_call | solution.py:103
  2.9 3.3 %collective-permute-start = (bf16[256,1024]{1,0:T(8,128)(2,1)S(1)}, bf16[256,1024]{1,0:T(8,128)(2,1)S(1)}, u32[]{:S(2)}, u32[]{:S(2)}) collective-permute-start(bf16[256,1024]{1,0:T(8,128)(2,1)S(1)} %get-tuple-element.26), channel_id=1, source_target_pairs={{0,1},{1,0},{2,3},{3,2},{4,5},{5,4},{6,7},{7,6},{8,9},{9,8},{10,11... | collective-permute-start | bytes 1572872 | tf_op jit(solution)/shard_map/ppermute | solution.py:45
  6.9 0.0 copy-done
  6.9 0.0 copy-done.1
  6.9 0.7 shard_map.60
  7.6 0.1 collective-permute-start.2
  7.7 0.5 collective-permute-start.1
  8.2 1.0 %collective-permute-done.2.mom_other = bf16[32,4096]{1,0:T(8,128)(2,1)S(1)} collective-permute-done((bf16[32,4096]{1,0:T(8,128)(2,1)S(1)}, bf16[32,4096]{1,0:T(8,128)(2,1)S(1)}, u32[]{:S(2)}, u32[]{:S(2)}) %collective-permute-start.2) | collective-permute-done | bytes 262176 | tf_op jit(solution)/shard_map/ppermute | solution.py:45
  9.2 0.4 collective-permute-done.1.lat
  9.6 0.0 collective-permute-done.grad
  9.6 0.1 collective-permute-start.3
  9.7 0.6 shard_map.61
  10.3 1.3 %collective-permute-start.7 = (bf16[3,512,256]{2,1,0:T(8,128)(2,1)S(1)}, bf16[3,512,256]{2,1,0:T(8,128)(2,1)S(1)}, u32[]{:S(2)}, u32[]{:S(2)}) collective-permute-start(bf16[3,512,256]{2,1,0:T(8,128)(2,1)S(1)} %shard_map.61), channel_id=1, source_target_pairs={{0,4},{1,17},{2,6},{3,19},{4,0},{5,21},{6,2},{7,23},{8,12},{9,25},... | collective-permute-start | bytes 2359304 | tf_op jit(solution)/shard_map/ppermute | solution.py:41
  11.6 2.5 %shard_map.62 = (bf16[4,512,256]{2,1,0:T(8,128)(2,1)S(1)}, bf16[4,512,256]{2,1,0:T(8,128)(2,1)S(1)}, bf16[4,512,256]{2,1,0:T(8,128)(2,1)S(1)}) custom-call(bf16[512,256]{1,0:T(8,128)(2,1)S(1)} %get-tuple-element.35.lat, bf16[256,8192]{1,0:T(8,128)(2,1)} %grad.3), custom_call_target="tpu_custom_call" | custom-call | flops 805306368 | bytes 4718592 | tf_op jit(solution)/shard_map/pallas_call | solution.py:174
  14.1 0.0 collective-permute-done.3.grad
  14.1 0.6 shard_map.66
  14.7 0.9 collective-permute-start.9
  15.6 0.6 shard_map.65
  16.2 0.8 collective-permute-start.8
  17.0 0.3 shard_map.64
  17.3 2.5 %collective-permute-start.4 = (bf16[1,512,256]{2,1,0:T(8,128)(2,1)S(1)}, bf16[1,512,256]{2,1,0:T(8,128)(2,1)S(1)}, u32[]{:S(2)}, u32[]{:S(2)}) collective-permute-start(bf16[1,512,256]{2,1,0:T(8,128)(2,1)S(1)} %shard_map.64), channel_id=1, source_target_pairs={{0,4},{1,17},{2,6},{3,19},{4,0},{5,21},{6,2},{7,23},{8,12},{9,25},... | collective-permute-start | bytes 786440 | tf_op jit(solution)/shard_map/ppermute | solution.py:41
  19.7 1.0 shard_map.63
  20.7 0.1 collective-permute-start.5
  20.8 2.3 %collective-permute-done.7 = bf16[3,512,256]{2,1,0:T(8,128)(2,1)S(1)} collective-permute-done((bf16[3,512,256]{2,1,0:T(8,128)(2,1)S(1)}, bf16[3,512,256]{2,1,0:T(8,128)(2,1)S(1)}, u32[]{:S(2)}, u32[]{:S(2)}) %collective-permute-start.7) | collective-permute-done | bytes 786464 | tf_op jit(solution)/shard_map/ppermute | solution.py:41
  23.1 1.0 collective-permute-start.6
  24.1 7.4 %collective-permute-done.9 = bf16[3,512,256]{2,1,0:T(8,128)(2,1)S(1)} collective-permute-done((bf16[3,512,256]{2,1,0:T(8,128)(2,1)S(1)}, bf16[3,512,256]{2,1,0:T(8,128)(2,1)S(1)}, u32[]{:S(2)}, u32[]{:S(2)}) %collective-permute-start.9) | collective-permute-done | bytes 786464 | tf_op jit(solution)/shard_map/ppermute | solution.py:41
  31.5 0.0 collective-permute-done.8
  31.5 0.5 add_convert_fusion
  32.0 0.1 slice_bitcast_fusion.2
  32.0 1.5 %collective-permute-start.10 = (bf16[512,256]{1,0:T(8,128)(2,1)S(1)}, bf16[512,256]{1,0:T(8,128)(2,1)S(1)}, u32[]{:S(2)}, u32[]{:S(2)}) collective-permute-start(bf16[512,256]{1,0:T(8,128)(2,1)S(1)} %get-tuple-element.44), channel_id=1, source_target_pairs={{0,16},{1,5},{2,18},{3,7},{4,20},{5,1},{6,22},{7,3},{8,24},{9,13},... | collective-permute-start | bytes 786440 | tf_op jit(solution)/shard_map/ppermute | solution.py:41
  33.5 0.9 collective-permute-start.12
  34.4 0.0 collective-permute-done.4
  34.4 0.4 collective-permute-start.11
  34.8 1.0 %collective-permute-done.5 = bf16[1,512,256]{2,1,0:T(8,128)(2,1)S(1)} collective-permute-done((bf16[1,512,256]{2,1,0:T(8,128)(2,1)S(1)}, bf16[1,512,256]{2,1,0:T(8,128)(2,1)S(1)}, u32[]{:S(2)}, u32[]{:S(2)}) %collective-permute-start.5) | collective-permute-done | bytes 262176 | tf_op jit(solution)/shard_map/ppermute | solution.py:41
  35.8 1.3 %collective-permute-done.6 = bf16[1,512,256]{2,1,0:T(8,128)(2,1)S(1)} collective-permute-done((bf16[1,512,256]{2,1,0:T(8,128)(2,1)S(1)}, bf16[1,512,256]{2,1,0:T(8,128)(2,1)S(1)}, u32[]{:S(2)}, u32[]{:S(2)}) %collective-permute-start.6) | collective-permute-done | bytes 262176 | tf_op jit(solution)/shard_map/ppermute | solution.py:41
  37.1 3.7 %collective-permute-done.10 = bf16[512,256]{1,0:T(8,128)(2,1)S(1)} collective-permute-done((bf16[512,256]{1,0:T(8,128)(2,1)S(1)}, bf16[512,256]{1,0:T(8,128)(2,1)S(1)}, u32[]{:S(2)}, u32[]{:S(2)}) %collective-permute-start.10) | collective-permute-done | bytes 262176 | tf_op jit(solution)/shard_map/ppermute | solution.py:41
  40.8 2.7 %collective-permute-done.12 = bf16[512,256]{1,0:T(8,128)(2,1)S(1)} collective-permute-done((bf16[512,256]{1,0:T(8,128)(2,1)S(1)}, bf16[512,256]{1,0:T(8,128)(2,1)S(1)}, u32[]{:S(2)}, u32[]{:S(2)}) %collective-permute-start.12) | collective-permute-done | bytes 262176 | tf_op jit(solution)/shard_map/ppermute | solution.py:41
  43.5 0.0 collective-permute-done.11
  43.5 0.2 fusion
  43.8 16.7 %all_to_all.15 = bf16[8,64,256]{2,1,0:T(8,128)(2,1)S(1)} all-to-all(bf16[8,64,256]{2,1,0:T(8,128)(2,1)S(1)} %bitcast.13), channel_id=1, replica_groups=mesh['z'=8,'y'=4,'x'=4,'c'=2] {'z'}, dimensions={0} | all-to-all | bytes 524288 | tf_op jit(solution)/shard_map/all_to_all | solution.py:349
  60.5 12.1 %all_to_all.16 = bf16[8,64,256]{2,1,0:T(8,128)(2,1)S(1)} all-to-all(bf16[8,64,256]{2,1,0:T(8,128)(2,1)S(1)} %broadcast_in_dim.3), channel_id=1, replica_groups=mesh['z'=8,'y'=4,'x'=4,'c'=2] {'z'}, dimensions={0} | all-to-all | bytes 524288 | tf_op jit(solution)/shard_map/all_to_all | solution.py:351
  72.6 5.7 %shard_map.67 = bf16[32,2,16,256]{3,2,1,0:T(8,128)(2,1)S(1)} custom-call(bf16[512,256]{1,0:T(8,128)(2,1)S(1)} %bitcast.12), custom_call_target="tpu_custom_call" | custom-call | tf_op jit(solution)/shard_map/pallas_call | solution.py:272
  78.3 22.6 %all_to_all.17.returned = bf16[32,2,16,256]{3,2,1,0:T(8,128)(2,1)S(1)} all-to-all(bf16[32,2,16,256]{3,2,1,0:T(8,128)(2,1)S(1)} %shard_map.67), channel_id=1, replica_groups=mesh['z'=8,'y'=4,'x'=4,'c'=2] {'c','y','x'}, dimensions={0} | all-to-all | bytes 1048576 | tf_op jit(solution)/shard_map/all_to_all | solution.py:355
  100.9 0.9 shard_map.68
  (2 shorter events, 0.1 us)
Async XLA Ops:
  0.6 6.3 %copy-start = (f32[16,8192]{1,0:T(8,128)S(1)}, f32[16,8192]{1,0:T(8,128)}, u32[]{:S(2)}) copy-start(f32[16,8192]{1,0:T(8,128)} %momentum.1) | copy-start | bytes 1572868
  0.6 6.3 %copy-start.1 = (bf16[256,512]{1,0:T(8,128)(2,1)S(1)}, bf16[256,512]{1,0:T(8,128)(2,1)}, u32[]{:S(2)}) copy-start(bf16[256,512]{1,0:T(8,128)(2,1)} %latent.1) | copy-start | bytes 786436
  2.9 6.7 %collective-permute-start = (bf16[256,1024]{1,0:T(8,128)(2,1)S(1)}, bf16[256,1024]{1,0:T(8,128)(2,1)S(1)}, u32[]{:S(2)}, u32[]{:S(2)}) collective-permute-start(bf16[256,1024]{1,0:T(8,128)(2,1)S(1)} %get-tuple-element.26), channel_id=1, source_target_pairs={{0,1},{1,0},{2,3},{3,2},{4,5},{5,4},{6,7},{7,6},{8,9},{9,8},{10,11... | collective-permute-start | bytes 1572872 | tf_op jit(solution)/shard_map/ppermute | solution.py:45
  7.6 1.6 %collective-permute-start.2 = (bf16[32,4096]{1,0:T(8,128)(2,1)S(1)}, bf16[32,4096]{1,0:T(8,128)(2,1)S(1)}, u32[]{:S(2)}, u32[]{:S(2)}) collective-permute-start(bf16[32,4096]{1,0:T(8,128)(2,1)S(1)} %get-tuple-element.28), channel_id=1, source_target_pairs={{0,1},{1,0},{2,3},{3,2},{4,5},{5,4},{6,7},{7,6},{8,9},{9,8},{10,11... | collective-permute-start | bytes 786440 | tf_op jit(solution)/shard_map/ppermute | solution.py:45
  7.7 1.9 %collective-permute-start.1 = (bf16[512,256]{1,0:T(8,128)(2,1)S(1)}, bf16[512,256]{1,0:T(8,128)(2,1)S(1)}, u32[]{:S(2)}, u32[]{:S(2)}) collective-permute-start(bf16[512,256]{1,0:T(8,128)(2,1)S(1)} %get-tuple-element.35.lat), channel_id=1, source_target_pairs={{0,1},{1,0},{2,3},{3,2},{4,5},{5,4},{6,7},{7,6},{8,9},{9,8},{10,11... | collective-permute-start | bytes 786440 | tf_op jit(solution)/shard_map/ppermute | solution.py:45
  9.6 4.5 %collective-permute-start.3 = (bf16[256,3072]{1,0:T(8,128)(2,1)S(1)}, bf16[256,3072]{1,0:T(8,128)(2,1)S(1)}, u32[]{:S(2)}, u32[]{:S(2)}) collective-permute-start(bf16[256,3072]{1,0:T(8,128)(2,1)S(1)} %get-tuple-element.32), channel_id=1, source_target_pairs={{0,1},{1,0},{2,3},{3,2},{4,5},{5,4},{6,7},{7,6},{8,9},{9,8},{10,11... | collective-permute-start | bytes 4718600 | tf_op jit(solution)/shard_map/ppermute | solution.py:45
  10.3 12.8 %collective-permute-start.7 = (bf16[3,512,256]{2,1,0:T(8,128)(2,1)S(1)}, bf16[3,512,256]{2,1,0:T(8,128)(2,1)S(1)}, u32[]{:S(2)}, u32[]{:S(2)}) collective-permute-start(bf16[3,512,256]{2,1,0:T(8,128)(2,1)S(1)} %shard_map.61), channel_id=1, source_target_pairs={{0,4},{1,17},{2,6},{3,19},{4,0},{5,21},{6,2},{7,23},{8,12},{9,25},... | collective-permute-start | bytes 2359304 | tf_op jit(solution)/shard_map/ppermute | solution.py:41
  14.7 16.7 %collective-permute-start.9 = (bf16[3,512,256]{2,1,0:T(8,128)(2,1)S(1)}, bf16[3,512,256]{2,1,0:T(8,128)(2,1)S(1)}, u32[]{:S(2)}, u32[]{:S(2)}) collective-permute-start(bf16[3,512,256]{2,1,0:T(8,128)(2,1)S(1)} %shard_map.66), channel_id=1, source_target_pairs={{0,6},{1,25},{2,4},{3,27},{4,2},{5,29},{6,0},{7,31},{8,14},{9,17},... | collective-permute-start | bytes 2359304 | tf_op jit(solution)/shard_map/ppermute | solution.py:41
  16.2 15.3 %collective-permute-start.8 = (bf16[3,512,256]{2,1,0:T(8,128)(2,1)S(1)}, bf16[3,512,256]{2,1,0:T(8,128)(2,1)S(1)}, u32[]{:S(2)}, u32[]{:S(2)}) collective-permute-start(bf16[3,512,256]{2,1,0:T(8,128)(2,1)S(1)} %shard_map.65), channel_id=1, source_target_pairs={{0,2},{1,9},{2,0},{3,11},{4,6},{5,13},{6,4},{7,15},{8,10},{9,1},{1... | collective-permute-start | bytes 2359304 | tf_op jit(solution)/shard_map/ppermute | solution.py:41
  17.3 17.1 %collective-permute-start.4 = (bf16[1,512,256]{2,1,0:T(8,128)(2,1)S(1)}, bf16[1,512,256]{2,1,0:T(8,128)(2,1)S(1)}, u32[]{:S(2)}, u32[]{:S(2)}) collective-permute-start(bf16[1,512,256]{2,1,0:T(8,128)(2,1)S(1)} %shard_map.64), channel_id=1, source_target_pairs={{0,4},{1,17},{2,6},{3,19},{4,0},{5,21},{6,2},{7,23},{8,12},{9,25},... | collective-permute-start | bytes 786440 | tf_op jit(solution)/shard_map/ppermute | solution.py:41
  20.7 15.1 %collective-permute-start.5 = (bf16[1,512,256]{2,1,0:T(8,128)(2,1)S(1)}, bf16[1,512,256]{2,1,0:T(8,128)(2,1)S(1)}, u32[]{:S(2)}, u32[]{:S(2)}) collective-permute-start(bf16[1,512,256]{2,1,0:T(8,128)(2,1)S(1)} %get-tuple-element.40), channel_id=1, source_target_pairs={{0,2},{1,9},{2,0},{3,11},{4,6},{5,13},{6,4},{7,15},{8,10},{9,1},{1... | collective-permute-start | bytes 786440 | tf_op jit(solution)/shard_map/ppermute | solution.py:41
  23.1 14.0 %collective-permute-start.6 = (bf16[1,512,256]{2,1,0:T(8,128)(2,1)S(1)}, bf16[1,512,256]{2,1,0:T(8,128)(2,1)S(1)}, u32[]{:S(2)}, u32[]{:S(2)}) collective-permute-start(bf16[1,512,256]{2,1,0:T(8,128)(2,1)S(1)} %get-tuple-element.41), channel_id=1, source_target_pairs={{0,6},{1,25},{2,4},{3,27},{4,2},{5,29},{6,0},{7,31},{8,14},{9,17},... | collective-permute-start | bytes 786440 | tf_op jit(solution)/shard_map/ppermute | solution.py:41
  32.0 8.8 %collective-permute-start.10 = (bf16[512,256]{1,0:T(8,128)(2,1)S(1)}, bf16[512,256]{1,0:T(8,128)(2,1)S(1)}, u32[]{:S(2)}, u32[]{:S(2)}) collective-permute-start(bf16[512,256]{1,0:T(8,128)(2,1)S(1)} %get-tuple-element.44), channel_id=1, source_target_pairs={{0,16},{1,5},{2,18},{3,7},{4,20},{5,1},{6,22},{7,3},{8,24},{9,13},... | collective-permute-start | bytes 786440 | tf_op jit(solution)/shard_map/ppermute | solution.py:41
  33.5 10.0 %collective-permute-start.12 = (bf16[512,256]{1,0:T(8,128)(2,1)S(1)}, bf16[512,256]{1,0:T(8,128)(2,1)S(1)}, u32[]{:S(2)}, u32[]{:S(2)}) collective-permute-start(bf16[512,256]{1,0:T(8,128)(2,1)S(1)} %get-tuple-element.45), channel_id=1, source_target_pairs={{0,24},{1,7},{2,26},{3,5},{4,28},{5,3},{6,30},{7,1},{8,16},{9,15},... | collective-permute-start | bytes 786440 | tf_op jit(solution)/shard_map/ppermute | solution.py:41
  34.4 9.2 %collective-permute-start.11 = (bf16[512,256]{1,0:T(8,128)(2,1)S(1)}, bf16[512,256]{1,0:T(8,128)(2,1)S(1)}, u32[]{:S(2)}, u32[]{:S(2)}) collective-permute-start(bf16[512,256]{1,0:T(8,128)(2,1)S(1)} %get-tuple-element.46), channel_id=1, source_target_pairs={{0,8},{1,3},{2,10},{3,1},{4,12},{5,7},{6,14},{7,5},{8,0},{9,11},{1... | collective-permute-start | bytes 786440 | tf_op jit(solution)/shard_map/ppermute | solution.py:41

commit v11 on v9

--- a/solution.py
+++ b/solution.py
@@ -31,13 +31,13 @@
     return [(z, y, x, c) for z in range(NZ) for y in range(NY) for x in range(NX) for c in range(NC)]
 
 
-def shift(value, axis, distance):
+def exchange(value, axis, distance):
     pairs = []
     for z, y, x, c in every_device():
         if axis == c:
-            to = (y, (x + distance) % NX)
+            to = (y, x ^ distance)
         else:
-            to = ((y + distance) % NY, x)
+            to = (y ^ distance, x)
         pairs.append((device_at(z, y, x, c), device_at(z, *to, c)))
     return lax.ppermute(value, AXES, pairs)
 
@@ -57,7 +57,7 @@
     first, second = places()
     if other:
         first, second = second, first
-    head = lax.rem(first + near, RING) * RING + lax.rem(second + far, RING)
+    head = (first ^ near) * RING + (second ^ far)
     return pl.multiple_of(head * HD, HD)
 
 
@@ -229,10 +229,10 @@
     for k in range(kept.shape[0]):
         kept_out[k, :half] = kept[k, :half] + upper[k].astype(f32)
         kept_out[k, half:] = kept[k, half:] + lower[k].astype(f32)
-    one_out[:half, :] = (one[0, :half] + two_a[0].astype(f32)).astype(bf16)
-    one_out[half:, :] = one[0, half:].astype(bf16)
-    three_out[:half, :] = three[0, :half].astype(bf16)
-    three_out[half:, :] = (three[0, half:] + two_b[0].astype(f32)).astype(bf16)
+    one_out[:half, :] = one[0, :half].astype(bf16)
+    one_out[half:, :] = (one[0, half:] + two_b[0].astype(f32)).astype(bf16)
+    three_out[:half, :] = (three[0, :half] + two_a[0].astype(f32)).astype(bf16)
+    three_out[half:, :] = three[0, half:].astype(bf16)
 
 
 def middle(kept, *parts):
@@ -387,15 +387,15 @@
     )
     lat_late, two_a, two_b = tie((lat_own, two_a, two_b))
     own[1], own[3], own[0] = own_products(lat_late, latent_grad, late)
-    (one_b,) = block(own, late, [(1, rest, *lower, bf16)], *shared, piece_late)
-    (three_a,) = block(own, late, [(3, rest, *upper, bf16)], *shared, piece_late)
-    own[0], one_b, three_a = tie((own[0], one_b, three_a))
-    one_a, three_b, one_stay, three_stay, kept_on, kept_stay = block(
+    (one_a,) = block(own, late, [(1, rest, *upper, bf16)], *shared, piece_late)
+    (three_b,) = block(own, late, [(3, rest, *lower, bf16)], *shared, piece_late)
+    own[0], one_a, three_b = tie((own[0], one_a, three_b))
+    one_b, three_a, one_stay, three_stay, kept_on, kept_stay = block(
         own,
         late,
         [
-            (1, rest, *upper, f32),
-            (3, rest, *lower, f32),
+            (1, rest, *lower, f32),
+            (3, rest, *upper, f32),
             (1, stay, *whole, f32),
             (3, stay, *whole, f32),
             (0, rest, *whole, f32),
@@ -404,17 +404,17 @@
         *shared,
         piece_late,
     )
-    two_a, two_b = shift(two_a, 0, 1), shift(two_b, 0, 3)
-    one_b, three_a = shift(one_b, 0, 1), shift(three_a, 0, 3)
-    one_a = shift((one_a + two_a[1:].astype(f32)).astype(bf16), 0, 1)
-    three_b = shift((three_b + two_b[1:].astype(f32)).astype(bf16), 0, 3)
+    two_a, two_b = exchange(two_a, 0, 1), exchange(two_b, 0, 3)
+    one_a, three_b = exchange(one_a, 0, 1), exchange(three_b, 0, 3)
+    three_a = exchange((three_a + two_a[1:].astype(f32)).astype(bf16), 0, 3)
+    one_b = exchange((one_b + two_b[1:].astype(f32)).astype(bf16), 0, 1)
     kept_on, one_stay, three_stay = middle(
-        kept_on, three_a, one_b, one_stay, three_stay, two_a, two_b
-    )
-    one_stay, three_stay = shift(one_stay, 0, 1), shift(three_stay, 0, 3)
-
-    sums = add_up(kept_on, one_a, three_b)
-    got = [shift(sums[k - 1], 1, k) for k in order]
+        kept_on, one_a, three_b, one_stay, three_stay, two_a, two_b
+    )
+    one_stay, three_stay = exchange(one_stay, 0, 1), exchange(three_stay, 0, 3)
+
+    sums = add_up(kept_on, three_a, one_b)
+    got = [exchange(sums[k - 1], 1, k) for k in order]
     head = stay_sum(kept_stay, one_stay, three_stay)
     head = (head + sum(value.astype(f32) for value in got)).astype(bf16)
 

time: 102 us -> 96.7 us (0.948)
  blocking collectives: 54 us -> 49.5 us
  starting transfers between devices: 18.8 us -> 15.2 us
  waiting for transfers between devices: 11.6 us -> 14.3 us
    all_to_all x1, blocking collectives: 25.2 us -> 20.4 us  [body(): returned = lax.all_to_all(outgoing, PLANE, 0, 0, tiled=True)]
    ppermute x11, starting transfers between devices: 14.8 us -> 11.2 us  [exchange(): return lax.ppermute(value, AXES, pairs)]
    ppermute x11, waiting for transfers between devices: 10.2 us -> 12.9 us  [exchange(): return lax.ppermute(value, AXES, pairs)]
  transfers between devices with their start and end apart: 15 -> 15, of which waited for: 7 -> 10; matrix products, arithmetic and copies ran while one was open for 0% -> 0% of each run, Pallas kernels for 6% -> 7%
where the time goes in v11:
time: 96.7 us; the launch traced here: 96.5 us
  blocking collectives  49.5 us (51%)
  Pallas kernels  15.4 us (16%)
  starting transfers between devices  15.2 us (16%)
  waiting for transfers between devices  14.3 us (15%)
  between operations  1.61 us (2%)
    all_to_all x1, blocking collectives, body(): returned = lax.all_to_all(outgoing, PLANE, 0, 0, tiled=True)  20.4 us
    all_to_all x1, blocking collectives, body(): pieces = lax.all_to_all(head.reshape(NZ, -1, HD), 'z', 0, 0, tiled=True)  17.2 us
    ppermute x11, waiting for transfers between devices, exchange(): return lax.ppermute(value, AXES, pairs)  12.9 us
    all_to_all x1, blocking collectives, body(): lax.all_to_all(jnp.broadcast_to(piece, (NZ,) + piece.shape), 'z', 0, 0, t...  11.9 us
    ppermute x11, starting transfers between devices, exchange(): return lax.ppermute(value, AXES, pairs)  11.2 us
    pallas_call x1, Pallas kernels, newton_schulz(): pl.pallas_call(newton_schulz_kernel, out_shape=jax.ShapeDtypeStruct((owne...  5.75 us
    ppermute x4, starting transfers between devices, swap_cores(): lax.ppermute(value, AXES, [(device_at(z, y, x, c), device_at(z, y, x, 1 -...  4.06 us
    pallas_call x4, Pallas kernels, block(): pl.pallas_call(functools.partial(block_kernel, tiles), out_shape=[jax.Sha...  2.88 us
  transfers between devices with their start and end apart: 15, of which 10 were waited for; matrix products, arithmetic and copies ran while one was open for 0% of the time, Pallas kernels for 7%

profile of v11, /device:TPU:1, one launch (start us, length us, event | category | flops | bytes accessed | tf_op | source)
XLA Modules:
  0.0 96.5 jit_solution(11105119282721920466)
XLA Ops:
  0.6 2.3 %shard_map.59 = (bf16[256,1024]{1,0:T(8,128)(2,1)S(1)}, bf16[256,3072]{1,0:T(8,128)(2,1)S(1)}, bf16[256,1024]{1,0:T(8,128)(2,1)S(1)}) custom-call(bf16[256,8192]{1,0:T(8,128)(2,1)} %grad.3), custom_call_target="tpu_custom_call" | custom-call | tf_op jit(solution)/shard_map/pallas_call | solution.py:104
  2.9 3.3 %collective-permute-start = (bf16[256,1024]{1,0:T(8,128)(2,1)S(1)}, bf16[256,1024]{1,0:T(8,128)(2,1)S(1)}, u32[]{:S(2)}, u32[]{:S(2)}) collective-permute-start(bf16[256,1024]{1,0:T(8,128)(2,1)S(1)} %get-tuple-element.40), channel_id=1, source_target_pairs={{0,1},{1,0},{2,3},{3,2},{4,5},{5,4},{6,7},{7,6},{8,9},{9,8},{10,11... | collective-permute-start | bytes 1572872 | tf_op jit(solution)/shard_map/ppermute | solution.py:46
  6.9 0.7 shard_map.60
  7.6 0.1 collective-permute-start.2
  7.7 0.5 collective-permute-start.1
  8.2 1.0 %collective-permute-done.2.mom_other = bf16[32,4096]{1,0:T(8,128)(2,1)S(1)} collective-permute-done((bf16[32,4096]{1,0:T(8,128)(2,1)S(1)}, bf16[32,4096]{1,0:T(8,128)(2,1)S(1)}, u32[]{:S(2)}, u32[]{:S(2)}) %collective-permute-start.2) | collective-permute-done | bytes 262176 | tf_op jit(solution)/shard_map/ppermute | solution.py:46
  9.2 0.4 collective-permute-done.1.lat
  9.6 0.0 collective-permute-done.grad
  9.6 0.1 collective-permute-start.3
  9.7 0.7 shard_map.61
  10.5 1.1 %collective-permute-start.7 = (bf16[4,256,256]{2,1,0:T(8,128)(2,1)S(1)}, bf16[4,256,256]{2,1,0:T(8,128)(2,1)S(1)}, u32[]{:S(2)}, u32[]{:S(2)}) collective-permute-start(bf16[4,256,256]{2,1,0:T(8,128)(2,1)S(1)} %get-tuple-element.63), channel_id=1, source_target_pairs={{0,6},{1,25},{2,4},{3,27},{4,2},{5,29},{6,0},{7,31},{8,14},{9,17},... | collective-permute-start | bytes 1572872 | tf_op jit(solution)/shard_map/ppermute | solution.py:42
  11.5 0.0 collective-permute-start.6
  11.5 2.5 %shard_map.62 = (bf16[4,512,256]{2,1,0:T(8,128)(2,1)S(1)}, bf16[4,512,256]{2,1,0:T(8,128)(2,1)S(1)}, bf16[4,512,256]{2,1,0:T(8,128)(2,1)S(1)}) custom-call(bf16[512,256]{1,0:T(8,128)(2,1)S(1)} %get-tuple-element.51.lat, bf16[256,8192]{1,0:T(8,128)(2,1)} %grad.3), custom_call_target="tpu_custom_call" | custom-call | flops 805306368 | bytes 4718592 | tf_op jit(solution)/shard_map/pallas_call | solution.py:175
  14.1 0.0 collective-permute-done.3.grad
  14.1 0.4 shard_map.63
  14.5 0.4 shard_map.64
  14.9 1.6 %collective-permute-start.4 = (bf16[3,256,256]{2,1,0:T(8,128)(2,1)S(1)}, bf16[3,256,256]{2,1,0:T(8,128)(2,1)S(1)}, u32[]{:S(2)}, u32[]{:S(2)}) collective-permute-start(bf16[3,256,256]{2,1,0:T(8,128)(2,1)S(1)} %shard_map.63), channel_id=1, source_target_pairs={{0,2},{1,9},{2,0},{3,11},{4,6},{5,13},{6,4},{7,15},{8,10},{9,1},{1... | collective-permute-start | bytes 1179656 | tf_op jit(solution)/shard_map/ppermute | solution.py:42
  16.4 1.7 %collective-permute-start.5 = (bf16[3,256,256]{2,1,0:T(8,128)(2,1)S(1)}, bf16[3,256,256]{2,1,0:T(8,128)(2,1)S(1)}, u32[]{:S(2)}, u32[]{:S(2)}) collective-permute-start(bf16[3,256,256]{2,1,0:T(8,128)(2,1)S(1)} %shard_map.64), channel_id=1, source_target_pairs={{0,6},{1,25},{2,4},{3,27},{4,2},{5,29},{6,0},{7,31},{8,14},{9,17},... | collective-permute-start | bytes 1179656 | tf_op jit(solution)/shard_map/ppermute | solution.py:42
  18.1 1.4 %shard_map.65 = (f32[3,256,256]{2,1,0:T(8,128)S(1)}, f32[3,256,256]{2,1,0:T(8,128)S(1)}, f32[1,512,256]{2,1,0:T(8,128)S(1)}, f32[1,512,256]{2,1,0:T(8,128)S(1)},...) custom-call(bf16[512,64]{1,0:T(8,128)(2,1)S(1)} %get-tuple-element.38.unit, ...), custom_call_target="tpu_custom_call" | custom-call | flops 754974720 | bytes 7864320 | tf_op jit(solution)/shard_map/pallas_call | solution.py:215
  19.5 0.6 collective-permute-done.7.two_b
  20.1 0.1 add_convert_fusion
  20.2 0.1 collective-permute-start.11
  20.3 0.0 collective-permute-done.6.two_a
  20.3 0.1 add_convert_fusion.1
  20.4 1.3 %collective-permute-start.10 = (bf16[3,256,256]{2,1,0:T(8,128)(2,1)S(1)}, bf16[3,256,256]{2,1,0:T(8,128)(2,1)S(1)}, u32[]{:S(2)}, u32[]{:S(2)}) collective-permute-start(bf16[3,256,256]{2,1,0:T(8,128)(2,1)S(1)} %add_convert_fusion.1), channel_id=1, source_target_pairs={{0,6},{1,25},{2,4},{3,27},{4,2},{5,29},{6,0},{7,31},{8,14},{9,17},... | collective-permute-start | bytes 1179656 | tf_op jit(solution)/shard_map/ppermute | solution.py:42
  21.7 2.4 %collective-permute-done.4.upper = bf16[3,256,256]{2,1,0:T(8,128)(2,1)S(1)} collective-permute-done((bf16[3,256,256]{2,1,0:T(8,128)(2,1)S(1)}, bf16[3,256,256]{2,1,0:T(8,128)(2,1)S(1)}, u32[]{:S(2)}, u32[]{:S(2)}) %collective-permute-start.4) | collective-permute-done | bytes 393248 | tf_op jit(solution)/shard_map/ppermute | solution.py:42
  24.1 0.5 collective-permute-done.5.lower
  24.6 0.2 shard_map.66
  24.8 0.1 collective-permute-start.8
  24.9 1.9 %collective-permute-start.9 = (bf16[512,256]{1,0:T(8,128)(2,1)S(1)}, bf16[512,256]{1,0:T(8,128)(2,1)S(1)}, u32[]{:S(2)}, u32[]{:S(2)}) collective-permute-start(bf16[512,256]{1,0:T(8,128)(2,1)S(1)} %get-tuple-element.65), channel_id=1, source_target_pairs={{0,6},{1,25},{2,4},{3,27},{4,2},{5,29},{6,0},{7,31},{8,14},{9,17},... | collective-permute-start | bytes 786440 | tf_op jit(solution)/shard_map/ppermute | solution.py:42
  26.8 1.5 %collective-permute-done.11.lower = bf16[3,256,256]{2,1,0:T(8,128)(2,1)S(1)} collective-permute-done((bf16[3,256,256]{2,1,0:T(8,128)(2,1)S(1)}, bf16[3,256,256]{2,1,0:T(8,128)(2,1)S(1)}, u32[]{:S(2)}, u32[]{:S(2)}) %collective-permute-start.11) | collective-permute-done | bytes 393248 | tf_op jit(solution)/shard_map/ppermute | solution.py:42
  28.3 0.5 collective-permute-done.10.upper
  28.8 0.1 shard_map.68
  28.9 2.5 %collective-permute-start.12 = (bf16[512,256]{1,0:T(8,128)(2,1)S(1)}, bf16[512,256]{1,0:T(8,128)(2,1)S(1)}, u32[]{:S(2)}, u32[]{:S(2)}) collective-permute-start(bf16[512,256]{1,0:T(8,128)(2,1)S(1)} %get-tuple-element.69), channel_id=1, source_target_pairs={{0,16},{1,5},{2,18},{3,7},{4,20},{5,1},{6,22},{7,3},{8,24},{9,13},... | collective-permute-start | bytes 786440 | tf_op jit(solution)/shard_map/ppermute | solution.py:42
  31.4 0.6 collective-permute-start.13
  32.0 0.2 collective-permute-start.14
  32.3 0.0 collective-permute-done.8.one
  32.3 0.0 collective-permute-done.9.three
  32.3 0.1 shard_map.67
  32.4 4.7 %collective-permute-done.12 = bf16[512,256]{1,0:T(8,128)(2,1)S(1)} collective-permute-done((bf16[512,256]{1,0:T(8,128)(2,1)S(1)}, bf16[512,256]{1,0:T(8,128)(2,1)S(1)}, u32[]{:S(2)}, u32[]{:S(2)}) %collective-permute-start.12) | collective-permute-done | bytes 262176 | tf_op jit(solution)/shard_map/ppermute | solution.py:42
  37.1 1.8 %collective-permute-done.13 = bf16[512,256]{1,0:T(8,128)(2,1)S(1)} collective-permute-done((bf16[512,256]{1,0:T(8,128)(2,1)S(1)}, bf16[512,256]{1,0:T(8,128)(2,1)S(1)}, u32[]{:S(2)}, u32[]{:S(2)}) %collective-permute-start.13) | collective-permute-done | bytes 262176 | tf_op jit(solution)/shard_map/ppermute | solution.py:42
  38.9 1.0 collective-permute-done.14
  39.9 0.1 add_convert_fusion.2
  40.0 17.2 %all_to_all.15 = bf16[8,64,256]{2,1,0:T(8,128)(2,1)S(1)} all-to-all(bf16[8,64,256]{2,1,0:T(8,128)(2,1)S(1)} %bitcast.3), channel_id=1, replica_groups=mesh['z'=8,'y'=4,'x'=4,'c'=2] {'z'}, dimensions={0} | all-to-all | bytes 524288 | tf_op jit(solution)/shard_map/all_to_all | solution.py:421
  57.3 11.9 %all_to_all.16 = bf16[8,64,256]{2,1,0:T(8,128)(2,1)S(1)} all-to-all(bf16[8,64,256]{2,1,0:T(8,128)(2,1)S(1)} %broadcast_in_dim.3), channel_id=1, replica_groups=mesh['z'=8,'y'=4,'x'=4,'c'=2] {'z'}, dimensions={0} | all-to-all | bytes 524288 | tf_op jit(solution)/shard_map/all_to_all | solution.py:423
  69.2 5.8 %shard_map.69 = bf16[32,2,16,256]{3,2,1,0:T(8,128)(2,1)S(1)} custom-call(bf16[512,256]{1,0:T(8,128)(2,1)S(1)} %bitcast.2), custom_call_target="tpu_custom_call" | custom-call | tf_op jit(solution)/shard_map/pallas_call | solution.py:321
  75.0 20.4 %all_to_all.17.returned = bf16[32,2,16,256]{3,2,1,0:T(8,128)(2,1)S(1)} all-to-all(bf16[32,2,16,256]{3,2,1,0:T(8,128)(2,1)S(1)} %shard_map.69), channel_id=1, replica_groups=mesh['z'=8,'y'=4,'x'=4,'c'=2] {'c','y','x'}, dimensions={0} | all-to-all | bytes 1048576 | tf_op jit(solution)/shard_map/all_to_all | solution.py:427
  95.4 0.9 shard_map.70
  (6 shorter events, 0.1 us)
Async XLA Ops:
  0.6 6.3 %copy-start = (f32[16,8192]{1,0:T(8,128)S(1)}, f32[16,8192]{1,0:T(8,128)}, u32[]{:S(2)}) copy-start(f32[16,8192]{1,0:T(8,128)} %momentum.1) | copy-start | bytes 1572868
  0.6 6.3 %copy-start.1 = (bf16[256,512]{1,0:T(8,128)(2,1)S(1)}, bf16[256,512]{1,0:T(8,128)(2,1)}, u32[]{:S(2)}) copy-start(bf16[256,512]{1,0:T(8,128)(2,1)} %latent.1) | copy-start | bytes 786436
  2.9 6.7 %collective-permute-start = (bf16[256,1024]{1,0:T(8,128)(2,1)S(1)}, bf16[256,1024]{1,0:T(8,128)(2,1)S(1)}, u32[]{:S(2)}, u32[]{:S(2)}) collective-permute-start(bf16[256,1024]{1,0:T(8,128)(2,1)S(1)} %get-tuple-element.40), channel_id=1, source_target_pairs={{0,1},{1,0},{2,3},{3,2},{4,5},{5,4},{6,7},{7,6},{8,9},{9,8},{10,11... | collective-permute-start | bytes 1572872 | tf_op jit(solution)/shard_map/ppermute | solution.py:46
  7.6 1.6 %collective-permute-start.2 = (bf16[32,4096]{1,0:T(8,128)(2,1)S(1)}, bf16[32,4096]{1,0:T(8,128)(2,1)S(1)}, u32[]{:S(2)}, u32[]{:S(2)}) collective-permute-start(bf16[32,4096]{1,0:T(8,128)(2,1)S(1)} %get-tuple-element.42), channel_id=1, source_target_pairs={{0,1},{1,0},{2,3},{3,2},{4,5},{5,4},{6,7},{7,6},{8,9},{9,8},{10,11... | collective-permute-start | bytes 786440 | tf_op jit(solution)/shard_map/ppermute | solution.py:46
  7.7 1.9 %collective-permute-start.1 = (bf16[512,256]{1,0:T(8,128)(2,1)S(1)}, bf16[512,256]{1,0:T(8,128)(2,1)S(1)}, u32[]{:S(2)}, u32[]{:S(2)}) collective-permute-start(bf16[512,256]{1,0:T(8,128)(2,1)S(1)} %get-tuple-element.51.lat), channel_id=1, source_target_pairs={{0,1},{1,0},{2,3},{3,2},{4,5},{5,4},{6,7},{7,6},{8,9},{9,8},{10,11... | collective-permute-start | bytes 786440 | tf_op jit(solution)/shard_map/ppermute | solution.py:46
  9.6 4.5 %collective-permute-start.3 = (bf16[256,3072]{1,0:T(8,128)(2,1)S(1)}, bf16[256,3072]{1,0:T(8,128)(2,1)S(1)}, u32[]{:S(2)}, u32[]{:S(2)}) collective-permute-start(bf16[256,3072]{1,0:T(8,128)(2,1)S(1)} %get-tuple-element.46), channel_id=1, source_target_pairs={{0,1},{1,0},{2,3},{3,2},{4,5},{5,4},{6,7},{7,6},{8,9},{9,8},{10,11... | collective-permute-start | bytes 4718600 | tf_op jit(solution)/shard_map/ppermute | solution.py:46
  10.5 9.6 %collective-permute-start.7 = (bf16[4,256,256]{2,1,0:T(8,128)(2,1)S(1)}, bf16[4,256,256]{2,1,0:T(8,128)(2,1)S(1)}, u32[]{:S(2)}, u32[]{:S(2)}) collective-permute-start(bf16[4,256,256]{2,1,0:T(8,128)(2,1)S(1)} %get-tuple-element.63), channel_id=1, source_target_pairs={{0,6},{1,25},{2,4},{3,27},{4,2},{5,29},{6,0},{7,31},{8,14},{9,17},... | collective-permute-start | bytes 1572872 | tf_op jit(solution)/shard_map/ppermute | solution.py:42
  11.5 8.7 %collective-permute-start.6 = (bf16[4,256,256]{2,1,0:T(8,128)(2,1)S(1)}, bf16[4,256,256]{2,1,0:T(8,128)(2,1)S(1)}, u32[]{:S(2)}, u32[]{:S(2)}) collective-permute-start(bf16[4,256,256]{2,1,0:T(8,128)(2,1)S(1)} %get-tuple-element.62), channel_id=1, source_target_pairs={{0,2},{1,9},{2,0},{3,11},{4,6},{5,13},{6,4},{7,15},{8,10},{9,1},{1... | collective-permute-start | bytes 1572872 | tf_op jit(solution)/shard_map/ppermute | solution.py:42
  14.9 9.2 %collective-permute-start.4 = (bf16[3,256,256]{2,1,0:T(8,128)(2,1)S(1)}, bf16[3,256,256]{2,1,0:T(8,128)(2,1)S(1)}, u32[]{:S(2)}, u32[]{:S(2)}) collective-permute-start(bf16[3,256,256]{2,1,0:T(8,128)(2,1)S(1)} %shard_map.63), channel_id=1, source_target_pairs={{0,2},{1,9},{2,0},{3,11},{4,6},{5,13},{6,4},{7,15},{8,10},{9,1},{1... | collective-permute-start | bytes 1179656 | tf_op jit(solution)/shard_map/ppermute | solution.py:42
  16.4 8.1 %collective-permute-start.5 = (bf16[3,256,256]{2,1,0:T(8,128)(2,1)S(1)}, bf16[3,256,256]{2,1,0:T(8,128)(2,1)S(1)}, u32[]{:S(2)}, u32[]{:S(2)}) collective-permute-start(bf16[3,256,256]{2,1,0:T(8,128)(2,1)S(1)} %shard_map.64), channel_id=1, source_target_pairs={{0,6},{1,25},{2,4},{3,27},{4,2},{5,29},{6,0},{7,31},{8,14},{9,17},... | collective-permute-start | bytes 1179656 | tf_op jit(solution)/shard_map/ppermute | solution.py:42
  20.2 8.1 %collective-permute-start.11 = (bf16[3,256,256]{2,1,0:T(8,128)(2,1)S(1)}, bf16[3,256,256]{2,1,0:T(8,128)(2,1)S(1)}, u32[]{:S(2)}, u32[]{:S(2)}) collective-permute-start(bf16[3,256,256]{2,1,0:T(8,128)(2,1)S(1)} %add_convert_fusion), channel_id=1, source_target_pairs={{0,2},{1,9},{2,0},{3,11},{4,6},{5,13},{6,4},{7,15},{8,10},{9,1},{1... | collective-permute-start | bytes 1179656 | tf_op jit(solution)/shard_map/ppermute | solution.py:42
  20.4 8.4 %collective-permute-start.10 = (bf16[3,256,256]{2,1,0:T(8,128)(2,1)S(1)}, bf16[3,256,256]{2,1,0:T(8,128)(2,1)S(1)}, u32[]{:S(2)}, u32[]{:S(2)}) collective-permute-start(bf16[3,256,256]{2,1,0:T(8,128)(2,1)S(1)} %add_convert_fusion.1), channel_id=1, source_target_pairs={{0,6},{1,25},{2,4},{3,27},{4,2},{5,29},{6,0},{7,31},{8,14},{9,17},... | collective-permute-start | bytes 1179656 | tf_op jit(solution)/shard_map/ppermute | solution.py:42
  24.8 7.5 %collective-permute-start.8 = (bf16[512,256]{1,0:T(8,128)(2,1)S(1)}, bf16[512,256]{1,0:T(8,128)(2,1)S(1)}, u32[]{:S(2)}, u32[]{:S(2)}) collective-permute-start(bf16[512,256]{1,0:T(8,128)(2,1)S(1)} %get-tuple-element.64), channel_id=1, source_target_pairs={{0,2},{1,9},{2,0},{3,11},{4,6},{5,13},{6,4},{7,15},{8,10},{9,1},{1... | collective-permute-start | bytes 786440 | tf_op jit(solution)/shard_map/ppermute | solution.py:42
  24.9 7.4 %collective-permute-start.9 = (bf16[512,256]{1,0:T(8,128)(2,1)S(1)}, bf16[512,256]{1,0:T(8,128)(2,1)S(1)}, u32[]{:S(2)}, u32[]{:S(2)}) collective-permute-start(bf16[512,256]{1,0:T(8,128)(2,1)S(1)} %get-tuple-element.65), channel_id=1, source_target_pairs={{0,6},{1,25},{2,4},{3,27},{4,2},{5,29},{6,0},{7,31},{8,14},{9,17},... | collective-permute-start | bytes 786440 | tf_op jit(solution)/shard_map/ppermute | solution.py:42
  28.9 8.2 %collective-permute-start.12 = (bf16[512,256]{1,0:T(8,128)(2,1)S(1)}, bf16[512,256]{1,0:T(8,128)(2,1)S(1)}, u32[]{:S(2)}, u32[]{:S(2)}) collective-permute-start(bf16[512,256]{1,0:T(8,128)(2,1)S(1)} %get-tuple-element.69), channel_id=1, source_target_pairs={{0,16},{1,5},{2,18},{3,7},{4,20},{5,1},{6,22},{7,3},{8,24},{9,13},... | collective-permute-start | bytes 786440 | tf_op jit(solution)/shard_map/ppermute | solution.py:42
  31.4 7.5 %collective-permute-start.13 = (bf16[512,256]{1,0:T(8,128)(2,1)S(1)}, bf16[512,256]{1,0:T(8,128)(2,1)S(1)}, u32[]{:S(2)}, u32[]{:S(2)}) collective-permute-start(bf16[512,256]{1,0:T(8,128)(2,1)S(1)} %get-tuple-element.70), channel_id=1, source_target_pairs={{0,8},{1,3},{2,10},{3,1},{4,12},{5,7},{6,14},{7,5},{8,0},{9,11},{1... | collective-permute-start | bytes 786440 | tf_op jit(solution)/shard_map/ppermute | solution.py:42
  32.0 7.9 %collective-permute-start.14 = (bf16[512,256]{1,0:T(8,128)(2,1)S(1)}, bf16[512,256]{1,0:T(8,128)(2,1)S(1)}, u32[]{:S(2)}, u32[]{:S(2)}) collective-permute-start(bf16[512,256]{1,0:T(8,128)(2,1)S(1)} %get-tuple-element.71), channel_id=1, source_target_pairs={{0,24},{1,7},{2,26},{3,5},{4,28},{5,3},{6,30},{7,1},{8,16},{9,15},... | collective-permute-start | bytes 786440 | tf_op jit(solution)/shard_map/ppermute | solution.py:42

commit v12 on v11

--- a/solution.py
+++ b/solution.py
@@ -20,6 +20,7 @@
 VMEM = 16 * 1024 * 1024
 MIDDLE = 5 * 10**9
 LARGE = 48 * 1024 * 1024
+LARGER = 52 * 1024 * 1024
 bf16, f32 = jnp.bfloat16, jnp.float32
 
 
@@ -75,10 +76,10 @@
     return copies
 
 
-def pieces_kernel(groups, grad, early, late, mine, held, sems_in, sems_out):
-    lists = [(groups[0], True), (groups[1], True), (groups[0], False)]
+def pieces_kernel(lists, grad, *refs):
+    outs, (held, sems_in, sems_out) = refs[: len(lists)], refs[len(lists) :]
     into, onto = [], []
-    for (nears, other), out in zip(lists, (early, late, mine)):
+    for (nears, other), out in zip(lists, outs):
         at = len(into)
         count = RING * len(nears)
         into += gather(grad, held.at[pl.ds(at, count)], sems_in.at[pl.ds(at, count)], nears, other)
@@ -97,21 +98,21 @@
         copy.wait()
 
 
-def column_pieces(grad, groups):
+def column_pieces(grad, lists):
     slots = grad.shape[0]
-    widths = [RING * len(nears) for nears in (groups[0], groups[1], groups[0])]
+    widths = [RING * len(nears) for nears, _ in lists]
     hbm = pl.BlockSpec(memory_space=pl.ANY)
     return pl.pallas_call(
-        functools.partial(pieces_kernel, groups),
+        functools.partial(pieces_kernel, lists),
         out_shape=[jax.ShapeDtypeStruct((slots, width * HD), bf16) for width in widths],
         in_specs=[hbm],
-        out_specs=[hbm] * 3,
+        out_specs=[hbm] * len(lists),
         scratch_shapes=[
             pltpu.VMEM((sum(widths), slots, HD), bf16),
             pltpu.SemaphoreType.DMA((sum(widths),)),
             pltpu.SemaphoreType.DMA((sum(widths),)),
         ],
-        compiler_params=pltpu.CompilerParams(vmem_limit_bytes=LARGE),
+        compiler_params=pltpu.CompilerParams(vmem_limit_bytes=LARGER),
     )(grad)
 
 
@@ -369,8 +370,10 @@
     tie = lax.optimization_barrier
 
     early, late = (2,), (1, 3, 0)
-    piece_early, piece_late, mine = column_pieces(latent_grad, (early, late))
+    piece_early, mine = column_pieces(latent_grad, [(early, True), (early, False)])
     lat_own, mom_own, mom_other, unit, own_early = first(row_counts, latent, momentum, mine)
+    grad_late, own_early = tie((latent_grad, own_early))
+    (piece_late,) = column_pieces(grad_late, [(late, True)])
     piece_early, lat_other, mom_other = (
         swap_cores(piece_early), swap_cores(lat_own), swap_cores(mom_other)
     )

time: 96.7 us -> 96.5 us (level)
  waiting for transfers between devices: 14.3 us -> 13 us
  Pallas kernels: 15.4 us -> 16.4 us
    ppermute x4, waiting for transfers between devices: 1.4 us -> 0.01 us  [swap_cores(): lax.ppermute(value, AXES, [(device_at(z, y, x, c), device_at(z, y, x, 1 -...]
    pallas_call x1 -> x2, Pallas kernels: 2.27 us -> 3.25 us  [column_pieces(): pl.pallas_call(functools.partial(pieces_kernel, lists), out_shape=[jax.Sh...]
  transfers between devices with their start and end apart: 15 -> 15, of which waited for: 10 -> 8; matrix products, arithmetic and copies ran while one was open for 0% -> 0% of each run, Pallas kernels for 7% -> 9%
where the time goes in v12:
time: 96.5 us; the launch traced here: 96.2 us
  blocking collectives  49.5 us (51%)
  Pallas kernels  16.4 us (17%)
  starting transfers between devices  15.3 us (16%)
  waiting for transfers between devices  13 us (13%)
  between operations  1.64 us (2%)
    all_to_all x1, blocking collectives, body(): returned = lax.all_to_all(outgoing, PLANE, 0, 0, tiled=True)  20.4 us
    all_to_all x1, blocking collectives, body(): pieces = lax.all_to_all(head.reshape(NZ, -1, HD), 'z', 0, 0, tiled=True)  17.2 us
    ppermute x11, waiting for transfers between devices, exchange(): return lax.ppermute(value, AXES, pairs)  13 us
    all_to_all x1, blocking collectives, body(): lax.all_to_all(jnp.broadcast_to(piece, (NZ,) + piece.shape), 'z', 0, 0, t...  11.9 us
    ppermute x11, starting transfers between devices, exchange(): return lax.ppermute(value, AXES, pairs)  11.2 us
    pallas_call x1, Pallas kernels, newton_schulz(): pl.pallas_call(newton_schulz_kernel, out_shape=jax.ShapeDtypeStruct((owne...  5.76 us
    ppermute x4, starting transfers between devices, swap_cores(): lax.ppermute(value, AXES, [(device_at(z, y, x, c), device_at(z, y, x, 1 -...  4.11 us
    pallas_call x2, Pallas kernels, column_pieces(): pl.pallas_call(functools.partial(pieces_kernel, lists), out_shape=[jax.Sh...  3.25 us
  transfers between devices with their start and end apart: 15, of which 8 were waited for; matrix products, arithmetic and copies ran while one was open for 0% of the time, Pallas kernels for 9%

profile of v12, /device:TPU:1, one launch (start us, length us, event | category | flops | bytes accessed | tf_op | source)
XLA Modules:
  0.0 96.2 jit_solution(12481431119107122789)
XLA Ops:
  0.6 1.5 %shard_map.59 = (bf16[256,1024]{1,0:T(8,128)(2,1)S(1)}, bf16[256,1024]{1,0:T(8,128)(2,1)S(1)}) custom-call(bf16[256,8192]{1,0:T(8,128)(2,1)} %grad.4), custom_call_target="tpu_custom_call" | custom-call | tf_op jit(solution)/shard_map/pallas_call | solution.py:105
  2.2 3.3 %collective-permute-start = (bf16[256,1024]{1,0:T(8,128)(2,1)S(1)}, bf16[256,1024]{1,0:T(8,128)(2,1)S(1)}, u32[]{:S(2)}, u32[]{:S(2)}) collective-permute-start(bf16[256,1024]{1,0:T(8,128)(2,1)S(1)} %get-tuple-element.42), channel_id=1, source_target_pairs={{0,1},{1,0},{2,3},{3,2},{4,5},{5,4},{6,7},{7,6},{8,9},{9,8},{10,11... | collective-permute-start | bytes 1572872 | tf_op jit(solution)/shard_map/ppermute | solution.py:47
  6.2 0.7 shard_map.60
  6.9 0.1 collective-permute-start.2
  7.0 0.5 collective-permute-start.1
  7.5 1.7 %shard_map.61 = bf16[256,3072]{1,0:T(8,128)(2,1)S(1)} custom-call(bf16[256,8192]{1,0:T(8,128)(2,1)} %grad.4), custom_call_target="tpu_custom_call" | custom-call | tf_op jit(solution)/shard_map/pallas_call | solution.py:105
  9.2 0.0 collective-permute-done.2.mom_other
  9.2 0.0 collective-permute-done.1.lat
  9.2 0.0 collective-permute-done.grad
  9.2 0.2 collective-permute-start.3
  9.4 0.7 shard_map.62
  10.1 1.1 %collective-permute-start.7 = (bf16[4,256,256]{2,1,0:T(8,128)(2,1)S(1)}, bf16[4,256,256]{2,1,0:T(8,128)(2,1)S(1)}, u32[]{:S(2)}, u32[]{:S(2)}) collective-permute-start(bf16[4,256,256]{2,1,0:T(8,128)(2,1)S(1)} %get-tuple-element.65), channel_id=1, source_target_pairs={{0,6},{1,25},{2,4},{3,27},{4,2},{5,29},{6,0},{7,31},{8,14},{9,17},... | collective-permute-start | bytes 1572872 | tf_op jit(solution)/shard_map/ppermute | solution.py:43
  11.2 0.0 collective-permute-start.6
  11.2 2.5 %shard_map.63 = (bf16[4,512,256]{2,1,0:T(8,128)(2,1)S(1)}, bf16[4,512,256]{2,1,0:T(8,128)(2,1)S(1)}, bf16[4,512,256]{2,1,0:T(8,128)(2,1)S(1)}) custom-call(bf16[512,256]{1,0:T(8,128)(2,1)S(1)} %get-tuple-element.53.lat, bf16[256,8192]{1,0:T(8,128)(2,1)} %grad.4), custom_call_target="tpu_custom_call" | custom-call | flops 805306368 | bytes 4718592 | tf_op jit(solution)/shard_map/pallas_call | solution.py:176
  13.8 0.0 collective-permute-done.3.grad
  13.8 0.4 shard_map.64
  14.2 0.4 shard_map.65
  14.5 1.6 %collective-permute-start.4 = (bf16[3,256,256]{2,1,0:T(8,128)(2,1)S(1)}, bf16[3,256,256]{2,1,0:T(8,128)(2,1)S(1)}, u32[]{:S(2)}, u32[]{:S(2)}) collective-permute-start(bf16[3,256,256]{2,1,0:T(8,128)(2,1)S(1)} %shard_map.64), channel_id=1, source_target_pairs={{0,2},{1,9},{2,0},{3,11},{4,6},{5,13},{6,4},{7,15},{8,10},{9,1},{1... | collective-permute-start | bytes 1179656 | tf_op jit(solution)/shard_map/ppermute | solution.py:43
  16.1 1.7 %collective-permute-start.5 = (bf16[3,256,256]{2,1,0:T(8,128)(2,1)S(1)}, bf16[3,256,256]{2,1,0:T(8,128)(2,1)S(1)}, u32[]{:S(2)}, u32[]{:S(2)}) collective-permute-start(bf16[3,256,256]{2,1,0:T(8,128)(2,1)S(1)} %shard_map.65), channel_id=1, source_target_pairs={{0,6},{1,25},{2,4},{3,27},{4,2},{5,29},{6,0},{7,31},{8,14},{9,17},... | collective-permute-start | bytes 1179656 | tf_op jit(solution)/shard_map/ppermute | solution.py:43
  17.8 1.4 %shard_map.66 = (f32[3,256,256]{2,1,0:T(8,128)S(1)}, f32[3,256,256]{2,1,0:T(8,128)S(1)}, f32[1,512,256]{2,1,0:T(8,128)S(1)}, f32[1,512,256]{2,1,0:T(8,128)S(1)},...) custom-call(bf16[512,64]{1,0:T(8,128)(2,1)S(1)} %get-tuple-element.39.unit, ...), custom_call_target="tpu_custom_call" | custom-call | flops 754974720 | bytes 7864320 | tf_op jit(solution)/shard_map/pallas_call | solution.py:216
  19.2 0.6 collective-permute-done.7.two_b
  19.8 0.1 add_convert_fusion
  19.8 0.1 collective-permute-start.11
  19.9 0.1 add_convert_fusion.1
  20.0 1.3 %collective-permute-start.10 = (bf16[3,256,256]{2,1,0:T(8,128)(2,1)S(1)}, bf16[3,256,256]{2,1,0:T(8,128)(2,1)S(1)}, u32[]{:S(2)}, u32[]{:S(2)}) collective-permute-start(bf16[3,256,256]{2,1,0:T(8,128)(2,1)S(1)} %add_convert_fusion.1), channel_id=1, source_target_pairs={{0,6},{1,25},{2,4},{3,27},{4,2},{5,29},{6,0},{7,31},{8,14},{9,17},... | collective-permute-start | bytes 1179656 | tf_op jit(solution)/shard_map/ppermute | solution.py:43
  21.4 2.4 %collective-permute-done.4.upper = bf16[3,256,256]{2,1,0:T(8,128)(2,1)S(1)} collective-permute-done((bf16[3,256,256]{2,1,0:T(8,128)(2,1)S(1)}, bf16[3,256,256]{2,1,0:T(8,128)(2,1)S(1)}, u32[]{:S(2)}, u32[]{:S(2)}) %collective-permute-start.4) | collective-permute-done | bytes 393248 | tf_op jit(solution)/shard_map/ppermute | solution.py:43
  23.8 0.5 collective-permute-done.5.lower
  24.2 0.2 shard_map.67
  24.4 0.1 collective-permute-start.8
  24.5 1.9 %collective-permute-start.9 = (bf16[512,256]{1,0:T(8,128)(2,1)S(1)}, bf16[512,256]{1,0:T(8,128)(2,1)S(1)}, u32[]{:S(2)}, u32[]{:S(2)}) collective-permute-start(bf16[512,256]{1,0:T(8,128)(2,1)S(1)} %get-tuple-element.67), channel_id=1, source_target_pairs={{0,6},{1,25},{2,4},{3,27},{4,2},{5,29},{6,0},{7,31},{8,14},{9,17},... | collective-permute-start | bytes 786440 | tf_op jit(solution)/shard_map/ppermute | solution.py:43
  26.5 1.5 %collective-permute-done.11.lower = bf16[3,256,256]{2,1,0:T(8,128)(2,1)S(1)} collective-permute-done((bf16[3,256,256]{2,1,0:T(8,128)(2,1)S(1)}, bf16[3,256,256]{2,1,0:T(8,128)(2,1)S(1)}, u32[]{:S(2)}, u32[]{:S(2)}) %collective-permute-start.11) | collective-permute-done | bytes 393248 | tf_op jit(solution)/shard_map/ppermute | solution.py:43
  28.0 0.5 collective-permute-done.10.upper
  28.4 0.1 shard_map.69
  28.6 2.5 %collective-permute-start.12 = (bf16[512,256]{1,0:T(8,128)(2,1)S(1)}, bf16[512,256]{1,0:T(8,128)(2,1)S(1)}, u32[]{:S(2)}, u32[]{:S(2)}) collective-permute-start(bf16[512,256]{1,0:T(8,128)(2,1)S(1)} %get-tuple-element.71), channel_id=1, source_target_pairs={{0,16},{1,5},{2,18},{3,7},{4,20},{5,1},{6,22},{7,3},{8,24},{9,13},... | collective-permute-start | bytes 786440 | tf_op jit(solution)/shard_map/ppermute | solution.py:43
  31.1 0.6 collective-permute-start.13
  31.7 0.3 collective-permute-start.14
  32.0 0.0 collective-permute-done.8.one
  32.0 0.0 collective-permute-done.9.three
  32.0 0.1 shard_map.68
  32.0 4.8 %collective-permute-done.12 = bf16[512,256]{1,0:T(8,128)(2,1)S(1)} collective-permute-done((bf16[512,256]{1,0:T(8,128)(2,1)S(1)}, bf16[512,256]{1,0:T(8,128)(2,1)S(1)}, u32[]{:S(2)}, u32[]{:S(2)}) %collective-permute-start.12) | collective-permute-done | bytes 262176 | tf_op jit(solution)/shard_map/ppermute | solution.py:43
  36.8 1.8 %collective-permute-done.13 = bf16[512,256]{1,0:T(8,128)(2,1)S(1)} collective-permute-done((bf16[512,256]{1,0:T(8,128)(2,1)S(1)}, bf16[512,256]{1,0:T(8,128)(2,1)S(1)}, u32[]{:S(2)}, u32[]{:S(2)}) %collective-permute-start.13) | collective-permute-done | bytes 262176 | tf_op jit(solution)/shard_map/ppermute | solution.py:43
  38.6 1.0 %collective-permute-done.14 = bf16[512,256]{1,0:T(8,128)(2,1)S(1)} collective-permute-done((bf16[512,256]{1,0:T(8,128)(2,1)S(1)}, bf16[512,256]{1,0:T(8,128)(2,1)S(1)}, u32[]{:S(2)}, u32[]{:S(2)}) %collective-permute-start.14) | collective-permute-done | bytes 262176 | tf_op jit(solution)/shard_map/ppermute | solution.py:43
  39.6 0.1 add_convert_fusion.2
  39.7 17.2 %all_to_all.15 = bf16[8,64,256]{2,1,0:T(8,128)(2,1)S(1)} all-to-all(bf16[8,64,256]{2,1,0:T(8,128)(2,1)S(1)} %bitcast.3), channel_id=1, replica_groups=mesh['z'=8,'y'=4,'x'=4,'c'=2] {'z'}, dimensions={0} | all-to-all | bytes 524288 | tf_op jit(solution)/shard_map/all_to_all | solution.py:424
  57.0 11.9 %all_to_all.16 = bf16[8,64,256]{2,1,0:T(8,128)(2,1)S(1)} all-to-all(bf16[8,64,256]{2,1,0:T(8,128)(2,1)S(1)} %broadcast_in_dim.3), channel_id=1, replica_groups=mesh['z'=8,'y'=4,'x'=4,'c'=2] {'z'}, dimensions={0} | all-to-all | bytes 524288 | tf_op jit(solution)/shard_map/all_to_all | solution.py:426
  68.9 5.8 %shard_map.70 = bf16[32,2,16,256]{3,2,1,0:T(8,128)(2,1)S(1)} custom-call(bf16[512,256]{1,0:T(8,128)(2,1)S(1)} %bitcast.2), custom_call_target="tpu_custom_call" | custom-call | tf_op jit(solution)/shard_map/pallas_call | solution.py:322
  74.7 20.4 %all_to_all.17.returned = bf16[32,2,16,256]{3,2,1,0:T(8,128)(2,1)S(1)} all-to-all(bf16[32,2,16,256]{3,2,1,0:T(8,128)(2,1)S(1)} %shard_map.70), channel_id=1, replica_groups=mesh['z'=8,'y'=4,'x'=4,'c'=2] {'c','y','x'}, dimensions={0} | all-to-all | bytes 1048576 | tf_op jit(solution)/shard_map/all_to_all | solution.py:430
  95.1 0.9 shard_map.71
  (7 shorter events, 0.1 us)
Async XLA Ops:
  0.6 5.6 %copy-start = (f32[16,8192]{1,0:T(8,128)S(1)}, f32[16,8192]{1,0:T(8,128)}, u32[]{:S(2)}) copy-start(f32[16,8192]{1,0:T(8,128)} %momentum.1) | copy-start | bytes 1572868
  0.6 5.6 %copy-start.1 = (bf16[256,512]{1,0:T(8,128)(2,1)S(1)}, bf16[256,512]{1,0:T(8,128)(2,1)}, u32[]{:S(2)}) copy-start(bf16[256,512]{1,0:T(8,128)(2,1)} %latent.1) | copy-start | bytes 786436
  2.2 7.0 %collective-permute-start = (bf16[256,1024]{1,0:T(8,128)(2,1)S(1)}, bf16[256,1024]{1,0:T(8,128)(2,1)S(1)}, u32[]{:S(2)}, u32[]{:S(2)}) collective-permute-start(bf16[256,1024]{1,0:T(8,128)(2,1)S(1)} %get-tuple-element.42), channel_id=1, source_target_pairs={{0,1},{1,0},{2,3},{3,2},{4,5},{5,4},{6,7},{7,6},{8,9},{9,8},{10,11... | collective-permute-start | bytes 1572872 | tf_op jit(solution)/shard_map/ppermute | solution.py:47
  6.9 2.3 %collective-permute-start.2 = (bf16[32,4096]{1,0:T(8,128)(2,1)S(1)}, bf16[32,4096]{1,0:T(8,128)(2,1)S(1)}, u32[]{:S(2)}, u32[]{:S(2)}) collective-permute-start(bf16[32,4096]{1,0:T(8,128)(2,1)S(1)} %get-tuple-element.44), channel_id=1, source_target_pairs={{0,1},{1,0},{2,3},{3,2},{4,5},{5,4},{6,7},{7,6},{8,9},{9,8},{10,11... | collective-permute-start | bytes 786440 | tf_op jit(solution)/shard_map/ppermute | solution.py:47
  7.0 2.2 %collective-permute-start.1 = (bf16[512,256]{1,0:T(8,128)(2,1)S(1)}, bf16[512,256]{1,0:T(8,128)(2,1)S(1)}, u32[]{:S(2)}, u32[]{:S(2)}) collective-permute-start(bf16[512,256]{1,0:T(8,128)(2,1)S(1)} %get-tuple-element.53.lat), channel_id=1, source_target_pairs={{0,1},{1,0},{2,3},{3,2},{4,5},{5,4},{6,7},{7,6},{8,9},{9,8},{10,11... | collective-permute-start | bytes 786440 | tf_op jit(solution)/shard_map/ppermute | solution.py:47
  9.2 4.6 %collective-permute-start.3 = (bf16[256,3072]{1,0:T(8,128)(2,1)S(1)}, bf16[256,3072]{1,0:T(8,128)(2,1)S(1)}, u32[]{:S(2)}, u32[]{:S(2)}) collective-permute-start(bf16[256,3072]{1,0:T(8,128)(2,1)S(1)} %shard_map.61), channel_id=1, source_target_pairs={{0,1},{1,0},{2,3},{3,2},{4,5},{5,4},{6,7},{7,6},{8,9},{9,8},{10,11... | collective-permute-start | bytes 4718600 | tf_op jit(solution)/shard_map/ppermute | solution.py:47
  10.1 9.6 %collective-permute-start.7 = (bf16[4,256,256]{2,1,0:T(8,128)(2,1)S(1)}, bf16[4,256,256]{2,1,0:T(8,128)(2,1)S(1)}, u32[]{:S(2)}, u32[]{:S(2)}) collective-permute-start(bf16[4,256,256]{2,1,0:T(8,128)(2,1)S(1)} %get-tuple-element.65), channel_id=1, source_target_pairs={{0,6},{1,25},{2,4},{3,27},{4,2},{5,29},{6,0},{7,31},{8,14},{9,17},... | collective-permute-start | bytes 1572872 | tf_op jit(solution)/shard_map/ppermute | solution.py:43
  11.2 8.7 %collective-permute-start.6 = (bf16[4,256,256]{2,1,0:T(8,128)(2,1)S(1)}, bf16[4,256,256]{2,1,0:T(8,128)(2,1)S(1)}, u32[]{:S(2)}, u32[]{:S(2)}) collective-permute-start(bf16[4,256,256]{2,1,0:T(8,128)(2,1)S(1)} %get-tuple-element.64), channel_id=1, source_target_pairs={{0,2},{1,9},{2,0},{3,11},{4,6},{5,13},{6,4},{7,15},{8,10},{9,1},{1... | collective-permute-start | bytes 1572872 | tf_op jit(solution)/shard_map/ppermute | solution.py:43
  14.5 9.2 %collective-permute-start.4 = (bf16[3,256,256]{2,1,0:T(8,128)(2,1)S(1)}, bf16[3,256,256]{2,1,0:T(8,128)(2,1)S(1)}, u32[]{:S(2)}, u32[]{:S(2)}) collective-permute-start(bf16[3,256,256]{2,1,0:T(8,128)(2,1)S(1)} %shard_map.64), channel_id=1, source_target_pairs={{0,2},{1,9},{2,0},{3,11},{4,6},{5,13},{6,4},{7,15},{8,10},{9,1},{1... | collective-permute-start | bytes 1179656 | tf_op jit(solution)/shard_map/ppermute | solution.py:43
  16.1 8.1 %collective-permute-start.5 = (bf16[3,256,256]{2,1,0:T(8,128)(2,1)S(1)}, bf16[3,256,256]{2,1,0:T(8,128)(2,1)S(1)}, u32[]{:S(2)}, u32[]{:S(2)}) collective-permute-start(bf16[3,256,256]{2,1,0:T(8,128)(2,1)S(1)} %shard_map.65), channel_id=1, source_target_pairs={{0,6},{1,25},{2,4},{3,27},{4,2},{5,29},{6,0},{7,31},{8,14},{9,17},... | collective-permute-start | bytes 1179656 | tf_op jit(solution)/shard_map/ppermute | solution.py:43
  19.8 8.1 %collective-permute-start.11 = (bf16[3,256,256]{2,1,0:T(8,128)(2,1)S(1)}, bf16[3,256,256]{2,1,0:T(8,128)(2,1)S(1)}, u32[]{:S(2)}, u32[]{:S(2)}) collective-permute-start(bf16[3,256,256]{2,1,0:T(8,128)(2,1)S(1)} %add_convert_fusion), channel_id=1, source_target_pairs={{0,2},{1,9},{2,0},{3,11},{4,6},{5,13},{6,4},{7,15},{8,10},{9,1},{1... | collective-permute-start | bytes 1179656 | tf_op jit(solution)/shard_map/ppermute | solution.py:43
  20.0 8.4 %collective-permute-start.10 = (bf16[3,256,256]{2,1,0:T(8,128)(2,1)S(1)}, bf16[3,256,256]{2,1,0:T(8,128)(2,1)S(1)}, u32[]{:S(2)}, u32[]{:S(2)}) collective-permute-start(bf16[3,256,256]{2,1,0:T(8,128)(2,1)S(1)} %add_convert_fusion.1), channel_id=1, source_target_pairs={{0,6},{1,25},{2,4},{3,27},{4,2},{5,29},{6,0},{7,31},{8,14},{9,17},... | collective-permute-start | bytes 1179656 | tf_op jit(solution)/shard_map/ppermute | solution.py:43
  24.4 7.5 %collective-permute-start.8 = (bf16[512,256]{1,0:T(8,128)(2,1)S(1)}, bf16[512,256]{1,0:T(8,128)(2,1)S(1)}, u32[]{:S(2)}, u32[]{:S(2)}) collective-permute-start(bf16[512,256]{1,0:T(8,128)(2,1)S(1)} %get-tuple-element.66), channel_id=1, source_target_pairs={{0,2},{1,9},{2,0},{3,11},{4,6},{5,13},{6,4},{7,15},{8,10},{9,1},{1... | collective-permute-start | bytes 786440 | tf_op jit(solution)/shard_map/ppermute | solution.py:43
  24.5 7.4 %collective-permute-start.9 = (bf16[512,256]{1,0:T(8,128)(2,1)S(1)}, bf16[512,256]{1,0:T(8,128)(2,1)S(1)}, u32[]{:S(2)}, u32[]{:S(2)}) collective-permute-start(bf16[512,256]{1,0:T(8,128)(2,1)S(1)} %get-tuple-element.67), channel_id=1, source_target_pairs={{0,6},{1,25},{2,4},{3,27},{4,2},{5,29},{6,0},{7,31},{8,14},{9,17},... | collective-permute-start | bytes 786440 | tf_op jit(solution)/shard_map/ppermute | solution.py:43
  28.6 8.2 %collective-permute-start.12 = (bf16[512,256]{1,0:T(8,128)(2,1)S(1)}, bf16[512,256]{1,0:T(8,128)(2,1)S(1)}, u32[]{:S(2)}, u32[]{:S(2)}) collective-permute-start(bf16[512,256]{1,0:T(8,128)(2,1)S(1)} %get-tuple-element.71), channel_id=1, source_target_pairs={{0,16},{1,5},{2,18},{3,7},{4,20},{5,1},{6,22},{7,3},{8,24},{9,13},... | collective-permute-start | bytes 786440 | tf_op jit(solution)/shard_map/ppermute | solution.py:43
  31.1 7.5 %collective-permute-start.13 = (bf16[512,256]{1,0:T(8,128)(2,1)S(1)}, bf16[512,256]{1,0:T(8,128)(2,1)S(1)}, u32[]{:S(2)}, u32[]{:S(2)}) collective-permute-start(bf16[512,256]{1,0:T(8,128)(2,1)S(1)} %get-tuple-element.72), channel_id=1, source_target_pairs={{0,8},{1,3},{2,10},{3,1},{4,12},{5,7},{6,14},{7,5},{8,0},{9,11},{1... | collective-permute-start | bytes 786440 | tf_op jit(solution)/shard_map/ppermute | solution.py:43
  31.7 7.9 %collective-permute-start.14 = (bf16[512,256]{1,0:T(8,128)(2,1)S(1)}, bf16[512,256]{1,0:T(8,128)(2,1)S(1)}, u32[]{:S(2)}, u32[]{:S(2)}) collective-permute-start(bf16[512,256]{1,0:T(8,128)(2,1)S(1)} %get-tuple-element.73), channel_id=1, source_target_pairs={{0,24},{1,7},{2,26},{3,5},{4,28},{5,3},{6,30},{7,1},{8,16},{9,15},... | collective-permute-start | bytes 786440 | tf_op jit(solution)/shard_map/ppermute | solution.py:43

commit v13 on v12

--- a/solution.py
+++ b/solution.py
@@ -230,49 +230,49 @@
     for k in range(kept.shape[0]):
         kept_out[k, :half] = kept[k, :half] + upper[k].astype(f32)
         kept_out[k, half:] = kept[k, half:] + lower[k].astype(f32)
-    one_out[:half, :] = one[0, :half].astype(bf16)
-    one_out[half:, :] = (one[0, half:] + two_b[0].astype(f32)).astype(bf16)
-    three_out[:half, :] = (three[0, :half] + two_a[0].astype(f32)).astype(bf16)
-    three_out[half:, :] = three[0, half:].astype(bf16)
-
-
-def middle(kept, *parts):
-    stay = jax.ShapeDtypeStruct(kept.shape[1:], bf16)
+    one_out[...] = (one[0] + two_b[0].astype(f32)).astype(bf16)
+    three_out[...] = (three[0] + two_a[0].astype(f32)).astype(bf16)
+
+
+def middle(kept, upper, *parts):
+    stay = jax.ShapeDtypeStruct(upper.shape[1:], bf16)
     return pl.pallas_call(
         middle_kernel,
         out_shape=[jax.ShapeDtypeStruct(kept.shape, f32), stay, stay],
         compiler_params=pltpu.CompilerParams(vmem_limit_bytes=VMEM),
         cost_estimate=pl.CostEstimate(flops=MIDDLE, bytes_accessed=0, transcendentals=0),
-    )(kept, *parts)
-
-
-def stay_kernel(kept, one, three, out):
-    out[...] = kept[0] + one[...].astype(f32) + three[...].astype(f32)
-
-
-def stay_sum(kept, one, three):
+    )(kept, upper, *parts)
+
+
+def stay_kernel(kept, upper, lower, out):
+    half = upper.shape[0]
+    out[:half, :] = kept[0, :half] + upper[...].astype(f32)
+    out[half:, :] = kept[0, half:] + lower[...].astype(f32)
+
+
+def stay_sum(kept, upper, lower):
     return pl.pallas_call(
         stay_kernel,
         out_shape=jax.ShapeDtypeStruct(kept.shape[1:], f32),
         compiler_params=pltpu.CompilerParams(vmem_limit_bytes=VMEM),
         cost_estimate=pl.CostEstimate(flops=MIDDLE, bytes_accessed=0, transcendentals=0),
-    )(kept, one, three)
+    )(kept, upper, lower)
 
 
 def add_kernel(kept, upper, lower, *outs):
     half = upper.shape[1]
     for k, out in enumerate(outs):
-        out[:half, :] = (kept[k, :half] + upper[k].astype(f32)).astype(out.dtype)
-        out[half:, :] = (kept[k, half:] + lower[k].astype(f32)).astype(out.dtype)
-
-
-def add_up(kept, *parts):
+        out[:half, :] = (kept[k + 1, :half] + upper[k].astype(f32)).astype(out.dtype)
+        out[half:, :] = (kept[k + 1, half:] + lower[k].astype(f32)).astype(out.dtype)
+
+
+def add_up(kept, upper, lower):
     heads, rows, columns = kept.shape
     return pl.pallas_call(
         add_kernel,
-        out_shape=[jax.ShapeDtypeStruct((rows, columns), bf16)] * heads,
-        compiler_params=pltpu.CompilerParams(vmem_limit_bytes=VMEM),
-    )(kept, *parts)
+        out_shape=[jax.ShapeDtypeStruct((rows, columns), bf16)] * (heads - 1),
+        compiler_params=pltpu.CompilerParams(vmem_limit_bytes=VMEM),
+    )(kept, upper, lower)
 
 
 def split(value):
@@ -383,42 +383,33 @@
 
     half = features // 2
     upper, lower, whole = (0, half), (half, half), (0, features)
-    every, rest, stay = (0, 1, 2, 3), (1, 2, 3), (0,)
+    every = (0, 1, 2, 3)
     own = {2: own_early}
     two_a, two_b = block(
         own, early, [(2, every, *upper, bf16), (2, every, *lower, bf16)], *shared, piece_early
     )
     lat_late, two_a, two_b = tie((lat_own, two_a, two_b))
     own[1], own[3], own[0] = own_products(lat_late, latent_grad, late)
-    (one_a,) = block(own, late, [(1, rest, *upper, bf16)], *shared, piece_late)
-    (three_b,) = block(own, late, [(3, rest, *lower, bf16)], *shared, piece_late)
+    (one_a,) = block(own, late, [(1, every, *upper, bf16)], *shared, piece_late)
+    (three_b,) = block(own, late, [(3, every, *lower, bf16)], *shared, piece_late)
     own[0], one_a, three_b = tie((own[0], one_a, three_b))
-    one_b, three_a, one_stay, three_stay, kept_on, kept_stay = block(
+    one_b, three_a, kept = block(
         own,
         late,
-        [
-            (1, rest, *lower, f32),
-            (3, rest, *upper, f32),
-            (1, stay, *whole, f32),
-            (3, stay, *whole, f32),
-            (0, rest, *whole, f32),
-            (0, stay, *whole, f32),
-        ],
+        [(1, every, *lower, f32), (3, every, *upper, f32), (0, every, *whole, f32)],
         *shared,
         piece_late,
     )
     two_a, two_b = exchange(two_a, 0, 1), exchange(two_b, 0, 3)
     one_a, three_b = exchange(one_a, 0, 1), exchange(three_b, 0, 3)
-    three_a = exchange((three_a + two_a[1:].astype(f32)).astype(bf16), 0, 3)
-    one_b = exchange((one_b + two_b[1:].astype(f32)).astype(bf16), 0, 1)
-    kept_on, one_stay, three_stay = middle(
-        kept_on, one_a, three_b, one_stay, three_stay, two_a, two_b
-    )
+    three_on = exchange((three_a[1:] + two_a[1:].astype(f32)).astype(bf16), 0, 3)
+    one_on = exchange((one_b[1:] + two_b[1:].astype(f32)).astype(bf16), 0, 1)
+    kept, one_stay, three_stay = middle(kept, one_a, three_b, one_b, three_a, two_a, two_b)
     one_stay, three_stay = exchange(one_stay, 0, 1), exchange(three_stay, 0, 3)
 
-    sums = add_up(kept_on, three_a, one_b)
+    sums = add_up(kept, three_on, one_on)
     got = [exchange(sums[k - 1], 1, k) for k in order]
-    head = stay_sum(kept_stay, one_stay, three_stay)
+    head = stay_sum(kept, three_stay, one_stay)
     head = (head + sum(value.astype(f32) for value in got)).astype(bf16)
 
     pieces = lax.all_to_all(head.reshape(NZ, -1, HD), "z", 0, 0, tiled=True)

time: 96.5 us -> 97.5 us (1.010)
  waiting for transfers between devices: 13 us -> 14.9 us
  starting transfers between devices: 15.3 us -> 13.9 us
    ppermute x11, waiting for transfers between devices: 13 us -> 14.9 us  [exchange(): return lax.ppermute(value, AXES, pairs)]
    ppermute x11, starting transfers between devices: 11.2 us -> 9.83 us  [exchange(): return lax.ppermute(value, AXES, pairs)]
  transfers between devices with their start and end apart: 15 -> 15, of which waited for: 8 -> 7; matrix products, arithmetic and copies ran while one was open for 0% -> 0% of each run, Pallas kernels for 9% -> 8%
where the time goes in v13:
time: 97.5 us; the launch traced here: 97.3 us
  blocking collectives  50 us (51%)
  Pallas kernels  16.4 us (17%)
  waiting for transfers between devices  14.9 us (15%)
  starting transfers between devices  13.9 us (14%)
  between operations  1.64 us (2%)
    all_to_all x1, blocking collectives, body(): returned = lax.all_to_all(outgoing, PLANE, 0, 0, tiled=True)  20.9 us
    all_to_all x1, blocking collectives, body(): pieces = lax.all_to_all(head.reshape(NZ, -1, HD), 'z', 0, 0, tiled=True)  17.4 us
    ppermute x11, waiting for transfers between devices, exchange(): return lax.ppermute(value, AXES, pairs)  14.9 us
    all_to_all x1, blocking collectives, body(): lax.all_to_all(jnp.broadcast_to(piece, (NZ,) + piece.shape), 'z', 0, 0, t...  11.7 us
    ppermute x11, starting transfers between devices, exchange(): return lax.ppermute(value, AXES, pairs)  9.83 us
    pallas_call x1, Pallas kernels, newton_schulz(): pl.pallas_call(newton_schulz_kernel, out_shape=jax.ShapeDtypeStruct((owne...  5.76 us
    ppermute x4, starting transfers between devices, swap_cores(): lax.ppermute(value, AXES, [(device_at(z, y, x, c), device_at(z, y, x, 1 -...  4.11 us
    pallas_call x2, Pallas kernels, column_pieces(): pl.pallas_call(functools.partial(pieces_kernel, lists), out_shape=[jax.Sh...  3.25 us
  transfers between devices with their start and end apart: 15, of which 7 were waited for; matrix products, arithmetic and copies ran while one was open for 0% of the time, Pallas kernels for 8%

profile of v13, /device:TPU:1, one launch (start us, length us, event | category | flops | bytes accessed | tf_op | source)
XLA Modules:
  0.0 97.3 jit_solution(17377086679552468566)
XLA Ops:
  0.6 1.5 %shard_map.59 = (bf16[256,1024]{1,0:T(8,128)(2,1)S(1)}, bf16[256,1024]{1,0:T(8,128)(2,1)S(1)}) custom-call(bf16[256,8192]{1,0:T(8,128)(2,1)} %grad.4), custom_call_target="tpu_custom_call" | custom-call | tf_op jit(solution)/shard_map/pallas_call | solution.py:105
  2.2 3.3 %collective-permute-start = (bf16[256,1024]{1,0:T(8,128)(2,1)S(1)}, bf16[256,1024]{1,0:T(8,128)(2,1)S(1)}, u32[]{:S(2)}, u32[]{:S(2)}) collective-permute-start(bf16[256,1024]{1,0:T(8,128)(2,1)S(1)} %get-tuple-element.39), channel_id=1, source_target_pairs={{0,1},{1,0},{2,3},{3,2},{4,5},{5,4},{6,7},{7,6},{8,9},{9,8},{10,11... | collective-permute-start | bytes 1572872 | tf_op jit(solution)/shard_map/ppermute | solution.py:47
  6.2 0.7 shard_map.60
  6.9 0.1 collective-permute-start.2
  7.0 0.5 collective-permute-start.1
  7.5 1.7 %shard_map.61 = bf16[256,3072]{1,0:T(8,128)(2,1)S(1)} custom-call(bf16[256,8192]{1,0:T(8,128)(2,1)} %grad.4), custom_call_target="tpu_custom_call" | custom-call | tf_op jit(solution)/shard_map/pallas_call | solution.py:105
  9.2 0.0 collective-permute-done.2.mom_other
  9.2 0.0 collective-permute-done.1.lat
  9.2 0.0 collective-permute-done.grad
  9.2 0.2 collective-permute-start.3
  9.4 0.7 shard_map.62
  10.1 0.1 collective-permute-start.6
  10.2 1.5 %collective-permute-start.7 = (bf16[4,256,256]{2,1,0:T(8,128)(2,1)S(1)}, bf16[4,256,256]{2,1,0:T(8,128)(2,1)S(1)}, u32[]{:S(2)}, u32[]{:S(2)}) collective-permute-start(bf16[4,256,256]{2,1,0:T(8,128)(2,1)S(1)} %get-tuple-element.61), channel_id=1, source_target_pairs={{0,6},{1,25},{2,4},{3,27},{4,2},{5,29},{6,0},{7,31},{8,14},{9,17},... | collective-permute-start | bytes 1572872 | tf_op jit(solution)/shard_map/ppermute | solution.py:43
  11.7 2.5 %shard_map.63 = (bf16[4,512,256]{2,1,0:T(8,128)(2,1)S(1)}, bf16[4,512,256]{2,1,0:T(8,128)(2,1)S(1)}, bf16[4,512,256]{2,1,0:T(8,128)(2,1)S(1)}) custom-call(bf16[512,256]{1,0:T(8,128)(2,1)S(1)} %get-tuple-element.50.lat, bf16[256,8192]{1,0:T(8,128)(2,1)} %grad.4), custom_call_target="tpu_custom_call" | custom-call | flops 805306368 | bytes 4718592 | tf_op jit(solution)/shard_map/pallas_call | solution.py:176
  14.2 0.0 collective-permute-done.3.grad
  14.2 0.4 shard_map.64
  14.7 0.4 shard_map.65
  15.1 0.5 collective-permute-start.4
  15.6 1.7 %collective-permute-start.5 = (bf16[4,256,256]{2,1,0:T(8,128)(2,1)S(1)}, bf16[4,256,256]{2,1,0:T(8,128)(2,1)S(1)}, u32[]{:S(2)}, u32[]{:S(2)}) collective-permute-start(bf16[4,256,256]{2,1,0:T(8,128)(2,1)S(1)} %shard_map.65), channel_id=1, source_target_pairs={{0,6},{1,25},{2,4},{3,27},{4,2},{5,29},{6,0},{7,31},{8,14},{9,17},... | collective-permute-start | bytes 1572872 | tf_op jit(solution)/shard_map/ppermute | solution.py:43
  17.3 1.3 %shard_map.66 = (f32[4,256,256]{2,1,0:T(8,128)S(1)}, f32[4,256,256]{2,1,0:T(8,128)S(1)}, f32[4,512,256]{2,1,0:T(8,128)S(1)}) custom-call(bf16[512,64]{1,0:T(8,128)(2,1)S(1)} %get-tuple-element.36.unit, bf16[512,256]{1,0:T(8,128)(2,1)S(1)} %collective-permute-done.1.lat, bf16[32,4096]{1,0:T(8,128)(2,1)S(1)} %get-tuple-element.43.mom_own, ...), custom_call_target="tpu_custom_call" | custom-call | flops 671088640 | bytes 5767168 | tf_op jit(solution)/shard_map/pallas_call | solution.py:216
  18.6 0.0 collective-permute-done.6.two_a
  18.6 0.1 add_convert_fusion.1
  18.7 1.1 %collective-permute-start.10 = (bf16[3,256,256]{2,1,0:T(8,128)(2,1)S(1)}, bf16[3,256,256]{2,1,0:T(8,128)(2,1)S(1)}, u32[]{:S(2)}, u32[]{:S(2)}) collective-permute-start(bf16[3,256,256]{2,1,0:T(8,128)(2,1)S(1)} %add_convert_fusion.1), channel_id=1, source_target_pairs={{0,6},{1,25},{2,4},{3,27},{4,2},{5,29},{6,0},{7,31},{8,14},{9,17},... | collective-permute-start | bytes 1179656 | tf_op jit(solution)/shard_map/ppermute | solution.py:43
  19.8 0.1 collective-permute-done.7.two_b
  19.9 0.1 add_convert_fusion
  19.9 0.2 collective-permute-start.11
  20.2 4.0 %collective-permute-done.4.upper = bf16[4,256,256]{2,1,0:T(8,128)(2,1)S(1)} collective-permute-done((bf16[4,256,256]{2,1,0:T(8,128)(2,1)S(1)}, bf16[4,256,256]{2,1,0:T(8,128)(2,1)S(1)}, u32[]{:S(2)}, u32[]{:S(2)}) %collective-permute-start.4) | collective-permute-done | bytes 524320 | tf_op jit(solution)/shard_map/ppermute | solution.py:43
  24.2 1.3 %collective-permute-done.5.lower = bf16[4,256,256]{2,1,0:T(8,128)(2,1)S(1)} collective-permute-done((bf16[4,256,256]{2,1,0:T(8,128)(2,1)S(1)}, bf16[4,256,256]{2,1,0:T(8,128)(2,1)S(1)}, u32[]{:S(2)}, u32[]{:S(2)}) %collective-permute-start.5) | collective-permute-done | bytes 524320 | tf_op jit(solution)/shard_map/ppermute | solution.py:43
  25.5 0.2 shard_map.67
  25.7 1.5 %collective-permute-start.8 = (bf16[256,256]{1,0:T(8,128)(2,1)S(1)}, bf16[256,256]{1,0:T(8,128)(2,1)S(1)}, u32[]{:S(2)}, u32[]{:S(2)}) collective-permute-start(bf16[256,256]{1,0:T(8,128)(2,1)S(1)} %get-tuple-element.63), channel_id=1, source_target_pairs={{0,6},{1,25},{2,4},{3,27},{4,2},{5,29},{6,0},{7,31},{8,14},{9,17},... | collective-permute-start | bytes 393224 | tf_op jit(solution)/shard_map/ppermute | solution.py:43
  27.1 0.0 collective-permute-start.9
  27.1 2.5 %collective-permute-done.10.upper = bf16[3,256,256]{2,1,0:T(8,128)(2,1)S(1)} collective-permute-done((bf16[3,256,256]{2,1,0:T(8,128)(2,1)S(1)}, bf16[3,256,256]{2,1,0:T(8,128)(2,1)S(1)}, u32[]{:S(2)}, u32[]{:S(2)}) %collective-permute-start.10) | collective-permute-done | bytes 393248 | tf_op jit(solution)/shard_map/ppermute | solution.py:43
  29.7 0.0 collective-permute-done.11.lower
  29.7 0.1 shard_map.69
  29.8 2.2 %collective-permute-start.12 = (bf16[512,256]{1,0:T(8,128)(2,1)S(1)}, bf16[512,256]{1,0:T(8,128)(2,1)S(1)}, u32[]{:S(2)}, u32[]{:S(2)}) collective-permute-start(bf16[512,256]{1,0:T(8,128)(2,1)S(1)} %get-tuple-element.65), channel_id=1, source_target_pairs={{0,16},{1,5},{2,18},{3,7},{4,20},{5,1},{6,22},{7,3},{8,24},{9,13},... | collective-permute-start | bytes 786440 | tf_op jit(solution)/shard_map/ppermute | solution.py:43
  32.0 0.6 collective-permute-start.13
  32.6 0.5 collective-permute-start.14
  33.2 0.0 collective-permute-done.8.upper
  33.2 0.0 collective-permute-done.9.lower
  33.2 4.2 %collective-permute-done.12 = bf16[512,256]{1,0:T(8,128)(2,1)S(1)} collective-permute-done((bf16[512,256]{1,0:T(8,128)(2,1)S(1)}, bf16[512,256]{1,0:T(8,128)(2,1)S(1)}, u32[]{:S(2)}, u32[]{:S(2)}) %collective-permute-start.12) | collective-permute-done | bytes 262176 | tf_op jit(solution)/shard_map/ppermute | solution.py:43
  37.4 2.4 %collective-permute-done.13 = bf16[512,256]{1,0:T(8,128)(2,1)S(1)} collective-permute-done((bf16[512,256]{1,0:T(8,128)(2,1)S(1)}, bf16[512,256]{1,0:T(8,128)(2,1)S(1)}, u32[]{:S(2)}, u32[]{:S(2)}) %collective-permute-start.13) | collective-permute-done | bytes 262176 | tf_op jit(solution)/shard_map/ppermute | solution.py:43
  39.8 0.4 collective-permute-done.14
  40.2 0.1 add_convert_fusion.2
  40.3 17.4 %all_to_all.15 = bf16[8,64,256]{2,1,0:T(8,128)(2,1)S(1)} all-to-all(bf16[8,64,256]{2,1,0:T(8,128)(2,1)S(1)} %bitcast.3), channel_id=1, replica_groups=mesh['z'=8,'y'=4,'x'=4,'c'=2] {'z'}, dimensions={0} | all-to-all | bytes 524288 | tf_op jit(solution)/shard_map/all_to_all | solution.py:415
  57.7 11.7 %all_to_all.16 = bf16[8,64,256]{2,1,0:T(8,128)(2,1)S(1)} all-to-all(bf16[8,64,256]{2,1,0:T(8,128)(2,1)S(1)} %broadcast_in_dim.3), channel_id=1, replica_groups=mesh['z'=8,'y'=4,'x'=4,'c'=2] {'z'}, dimensions={0} | all-to-all | bytes 524288 | tf_op jit(solution)/shard_map/all_to_all | solution.py:417
  69.5 5.8 %shard_map.70 = bf16[32,2,16,256]{3,2,1,0:T(8,128)(2,1)S(1)} custom-call(bf16[512,256]{1,0:T(8,128)(2,1)S(1)} %bitcast.2), custom_call_target="tpu_custom_call" | custom-call | tf_op jit(solution)/shard_map/pallas_call | solution.py:322
  75.2 20.9 %all_to_all.17.returned = bf16[32,2,16,256]{3,2,1,0:T(8,128)(2,1)S(1)} all-to-all(bf16[32,2,16,256]{3,2,1,0:T(8,128)(2,1)S(1)} %shard_map.70), channel_id=1, replica_groups=mesh['z'=8,'y'=4,'x'=4,'c'=2] {'c','y','x'}, dimensions={0} | all-to-all | bytes 1048576 | tf_op jit(solution)/shard_map/all_to_all | solution.py:421
  96.2 0.9 shard_map.71
  (7 shorter events, 0.1 us)
Async XLA Ops:
  0.6 5.6 %copy-start = (f32[16,8192]{1,0:T(8,128)S(1)}, f32[16,8192]{1,0:T(8,128)}, u32[]{:S(2)}) copy-start(f32[16,8192]{1,0:T(8,128)} %momentum.1) | copy-start | bytes 1572868
  0.6 5.6 %copy-start.1 = (bf16[256,512]{1,0:T(8,128)(2,1)S(1)}, bf16[256,512]{1,0:T(8,128)(2,1)}, u32[]{:S(2)}) copy-start(bf16[256,512]{1,0:T(8,128)(2,1)} %latent.1) | copy-start | bytes 786436
  2.2 7.0 %collective-permute-start = (bf16[256,1024]{1,0:T(8,128)(2,1)S(1)}, bf16[256,1024]{1,0:T(8,128)(2,1)S(1)}, u32[]{:S(2)}, u32[]{:S(2)}) collective-permute-start(bf16[256,1024]{1,0:T(8,128)(2,1)S(1)} %get-tuple-element.39), channel_id=1, source_target_pairs={{0,1},{1,0},{2,3},{3,2},{4,5},{5,4},{6,7},{7,6},{8,9},{9,8},{10,11... | collective-permute-start | bytes 1572872 | tf_op jit(solution)/shard_map/ppermute | solution.py:47
  6.9 2.3 %collective-permute-start.2 = (bf16[32,4096]{1,0:T(8,128)(2,1)S(1)}, bf16[32,4096]{1,0:T(8,128)(2,1)S(1)}, u32[]{:S(2)}, u32[]{:S(2)}) collective-permute-start(bf16[32,4096]{1,0:T(8,128)(2,1)S(1)} %get-tuple-element.41), channel_id=1, source_target_pairs={{0,1},{1,0},{2,3},{3,2},{4,5},{5,4},{6,7},{7,6},{8,9},{9,8},{10,11... | collective-permute-start | bytes 786440 | tf_op jit(solution)/shard_map/ppermute | solution.py:47
  7.0 2.2 %collective-permute-start.1 = (bf16[512,256]{1,0:T(8,128)(2,1)S(1)}, bf16[512,256]{1,0:T(8,128)(2,1)S(1)}, u32[]{:S(2)}, u32[]{:S(2)}) collective-permute-start(bf16[512,256]{1,0:T(8,128)(2,1)S(1)} %get-tuple-element.50.lat), channel_id=1, source_target_pairs={{0,1},{1,0},{2,3},{3,2},{4,5},{5,4},{6,7},{7,6},{8,9},{9,8},{10,11... | collective-permute-start | bytes 786440 | tf_op jit(solution)/shard_map/ppermute | solution.py:47
  9.2 5.0 %collective-permute-start.3 = (bf16[256,3072]{1,0:T(8,128)(2,1)S(1)}, bf16[256,3072]{1,0:T(8,128)(2,1)S(1)}, u32[]{:S(2)}, u32[]{:S(2)}) collective-permute-start(bf16[256,3072]{1,0:T(8,128)(2,1)S(1)} %shard_map.61), channel_id=1, source_target_pairs={{0,1},{1,0},{2,3},{3,2},{4,5},{5,4},{6,7},{7,6},{8,9},{9,8},{10,11... | collective-permute-start | bytes 4718600 | tf_op jit(solution)/shard_map/ppermute | solution.py:47
  10.1 8.5 %collective-permute-start.6 = (bf16[4,256,256]{2,1,0:T(8,128)(2,1)S(1)}, bf16[4,256,256]{2,1,0:T(8,128)(2,1)S(1)}, u32[]{:S(2)}, u32[]{:S(2)}) collective-permute-start(bf16[4,256,256]{2,1,0:T(8,128)(2,1)S(1)} %get-tuple-element.60), channel_id=1, source_target_pairs={{0,2},{1,9},{2,0},{3,11},{4,6},{5,13},{6,4},{7,15},{8,10},{9,1},{1... | collective-permute-start | bytes 1572872 | tf_op jit(solution)/shard_map/ppermute | solution.py:43
  10.2 9.6 %collective-permute-start.7 = (bf16[4,256,256]{2,1,0:T(8,128)(2,1)S(1)}, bf16[4,256,256]{2,1,0:T(8,128)(2,1)S(1)}, u32[]{:S(2)}, u32[]{:S(2)}) collective-permute-start(bf16[4,256,256]{2,1,0:T(8,128)(2,1)S(1)} %get-tuple-element.61), channel_id=1, source_target_pairs={{0,6},{1,25},{2,4},{3,27},{4,2},{5,29},{6,0},{7,31},{8,14},{9,17},... | collective-permute-start | bytes 1572872 | tf_op jit(solution)/shard_map/ppermute | solution.py:43
  15.1 9.0 %collective-permute-start.4 = (bf16[4,256,256]{2,1,0:T(8,128)(2,1)S(1)}, bf16[4,256,256]{2,1,0:T(8,128)(2,1)S(1)}, u32[]{:S(2)}, u32[]{:S(2)}) collective-permute-start(bf16[4,256,256]{2,1,0:T(8,128)(2,1)S(1)} %shard_map.64), channel_id=1, source_target_pairs={{0,2},{1,9},{2,0},{3,11},{4,6},{5,13},{6,4},{7,15},{8,10},{9,1},{1... | collective-permute-start | bytes 1572872 | tf_op jit(solution)/shard_map/ppermute | solution.py:43
  15.6 9.8 %collective-permute-start.5 = (bf16[4,256,256]{2,1,0:T(8,128)(2,1)S(1)}, bf16[4,256,256]{2,1,0:T(8,128)(2,1)S(1)}, u32[]{:S(2)}, u32[]{:S(2)}) collective-permute-start(bf16[4,256,256]{2,1,0:T(8,128)(2,1)S(1)} %shard_map.65), channel_id=1, source_target_pairs={{0,6},{1,25},{2,4},{3,27},{4,2},{5,29},{6,0},{7,31},{8,14},{9,17},... | collective-permute-start | bytes 1572872 | tf_op jit(solution)/shard_map/ppermute | solution.py:43
  18.7 11.0 %collective-permute-start.10 = (bf16[3,256,256]{2,1,0:T(8,128)(2,1)S(1)}, bf16[3,256,256]{2,1,0:T(8,128)(2,1)S(1)}, u32[]{:S(2)}, u32[]{:S(2)}) collective-permute-start(bf16[3,256,256]{2,1,0:T(8,128)(2,1)S(1)} %add_convert_fusion.1), channel_id=1, source_target_pairs={{0,6},{1,25},{2,4},{3,27},{4,2},{5,29},{6,0},{7,31},{8,14},{9,17},... | collective-permute-start | bytes 1179656 | tf_op jit(solution)/shard_map/ppermute | solution.py:43
  19.9 9.7 %collective-permute-start.11 = (bf16[3,256,256]{2,1,0:T(8,128)(2,1)S(1)}, bf16[3,256,256]{2,1,0:T(8,128)(2,1)S(1)}, u32[]{:S(2)}, u32[]{:S(2)}) collective-permute-start(bf16[3,256,256]{2,1,0:T(8,128)(2,1)S(1)} %add_convert_fusion), channel_id=1, source_target_pairs={{0,2},{1,9},{2,0},{3,11},{4,6},{5,13},{6,4},{7,15},{8,10},{9,1},{1... | collective-permute-start | bytes 1179656 | tf_op jit(solution)/shard_map/ppermute | solution.py:43
  25.7 7.5 %collective-permute-start.8 = (bf16[256,256]{1,0:T(8,128)(2,1)S(1)}, bf16[256,256]{1,0:T(8,128)(2,1)S(1)}, u32[]{:S(2)}, u32[]{:S(2)}) collective-permute-start(bf16[256,256]{1,0:T(8,128)(2,1)S(1)} %get-tuple-element.63), channel_id=1, source_target_pairs={{0,6},{1,25},{2,4},{3,27},{4,2},{5,29},{6,0},{7,31},{8,14},{9,17},... | collective-permute-start | bytes 393224 | tf_op jit(solution)/shard_map/ppermute | solution.py:43
  27.1 6.0 %collective-permute-start.9 = (bf16[256,256]{1,0:T(8,128)(2,1)S(1)}, bf16[256,256]{1,0:T(8,128)(2,1)S(1)}, u32[]{:S(2)}, u32[]{:S(2)}) collective-permute-start(bf16[256,256]{1,0:T(8,128)(2,1)S(1)} %get-tuple-element.64), channel_id=1, source_target_pairs={{0,2},{1,9},{2,0},{3,11},{4,6},{5,13},{6,4},{7,15},{8,10},{9,1},{1... | collective-permute-start | bytes 393224 | tf_op jit(solution)/shard_map/ppermute | solution.py:43
  29.8 7.6 %collective-permute-start.12 = (bf16[512,256]{1,0:T(8,128)(2,1)S(1)}, bf16[512,256]{1,0:T(8,128)(2,1)S(1)}, u32[]{:S(2)}, u32[]{:S(2)}) collective-permute-start(bf16[512,256]{1,0:T(8,128)(2,1)S(1)} %get-tuple-element.65), channel_id=1, source_target_pairs={{0,16},{1,5},{2,18},{3,7},{4,20},{5,1},{6,22},{7,3},{8,24},{9,13},... | collective-permute-start | bytes 786440 | tf_op jit(solution)/shard_map/ppermute | solution.py:43
  32.0 7.7 %collective-permute-start.13 = (bf16[512,256]{1,0:T(8,128)(2,1)S(1)}, bf16[512,256]{1,0:T(8,128)(2,1)S(1)}, u32[]{:S(2)}, u32[]{:S(2)}) collective-permute-start(bf16[512,256]{1,0:T(8,128)(2,1)S(1)} %get-tuple-element.66), channel_id=1, source_target_pairs={{0,8},{1,3},{2,10},{3,1},{4,12},{5,7},{6,14},{7,5},{8,0},{9,11},{1... | collective-permute-start | bytes 786440 | tf_op jit(solution)/shard_map/ppermute | solution.py:43
  32.6 7.5 %collective-permute-start.14 = (bf16[512,256]{1,0:T(8,128)(2,1)S(1)}, bf16[512,256]{1,0:T(8,128)(2,1)S(1)}, u32[]{:S(2)}, u32[]{:S(2)}) collective-permute-start(bf16[512,256]{1,0:T(8,128)(2,1)S(1)} %get-tuple-element.67), channel_id=1, source_target_pairs={{0,24},{1,7},{2,26},{3,5},{4,28},{5,3},{6,30},{7,1},{8,16},{9,15},... | collective-permute-start | bytes 786440 | tf_op jit(solution)/shard_map/ppermute | solution.py:43

commit v14 on v12

--- a/solution.py
+++ b/solution.py
@@ -225,38 +225,33 @@
     )(unit, lat, mom_own, mom_other, grad, *[own[near] for near in nears])
 
 
-def middle_kernel(kept, upper, lower, one, three, two_a, two_b, kept_out, one_out, three_out):
+def middle_kernel(kept, upper, lower, out):
     half = upper.shape[1]
     for k in range(kept.shape[0]):
-        kept_out[k, :half] = kept[k, :half] + upper[k].astype(f32)
-        kept_out[k, half:] = kept[k, half:] + lower[k].astype(f32)
-    one_out[:half, :] = one[0, :half].astype(bf16)
-    one_out[half:, :] = (one[0, half:] + two_b[0].astype(f32)).astype(bf16)
-    three_out[:half, :] = (three[0, :half] + two_a[0].astype(f32)).astype(bf16)
-    three_out[half:, :] = three[0, half:].astype(bf16)
-
-
-def middle(kept, *parts):
-    stay = jax.ShapeDtypeStruct(kept.shape[1:], bf16)
+        out[k, :half] = kept[k, :half] + upper[k].astype(f32)
+        out[k, half:] = kept[k, half:] + lower[k].astype(f32)
+
+
+def middle(kept, upper, lower):
     return pl.pallas_call(
         middle_kernel,
-        out_shape=[jax.ShapeDtypeStruct(kept.shape, f32), stay, stay],
+        out_shape=jax.ShapeDtypeStruct(kept.shape, f32),
+        compiler_params=pltpu.CompilerParams(vmem_limit_bytes=VMEM),
+        cost_estimate=pl.CostEstimate(flops=MIDDLE, bytes_accessed=0, transcendentals=0),
+    )(kept, upper, lower)
+
+
+def stay_kernel(kept, one, two, three, out):
+    out[...] = kept[0] + one[0].astype(f32) + two[0].astype(f32) + three[0].astype(f32)
+
+
+def stay_sum(kept, *parts):
+    return pl.pallas_call(
+        stay_kernel,
+        out_shape=jax.ShapeDtypeStruct(kept.shape[1:], f32),
         compiler_params=pltpu.CompilerParams(vmem_limit_bytes=VMEM),
         cost_estimate=pl.CostEstimate(flops=MIDDLE, bytes_accessed=0, transcendentals=0),
     )(kept, *parts)
-
-
-def stay_kernel(kept, one, three, out):
-    out[...] = kept[0] + one[...].astype(f32) + three[...].astype(f32)
-
-
-def stay_sum(kept, one, three):
-    return pl.pallas_call(
-        stay_kernel,
-        out_shape=jax.ShapeDtypeStruct(kept.shape[1:], f32),
-        compiler_params=pltpu.CompilerParams(vmem_limit_bytes=VMEM),
-        cost_estimate=pl.CostEstimate(flops=MIDDLE, bytes_accessed=0, transcendentals=0),
-    )(kept, one, three)
 
 
 def add_kernel(kept, upper, lower, *outs):
@@ -383,42 +378,44 @@
 
     half = features // 2
     upper, lower, whole = (0, half), (half, half), (0, features)
-    every, rest, stay = (0, 1, 2, 3), (1, 2, 3), (0,)
+    rest, stay = (1, 2, 3), (0,)
     own = {2: own_early}
     two_a, two_b = block(
-        own, early, [(2, every, *upper, bf16), (2, every, *lower, bf16)], *shared, piece_early
+        own, early, [(2, rest, *upper, bf16), (2, rest, *lower, bf16)], *shared, piece_early
     )
     lat_late, two_a, two_b = tie((lat_own, two_a, two_b))
     own[1], own[3], own[0] = own_products(lat_late, latent_grad, late)
     (one_a,) = block(own, late, [(1, rest, *upper, bf16)], *shared, piece_late)
     (three_b,) = block(own, late, [(3, rest, *lower, bf16)], *shared, piece_late)
-    own[0], one_a, three_b = tie((own[0], one_a, three_b))
+    own[0], own[2], one_a, three_b = tie((own[0], own[2], one_a, three_b))
     one_b, three_a, one_stay, three_stay, kept_on, kept_stay = block(
         own,
         late,
         [
             (1, rest, *lower, f32),
             (3, rest, *upper, f32),
-            (1, stay, *whole, f32),
-            (3, stay, *whole, f32),
+            (1, stay, *whole, bf16),
+            (3, stay, *whole, bf16),
             (0, rest, *whole, f32),
             (0, stay, *whole, f32),
         ],
         *shared,
         piece_late,
     )
+    (two_stay,) = block(own, early, [(2, stay, *whole, bf16)], *shared, piece_early)
     two_a, two_b = exchange(two_a, 0, 1), exchange(two_b, 0, 3)
     one_a, three_b = exchange(one_a, 0, 1), exchange(three_b, 0, 3)
-    three_a = exchange((three_a + two_a[1:].astype(f32)).astype(bf16), 0, 3)
-    one_b = exchange((one_b + two_b[1:].astype(f32)).astype(bf16), 0, 1)
-    kept_on, one_stay, three_stay = middle(
-        kept_on, one_a, three_b, one_stay, three_stay, two_a, two_b
-    )
-    one_stay, three_stay = exchange(one_stay, 0, 1), exchange(three_stay, 0, 3)
+    three_a = exchange((three_a + two_a.astype(f32)).astype(bf16), 0, 3)
+    one_b = exchange((one_b + two_b.astype(f32)).astype(bf16), 0, 1)
+    kept_on = middle(kept_on, one_a, three_b)
+    one_stay, two_stay, three_stay, kept_on = tie((one_stay, two_stay, three_stay, kept_on))
+    one_stay, two_stay, three_stay = (
+        exchange(one_stay, 0, 1), exchange(two_stay, 0, 2), exchange(three_stay, 0, 3)
+    )
 
     sums = add_up(kept_on, three_a, one_b)
     got = [exchange(sums[k - 1], 1, k) for k in order]
-    head = stay_sum(kept_stay, one_stay, three_stay)
+    head = stay_sum(kept_stay, one_stay, two_stay, three_stay)
     head = (head + sum(value.astype(f32) for value in got)).astype(bf16)
 
     pieces = lax.all_to_all(head.reshape(NZ, -1, HD), "z", 0, 0, tiled=True)

time: 96.5 us -> 100 us (1.036)
  waiting for transfers between devices: 13 us -> 15.2 us
  starting transfers between devices: 15.3 us -> 17.1 us
    ppermute x11 -> x12, waiting for transfers between devices: 13 us -> 15.2 us  [exchange(): return lax.ppermute(value, AXES, pairs)]
    ppermute x11 -> x12, starting transfers between devices: 11.2 us -> 13 us  [exchange(): return lax.ppermute(value, AXES, pairs)]
    pallas_call x4 -> x5, Pallas kernels: 2.88 us -> 3.05 us  [block(): pl.pallas_call(functools.partial(block_kernel, tiles), out_shape=[jax.Sha...]
  transfers between devices with their start and end apart: 15 -> 16, of which waited for: 8 -> 7; matrix products, arithmetic and copies ran while one was open for 0% -> 0% of each run, Pallas kernels for 9% -> 8%
where the time goes in v14:
time: 100 us
  blocking collectives  49.1 us (49%)
  starting transfers between devices  17.1 us (17%)
  Pallas kernels  16.5 us (16%)
  waiting for transfers between devices  15.2 us (15%)
  between operations  1.66 us (2%)
    all_to_all x1, blocking collectives, body(): returned = lax.all_to_all(outgoing, PLANE, 0, 0, tiled=True)  19.6 us
    all_to_all x1, blocking collectives, body(): pieces = lax.all_to_all(head.reshape(NZ, -1, HD), 'z', 0, 0, tiled=True)  17.5 us
    ppermute x12, waiting for transfers between devices, exchange(): return lax.ppermute(value, AXES, pairs)  15.2 us
    ppermute x12, starting transfers between devices, exchange(): return lax.ppermute(value, AXES, pairs)  13 us
    all_to_all x1, blocking collectives, body(): lax.all_to_all(jnp.broadcast_to(piece, (NZ,) + piece.shape), 'z', 0, 0, t...  11.9 us
    pallas_call x1, Pallas kernels, newton_schulz(): pl.pallas_call(newton_schulz_kernel, out_shape=jax.ShapeDtypeStruct((owne...  5.75 us
    ppermute x4, starting transfers between devices, swap_cores(): lax.ppermute(value, AXES, [(device_at(z, y, x, c), device_at(z, y, x, 1 -...  4.11 us
    pallas_call x2, Pallas kernels, column_pieces(): pl.pallas_call(functools.partial(pieces_kernel, lists), out_shape=[jax.Sh...  3.25 us
  transfers between devices with their start and end apart: 16, of which 7 were waited for; matrix products, arithmetic and copies ran while one was open for 0% of the time, Pallas kernels for 8%

profile of v14, /device:TPU:1, one launch (start us, length us, event | category | flops | bytes accessed | tf_op | source)
XLA Modules:
  0.0 100.0 jit_solution(5366117470604250733)
XLA Ops:
  0.6 1.5 %shard_map.59 = (bf16[256,1024]{1,0:T(8,128)(2,1)S(1)}, bf16[256,1024]{1,0:T(8,128)(2,1)S(1)}) custom-call(bf16[256,8192]{1,0:T(8,128)(2,1)} %grad.4), custom_call_target="tpu_custom_call" | custom-call | tf_op jit(solution)/shard_map/pallas_call | solution.py:105
  2.2 3.3 %collective-permute-start = (bf16[256,1024]{1,0:T(8,128)(2,1)S(1)}, bf16[256,1024]{1,0:T(8,128)(2,1)S(1)}, u32[]{:S(2)}, u32[]{:S(2)}) collective-permute-start(bf16[256,1024]{1,0:T(8,128)(2,1)S(1)} %get-tuple-element.44), channel_id=1, source_target_pairs={{0,1},{1,0},{2,3},{3,2},{4,5},{5,4},{6,7},{7,6},{8,9},{9,8},{10,11... | collective-permute-start | bytes 1572872 | tf_op jit(solution)/shard_map/ppermute | solution.py:47
  6.2 0.7 shard_map.60
  6.9 0.1 collective-permute-start.2
  7.0 0.5 collective-permute-start.1
  7.5 1.7 %shard_map.61 = bf16[256,3072]{1,0:T(8,128)(2,1)S(1)} custom-call(bf16[256,8192]{1,0:T(8,128)(2,1)} %grad.4), custom_call_target="tpu_custom_call" | custom-call | tf_op jit(solution)/shard_map/pallas_call | solution.py:105
  9.2 0.0 collective-permute-done.2.mom_other
  9.2 0.0 collective-permute-done.1.lat
  9.2 0.0 collective-permute-done.grad
  9.2 0.2 collective-permute-start.3
  9.4 0.6 shard_map.62
  10.0 0.1 collective-permute-start.9
  10.1 1.5 %collective-permute-start.11 = (bf16[3,256,256]{2,1,0:T(8,128)(2,1)S(1)}, bf16[3,256,256]{2,1,0:T(8,128)(2,1)S(1)}, u32[]{:S(2)}, u32[]{:S(2)}) collective-permute-start(bf16[3,256,256]{2,1,0:T(8,128)(2,1)S(1)} %get-tuple-element.74), channel_id=1, source_target_pairs={{0,6},{1,25},{2,4},{3,27},{4,2},{5,29},{6,0},{7,31},{8,14},{9,17},... | collective-permute-start | bytes 1179656 | tf_op jit(solution)/shard_map/ppermute | solution.py:43
  11.5 2.5 %shard_map.63 = (bf16[4,512,256]{2,1,0:T(8,128)(2,1)S(1)}, bf16[4,512,256]{2,1,0:T(8,128)(2,1)S(1)}, bf16[4,512,256]{2,1,0:T(8,128)(2,1)S(1)}) custom-call(bf16[512,256]{1,0:T(8,128)(2,1)S(1)} %get-tuple-element.55.lat, bf16[256,8192]{1,0:T(8,128)(2,1)} %grad.4), custom_call_target="tpu_custom_call" | custom-call | flops 805306368 | bytes 4718592 | tf_op jit(solution)/shard_map/pallas_call | solution.py:176
  14.1 0.4 shard_map.64
  14.5 0.4 shard_map.65
  14.9 0.5 collective-permute-start.4
  15.4 1.7 %collective-permute-start.5 = (bf16[3,256,256]{2,1,0:T(8,128)(2,1)S(1)}, bf16[3,256,256]{2,1,0:T(8,128)(2,1)S(1)}, u32[]{:S(2)}, u32[]{:S(2)}) collective-permute-start(bf16[3,256,256]{2,1,0:T(8,128)(2,1)S(1)} %shard_map.65), channel_id=1, source_target_pairs={{0,6},{1,25},{2,4},{3,27},{4,2},{5,29},{6,0},{7,31},{8,14},{9,17},... | collective-permute-start | bytes 1179656 | tf_op jit(solution)/shard_map/ppermute | solution.py:43
  17.0 1.4 %shard_map.66 = (f32[3,256,256]{2,1,0:T(8,128)S(1)}, f32[3,256,256]{2,1,0:T(8,128)S(1)}, bf16[1,512,256]{2,1,0:T(8,128)(2,1)S(1)}, bf16[1,512,256]{2,1,0:T(8,128...) custom-call(bf16[512,64]{1,0:T(8,128)(2,1)S(1)} %get-tuple-element.41.unit, ...), custom_call_target="tpu_custom_call" | custom-call | flops 754974720 | bytes 7864320 | tf_op jit(solution)/shard_map/pallas_call | solution.py:216
  18.5 0.1 add_convert_fusion.1
  18.5 1.1 %collective-permute-start.10 = (bf16[3,256,256]{2,1,0:T(8,128)(2,1)S(1)}, bf16[3,256,256]{2,1,0:T(8,128)(2,1)S(1)}, u32[]{:S(2)}, u32[]{:S(2)}) collective-permute-start(bf16[3,256,256]{2,1,0:T(8,128)(2,1)S(1)} %add_convert_fusion.1), channel_id=1, source_target_pairs={{0,6},{1,25},{2,4},{3,27},{4,2},{5,29},{6,0},{7,31},{8,14},{9,17},... | collective-permute-start | bytes 1179656 | tf_op jit(solution)/shard_map/ppermute | solution.py:43
  19.6 0.1 add_convert_fusion
  19.7 0.1 collective-permute-start.12
  19.8 0.3 shard_map.67
  20.1 1.7 %collective-permute-done.4.upper = bf16[3,256,256]{2,1,0:T(8,128)(2,1)S(1)} collective-permute-done((bf16[3,256,256]{2,1,0:T(8,128)(2,1)S(1)}, bf16[3,256,256]{2,1,0:T(8,128)(2,1)S(1)}, u32[]{:S(2)}, u32[]{:S(2)}) %collective-permute-start.4) | collective-permute-done | bytes 393248 | tf_op jit(solution)/shard_map/ppermute | solution.py:43
  21.9 1.6 %collective-permute-done.5.lower = bf16[3,256,256]{2,1,0:T(8,128)(2,1)S(1)} collective-permute-done((bf16[3,256,256]{2,1,0:T(8,128)(2,1)S(1)}, bf16[3,256,256]{2,1,0:T(8,128)(2,1)S(1)}, u32[]{:S(2)}, u32[]{:S(2)}) %collective-permute-start.5) | collective-permute-done | bytes 393248 | tf_op jit(solution)/shard_map/ppermute | solution.py:43
  23.5 0.1 shard_map.68.kept
  23.6 0.1 collective-permute-start.6
  23.7 2.8 %collective-permute-start.7 = (bf16[1,512,256]{2,1,0:T(8,128)(2,1)S(1)}, bf16[1,512,256]{2,1,0:T(8,128)(2,1)S(1)}, u32[]{:S(2)}, u32[]{:S(2)}) collective-permute-start(bf16[1,512,256]{2,1,0:T(8,128)(2,1)S(1)} %shard_map.67), channel_id=1, source_target_pairs={{0,4},{1,17},{2,6},{3,19},{4,0},{5,21},{6,2},{7,23},{8,12},{9,25},... | collective-permute-start | bytes 786440 | tf_op jit(solution)/shard_map/ppermute | solution.py:43
  26.6 1.0 %collective-permute-start.8 = (bf16[1,512,256]{2,1,0:T(8,128)(2,1)S(1)}, bf16[1,512,256]{2,1,0:T(8,128)(2,1)S(1)}, u32[]{:S(2)}, u32[]{:S(2)}) collective-permute-start(bf16[1,512,256]{2,1,0:T(8,128)(2,1)S(1)} %get-tuple-element.69), channel_id=1, source_target_pairs={{0,6},{1,25},{2,4},{3,27},{4,2},{5,29},{6,0},{7,31},{8,14},{9,17},... | collective-permute-start | bytes 786440 | tf_op jit(solution)/shard_map/ppermute | solution.py:43
  27.6 0.1 collective-permute-done.10.upper
  27.7 0.1 shard_map.70
  27.8 2.5 %collective-permute-start.13 = (bf16[512,256]{1,0:T(8,128)(2,1)S(1)}, bf16[512,256]{1,0:T(8,128)(2,1)S(1)}, u32[]{:S(2)}, u32[]{:S(2)}) collective-permute-start(bf16[512,256]{1,0:T(8,128)(2,1)S(1)} %get-tuple-element.75), channel_id=1, source_target_pairs={{0,16},{1,5},{2,18},{3,7},{4,20},{5,1},{6,22},{7,3},{8,24},{9,13},... | collective-permute-start | bytes 786440 | tf_op jit(solution)/shard_map/ppermute | solution.py:43
  30.4 0.6 collective-permute-start.14
  31.0 0.0 collective-permute-done.6.one
  31.0 1.0 %collective-permute-start.15 = (bf16[512,256]{1,0:T(8,128)(2,1)S(1)}, bf16[512,256]{1,0:T(8,128)(2,1)S(1)}, u32[]{:S(2)}, u32[]{:S(2)}) collective-permute-start(bf16[512,256]{1,0:T(8,128)(2,1)S(1)} %get-tuple-element.77), channel_id=1, source_target_pairs={{0,24},{1,7},{2,26},{3,5},{4,28},{5,3},{6,30},{7,1},{8,16},{9,15},... | collective-permute-start | bytes 786440 | tf_op jit(solution)/shard_map/ppermute | solution.py:43
  32.0 1.6 %collective-permute-done.7.two = bf16[1,512,256]{2,1,0:T(8,128)(2,1)S(1)} collective-permute-done((bf16[1,512,256]{2,1,0:T(8,128)(2,1)S(1)}, bf16[1,512,256]{2,1,0:T(8,128)(2,1)S(1)}, u32[]{:S(2)}, u32[]{:S(2)}) %collective-permute-start.7) | collective-permute-done | bytes 262176 | tf_op jit(solution)/shard_map/ppermute | solution.py:43
  33.6 5.5 %collective-permute-done.8.three = bf16[1,512,256]{2,1,0:T(8,128)(2,1)S(1)} collective-permute-done((bf16[1,512,256]{2,1,0:T(8,128)(2,1)S(1)}, bf16[1,512,256]{2,1,0:T(8,128)(2,1)S(1)}, u32[]{:S(2)}, u32[]{:S(2)}) %collective-permute-start.8) | collective-permute-done | bytes 262176 | tf_op jit(solution)/shard_map/ppermute | solution.py:43
  39.0 0.1 shard_map.69
  39.1 0.0 collective-permute-done.13
  39.1 0.9 collective-permute-done.14
  40.0 3.8 %collective-permute-done.15 = bf16[512,256]{1,0:T(8,128)(2,1)S(1)} collective-permute-done((bf16[512,256]{1,0:T(8,128)(2,1)S(1)}, bf16[512,256]{1,0:T(8,128)(2,1)S(1)}, u32[]{:S(2)}, u32[]{:S(2)}) %collective-permute-start.15) | collective-permute-done | bytes 262176 | tf_op jit(solution)/shard_map/ppermute | solution.py:43
  43.8 0.1 add_convert_fusion.2
  44.0 17.5 %all_to_all.15 = bf16[8,64,256]{2,1,0:T(8,128)(2,1)S(1)} all-to-all(bf16[8,64,256]{2,1,0:T(8,128)(2,1)S(1)} %bitcast.3), channel_id=1, replica_groups=mesh['z'=8,'y'=4,'x'=4,'c'=2] {'z'}, dimensions={0} | all-to-all | bytes 524288 | tf_op jit(solution)/shard_map/all_to_all | solution.py:421
  61.6 11.9 %all_to_all.16 = bf16[8,64,256]{2,1,0:T(8,128)(2,1)S(1)} all-to-all(bf16[8,64,256]{2,1,0:T(8,128)(2,1)S(1)} %broadcast_in_dim.3), channel_id=1, replica_groups=mesh['z'=8,'y'=4,'x'=4,'c'=2] {'z'}, dimensions={0} | all-to-all | bytes 524288 | tf_op jit(solution)/shard_map/all_to_all | solution.py:423
  73.5 5.7 %shard_map.71 = bf16[32,2,16,256]{3,2,1,0:T(8,128)(2,1)S(1)} custom-call(bf16[512,256]{1,0:T(8,128)(2,1)S(1)} %bitcast.2), custom_call_target="tpu_custom_call" | custom-call | tf_op jit(solution)/shard_map/pallas_call | solution.py:317
  79.3 19.6 %all_to_all.17.returned = bf16[32,2,16,256]{3,2,1,0:T(8,128)(2,1)S(1)} all-to-all(bf16[32,2,16,256]{3,2,1,0:T(8,128)(2,1)S(1)} %shard_map.71), channel_id=1, replica_groups=mesh['z'=8,'y'=4,'x'=4,'c'=2] {'c','y','x'}, dimensions={0} | all-to-all | bytes 1048576 | tf_op jit(solution)/shard_map/all_to_all | solution.py:427
  98.9 0.9 shard_map.72
  (10 shorter events, 0.1 us)
Async XLA Ops:
  0.6 5.6 %copy-start = (f32[16,8192]{1,0:T(8,128)S(1)}, f32[16,8192]{1,0:T(8,128)}, u32[]{:S(2)}) copy-start(f32[16,8192]{1,0:T(8,128)} %momentum.1) | copy-start | bytes 1572868
  0.6 5.6 %copy-start.1 = (bf16[256,512]{1,0:T(8,128)(2,1)S(1)}, bf16[256,512]{1,0:T(8,128)(2,1)}, u32[]{:S(2)}) copy-start(bf16[256,512]{1,0:T(8,128)(2,1)} %latent.1) | copy-start | bytes 786436
  2.2 7.0 %collective-permute-start = (bf16[256,1024]{1,0:T(8,128)(2,1)S(1)}, bf16[256,1024]{1,0:T(8,128)(2,1)S(1)}, u32[]{:S(2)}, u32[]{:S(2)}) collective-permute-start(bf16[256,1024]{1,0:T(8,128)(2,1)S(1)} %get-tuple-element.44), channel_id=1, source_target_pairs={{0,1},{1,0},{2,3},{3,2},{4,5},{5,4},{6,7},{7,6},{8,9},{9,8},{10,11... | collective-permute-start | bytes 1572872 | tf_op jit(solution)/shard_map/ppermute | solution.py:47
  6.9 2.3 %collective-permute-start.2 = (bf16[32,4096]{1,0:T(8,128)(2,1)S(1)}, bf16[32,4096]{1,0:T(8,128)(2,1)S(1)}, u32[]{:S(2)}, u32[]{:S(2)}) collective-permute-start(bf16[32,4096]{1,0:T(8,128)(2,1)S(1)} %get-tuple-element.46), channel_id=1, source_target_pairs={{0,1},{1,0},{2,3},{3,2},{4,5},{5,4},{6,7},{7,6},{8,9},{9,8},{10,11... | collective-permute-start | bytes 786440 | tf_op jit(solution)/shard_map/ppermute | solution.py:47
  7.0 2.2 %collective-permute-start.1 = (bf16[512,256]{1,0:T(8,128)(2,1)S(1)}, bf16[512,256]{1,0:T(8,128)(2,1)S(1)}, u32[]{:S(2)}, u32[]{:S(2)}) collective-permute-start(bf16[512,256]{1,0:T(8,128)(2,1)S(1)} %get-tuple-element.55.lat), channel_id=1, source_target_pairs={{0,1},{1,0},{2,3},{3,2},{4,5},{5,4},{6,7},{7,6},{8,9},{9,8},{10,11... | collective-permute-start | bytes 786440 | tf_op jit(solution)/shard_map/ppermute | solution.py:47
  9.2 4.9 %collective-permute-start.3 = (bf16[256,3072]{1,0:T(8,128)(2,1)S(1)}, bf16[256,3072]{1,0:T(8,128)(2,1)S(1)}, u32[]{:S(2)}, u32[]{:S(2)}) collective-permute-start(bf16[256,3072]{1,0:T(8,128)(2,1)S(1)} %shard_map.61), channel_id=1, source_target_pairs={{0,1},{1,0},{2,3},{3,2},{4,5},{5,4},{6,7},{7,6},{8,9},{9,8},{10,11... | collective-permute-start | bytes 4718600 | tf_op jit(solution)/shard_map/ppermute | solution.py:47
  10.0 8.5 %collective-permute-start.9 = (bf16[3,256,256]{2,1,0:T(8,128)(2,1)S(1)}, bf16[3,256,256]{2,1,0:T(8,128)(2,1)S(1)}, u32[]{:S(2)}, u32[]{:S(2)}) collective-permute-start(bf16[3,256,256]{2,1,0:T(8,128)(2,1)S(1)} %get-tuple-element.72), channel_id=1, source_target_pairs={{0,2},{1,9},{2,0},{3,11},{4,6},{5,13},{6,4},{7,15},{8,10},{9,1},{1... | collective-permute-start | bytes 1179656 | tf_op jit(solution)/shard_map/ppermute | solution.py:43
  10.1 9.5 %collective-permute-start.11 = (bf16[3,256,256]{2,1,0:T(8,128)(2,1)S(1)}, bf16[3,256,256]{2,1,0:T(8,128)(2,1)S(1)}, u32[]{:S(2)}, u32[]{:S(2)}) collective-permute-start(bf16[3,256,256]{2,1,0:T(8,128)(2,1)S(1)} %get-tuple-element.74), channel_id=1, source_target_pairs={{0,6},{1,25},{2,4},{3,27},{4,2},{5,29},{6,0},{7,31},{8,14},{9,17},... | collective-permute-start | bytes 1179656 | tf_op jit(solution)/shard_map/ppermute | solution.py:43
  14.9 7.0 %collective-permute-start.4 = (bf16[3,256,256]{2,1,0:T(8,128)(2,1)S(1)}, bf16[3,256,256]{2,1,0:T(8,128)(2,1)S(1)}, u32[]{:S(2)}, u32[]{:S(2)}) collective-permute-start(bf16[3,256,256]{2,1,0:T(8,128)(2,1)S(1)} %shard_map.64), channel_id=1, source_target_pairs={{0,2},{1,9},{2,0},{3,11},{4,6},{5,13},{6,4},{7,15},{8,10},{9,1},{1... | collective-permute-start | bytes 1179656 | tf_op jit(solution)/shard_map/ppermute | solution.py:43
  15.4 8.1 %collective-permute-start.5 = (bf16[3,256,256]{2,1,0:T(8,128)(2,1)S(1)}, bf16[3,256,256]{2,1,0:T(8,128)(2,1)S(1)}, u32[]{:S(2)}, u32[]{:S(2)}) collective-permute-start(bf16[3,256,256]{2,1,0:T(8,128)(2,1)S(1)} %shard_map.65), channel_id=1, source_target_pairs={{0,6},{1,25},{2,4},{3,27},{4,2},{5,29},{6,0},{7,31},{8,14},{9,17},... | collective-permute-start | bytes 1179656 | tf_op jit(solution)/shard_map/ppermute | solution.py:43
  18.5 9.2 %collective-permute-start.10 = (bf16[3,256,256]{2,1,0:T(8,128)(2,1)S(1)}, bf16[3,256,256]{2,1,0:T(8,128)(2,1)S(1)}, u32[]{:S(2)}, u32[]{:S(2)}) collective-permute-start(bf16[3,256,256]{2,1,0:T(8,128)(2,1)S(1)} %add_convert_fusion.1), channel_id=1, source_target_pairs={{0,6},{1,25},{2,4},{3,27},{4,2},{5,29},{6,0},{7,31},{8,14},{9,17},... | collective-permute-start | bytes 1179656 | tf_op jit(solution)/shard_map/ppermute | solution.py:43
  19.7 8.0 %collective-permute-start.12 = (bf16[3,256,256]{2,1,0:T(8,128)(2,1)S(1)}, bf16[3,256,256]{2,1,0:T(8,128)(2,1)S(1)}, u32[]{:S(2)}, u32[]{:S(2)}) collective-permute-start(bf16[3,256,256]{2,1,0:T(8,128)(2,1)S(1)} %add_convert_fusion), channel_id=1, source_target_pairs={{0,2},{1,9},{2,0},{3,11},{4,6},{5,13},{6,4},{7,15},{8,10},{9,1},{1... | collective-permute-start | bytes 1179656 | tf_op jit(solution)/shard_map/ppermute | solution.py:43
  23.6 7.3 %collective-permute-start.6 = (bf16[1,512,256]{2,1,0:T(8,128)(2,1)S(1)}, bf16[1,512,256]{2,1,0:T(8,128)(2,1)S(1)}, u32[]{:S(2)}, u32[]{:S(2)}) collective-permute-start(bf16[1,512,256]{2,1,0:T(8,128)(2,1)S(1)} %get-tuple-element.67), channel_id=1, source_target_pairs={{0,2},{1,9},{2,0},{3,11},{4,6},{5,13},{6,4},{7,15},{8,10},{9,1},{1... | collective-permute-start | bytes 786440 | tf_op jit(solution)/shard_map/ppermute | solution.py:43
  23.7 9.8 %collective-permute-start.7 = (bf16[1,512,256]{2,1,0:T(8,128)(2,1)S(1)}, bf16[1,512,256]{2,1,0:T(8,128)(2,1)S(1)}, u32[]{:S(2)}, u32[]{:S(2)}) collective-permute-start(bf16[1,512,256]{2,1,0:T(8,128)(2,1)S(1)} %shard_map.67), channel_id=1, source_target_pairs={{0,4},{1,17},{2,6},{3,19},{4,0},{5,21},{6,2},{7,23},{8,12},{9,25},... | collective-permute-start | bytes 786440 | tf_op jit(solution)/shard_map/ppermute | solution.py:43
  26.6 12.5 %collective-permute-start.8 = (bf16[1,512,256]{2,1,0:T(8,128)(2,1)S(1)}, bf16[1,512,256]{2,1,0:T(8,128)(2,1)S(1)}, u32[]{:S(2)}, u32[]{:S(2)}) collective-permute-start(bf16[1,512,256]{2,1,0:T(8,128)(2,1)S(1)} %get-tuple-element.69), channel_id=1, source_target_pairs={{0,6},{1,25},{2,4},{3,27},{4,2},{5,29},{6,0},{7,31},{8,14},{9,17},... | collective-permute-start | bytes 786440 | tf_op jit(solution)/shard_map/ppermute | solution.py:43
  27.8 11.3 %collective-permute-start.13 = (bf16[512,256]{1,0:T(8,128)(2,1)S(1)}, bf16[512,256]{1,0:T(8,128)(2,1)S(1)}, u32[]{:S(2)}, u32[]{:S(2)}) collective-permute-start(bf16[512,256]{1,0:T(8,128)(2,1)S(1)} %get-tuple-element.75), channel_id=1, source_target_pairs={{0,16},{1,5},{2,18},{3,7},{4,20},{5,1},{6,22},{7,3},{8,24},{9,13},... | collective-permute-start | bytes 786440 | tf_op jit(solution)/shard_map/ppermute | solution.py:43
  30.4 9.7 %collective-permute-start.14 = (bf16[512,256]{1,0:T(8,128)(2,1)S(1)}, bf16[512,256]{1,0:T(8,128)(2,1)S(1)}, u32[]{:S(2)}, u32[]{:S(2)}) collective-permute-start(bf16[512,256]{1,0:T(8,128)(2,1)S(1)} %get-tuple-element.76), channel_id=1, source_target_pairs={{0,8},{1,3},{2,10},{3,1},{4,12},{5,7},{6,14},{7,5},{8,0},{9,11},{1... | collective-permute-start | bytes 786440 | tf_op jit(solution)/shard_map/ppermute | solution.py:43
  31.0 12.9 %collective-permute-start.15 = (bf16[512,256]{1,0:T(8,128)(2,1)S(1)}, bf16[512,256]{1,0:T(8,128)(2,1)S(1)}, u32[]{:S(2)}, u32[]{:S(2)}) collective-permute-start(bf16[512,256]{1,0:T(8,128)(2,1)S(1)} %get-tuple-element.77), channel_id=1, source_target_pairs={{0,24},{1,7},{2,26},{3,5},{4,28},{5,3},{6,30},{7,1},{8,16},{9,15},... | collective-permute-start | bytes 786440 | tf_op jit(solution)/shard_map/ppermute | solution.py:43

commit v15 on v12

--- a/solution.py
+++ b/solution.py
@@ -296,17 +296,26 @@
     scale = 0.2 * math.sqrt(max(rows, columns))
     wide = moment.T
     gram = lax.dot_general(wide, wide, (((1,), (1,)), ((), ())), preferred_element_type=f32)
-    wide = wide.astype(f32)
-    inverse = 1.0 / (jnp.sqrt(jnp.sum(wide * wide)) + 1e-7)
+    squares = wide.astype(f32) * wide.astype(f32)
+    inverse = 1.0 / (jnp.sqrt(jnp.sum(squares)) + 1e-7)
     gram = (gram * inverse) * inverse
-    x = wide * inverse
+    at = [lax.broadcasted_iota(jnp.int32, gram.shape, axis) for axis in range(2)]
+    identity = jnp.where(at[0] == at[1], COEF_A, 0.0)
+    x = None
     for step in range(NS_STEPS):
-        pair = split(x)
         if step > 0:
+            pair = split(x)
             gram = product(pair, pair, ((1,), (1,)))
         gram_pair = split(gram)
-        poly = COEF_B * gram + COEF_C * product(gram_pair, gram_pair, ((1,), (0,)))
-        x = COEF_A * x + product(split(poly), pair, ((1,), (0,)))
+        poly = identity + COEF_B * gram + COEF_C * product(gram_pair, gram_pair, ((1,), (0,)))
+        if step > 0:
+            x = product(split(poly), pair, ((1,), (0,)))
+        else:
+            x = inverse * jnp.dot(
+                jnp.concatenate(split(poly), axis=1),
+                jnp.concatenate([wide, wide], axis=0),
+                preferred_element_type=f32,
+            )
     update = (scale * x).T.astype(bf16)
     owners = out_ref.shape[0]
     depth = rows // owners
@@ -389,16 +398,24 @@
         own, early, [(2, every, *upper, bf16), (2, every, *lower, bf16)], *shared, piece_early
     )
     lat_late, two_a, two_b = tie((lat_own, two_a, two_b))
-    own[1], own[3], own[0] = own_products(lat_late, latent_grad, late)
+    own[1], own[3] = own_products(lat_late, grad_late, late[:2])
     (one_a,) = block(own, late, [(1, rest, *upper, bf16)], *shared, piece_late)
     (three_b,) = block(own, late, [(3, rest, *lower, bf16)], *shared, piece_late)
-    own[0], one_a, three_b = tie((own[0], one_a, three_b))
-    one_b, three_a, one_stay, three_stay, kept_on, kept_stay = block(
+    own[1], own[3], one_a, three_b = tie((own[1], own[3], one_a, three_b))
+    one_b, three_a = block(
+        own, late, [(1, rest, *lower, f32), (3, rest, *upper, f32)], *shared, piece_late
+    )
+    two_a, two_b = exchange(two_a, 0, 1), exchange(two_b, 0, 3)
+    one_a, three_b = exchange(one_a, 0, 1), exchange(three_b, 0, 3)
+    three_a = (three_a + two_a[1:].astype(f32)).astype(bf16)
+    one_b = (one_b + two_b[1:].astype(f32)).astype(bf16)
+    lat_last, own[1], one_b = tie((lat_late, own[1], one_b))
+    three_a, one_b = exchange(three_a, 0, 3), exchange(one_b, 0, 1)
+    (own[0],) = own_products(lat_last, grad_late, late[2:])
+    one_stay, three_stay, kept_on, kept_stay = block(
         own,
         late,
         [
-            (1, rest, *lower, f32),
-            (3, rest, *upper, f32),
             (1, stay, *whole, f32),
             (3, stay, *whole, f32),
             (0, rest, *whole, f32),
@@ -407,10 +424,6 @@
         *shared,
         piece_late,
     )
-    two_a, two_b = exchange(two_a, 0, 1), exchange(two_b, 0, 3)
-    one_a, three_b = exchange(one_a, 0, 1), exchange(three_b, 0, 3)
-    three_a = exchange((three_a + two_a[1:].astype(f32)).astype(bf16), 0, 3)
-    one_b = exchange((one_b + two_b[1:].astype(f32)).astype(bf16), 0, 1)
     kept_on, one_stay, three_stay = middle(
         kept_on, one_a, three_b, one_stay, three_stay, two_a, two_b
     )

time: 96.5 us -> 97.1 us (level)
    pallas_call x4 -> x5, Pallas kernels: 2.88 us -> 3.05 us  [block(): pl.pallas_call(functools.partial(block_kernel, tiles), out_shape=[jax.Sha...]
    pallas_call x1 -> x2, Pallas kernels: 2.54 us -> 2.61 us  [own_products(): pl.pallas_call(functools.partial(own_kernel, nears), out_shape=[jax.Shape...]
where the time goes in v15:
time: 97.1 us; the launch traced here: 96.9 us
  blocking collectives  50 us (51%)
  Pallas kernels  16.5 us (17%)
  starting transfers between devices  15.1 us (16%)
  waiting for transfers between devices  13.2 us (14%)
  between operations  1.64 us (2%)
    all_to_all x1, blocking collectives, body(): returned = lax.all_to_all(outgoing, PLANE, 0, 0, tiled=True)  21.2 us
    all_to_all x1, blocking collectives, body(): pieces = lax.all_to_all(head.reshape(NZ, -1, HD), 'z', 0, 0, tiled=True)  16.9 us
    ppermute x11, waiting for transfers between devices, exchange(): return lax.ppermute(value, AXES, pairs)  13.2 us
    all_to_all x1, blocking collectives, body(): lax.all_to_all(jnp.broadcast_to(piece, (NZ,) + piece.shape), 'z', 0, 0, t...  11.9 us
    ppermute x11, starting transfers between devices, exchange(): return lax.ppermute(value, AXES, pairs)  11 us
    pallas_call x1, Pallas kernels, newton_schulz(): pl.pallas_call(newton_schulz_kernel, out_shape=jax.ShapeDtypeStruct((owne...  5.63 us
    ppermute x4, starting transfers between devices, swap_cores(): lax.ppermute(value, AXES, [(device_at(z, y, x, c), device_at(z, y, x, 1 -...  4.11 us
    pallas_call x2, Pallas kernels, column_pieces(): pl.pallas_call(functools.partial(pieces_kernel, lists), out_shape=[jax.Sh...  3.25 us
  transfers between devices with their start and end apart: 15, of which 8 were waited for; matrix products, arithmetic and copies ran while one was open for 0% of the time, Pallas kernels for 9%

profile of v15, /device:TPU:1, one launch (start us, length us, event | category | flops | bytes accessed | tf_op | source)
XLA Modules:
  0.0 96.9 jit_solution(13542799996034678353)
XLA Ops:
  0.6 1.5 %shard_map.59 = (bf16[256,1024]{1,0:T(8,128)(2,1)S(1)}, bf16[256,1024]{1,0:T(8,128)(2,1)S(1)}) custom-call(bf16[256,8192]{1,0:T(8,128)(2,1)} %grad.4), custom_call_target="tpu_custom_call" | custom-call | tf_op jit(solution)/shard_map/pallas_call | solution.py:105
  2.2 3.3 %collective-permute-start = (bf16[256,1024]{1,0:T(8,128)(2,1)S(1)}, bf16[256,1024]{1,0:T(8,128)(2,1)S(1)}, u32[]{:S(2)}, u32[]{:S(2)}) collective-permute-start(bf16[256,1024]{1,0:T(8,128)(2,1)S(1)} %get-tuple-element.45), channel_id=1, source_target_pairs={{0,1},{1,0},{2,3},{3,2},{4,5},{5,4},{6,7},{7,6},{8,9},{9,8},{10,11... | collective-permute-start | bytes 1572872 | tf_op jit(solution)/shard_map/ppermute | solution.py:47
  6.2 0.7 shard_map.60
  6.9 0.1 collective-permute-start.2
  7.0 0.5 collective-permute-start.1
  7.5 1.7 %shard_map.61 = bf16[256,3072]{1,0:T(8,128)(2,1)S(1)} custom-call(bf16[256,8192]{1,0:T(8,128)(2,1)} %grad.4), custom_call_target="tpu_custom_call" | custom-call | tf_op jit(solution)/shard_map/pallas_call | solution.py:105
  9.2 0.0 collective-permute-done.2.mom_other
  9.2 0.0 collective-permute-done.1.lat
  9.2 0.0 collective-permute-done.grad
  9.2 0.2 collective-permute-start.3
  9.4 0.7 shard_map.62
  10.1 1.1 %collective-permute-start.4 = (bf16[4,256,256]{2,1,0:T(8,128)(2,1)S(1)}, bf16[4,256,256]{2,1,0:T(8,128)(2,1)S(1)}, u32[]{:S(2)}, u32[]{:S(2)}) collective-permute-start(bf16[4,256,256]{2,1,0:T(8,128)(2,1)S(1)} %get-tuple-element.62), channel_id=1, source_target_pairs={{0,6},{1,25},{2,4},{3,27},{4,2},{5,29},{6,0},{7,31},{8,14},{9,17},... | collective-permute-start | bytes 1572872 | tf_op jit(solution)/shard_map/ppermute | solution.py:43
  11.2 2.1 %shard_map.63 = (bf16[4,512,256]{2,1,0:T(8,128)(2,1)S(1)}, bf16[4,512,256]{2,1,0:T(8,128)(2,1)S(1)}) custom-call(bf16[512,256]{1,0:T(8,128)(2,1)S(1)} %get-tuple-element.63.lat, bf16[256,8192]{1,0:T(8,128)(2,1)} %grad.4), custom_call_target="tpu_custom_call" | custom-call | flops 536870912 | bytes 3145728 | tf_op jit(solution)/shard_map/pallas_call | solution.py:176
  13.3 0.0 collective-permute-done.3.grad
  13.3 0.4 shard_map.64
  13.7 0.4 shard_map.65
  14.1 1.5 %collective-permute-start.5 = (bf16[3,256,256]{2,1,0:T(8,128)(2,1)S(1)}, bf16[3,256,256]{2,1,0:T(8,128)(2,1)S(1)}, u32[]{:S(2)}, u32[]{:S(2)}) collective-permute-start(bf16[3,256,256]{2,1,0:T(8,128)(2,1)S(1)} %shard_map.64), channel_id=1, source_target_pairs={{0,2},{1,9},{2,0},{3,11},{4,6},{5,13},{6,4},{7,15},{8,10},{9,1},{1... | collective-permute-start | bytes 1179656 | tf_op jit(solution)/shard_map/ppermute | solution.py:43
  15.6 1.7 %collective-permute-start.6 = (bf16[3,256,256]{2,1,0:T(8,128)(2,1)S(1)}, bf16[3,256,256]{2,1,0:T(8,128)(2,1)S(1)}, u32[]{:S(2)}, u32[]{:S(2)}) collective-permute-start(bf16[3,256,256]{2,1,0:T(8,128)(2,1)S(1)} %shard_map.65), channel_id=1, source_target_pairs={{0,6},{1,25},{2,4},{3,27},{4,2},{5,29},{6,0},{7,31},{8,14},{9,17},... | collective-permute-start | bytes 1179656 | tf_op jit(solution)/shard_map/ppermute | solution.py:43
  17.3 0.6 shard_map.66
  17.9 1.9 %collective-permute-done.4.two_b = bf16[4,256,256]{2,1,0:T(8,128)(2,1)S(1)} collective-permute-done((bf16[4,256,256]{2,1,0:T(8,128)(2,1)S(1)}, bf16[4,256,256]{2,1,0:T(8,128)(2,1)S(1)}, u32[]{:S(2)}, u32[]{:S(2)}) %collective-permute-start.4) | collective-permute-done | bytes 524320 | tf_op jit(solution)/shard_map/ppermute | solution.py:43
  19.8 0.1 add_convert_fusion.1
  19.8 0.0 collective-permute-done.7.two_a
  19.8 0.1 add_convert_fusion
  19.9 1.4 %collective-permute-start.10 = (bf16[3,256,256]{2,1,0:T(8,128)(2,1)S(1)}, bf16[3,256,256]{2,1,0:T(8,128)(2,1)S(1)}, u32[]{:S(2)}, u32[]{:S(2)}) collective-permute-start(bf16[3,256,256]{2,1,0:T(8,128)(2,1)S(1)} %add_convert_fusion), channel_id=1, source_target_pairs={{0,6},{1,25},{2,4},{3,27},{4,2},{5,29},{6,0},{7,31},{8,14},{9,17},... | collective-permute-start | bytes 1179656 | tf_op jit(solution)/shard_map/ppermute | solution.py:43
  21.4 0.6 shard_map.67.refs_0_
  22.0 1.0 %shard_map.68 = (f32[1,512,256]{2,1,0:T(8,128)S(1)}, f32[1,512,256]{2,1,0:T(8,128)S(1)}, f32[3,512,256]{2,1,0:T(8,128)S(1)}, f32[1,512,256]{2,1,0:T(8,128)S(1)}) custom-call(bf16[512,64]{1,0:T(8,128)(2,1)S(1)} %get-tuple-element.42.unit, bf16[512,256]{1,0:T(8,128)(2,1)S(1)} %collective-permute-done.1.lat, bf16[32,4096]{1,0:T(8,128)(2,1)S(1)} %get-tuple-element.49.mom_own, ...), custom_call_target="tpu_custom_call" | custom-call | flops 503316480 | bytes 5242880 | tf_op jit(solution)/shard_map/pallas_call | solution.py:216
  23.0 0.8 collective-permute-done.5.upper
  23.8 0.2 collective-permute-done.6.lower
  24.0 0.2 shard_map.69
  24.2 0.6 collective-permute-start.8
  24.7 1.3 %collective-permute-start.9 = (bf16[512,256]{1,0:T(8,128)(2,1)S(1)}, bf16[512,256]{1,0:T(8,128)(2,1)S(1)}, u32[]{:S(2)}, u32[]{:S(2)}) collective-permute-start(bf16[512,256]{1,0:T(8,128)(2,1)S(1)} %get-tuple-element.73), channel_id=1, source_target_pairs={{0,6},{1,25},{2,4},{3,27},{4,2},{5,29},{6,0},{7,31},{8,14},{9,17},... | collective-permute-start | bytes 786440 | tf_op jit(solution)/shard_map/ppermute | solution.py:43
  26.0 2.1 %collective-permute-done.10.upper = bf16[3,256,256]{2,1,0:T(8,128)(2,1)S(1)} collective-permute-done((bf16[3,256,256]{2,1,0:T(8,128)(2,1)S(1)}, bf16[3,256,256]{2,1,0:T(8,128)(2,1)S(1)}, u32[]{:S(2)}, u32[]{:S(2)}) %collective-permute-start.10) | collective-permute-done | bytes 393248 | tf_op jit(solution)/shard_map/ppermute | solution.py:43
  28.2 0.1 collective-permute-done.11.lower
  28.3 0.1 shard_map.71
  28.4 2.5 %collective-permute-start.12 = (bf16[512,256]{1,0:T(8,128)(2,1)S(1)}, bf16[512,256]{1,0:T(8,128)(2,1)S(1)}, u32[]{:S(2)}, u32[]{:S(2)}) collective-permute-start(bf16[512,256]{1,0:T(8,128)(2,1)S(1)} %get-tuple-element.77), channel_id=1, source_target_pairs={{0,16},{1,5},{2,18},{3,7},{4,20},{5,1},{6,22},{7,3},{8,24},{9,13},... | collective-permute-start | bytes 786440 | tf_op jit(solution)/shard_map/ppermute | solution.py:43
  30.9 0.3 collective-permute-start.13
  31.2 0.5 collective-permute-start.14
  31.8 0.0 collective-permute-done.9.three
  31.8 0.1 shard_map.70
  31.9 5.1 %collective-permute-done.12 = bf16[512,256]{1,0:T(8,128)(2,1)S(1)} collective-permute-done((bf16[512,256]{1,0:T(8,128)(2,1)S(1)}, bf16[512,256]{1,0:T(8,128)(2,1)S(1)}, u32[]{:S(2)}, u32[]{:S(2)}) %collective-permute-start.12) | collective-permute-done | bytes 262176 | tf_op jit(solution)/shard_map/ppermute | solution.py:43
  37.0 2.1 %collective-permute-done.13 = bf16[512,256]{1,0:T(8,128)(2,1)S(1)} collective-permute-done((bf16[512,256]{1,0:T(8,128)(2,1)S(1)}, bf16[512,256]{1,0:T(8,128)(2,1)S(1)}, u32[]{:S(2)}, u32[]{:S(2)}) %collective-permute-start.13) | collective-permute-done | bytes 262176 | tf_op jit(solution)/shard_map/ppermute | solution.py:43
  39.1 0.9 collective-permute-done.14
  39.9 0.1 add_convert_fusion.2
  40.0 16.9 %all_to_all.15 = bf16[8,64,256]{2,1,0:T(8,128)(2,1)S(1)} all-to-all(bf16[8,64,256]{2,1,0:T(8,128)(2,1)S(1)} %bitcast.3), channel_id=1, replica_groups=mesh['z'=8,'y'=4,'x'=4,'c'=2] {'z'}, dimensions={0} | all-to-all | bytes 524288 | tf_op jit(solution)/shard_map/all_to_all | solution.py:437
  57.0 11.9 %all_to_all.16 = bf16[8,64,256]{2,1,0:T(8,128)(2,1)S(1)} all-to-all(bf16[8,64,256]{2,1,0:T(8,128)(2,1)S(1)} %broadcast_in_dim.3), channel_id=1, replica_groups=mesh['z'=8,'y'=4,'x'=4,'c'=2] {'z'}, dimensions={0} | all-to-all | bytes 524288 | tf_op jit(solution)/shard_map/all_to_all | solution.py:439
  68.9 5.6 %shard_map.72 = bf16[32,2,16,256]{3,2,1,0:T(8,128)(2,1)S(1)} custom-call(bf16[512,256]{1,0:T(8,128)(2,1)S(1)} %bitcast.2), custom_call_target="tpu_custom_call" | custom-call | tf_op jit(solution)/shard_map/pallas_call | solution.py:331
  74.5 21.2 %all_to_all.17.returned = bf16[32,2,16,256]{3,2,1,0:T(8,128)(2,1)S(1)} all-to-all(bf16[32,2,16,256]{3,2,1,0:T(8,128)(2,1)S(1)} %shard_map.72), channel_id=1, replica_groups=mesh['z'=8,'y'=4,'x'=4,'c'=2] {'c','y','x'}, dimensions={0} | all-to-all | bytes 1048576 | tf_op jit(solution)/shard_map/all_to_all | solution.py:443
  95.8 0.9 shard_map.73
  (11 shorter events, 0.1 us)
Async XLA Ops:
  0.6 5.6 %copy-start.1 = (f32[16,8192]{1,0:T(8,128)S(1)}, f32[16,8192]{1,0:T(8,128)}, u32[]{:S(2)}) copy-start(f32[16,8192]{1,0:T(8,128)} %momentum.1) | copy-start | bytes 1572868
  0.6 5.6 %copy-start.2 = (bf16[256,512]{1,0:T(8,128)(2,1)S(1)}, bf16[256,512]{1,0:T(8,128)(2,1)}, u32[]{:S(2)}) copy-start(bf16[256,512]{1,0:T(8,128)(2,1)} %latent.1) | copy-start | bytes 786436
  2.2 7.0 %collective-permute-start = (bf16[256,1024]{1,0:T(8,128)(2,1)S(1)}, bf16[256,1024]{1,0:T(8,128)(2,1)S(1)}, u32[]{:S(2)}, u32[]{:S(2)}) collective-permute-start(bf16[256,1024]{1,0:T(8,128)(2,1)S(1)} %get-tuple-element.45), channel_id=1, source_target_pairs={{0,1},{1,0},{2,3},{3,2},{4,5},{5,4},{6,7},{7,6},{8,9},{9,8},{10,11... | collective-permute-start | bytes 1572872 | tf_op jit(solution)/shard_map/ppermute | solution.py:47
  6.9 2.3 %collective-permute-start.2 = (bf16[32,4096]{1,0:T(8,128)(2,1)S(1)}, bf16[32,4096]{1,0:T(8,128)(2,1)S(1)}, u32[]{:S(2)}, u32[]{:S(2)}) collective-permute-start(bf16[32,4096]{1,0:T(8,128)(2,1)S(1)} %get-tuple-element.47), channel_id=1, source_target_pairs={{0,1},{1,0},{2,3},{3,2},{4,5},{5,4},{6,7},{7,6},{8,9},{9,8},{10,11... | collective-permute-start | bytes 786440 | tf_op jit(solution)/shard_map/ppermute | solution.py:47
  7.0 2.2 %collective-permute-start.1 = (bf16[512,256]{1,0:T(8,128)(2,1)S(1)}, bf16[512,256]{1,0:T(8,128)(2,1)S(1)}, u32[]{:S(2)}, u32[]{:S(2)}) collective-permute-start(bf16[512,256]{1,0:T(8,128)(2,1)S(1)} %get-tuple-element.63.lat), channel_id=1, source_target_pairs={{0,1},{1,0},{2,3},{3,2},{4,5},{5,4},{6,7},{7,6},{8,9},{9,8},{10,11... | collective-permute-start | bytes 786440 | tf_op jit(solution)/shard_map/ppermute | solution.py:47
  9.2 4.1 %collective-permute-start.3 = (bf16[256,3072]{1,0:T(8,128)(2,1)S(1)}, bf16[256,3072]{1,0:T(8,128)(2,1)S(1)}, u32[]{:S(2)}, u32[]{:S(2)}) collective-permute-start(bf16[256,3072]{1,0:T(8,128)(2,1)S(1)} %shard_map.61), channel_id=1, source_target_pairs={{0,1},{1,0},{2,3},{3,2},{4,5},{5,4},{6,7},{7,6},{8,9},{9,8},{10,11... | collective-permute-start | bytes 4718600 | tf_op jit(solution)/shard_map/ppermute | solution.py:47
  10.1 9.6 %collective-permute-start.4 = (bf16[4,256,256]{2,1,0:T(8,128)(2,1)S(1)}, bf16[4,256,256]{2,1,0:T(8,128)(2,1)S(1)}, u32[]{:S(2)}, u32[]{:S(2)}) collective-permute-start(bf16[4,256,256]{2,1,0:T(8,128)(2,1)S(1)} %get-tuple-element.62), channel_id=1, source_target_pairs={{0,6},{1,25},{2,4},{3,27},{4,2},{5,29},{6,0},{7,31},{8,14},{9,17},... | collective-permute-start | bytes 1572872 | tf_op jit(solution)/shard_map/ppermute | solution.py:43
  11.2 8.6 %collective-permute-start.7 = (bf16[4,256,256]{2,1,0:T(8,128)(2,1)S(1)}, bf16[4,256,256]{2,1,0:T(8,128)(2,1)S(1)}, u32[]{:S(2)}, u32[]{:S(2)}) collective-permute-start(bf16[4,256,256]{2,1,0:T(8,128)(2,1)S(1)} %get-tuple-element.71), channel_id=1, source_target_pairs={{0,2},{1,9},{2,0},{3,11},{4,6},{5,13},{6,4},{7,15},{8,10},{9,1},{1... | collective-permute-start | bytes 1572872 | tf_op jit(solution)/shard_map/ppermute | solution.py:43
  14.1 9.7 %collective-permute-start.5 = (bf16[3,256,256]{2,1,0:T(8,128)(2,1)S(1)}, bf16[3,256,256]{2,1,0:T(8,128)(2,1)S(1)}, u32[]{:S(2)}, u32[]{:S(2)}) collective-permute-start(bf16[3,256,256]{2,1,0:T(8,128)(2,1)S(1)} %shard_map.64), channel_id=1, source_target_pairs={{0,2},{1,9},{2,0},{3,11},{4,6},{5,13},{6,4},{7,15},{8,10},{9,1},{1... | collective-permute-start | bytes 1179656 | tf_op jit(solution)/shard_map/ppermute | solution.py:43
  15.6 8.4 %collective-permute-start.6 = (bf16[3,256,256]{2,1,0:T(8,128)(2,1)S(1)}, bf16[3,256,256]{2,1,0:T(8,128)(2,1)S(1)}, u32[]{:S(2)}, u32[]{:S(2)}) collective-permute-start(bf16[3,256,256]{2,1,0:T(8,128)(2,1)S(1)} %shard_map.65), channel_id=1, source_target_pairs={{0,6},{1,25},{2,4},{3,27},{4,2},{5,29},{6,0},{7,31},{8,14},{9,17},... | collective-permute-start | bytes 1179656 | tf_op jit(solution)/shard_map/ppermute | solution.py:43
  17.3 4.1 %copy-start = (bf16[256,8192]{1,0:T(8,128)(2,1)S(1)}, bf16[256,8192]{1,0:T(8,128)(2,1)}, u32[]{:S(2)}) copy-start(bf16[256,8192]{1,0:T(8,128)(2,1)} %grad.4) | copy-start | bytes 12582916
  19.9 8.2 %collective-permute-start.10 = (bf16[3,256,256]{2,1,0:T(8,128)(2,1)S(1)}, bf16[3,256,256]{2,1,0:T(8,128)(2,1)S(1)}, u32[]{:S(2)}, u32[]{:S(2)}) collective-permute-start(bf16[3,256,256]{2,1,0:T(8,128)(2,1)S(1)} %add_convert_fusion), channel_id=1, source_target_pairs={{0,6},{1,25},{2,4},{3,27},{4,2},{5,29},{6,0},{7,31},{8,14},{9,17},... | collective-permute-start | bytes 1179656 | tf_op jit(solution)/shard_map/ppermute | solution.py:43
  21.4 6.9 %collective-permute-start.11 = (bf16[3,256,256]{2,1,0:T(8,128)(2,1)S(1)}, bf16[3,256,256]{2,1,0:T(8,128)(2,1)S(1)}, u32[]{:S(2)}, u32[]{:S(2)}) collective-permute-start(bf16[3,256,256]{2,1,0:T(8,128)(2,1)S(1)} %add_convert_fusion.1), channel_id=1, source_target_pairs={{0,2},{1,9},{2,0},{3,11},{4,6},{5,13},{6,4},{7,15},{8,10},{9,1},{1... | collective-permute-start | bytes 1179656 | tf_op jit(solution)/shard_map/ppermute | solution.py:43
  24.2 7.6 %collective-permute-start.8 = (bf16[512,256]{1,0:T(8,128)(2,1)S(1)}, bf16[512,256]{1,0:T(8,128)(2,1)S(1)}, u32[]{:S(2)}, u32[]{:S(2)}) collective-permute-start(bf16[512,256]{1,0:T(8,128)(2,1)S(1)} %get-tuple-element.72), channel_id=1, source_target_pairs={{0,2},{1,9},{2,0},{3,11},{4,6},{5,13},{6,4},{7,15},{8,10},{9,1},{1... | collective-permute-start | bytes 786440 | tf_op jit(solution)/shard_map/ppermute | solution.py:43
  24.7 7.1 %collective-permute-start.9 = (bf16[512,256]{1,0:T(8,128)(2,1)S(1)}, bf16[512,256]{1,0:T(8,128)(2,1)S(1)}, u32[]{:S(2)}, u32[]{:S(2)}) collective-permute-start(bf16[512,256]{1,0:T(8,128)(2,1)S(1)} %get-tuple-element.73), channel_id=1, source_target_pairs={{0,6},{1,25},{2,4},{3,27},{4,2},{5,29},{6,0},{7,31},{8,14},{9,17},... | collective-permute-start | bytes 786440 | tf_op jit(solution)/shard_map/ppermute | solution.py:43
  28.4 8.6 %collective-permute-start.12 = (bf16[512,256]{1,0:T(8,128)(2,1)S(1)}, bf16[512,256]{1,0:T(8,128)(2,1)S(1)}, u32[]{:S(2)}, u32[]{:S(2)}) collective-permute-start(bf16[512,256]{1,0:T(8,128)(2,1)S(1)} %get-tuple-element.77), channel_id=1, source_target_pairs={{0,16},{1,5},{2,18},{3,7},{4,20},{5,1},{6,22},{7,3},{8,24},{9,13},... | collective-permute-start | bytes 786440 | tf_op jit(solution)/shard_map/ppermute | solution.py:43
  30.9 8.1 %collective-permute-start.13 = (bf16[512,256]{1,0:T(8,128)(2,1)S(1)}, bf16[512,256]{1,0:T(8,128)(2,1)S(1)}, u32[]{:S(2)}, u32[]{:S(2)}) collective-permute-start(bf16[512,256]{1,0:T(8,128)(2,1)S(1)} %get-tuple-element.78), channel_id=1, source_target_pairs={{0,8},{1,3},{2,10},{3,1},{4,12},{5,7},{6,14},{7,5},{8,0},{9,11},{1... | collective-permute-start | bytes 786440 | tf_op jit(solution)/shard_map/ppermute | solution.py:43
  31.2 8.7 %collective-permute-start.14 = (bf16[512,256]{1,0:T(8,128)(2,1)S(1)}, bf16[512,256]{1,0:T(8,128)(2,1)S(1)}, u32[]{:S(2)}, u32[]{:S(2)}) collective-permute-start(bf16[512,256]{1,0:T(8,128)(2,1)S(1)} %get-tuple-element.79), channel_id=1, source_target_pairs={{0,24},{1,7},{2,26},{3,5},{4,28},{5,3},{6,30},{7,1},{8,16},{9,15},... | collective-permute-start | bytes 786440 | tf_op jit(solution)/shard_map/ppermute | solution.py:43

commit v16 on v15

--- a/solution.py
+++ b/solution.py
@@ -375,7 +375,7 @@
 
 def body(latent, latent_grad, row_counts, momentum):
     features = latent.shape[1]
-    order = (2, 1, 3)
+    order = (1, 3, 2)
     tie = lax.optimization_barrier
 
     early, late = (2,), (1, 3, 0)

time: 97.1 us -> 97 us (level)
  transfers between devices with their start and end apart: 15 -> 15, of which waited for: 8 -> 7; matrix products, arithmetic and copies ran while one was open for 0% -> 0% of each run, Pallas kernels for 9% -> 9%
where the time goes in v16:
time: 97 us; the launch traced here: 96.7 us
  blocking collectives  49.9 us (51%)
  Pallas kernels  16.5 us (17%)
  starting transfers between devices  15.2 us (16%)
  waiting for transfers between devices  13.2 us (14%)
  between operations  1.64 us (2%)
    all_to_all x1, blocking collectives, body(): returned = lax.all_to_all(outgoing, PLANE, 0, 0, tiled=True)  21.1 us
    all_to_all x1, blocking collectives, body(): pieces = lax.all_to_all(head.reshape(NZ, -1, HD), 'z', 0, 0, tiled=True)  17 us
    ppermute x11, waiting for transfers between devices, exchange(): return lax.ppermute(value, AXES, pairs)  13.2 us
    all_to_all x1, blocking collectives, body(): lax.all_to_all(jnp.broadcast_to(piece, (NZ,) + piece.shape), 'z', 0, 0, t...  11.7 us
    ppermute x11, starting transfers between devices, exchange(): return lax.ppermute(value, AXES, pairs)  11 us
    pallas_call x1, Pallas kernels, newton_schulz(): pl.pallas_call(newton_schulz_kernel, out_shape=jax.ShapeDtypeStruct((owne...  5.63 us
    ppermute x4, starting transfers between devices, swap_cores(): lax.ppermute(value, AXES, [(device_at(z, y, x, c), device_at(z, y, x, 1 -...  4.11 us
    pallas_call x2, Pallas kernels, column_pieces(): pl.pallas_call(functools.partial(pieces_kernel, lists), out_shape=[jax.Sh...  3.25 us
  transfers between devices with their start and end apart: 15, of which 7 were waited for; matrix products, arithmetic and copies ran while one was open for 0% of the time, Pallas kernels for 9%

profile of v16, /device:TPU:1, one launch (start us, length us, event | category | flops | bytes accessed | tf_op | source)
XLA Modules:
  0.0 96.7 jit_solution(12318984333387118796)
XLA Ops:
  0.6 1.5 %shard_map.59 = (bf16[256,1024]{1,0:T(8,128)(2,1)S(1)}, bf16[256,1024]{1,0:T(8,128)(2,1)S(1)}) custom-call(bf16[256,8192]{1,0:T(8,128)(2,1)} %grad.4), custom_call_target="tpu_custom_call" | custom-call | tf_op jit(solution)/shard_map/pallas_call | solution.py:105
  2.2 3.3 %collective-permute-start = (bf16[256,1024]{1,0:T(8,128)(2,1)S(1)}, bf16[256,1024]{1,0:T(8,128)(2,1)S(1)}, u32[]{:S(2)}, u32[]{:S(2)}) collective-permute-start(bf16[256,1024]{1,0:T(8,128)(2,1)S(1)} %get-tuple-element.45), channel_id=1, source_target_pairs={{0,1},{1,0},{2,3},{3,2},{4,5},{5,4},{6,7},{7,6},{8,9},{9,8},{10,11... | collective-permute-start | bytes 1572872 | tf_op jit(solution)/shard_map/ppermute | solution.py:47
  6.2 0.7 shard_map.60
  6.9 0.1 collective-permute-start.2
  7.0 0.5 collective-permute-start.1
  7.5 1.7 %shard_map.61 = bf16[256,3072]{1,0:T(8,128)(2,1)S(1)} custom-call(bf16[256,8192]{1,0:T(8,128)(2,1)} %grad.4), custom_call_target="tpu_custom_call" | custom-call | tf_op jit(solution)/shard_map/pallas_call | solution.py:105
  9.2 0.0 collective-permute-done.2.mom_other
  9.2 0.0 collective-permute-done.1.lat
  9.2 0.0 collective-permute-done.grad
  9.2 0.2 collective-permute-start.3
  9.4 0.7 shard_map.62
  10.1 1.1 %collective-permute-start.4 = (bf16[4,256,256]{2,1,0:T(8,128)(2,1)S(1)}, bf16[4,256,256]{2,1,0:T(8,128)(2,1)S(1)}, u32[]{:S(2)}, u32[]{:S(2)}) collective-permute-start(bf16[4,256,256]{2,1,0:T(8,128)(2,1)S(1)} %get-tuple-element.62), channel_id=1, source_target_pairs={{0,6},{1,25},{2,4},{3,27},{4,2},{5,29},{6,0},{7,31},{8,14},{9,17},... | collective-permute-start | bytes 1572872 | tf_op jit(solution)/shard_map/ppermute | solution.py:43
  11.2 2.1 %shard_map.63 = (bf16[4,512,256]{2,1,0:T(8,128)(2,1)S(1)}, bf16[4,512,256]{2,1,0:T(8,128)(2,1)S(1)}) custom-call(bf16[512,256]{1,0:T(8,128)(2,1)S(1)} %get-tuple-element.63.lat, bf16[256,8192]{1,0:T(8,128)(2,1)} %grad.4), custom_call_target="tpu_custom_call" | custom-call | flops 536870912 | bytes 3145728 | tf_op jit(solution)/shard_map/pallas_call | solution.py:176
  13.3 0.0 collective-permute-done.3.grad
  13.3 0.4 shard_map.64
  13.7 0.4 shard_map.65
  14.1 1.5 %collective-permute-start.5 = (bf16[3,256,256]{2,1,0:T(8,128)(2,1)S(1)}, bf16[3,256,256]{2,1,0:T(8,128)(2,1)S(1)}, u32[]{:S(2)}, u32[]{:S(2)}) collective-permute-start(bf16[3,256,256]{2,1,0:T(8,128)(2,1)S(1)} %shard_map.64), channel_id=1, source_target_pairs={{0,2},{1,9},{2,0},{3,11},{4,6},{5,13},{6,4},{7,15},{8,10},{9,1},{1... | collective-permute-start | bytes 1179656 | tf_op jit(solution)/shard_map/ppermute | solution.py:43
  15.6 1.7 %collective-permute-start.6 = (bf16[3,256,256]{2,1,0:T(8,128)(2,1)S(1)}, bf16[3,256,256]{2,1,0:T(8,128)(2,1)S(1)}, u32[]{:S(2)}, u32[]{:S(2)}) collective-permute-start(bf16[3,256,256]{2,1,0:T(8,128)(2,1)S(1)} %shard_map.65), channel_id=1, source_target_pairs={{0,6},{1,25},{2,4},{3,27},{4,2},{5,29},{6,0},{7,31},{8,14},{9,17},... | collective-permute-start | bytes 1179656 | tf_op jit(solution)/shard_map/ppermute | solution.py:43
  17.3 0.6 shard_map.66
  17.9 1.9 %collective-permute-done.4.two_b = bf16[4,256,256]{2,1,0:T(8,128)(2,1)S(1)} collective-permute-done((bf16[4,256,256]{2,1,0:T(8,128)(2,1)S(1)}, bf16[4,256,256]{2,1,0:T(8,128)(2,1)S(1)}, u32[]{:S(2)}, u32[]{:S(2)}) %collective-permute-start.4) | collective-permute-done | bytes 524320 | tf_op jit(solution)/shard_map/ppermute | solution.py:43
  19.8 0.1 add_convert_fusion.1
  19.8 0.0 collective-permute-done.7.two_a
  19.8 0.1 add_convert_fusion
  19.9 1.4 %collective-permute-start.10 = (bf16[3,256,256]{2,1,0:T(8,128)(2,1)S(1)}, bf16[3,256,256]{2,1,0:T(8,128)(2,1)S(1)}, u32[]{:S(2)}, u32[]{:S(2)}) collective-permute-start(bf16[3,256,256]{2,1,0:T(8,128)(2,1)S(1)} %add_convert_fusion), channel_id=1, source_target_pairs={{0,6},{1,25},{2,4},{3,27},{4,2},{5,29},{6,0},{7,31},{8,14},{9,17},... | collective-permute-start | bytes 1179656 | tf_op jit(solution)/shard_map/ppermute | solution.py:43
  21.4 0.6 shard_map.67.refs_0_
  22.0 1.0 %shard_map.68 = (f32[1,512,256]{2,1,0:T(8,128)S(1)}, f32[1,512,256]{2,1,0:T(8,128)S(1)}, f32[3,512,256]{2,1,0:T(8,128)S(1)}, f32[1,512,256]{2,1,0:T(8,128)S(1)}) custom-call(bf16[512,64]{1,0:T(8,128)(2,1)S(1)} %get-tuple-element.42.unit, bf16[512,256]{1,0:T(8,128)(2,1)S(1)} %collective-permute-done.1.lat, bf16[32,4096]{1,0:T(8,128)(2,1)S(1)} %get-tuple-element.49.mom_own, ...), custom_call_target="tpu_custom_call" | custom-call | flops 503316480 | bytes 5242880 | tf_op jit(solution)/shard_map/pallas_call | solution.py:216
  23.0 0.8 collective-permute-done.5.upper
  23.8 0.2 collective-permute-done.6.lower
  24.0 0.2 shard_map.69
  24.2 0.6 collective-permute-start.8
  24.7 1.3 %collective-permute-start.9 = (bf16[512,256]{1,0:T(8,128)(2,1)S(1)}, bf16[512,256]{1,0:T(8,128)(2,1)S(1)}, u32[]{:S(2)}, u32[]{:S(2)}) collective-permute-start(bf16[512,256]{1,0:T(8,128)(2,1)S(1)} %get-tuple-element.73), channel_id=1, source_target_pairs={{0,6},{1,25},{2,4},{3,27},{4,2},{5,29},{6,0},{7,31},{8,14},{9,17},... | collective-permute-start | bytes 786440 | tf_op jit(solution)/shard_map/ppermute | solution.py:43
  26.0 2.1 %collective-permute-done.10.upper = bf16[3,256,256]{2,1,0:T(8,128)(2,1)S(1)} collective-permute-done((bf16[3,256,256]{2,1,0:T(8,128)(2,1)S(1)}, bf16[3,256,256]{2,1,0:T(8,128)(2,1)S(1)}, u32[]{:S(2)}, u32[]{:S(2)}) %collective-permute-start.10) | collective-permute-done | bytes 393248 | tf_op jit(solution)/shard_map/ppermute | solution.py:43
  28.2 0.1 collective-permute-done.11.lower
  28.3 0.1 shard_map.71
  28.4 0.9 collective-permute-start.12
  29.4 1.8 %collective-permute-start.13 = (bf16[512,256]{1,0:T(8,128)(2,1)S(1)}, bf16[512,256]{1,0:T(8,128)(2,1)S(1)}, u32[]{:S(2)}, u32[]{:S(2)}) collective-permute-start(bf16[512,256]{1,0:T(8,128)(2,1)S(1)} %get-tuple-element.78), channel_id=1, source_target_pairs={{0,24},{1,7},{2,26},{3,5},{4,28},{5,3},{6,30},{7,1},{8,16},{9,15},... | collective-permute-start | bytes 786440 | tf_op jit(solution)/shard_map/ppermute | solution.py:43
  31.2 0.6 collective-permute-start.14
  31.8 0.0 collective-permute-done.8.one
  31.9 0.1 shard_map.70
  31.9 4.3 %collective-permute-done.12 = bf16[512,256]{1,0:T(8,128)(2,1)S(1)} collective-permute-done((bf16[512,256]{1,0:T(8,128)(2,1)S(1)}, bf16[512,256]{1,0:T(8,128)(2,1)S(1)}, u32[]{:S(2)}, u32[]{:S(2)}) %collective-permute-start.12) | collective-permute-done | bytes 262176 | tf_op jit(solution)/shard_map/ppermute | solution.py:43
  36.2 3.7 %collective-permute-done.13 = bf16[512,256]{1,0:T(8,128)(2,1)S(1)} collective-permute-done((bf16[512,256]{1,0:T(8,128)(2,1)S(1)}, bf16[512,256]{1,0:T(8,128)(2,1)S(1)}, u32[]{:S(2)}, u32[]{:S(2)}) %collective-permute-start.13) | collective-permute-done | bytes 262176 | tf_op jit(solution)/shard_map/ppermute | solution.py:43
  39.9 0.0 collective-permute-done.14
  39.9 0.1 add_convert_fusion.2
  40.0 17.0 %all_to_all.15 = bf16[8,64,256]{2,1,0:T(8,128)(2,1)S(1)} all-to-all(bf16[8,64,256]{2,1,0:T(8,128)(2,1)S(1)} %bitcast.3), channel_id=1, replica_groups=mesh['z'=8,'y'=4,'x'=4,'c'=2] {'z'}, dimensions={0} | all-to-all | bytes 524288 | tf_op jit(solution)/shard_map/all_to_all | solution.py:437
  57.1 11.7 %all_to_all.16 = bf16[8,64,256]{2,1,0:T(8,128)(2,1)S(1)} all-to-all(bf16[8,64,256]{2,1,0:T(8,128)(2,1)S(1)} %broadcast_in_dim.3), channel_id=1, replica_groups=mesh['z'=8,'y'=4,'x'=4,'c'=2] {'z'}, dimensions={0} | all-to-all | bytes 524288 | tf_op jit(solution)/shard_map/all_to_all | solution.py:439
  68.8 5.6 %shard_map.72 = bf16[32,2,16,256]{3,2,1,0:T(8,128)(2,1)S(1)} custom-call(bf16[512,256]{1,0:T(8,128)(2,1)S(1)} %bitcast.2), custom_call_target="tpu_custom_call" | custom-call | tf_op jit(solution)/shard_map/pallas_call | solution.py:331
  74.5 21.1 %all_to_all.17.returned = bf16[32,2,16,256]{3,2,1,0:T(8,128)(2,1)S(1)} all-to-all(bf16[32,2,16,256]{3,2,1,0:T(8,128)(2,1)S(1)} %shard_map.72), channel_id=1, replica_groups=mesh['z'=8,'y'=4,'x'=4,'c'=2] {'c','y','x'}, dimensions={0} | all-to-all | bytes 1048576 | tf_op jit(solution)/shard_map/all_to_all | solution.py:443
  95.6 0.9 shard_map.73
  (11 shorter events, 0.1 us)
Async XLA Ops:
  0.6 5.6 %copy-start.1 = (f32[16,8192]{1,0:T(8,128)S(1)}, f32[16,8192]{1,0:T(8,128)}, u32[]{:S(2)}) copy-start(f32[16,8192]{1,0:T(8,128)} %momentum.1) | copy-start | bytes 1572868
  0.6 5.6 %copy-start.2 = (bf16[256,512]{1,0:T(8,128)(2,1)S(1)}, bf16[256,512]{1,0:T(8,128)(2,1)}, u32[]{:S(2)}) copy-start(bf16[256,512]{1,0:T(8,128)(2,1)} %latent.1) | copy-start | bytes 786436
  2.2 7.0 %collective-permute-start = (bf16[256,1024]{1,0:T(8,128)(2,1)S(1)}, bf16[256,1024]{1,0:T(8,128)(2,1)S(1)}, u32[]{:S(2)}, u32[]{:S(2)}) collective-permute-start(bf16[256,1024]{1,0:T(8,128)(2,1)S(1)} %get-tuple-element.45), channel_id=1, source_target_pairs={{0,1},{1,0},{2,3},{3,2},{4,5},{5,4},{6,7},{7,6},{8,9},{9,8},{10,11... | collective-permute-start | bytes 1572872 | tf_op jit(solution)/shard_map/ppermute | solution.py:47
  6.9 2.3 %collective-permute-start.2 = (bf16[32,4096]{1,0:T(8,128)(2,1)S(1)}, bf16[32,4096]{1,0:T(8,128)(2,1)S(1)}, u32[]{:S(2)}, u32[]{:S(2)}) collective-permute-start(bf16[32,4096]{1,0:T(8,128)(2,1)S(1)} %get-tuple-element.47), channel_id=1, source_target_pairs={{0,1},{1,0},{2,3},{3,2},{4,5},{5,4},{6,7},{7,6},{8,9},{9,8},{10,11... | collective-permute-start | bytes 786440 | tf_op jit(solution)/shard_map/ppermute | solution.py:47
  7.0 2.2 %collective-permute-start.1 = (bf16[512,256]{1,0:T(8,128)(2,1)S(1)}, bf16[512,256]{1,0:T(8,128)(2,1)S(1)}, u32[]{:S(2)}, u32[]{:S(2)}) collective-permute-start(bf16[512,256]{1,0:T(8,128)(2,1)S(1)} %get-tuple-element.63.lat), channel_id=1, source_target_pairs={{0,1},{1,0},{2,3},{3,2},{4,5},{5,4},{6,7},{7,6},{8,9},{9,8},{10,11... | collective-permute-start | bytes 786440 | tf_op jit(solution)/shard_map/ppermute | solution.py:47
  9.2 4.1 %collective-permute-start.3 = (bf16[256,3072]{1,0:T(8,128)(2,1)S(1)}, bf16[256,3072]{1,0:T(8,128)(2,1)S(1)}, u32[]{:S(2)}, u32[]{:S(2)}) collective-permute-start(bf16[256,3072]{1,0:T(8,128)(2,1)S(1)} %shard_map.61), channel_id=1, source_target_pairs={{0,1},{1,0},{2,3},{3,2},{4,5},{5,4},{6,7},{7,6},{8,9},{9,8},{10,11... | collective-permute-start | bytes 4718600 | tf_op jit(solution)/shard_map/ppermute | solution.py:47
  10.1 9.6 %collective-permute-start.4 = (bf16[4,256,256]{2,1,0:T(8,128)(2,1)S(1)}, bf16[4,256,256]{2,1,0:T(8,128)(2,1)S(1)}, u32[]{:S(2)}, u32[]{:S(2)}) collective-permute-start(bf16[4,256,256]{2,1,0:T(8,128)(2,1)S(1)} %get-tuple-element.62), channel_id=1, source_target_pairs={{0,6},{1,25},{2,4},{3,27},{4,2},{5,29},{6,0},{7,31},{8,14},{9,17},... | collective-permute-start | bytes 1572872 | tf_op jit(solution)/shard_map/ppermute | solution.py:43
  11.2 8.6 %collective-permute-start.7 = (bf16[4,256,256]{2,1,0:T(8,128)(2,1)S(1)}, bf16[4,256,256]{2,1,0:T(8,128)(2,1)S(1)}, u32[]{:S(2)}, u32[]{:S(2)}) collective-permute-start(bf16[4,256,256]{2,1,0:T(8,128)(2,1)S(1)} %get-tuple-element.71), channel_id=1, source_target_pairs={{0,2},{1,9},{2,0},{3,11},{4,6},{5,13},{6,4},{7,15},{8,10},{9,1},{1... | collective-permute-start | bytes 1572872 | tf_op jit(solution)/shard_map/ppermute | solution.py:43
  14.1 9.7 %collective-permute-start.5 = (bf16[3,256,256]{2,1,0:T(8,128)(2,1)S(1)}, bf16[3,256,256]{2,1,0:T(8,128)(2,1)S(1)}, u32[]{:S(2)}, u32[]{:S(2)}) collective-permute-start(bf16[3,256,256]{2,1,0:T(8,128)(2,1)S(1)} %shard_map.64), channel_id=1, source_target_pairs={{0,2},{1,9},{2,0},{3,11},{4,6},{5,13},{6,4},{7,15},{8,10},{9,1},{1... | collective-permute-start | bytes 1179656 | tf_op jit(solution)/shard_map/ppermute | solution.py:43
  15.6 8.4 %collective-permute-start.6 = (bf16[3,256,256]{2,1,0:T(8,128)(2,1)S(1)}, bf16[3,256,256]{2,1,0:T(8,128)(2,1)S(1)}, u32[]{:S(2)}, u32[]{:S(2)}) collective-permute-start(bf16[3,256,256]{2,1,0:T(8,128)(2,1)S(1)} %shard_map.65), channel_id=1, source_target_pairs={{0,6},{1,25},{2,4},{3,27},{4,2},{5,29},{6,0},{7,31},{8,14},{9,17},... | collective-permute-start | bytes 1179656 | tf_op jit(solution)/shard_map/ppermute | solution.py:43
  17.3 4.1 %copy-start = (bf16[256,8192]{1,0:T(8,128)(2,1)S(1)}, bf16[256,8192]{1,0:T(8,128)(2,1)}, u32[]{:S(2)}) copy-start(bf16[256,8192]{1,0:T(8,128)(2,1)} %grad.4) | copy-start | bytes 12582916
  19.9 8.2 %collective-permute-start.10 = (bf16[3,256,256]{2,1,0:T(8,128)(2,1)S(1)}, bf16[3,256,256]{2,1,0:T(8,128)(2,1)S(1)}, u32[]{:S(2)}, u32[]{:S(2)}) collective-permute-start(bf16[3,256,256]{2,1,0:T(8,128)(2,1)S(1)} %add_convert_fusion), channel_id=1, source_target_pairs={{0,6},{1,25},{2,4},{3,27},{4,2},{5,29},{6,0},{7,31},{8,14},{9,17},... | collective-permute-start | bytes 1179656 | tf_op jit(solution)/shard_map/ppermute | solution.py:43
  21.4 6.9 %collective-permute-start.11 = (bf16[3,256,256]{2,1,0:T(8,128)(2,1)S(1)}, bf16[3,256,256]{2,1,0:T(8,128)(2,1)S(1)}, u32[]{:S(2)}, u32[]{:S(2)}) collective-permute-start(bf16[3,256,256]{2,1,0:T(8,128)(2,1)S(1)} %add_convert_fusion.1), channel_id=1, source_target_pairs={{0,2},{1,9},{2,0},{3,11},{4,6},{5,13},{6,4},{7,15},{8,10},{9,1},{1... | collective-permute-start | bytes 1179656 | tf_op jit(solution)/shard_map/ppermute | solution.py:43
  24.2 7.7 %collective-permute-start.8 = (bf16[512,256]{1,0:T(8,128)(2,1)S(1)}, bf16[512,256]{1,0:T(8,128)(2,1)S(1)}, u32[]{:S(2)}, u32[]{:S(2)}) collective-permute-start(bf16[512,256]{1,0:T(8,128)(2,1)S(1)} %get-tuple-element.72), channel_id=1, source_target_pairs={{0,2},{1,9},{2,0},{3,11},{4,6},{5,13},{6,4},{7,15},{8,10},{9,1},{1... | collective-permute-start | bytes 786440 | tf_op jit(solution)/shard_map/ppermute | solution.py:43
  24.7 7.1 %collective-permute-start.9 = (bf16[512,256]{1,0:T(8,128)(2,1)S(1)}, bf16[512,256]{1,0:T(8,128)(2,1)S(1)}, u32[]{:S(2)}, u32[]{:S(2)}) collective-permute-start(bf16[512,256]{1,0:T(8,128)(2,1)S(1)} %get-tuple-element.73), channel_id=1, source_target_pairs={{0,6},{1,25},{2,4},{3,27},{4,2},{5,29},{6,0},{7,31},{8,14},{9,17},... | collective-permute-start | bytes 786440 | tf_op jit(solution)/shard_map/ppermute | solution.py:43
  28.4 7.8 %collective-permute-start.12 = (bf16[512,256]{1,0:T(8,128)(2,1)S(1)}, bf16[512,256]{1,0:T(8,128)(2,1)S(1)}, u32[]{:S(2)}, u32[]{:S(2)}) collective-permute-start(bf16[512,256]{1,0:T(8,128)(2,1)S(1)} %get-tuple-element.77), channel_id=1, source_target_pairs={{0,8},{1,3},{2,10},{3,1},{4,12},{5,7},{6,14},{7,5},{8,0},{9,11},{1... | collective-permute-start | bytes 786440 | tf_op jit(solution)/shard_map/ppermute | solution.py:43
  29.4 10.5 %collective-permute-start.13 = (bf16[512,256]{1,0:T(8,128)(2,1)S(1)}, bf16[512,256]{1,0:T(8,128)(2,1)S(1)}, u32[]{:S(2)}, u32[]{:S(2)}) collective-permute-start(bf16[512,256]{1,0:T(8,128)(2,1)S(1)} %get-tuple-element.78), channel_id=1, source_target_pairs={{0,24},{1,7},{2,26},{3,5},{4,28},{5,3},{6,30},{7,1},{8,16},{9,15},... | collective-permute-start | bytes 786440 | tf_op jit(solution)/shard_map/ppermute | solution.py:43
  31.2 8.7 %collective-permute-start.14 = (bf16[512,256]{1,0:T(8,128)(2,1)S(1)}, bf16[512,256]{1,0:T(8,128)(2,1)S(1)}, u32[]{:S(2)}, u32[]{:S(2)}) collective-permute-start(bf16[512,256]{1,0:T(8,128)(2,1)S(1)} %get-tuple-element.79), channel_id=1, source_target_pairs={{0,16},{1,5},{2,18},{3,7},{4,20},{5,1},{6,22},{7,3},{8,24},{9,13},... | collective-permute-start | bytes 786440 | tf_op jit(solution)/shard_map/ppermute | solution.py:43

commit v17 on v12

--- a/solution.py
+++ b/solution.py
@@ -296,17 +296,26 @@
     scale = 0.2 * math.sqrt(max(rows, columns))
     wide = moment.T
     gram = lax.dot_general(wide, wide, (((1,), (1,)), ((), ())), preferred_element_type=f32)
-    wide = wide.astype(f32)
-    inverse = 1.0 / (jnp.sqrt(jnp.sum(wide * wide)) + 1e-7)
+    squares = wide.astype(f32) * wide.astype(f32)
+    inverse = 1.0 / (jnp.sqrt(jnp.sum(squares)) + 1e-7)
     gram = (gram * inverse) * inverse
-    x = wide * inverse
+    at = [lax.broadcasted_iota(jnp.int32, gram.shape, axis) for axis in range(2)]
+    identity = jnp.where(at[0] == at[1], COEF_A, 0.0)
+    x = None
     for step in range(NS_STEPS):
-        pair = split(x)
         if step > 0:
+            pair = split(x)
             gram = product(pair, pair, ((1,), (1,)))
         gram_pair = split(gram)
-        poly = COEF_B * gram + COEF_C * product(gram_pair, gram_pair, ((1,), (0,)))
-        x = COEF_A * x + product(split(poly), pair, ((1,), (0,)))
+        poly = identity + COEF_B * gram + COEF_C * product(gram_pair, gram_pair, ((1,), (0,)))
+        if step > 0:
+            x = product(split(poly), pair, ((1,), (0,)))
+        else:
+            x = inverse * jnp.dot(
+                jnp.concatenate(split(poly), axis=1),
+                jnp.concatenate([wide, wide], axis=0),
+                preferred_element_type=f32,
+            )
     update = (scale * x).T.astype(bf16)
     owners = out_ref.shape[0]
     depth = rows // owners

time: 96.5 us -> 96.3 us (level)
  no operation moved by 1% of the time
where the time goes in v17:
time: 96.3 us; the launch traced here: 96.1 us
  blocking collectives  49.5 us (51%)
  Pallas kernels  16.3 us (17%)
  starting transfers between devices  15.3 us (16%)
  waiting for transfers between devices  13 us (13%)
  between operations  1.64 us (2%)
    all_to_all x1, blocking collectives, body(): returned = lax.all_to_all(outgoing, PLANE, 0, 0, tiled=True)  20.4 us
    all_to_all x1, blocking collectives, body(): pieces = lax.all_to_all(head.reshape(NZ, -1, HD), 'z', 0, 0, tiled=True)  17.2 us
    ppermute x11, waiting for transfers between devices, exchange(): return lax.ppermute(value, AXES, pairs)  13 us
    all_to_all x1, blocking collectives, body(): lax.all_to_all(jnp.broadcast_to(piece, (NZ,) + piece.shape), 'z', 0, 0, t...  11.9 us
    ppermute x11, starting transfers between devices, exchange(): return lax.ppermute(value, AXES, pairs)  11.2 us
    pallas_call x1, Pallas kernels, newton_schulz(): pl.pallas_call(newton_schulz_kernel, out_shape=jax.ShapeDtypeStruct((owne...  5.63 us
    ppermute x4, starting transfers between devices, swap_cores(): lax.ppermute(value, AXES, [(device_at(z, y, x, c), device_at(z, y, x, 1 -...  4.11 us
    pallas_call x2, Pallas kernels, column_pieces(): pl.pallas_call(functools.partial(pieces_kernel, lists), out_shape=[jax.Sh...  3.25 us
  transfers between devices with their start and end apart: 15, of which 8 were waited for; matrix products, arithmetic and copies ran while one was open for 0% of the time, Pallas kernels for 9%

profile of v17, /device:TPU:1, one launch (start us, length us, event | category | flops | bytes accessed | tf_op | source)
XLA Modules:
  0.0 96.1 jit_solution(1694342426539962381)
XLA Ops:
  0.6 1.5 %shard_map.59 = (bf16[256,1024]{1,0:T(8,128)(2,1)S(1)}, bf16[256,1024]{1,0:T(8,128)(2,1)S(1)}) custom-call(bf16[256,8192]{1,0:T(8,128)(2,1)} %grad.4), custom_call_target="tpu_custom_call" | custom-call | tf_op jit(solution)/shard_map/pallas_call | solution.py:105
  2.2 3.3 %collective-permute-start = (bf16[256,1024]{1,0:T(8,128)(2,1)S(1)}, bf16[256,1024]{1,0:T(8,128)(2,1)S(1)}, u32[]{:S(2)}, u32[]{:S(2)}) collective-permute-start(bf16[256,1024]{1,0:T(8,128)(2,1)S(1)} %get-tuple-element.42), channel_id=1, source_target_pairs={{0,1},{1,0},{2,3},{3,2},{4,5},{5,4},{6,7},{7,6},{8,9},{9,8},{10,11... | collective-permute-start | bytes 1572872 | tf_op jit(solution)/shard_map/ppermute | solution.py:47
  6.2 0.7 shard_map.60
  6.9 0.1 collective-permute-start.2
  7.0 0.5 collective-permute-start.1
  7.5 1.7 %shard_map.61 = bf16[256,3072]{1,0:T(8,128)(2,1)S(1)} custom-call(bf16[256,8192]{1,0:T(8,128)(2,1)} %grad.4), custom_call_target="tpu_custom_call" | custom-call | tf_op jit(solution)/shard_map/pallas_call | solution.py:105
  9.2 0.0 collective-permute-done.2.mom_other
  9.2 0.0 collective-permute-done.1.lat
  9.2 0.0 collective-permute-done.grad
  9.2 0.2 collective-permute-start.3
  9.4 0.7 shard_map.62
  10.1 1.1 %collective-permute-start.7 = (bf16[4,256,256]{2,1,0:T(8,128)(2,1)S(1)}, bf16[4,256,256]{2,1,0:T(8,128)(2,1)S(1)}, u32[]{:S(2)}, u32[]{:S(2)}) collective-permute-start(bf16[4,256,256]{2,1,0:T(8,128)(2,1)S(1)} %get-tuple-element.65), channel_id=1, source_target_pairs={{0,6},{1,25},{2,4},{3,27},{4,2},{5,29},{6,0},{7,31},{8,14},{9,17},... | collective-permute-start | bytes 1572872 | tf_op jit(solution)/shard_map/ppermute | solution.py:43
  11.2 0.0 collective-permute-start.6
  11.2 2.5 %shard_map.63 = (bf16[4,512,256]{2,1,0:T(8,128)(2,1)S(1)}, bf16[4,512,256]{2,1,0:T(8,128)(2,1)S(1)}, bf16[4,512,256]{2,1,0:T(8,128)(2,1)S(1)}) custom-call(bf16[512,256]{1,0:T(8,128)(2,1)S(1)} %get-tuple-element.53.lat, bf16[256,8192]{1,0:T(8,128)(2,1)} %grad.4), custom_call_target="tpu_custom_call" | custom-call | flops 805306368 | bytes 4718592 | tf_op jit(solution)/shard_map/pallas_call | solution.py:176
  13.8 0.0 collective-permute-done.3.grad
  13.8 0.4 shard_map.64
  14.2 0.4 shard_map.65
  14.5 1.6 %collective-permute-start.4 = (bf16[3,256,256]{2,1,0:T(8,128)(2,1)S(1)}, bf16[3,256,256]{2,1,0:T(8,128)(2,1)S(1)}, u32[]{:S(2)}, u32[]{:S(2)}) collective-permute-start(bf16[3,256,256]{2,1,0:T(8,128)(2,1)S(1)} %shard_map.64), channel_id=1, source_target_pairs={{0,2},{1,9},{2,0},{3,11},{4,6},{5,13},{6,4},{7,15},{8,10},{9,1},{1... | collective-permute-start | bytes 1179656 | tf_op jit(solution)/shard_map/ppermute | solution.py:43
  16.1 1.7 %collective-permute-start.5 = (bf16[3,256,256]{2,1,0:T(8,128)(2,1)S(1)}, bf16[3,256,256]{2,1,0:T(8,128)(2,1)S(1)}, u32[]{:S(2)}, u32[]{:S(2)}) collective-permute-start(bf16[3,256,256]{2,1,0:T(8,128)(2,1)S(1)} %shard_map.65), channel_id=1, source_target_pairs={{0,6},{1,25},{2,4},{3,27},{4,2},{5,29},{6,0},{7,31},{8,14},{9,17},... | collective-permute-start | bytes 1179656 | tf_op jit(solution)/shard_map/ppermute | solution.py:43
  17.8 1.4 %shard_map.66 = (f32[3,256,256]{2,1,0:T(8,128)S(1)}, f32[3,256,256]{2,1,0:T(8,128)S(1)}, f32[1,512,256]{2,1,0:T(8,128)S(1)}, f32[1,512,256]{2,1,0:T(8,128)S(1)},...) custom-call(bf16[512,64]{1,0:T(8,128)(2,1)S(1)} %get-tuple-element.39.unit, ...), custom_call_target="tpu_custom_call" | custom-call | flops 754974720 | bytes 7864320 | tf_op jit(solution)/shard_map/pallas_call | solution.py:216
  19.2 0.6 collective-permute-done.7.two_b
  19.8 0.1 add_convert_fusion
  19.8 0.1 collective-permute-start.11
  19.9 0.1 add_convert_fusion.1
  20.0 1.3 %collective-permute-start.10 = (bf16[3,256,256]{2,1,0:T(8,128)(2,1)S(1)}, bf16[3,256,256]{2,1,0:T(8,128)(2,1)S(1)}, u32[]{:S(2)}, u32[]{:S(2)}) collective-permute-start(bf16[3,256,256]{2,1,0:T(8,128)(2,1)S(1)} %add_convert_fusion.1), channel_id=1, source_target_pairs={{0,6},{1,25},{2,4},{3,27},{4,2},{5,29},{6,0},{7,31},{8,14},{9,17},... | collective-permute-start | bytes 1179656 | tf_op jit(solution)/shard_map/ppermute | solution.py:43
  21.4 2.4 %collective-permute-done.4.upper = bf16[3,256,256]{2,1,0:T(8,128)(2,1)S(1)} collective-permute-done((bf16[3,256,256]{2,1,0:T(8,128)(2,1)S(1)}, bf16[3,256,256]{2,1,0:T(8,128)(2,1)S(1)}, u32[]{:S(2)}, u32[]{:S(2)}) %collective-permute-start.4) | collective-permute-done | bytes 393248 | tf_op jit(solution)/shard_map/ppermute | solution.py:43
  23.8 0.5 collective-permute-done.5.lower
  24.2 0.2 shard_map.67
  24.4 0.1 collective-permute-start.8
  24.5 1.9 %collective-permute-start.9 = (bf16[512,256]{1,0:T(8,128)(2,1)S(1)}, bf16[512,256]{1,0:T(8,128)(2,1)S(1)}, u32[]{:S(2)}, u32[]{:S(2)}) collective-permute-start(bf16[512,256]{1,0:T(8,128)(2,1)S(1)} %get-tuple-element.67), channel_id=1, source_target_pairs={{0,6},{1,25},{2,4},{3,27},{4,2},{5,29},{6,0},{7,31},{8,14},{9,17},... | collective-permute-start | bytes 786440 | tf_op jit(solution)/shard_map/ppermute | solution.py:43
  26.5 1.5 %collective-permute-done.11.lower = bf16[3,256,256]{2,1,0:T(8,128)(2,1)S(1)} collective-permute-done((bf16[3,256,256]{2,1,0:T(8,128)(2,1)S(1)}, bf16[3,256,256]{2,1,0:T(8,128)(2,1)S(1)}, u32[]{:S(2)}, u32[]{:S(2)}) %collective-permute-start.11) | collective-permute-done | bytes 393248 | tf_op jit(solution)/shard_map/ppermute | solution.py:43
  28.0 0.5 collective-permute-done.10.upper
  28.4 0.1 shard_map.69
  28.6 2.5 %collective-permute-start.12 = (bf16[512,256]{1,0:T(8,128)(2,1)S(1)}, bf16[512,256]{1,0:T(8,128)(2,1)S(1)}, u32[]{:S(2)}, u32[]{:S(2)}) collective-permute-start(bf16[512,256]{1,0:T(8,128)(2,1)S(1)} %get-tuple-element.71), channel_id=1, source_target_pairs={{0,16},{1,5},{2,18},{3,7},{4,20},{5,1},{6,22},{7,3},{8,24},{9,13},... | collective-permute-start | bytes 786440 | tf_op jit(solution)/shard_map/ppermute | solution.py:43
  31.1 0.6 collective-permute-start.13
  31.7 0.3 collective-permute-start.14
  32.0 0.0 collective-permute-done.8.one
  32.0 0.0 collective-permute-done.9.three
  32.0 0.1 shard_map.68
  32.0 4.8 %collective-permute-done.12 = bf16[512,256]{1,0:T(8,128)(2,1)S(1)} collective-permute-done((bf16[512,256]{1,0:T(8,128)(2,1)S(1)}, bf16[512,256]{1,0:T(8,128)(2,1)S(1)}, u32[]{:S(2)}, u32[]{:S(2)}) %collective-permute-start.12) | collective-permute-done | bytes 262176 | tf_op jit(solution)/shard_map/ppermute | solution.py:43
  36.8 1.8 %collective-permute-done.13 = bf16[512,256]{1,0:T(8,128)(2,1)S(1)} collective-permute-done((bf16[512,256]{1,0:T(8,128)(2,1)S(1)}, bf16[512,256]{1,0:T(8,128)(2,1)S(1)}, u32[]{:S(2)}, u32[]{:S(2)}) %collective-permute-start.13) | collective-permute-done | bytes 262176 | tf_op jit(solution)/shard_map/ppermute | solution.py:43
  38.6 1.0 %collective-permute-done.14 = bf16[512,256]{1,0:T(8,128)(2,1)S(1)} collective-permute-done((bf16[512,256]{1,0:T(8,128)(2,1)S(1)}, bf16[512,256]{1,0:T(8,128)(2,1)S(1)}, u32[]{:S(2)}, u32[]{:S(2)}) %collective-permute-start.14) | collective-permute-done | bytes 262176 | tf_op jit(solution)/shard_map/ppermute | solution.py:43
  39.6 0.1 add_convert_fusion.2
  39.7 17.2 %all_to_all.15 = bf16[8,64,256]{2,1,0:T(8,128)(2,1)S(1)} all-to-all(bf16[8,64,256]{2,1,0:T(8,128)(2,1)S(1)} %bitcast.3), channel_id=1, replica_groups=mesh['z'=8,'y'=4,'x'=4,'c'=2] {'z'}, dimensions={0} | all-to-all | bytes 524288 | tf_op jit(solution)/shard_map/all_to_all | solution.py:433
  57.0 11.9 %all_to_all.16 = bf16[8,64,256]{2,1,0:T(8,128)(2,1)S(1)} all-to-all(bf16[8,64,256]{2,1,0:T(8,128)(2,1)S(1)} %broadcast_in_dim.3), channel_id=1, replica_groups=mesh['z'=8,'y'=4,'x'=4,'c'=2] {'z'}, dimensions={0} | all-to-all | bytes 524288 | tf_op jit(solution)/shard_map/all_to_all | solution.py:435
  68.9 5.6 %shard_map.70 = bf16[32,2,16,256]{3,2,1,0:T(8,128)(2,1)S(1)} custom-call(bf16[512,256]{1,0:T(8,128)(2,1)S(1)} %bitcast.2), custom_call_target="tpu_custom_call" | custom-call | tf_op jit(solution)/shard_map/pallas_call | solution.py:331
  74.5 20.4 %all_to_all.17.returned = bf16[32,2,16,256]{3,2,1,0:T(8,128)(2,1)S(1)} all-to-all(bf16[32,2,16,256]{3,2,1,0:T(8,128)(2,1)S(1)} %shard_map.70), channel_id=1, replica_groups=mesh['z'=8,'y'=4,'x'=4,'c'=2] {'c','y','x'}, dimensions={0} | all-to-all | bytes 1048576 | tf_op jit(solution)/shard_map/all_to_all | solution.py:439
  95.0 0.9 shard_map.71
  (7 shorter events, 0.1 us)
Async XLA Ops:
  0.6 5.6 %copy-start = (f32[16,8192]{1,0:T(8,128)S(1)}, f32[16,8192]{1,0:T(8,128)}, u32[]{:S(2)}) copy-start(f32[16,8192]{1,0:T(8,128)} %momentum.1) | copy-start | bytes 1572868
  0.6 5.6 %copy-start.1 = (bf16[256,512]{1,0:T(8,128)(2,1)S(1)}, bf16[256,512]{1,0:T(8,128)(2,1)}, u32[]{:S(2)}) copy-start(bf16[256,512]{1,0:T(8,128)(2,1)} %latent.1) | copy-start | bytes 786436
  2.2 7.0 %collective-permute-start = (bf16[256,1024]{1,0:T(8,128)(2,1)S(1)}, bf16[256,1024]{1,0:T(8,128)(2,1)S(1)}, u32[]{:S(2)}, u32[]{:S(2)}) collective-permute-start(bf16[256,1024]{1,0:T(8,128)(2,1)S(1)} %get-tuple-element.42), channel_id=1, source_target_pairs={{0,1},{1,0},{2,3},{3,2},{4,5},{5,4},{6,7},{7,6},{8,9},{9,8},{10,11... | collective-permute-start | bytes 1572872 | tf_op jit(solution)/shard_map/ppermute | solution.py:47
  6.9 2.3 %collective-permute-start.2 = (bf16[32,4096]{1,0:T(8,128)(2,1)S(1)}, bf16[32,4096]{1,0:T(8,128)(2,1)S(1)}, u32[]{:S(2)}, u32[]{:S(2)}) collective-permute-start(bf16[32,4096]{1,0:T(8,128)(2,1)S(1)} %get-tuple-element.44), channel_id=1, source_target_pairs={{0,1},{1,0},{2,3},{3,2},{4,5},{5,4},{6,7},{7,6},{8,9},{9,8},{10,11... | collective-permute-start | bytes 786440 | tf_op jit(solution)/shard_map/ppermute | solution.py:47
  7.0 2.2 %collective-permute-start.1 = (bf16[512,256]{1,0:T(8,128)(2,1)S(1)}, bf16[512,256]{1,0:T(8,128)(2,1)S(1)}, u32[]{:S(2)}, u32[]{:S(2)}) collective-permute-start(bf16[512,256]{1,0:T(8,128)(2,1)S(1)} %get-tuple-element.53.lat), channel_id=1, source_target_pairs={{0,1},{1,0},{2,3},{3,2},{4,5},{5,4},{6,7},{7,6},{8,9},{9,8},{10,11... | collective-permute-start | bytes 786440 | tf_op jit(solution)/shard_map/ppermute | solution.py:47
  9.2 4.6 %collective-permute-start.3 = (bf16[256,3072]{1,0:T(8,128)(2,1)S(1)}, bf16[256,3072]{1,0:T(8,128)(2,1)S(1)}, u32[]{:S(2)}, u32[]{:S(2)}) collective-permute-start(bf16[256,3072]{1,0:T(8,128)(2,1)S(1)} %shard_map.61), channel_id=1, source_target_pairs={{0,1},{1,0},{2,3},{3,2},{4,5},{5,4},{6,7},{7,6},{8,9},{9,8},{10,11... | collective-permute-start | bytes 4718600 | tf_op jit(solution)/shard_map/ppermute | solution.py:47
  10.1 9.6 %collective-permute-start.7 = (bf16[4,256,256]{2,1,0:T(8,128)(2,1)S(1)}, bf16[4,256,256]{2,1,0:T(8,128)(2,1)S(1)}, u32[]{:S(2)}, u32[]{:S(2)}) collective-permute-start(bf16[4,256,256]{2,1,0:T(8,128)(2,1)S(1)} %get-tuple-element.65), channel_id=1, source_target_pairs={{0,6},{1,25},{2,4},{3,27},{4,2},{5,29},{6,0},{7,31},{8,14},{9,17},... | collective-permute-start | bytes 1572872 | tf_op jit(solution)/shard_map/ppermute | solution.py:43
  11.2 8.7 %collective-permute-start.6 = (bf16[4,256,256]{2,1,0:T(8,128)(2,1)S(1)}, bf16[4,256,256]{2,1,0:T(8,128)(2,1)S(1)}, u32[]{:S(2)}, u32[]{:S(2)}) collective-permute-start(bf16[4,256,256]{2,1,0:T(8,128)(2,1)S(1)} %get-tuple-element.64), channel_id=1, source_target_pairs={{0,2},{1,9},{2,0},{3,11},{4,6},{5,13},{6,4},{7,15},{8,10},{9,1},{1... | collective-permute-start | bytes 1572872 | tf_op jit(solution)/shard_map/ppermute | solution.py:43
  14.5 9.2 %collective-permute-start.4 = (bf16[3,256,256]{2,1,0:T(8,128)(2,1)S(1)}, bf16[3,256,256]{2,1,0:T(8,128)(2,1)S(1)}, u32[]{:S(2)}, u32[]{:S(2)}) collective-permute-start(bf16[3,256,256]{2,1,0:T(8,128)(2,1)S(1)} %shard_map.64), channel_id=1, source_target_pairs={{0,2},{1,9},{2,0},{3,11},{4,6},{5,13},{6,4},{7,15},{8,10},{9,1},{1... | collective-permute-start | bytes 1179656 | tf_op jit(solution)/shard_map/ppermute | solution.py:43
  16.1 8.1 %collective-permute-start.5 = (bf16[3,256,256]{2,1,0:T(8,128)(2,1)S(1)}, bf16[3,256,256]{2,1,0:T(8,128)(2,1)S(1)}, u32[]{:S(2)}, u32[]{:S(2)}) collective-permute-start(bf16[3,256,256]{2,1,0:T(8,128)(2,1)S(1)} %shard_map.65), channel_id=1, source_target_pairs={{0,6},{1,25},{2,4},{3,27},{4,2},{5,29},{6,0},{7,31},{8,14},{9,17},... | collective-permute-start | bytes 1179656 | tf_op jit(solution)/shard_map/ppermute | solution.py:43
  19.8 8.1 %collective-permute-start.11 = (bf16[3,256,256]{2,1,0:T(8,128)(2,1)S(1)}, bf16[3,256,256]{2,1,0:T(8,128)(2,1)S(1)}, u32[]{:S(2)}, u32[]{:S(2)}) collective-permute-start(bf16[3,256,256]{2,1,0:T(8,128)(2,1)S(1)} %add_convert_fusion), channel_id=1, source_target_pairs={{0,2},{1,9},{2,0},{3,11},{4,6},{5,13},{6,4},{7,15},{8,10},{9,1},{1... | collective-permute-start | bytes 1179656 | tf_op jit(solution)/shard_map/ppermute | solution.py:43
  20.0 8.4 %collective-permute-start.10 = (bf16[3,256,256]{2,1,0:T(8,128)(2,1)S(1)}, bf16[3,256,256]{2,1,0:T(8,128)(2,1)S(1)}, u32[]{:S(2)}, u32[]{:S(2)}) collective-permute-start(bf16[3,256,256]{2,1,0:T(8,128)(2,1)S(1)} %add_convert_fusion.1), channel_id=1, source_target_pairs={{0,6},{1,25},{2,4},{3,27},{4,2},{5,29},{6,0},{7,31},{8,14},{9,17},... | collective-permute-start | bytes 1179656 | tf_op jit(solution)/shard_map/ppermute | solution.py:43
  24.4 7.5 %collective-permute-start.8 = (bf16[512,256]{1,0:T(8,128)(2,1)S(1)}, bf16[512,256]{1,0:T(8,128)(2,1)S(1)}, u32[]{:S(2)}, u32[]{:S(2)}) collective-permute-start(bf16[512,256]{1,0:T(8,128)(2,1)S(1)} %get-tuple-element.66), channel_id=1, source_target_pairs={{0,2},{1,9},{2,0},{3,11},{4,6},{5,13},{6,4},{7,15},{8,10},{9,1},{1... | collective-permute-start | bytes 786440 | tf_op jit(solution)/shard_map/ppermute | solution.py:43
  24.5 7.4 %collective-permute-start.9 = (bf16[512,256]{1,0:T(8,128)(2,1)S(1)}, bf16[512,256]{1,0:T(8,128)(2,1)S(1)}, u32[]{:S(2)}, u32[]{:S(2)}) collective-permute-start(bf16[512,256]{1,0:T(8,128)(2,1)S(1)} %get-tuple-element.67), channel_id=1, source_target_pairs={{0,6},{1,25},{2,4},{3,27},{4,2},{5,29},{6,0},{7,31},{8,14},{9,17},... | collective-permute-start | bytes 786440 | tf_op jit(solution)/shard_map/ppermute | solution.py:43
  28.6 8.2 %collective-permute-start.12 = (bf16[512,256]{1,0:T(8,128)(2,1)S(1)}, bf16[512,256]{1,0:T(8,128)(2,1)S(1)}, u32[]{:S(2)}, u32[]{:S(2)}) collective-permute-start(bf16[512,256]{1,0:T(8,128)(2,1)S(1)} %get-tuple-element.71), channel_id=1, source_target_pairs={{0,16},{1,5},{2,18},{3,7},{4,20},{5,1},{6,22},{7,3},{8,24},{9,13},... | collective-permute-start | bytes 786440 | tf_op jit(solution)/shard_map/ppermute | solution.py:43
  31.1 7.5 %collective-permute-start.13 = (bf16[512,256]{1,0:T(8,128)(2,1)S(1)}, bf16[512,256]{1,0:T(8,128)(2,1)S(1)}, u32[]{:S(2)}, u32[]{:S(2)}) collective-permute-start(bf16[512,256]{1,0:T(8,128)(2,1)S(1)} %get-tuple-element.72), channel_id=1, source_target_pairs={{0,8},{1,3},{2,10},{3,1},{4,12},{5,7},{6,14},{7,5},{8,0},{9,11},{1... | collective-permute-start | bytes 786440 | tf_op jit(solution)/shard_map/ppermute | solution.py:43
  31.7 7.9 %collective-permute-start.14 = (bf16[512,256]{1,0:T(8,128)(2,1)S(1)}, bf16[512,256]{1,0:T(8,128)(2,1)S(1)}, u32[]{:S(2)}, u32[]{:S(2)}) collective-permute-start(bf16[512,256]{1,0:T(8,128)(2,1)S(1)} %get-tuple-element.73), channel_id=1, source_target_pairs={{0,24},{1,7},{2,26},{3,5},{4,28},{5,3},{6,30},{7,1},{8,16},{9,15},... | collective-permute-start | bytes 786440 | tf_op jit(solution)/shard_map/ppermute | solution.py:43

commit v18 on v12

--- a/solution.py
+++ b/solution.py
@@ -390,8 +390,9 @@
     )
     lat_late, two_a, two_b = tie((lat_own, two_a, two_b))
     own[1], own[3], own[0] = own_products(lat_late, latent_grad, late)
-    (one_a,) = block(own, late, [(1, rest, *upper, bf16)], *shared, piece_late)
-    (three_b,) = block(own, late, [(3, rest, *lower, bf16)], *shared, piece_late)
+    one_a, three_b = block(
+        own, late, [(1, rest, *upper, bf16), (3, rest, *lower, bf16)], *shared, piece_late
+    )
     own[0], one_a, three_b = tie((own[0], one_a, three_b))
     one_b, three_a, one_stay, three_stay, kept_on, kept_stay = block(
         own,

time: 96.5 us -> 96.5 us (level)
    pallas_call x4 -> x3, Pallas kernels: 2.88 us -> 2.71 us  [block(): pl.pallas_call(functools.partial(block_kernel, tiles), out_shape=[jax.Sha...]
  transfers between devices with their start and end apart: 15 -> 15, of which waited for: 8 -> 8; matrix products, arithmetic and copies ran while one was open for 0% -> 0% of each run, Pallas kernels for 9% -> 8%
where the time goes in v18:
time: 96.5 us; the launch traced here: 96.2 us
  blocking collectives  49.7 us (52%)
  Pallas kernels  16.2 us (17%)
  starting transfers between devices  15.3 us (16%)
  waiting for transfers between devices  13 us (13%)
  between operations  1.64 us (2%)
    all_to_all x1, blocking collectives, body(): returned = lax.all_to_all(outgoing, PLANE, 0, 0, tiled=True)  20.6 us
    all_to_all x1, blocking collectives, body(): pieces = lax.all_to_all(head.reshape(NZ, -1, HD), 'z', 0, 0, tiled=True)  17.2 us
    ppermute x11, waiting for transfers between devices, exchange(): return lax.ppermute(value, AXES, pairs)  13 us
    all_to_all x1, blocking collectives, body(): lax.all_to_all(jnp.broadcast_to(piece, (NZ,) + piece.shape), 'z', 0, 0, t...  11.9 us
    ppermute x11, starting transfers between devices, exchange(): return lax.ppermute(value, AXES, pairs)  11.2 us
    pallas_call x1, Pallas kernels, newton_schulz(): pl.pallas_call(newton_schulz_kernel, out_shape=jax.ShapeDtypeStruct((owne...  5.75 us
    ppermute x4, starting transfers between devices, swap_cores(): lax.ppermute(value, AXES, [(device_at(z, y, x, c), device_at(z, y, x, 1 -...  4.11 us
    pallas_call x2, Pallas kernels, column_pieces(): pl.pallas_call(functools.partial(pieces_kernel, lists), out_shape=[jax.Sh...  3.25 us
  transfers between devices with their start and end apart: 15, of which 8 were waited for; matrix products, arithmetic and copies ran while one was open for 0% of the time, Pallas kernels for 8%

profile of v18, /device:TPU:1, one launch (start us, length us, event | category | flops | bytes accessed | tf_op | source)
XLA Modules:
  0.0 96.2 jit_solution(16381526959542291996)
XLA Ops:
  0.6 1.5 %shard_map.59 = (bf16[256,1024]{1,0:T(8,128)(2,1)S(1)}, bf16[256,1024]{1,0:T(8,128)(2,1)S(1)}) custom-call(bf16[256,8192]{1,0:T(8,128)(2,1)} %grad.4), custom_call_target="tpu_custom_call" | custom-call | tf_op jit(solution)/shard_map/pallas_call | solution.py:105
  2.2 3.3 %collective-permute-start = (bf16[256,1024]{1,0:T(8,128)(2,1)S(1)}, bf16[256,1024]{1,0:T(8,128)(2,1)S(1)}, u32[]{:S(2)}, u32[]{:S(2)}) collective-permute-start(bf16[256,1024]{1,0:T(8,128)(2,1)S(1)} %get-tuple-element.44), channel_id=1, source_target_pairs={{0,1},{1,0},{2,3},{3,2},{4,5},{5,4},{6,7},{7,6},{8,9},{9,8},{10,11... | collective-permute-start | bytes 1572872 | tf_op jit(solution)/shard_map/ppermute | solution.py:47
  6.2 0.7 shard_map.60
  6.9 0.1 collective-permute-start.2
  7.0 0.5 collective-permute-start.1
  7.5 1.7 %shard_map.61 = bf16[256,3072]{1,0:T(8,128)(2,1)S(1)} custom-call(bf16[256,8192]{1,0:T(8,128)(2,1)} %grad.4), custom_call_target="tpu_custom_call" | custom-call | tf_op jit(solution)/shard_map/pallas_call | solution.py:105
  9.2 0.0 collective-permute-done.2.mom_other
  9.2 0.0 collective-permute-done.1.lat
  9.2 0.0 collective-permute-done.grad
  9.2 0.2 collective-permute-start.3
  9.4 0.7 shard_map.62
  10.1 1.1 %collective-permute-start.7 = (bf16[4,256,256]{2,1,0:T(8,128)(2,1)S(1)}, bf16[4,256,256]{2,1,0:T(8,128)(2,1)S(1)}, u32[]{:S(2)}, u32[]{:S(2)}) collective-permute-start(bf16[4,256,256]{2,1,0:T(8,128)(2,1)S(1)} %get-tuple-element.69), channel_id=1, source_target_pairs={{0,6},{1,25},{2,4},{3,27},{4,2},{5,29},{6,0},{7,31},{8,14},{9,17},... | collective-permute-start | bytes 1572872 | tf_op jit(solution)/shard_map/ppermute | solution.py:43
  11.2 0.0 collective-permute-start.6
  11.2 2.5 %shard_map.63 = (bf16[4,512,256]{2,1,0:T(8,128)(2,1)S(1)}, bf16[4,512,256]{2,1,0:T(8,128)(2,1)S(1)}, bf16[4,512,256]{2,1,0:T(8,128)(2,1)S(1)}) custom-call(bf16[512,256]{1,0:T(8,128)(2,1)S(1)} %get-tuple-element.55.lat, bf16[256,8192]{1,0:T(8,128)(2,1)} %grad.4), custom_call_target="tpu_custom_call" | custom-call | flops 805306368 | bytes 4718592 | tf_op jit(solution)/shard_map/pallas_call | solution.py:176
  13.8 0.0 collective-permute-done.3.grad
  13.8 0.6 shard_map.64
  14.4 1.6 %collective-permute-start.4 = (bf16[3,256,256]{2,1,0:T(8,128)(2,1)S(1)}, bf16[3,256,256]{2,1,0:T(8,128)(2,1)S(1)}, u32[]{:S(2)}, u32[]{:S(2)}) collective-permute-start(bf16[3,256,256]{2,1,0:T(8,128)(2,1)S(1)} %get-tuple-element.64), channel_id=1, source_target_pairs={{0,2},{1,9},{2,0},{3,11},{4,6},{5,13},{6,4},{7,15},{8,10},{9,1},{1... | collective-permute-start | bytes 1179656 | tf_op jit(solution)/shard_map/ppermute | solution.py:43
  15.9 1.7 %collective-permute-start.5 = (bf16[3,256,256]{2,1,0:T(8,128)(2,1)S(1)}, bf16[3,256,256]{2,1,0:T(8,128)(2,1)S(1)}, u32[]{:S(2)}, u32[]{:S(2)}) collective-permute-start(bf16[3,256,256]{2,1,0:T(8,128)(2,1)S(1)} %get-tuple-element.65), channel_id=1, source_target_pairs={{0,6},{1,25},{2,4},{3,27},{4,2},{5,29},{6,0},{7,31},{8,14},{9,17},... | collective-permute-start | bytes 1179656 | tf_op jit(solution)/shard_map/ppermute | solution.py:43
  17.6 1.4 %shard_map.65 = (f32[3,256,256]{2,1,0:T(8,128)S(1)}, f32[3,256,256]{2,1,0:T(8,128)S(1)}, f32[1,512,256]{2,1,0:T(8,128)S(1)}, f32[1,512,256]{2,1,0:T(8,128)S(1)},...) custom-call(bf16[512,64]{1,0:T(8,128)(2,1)S(1)} %get-tuple-element.41.unit, ...), custom_call_target="tpu_custom_call" | custom-call | flops 754974720 | bytes 7864320 | tf_op jit(solution)/shard_map/pallas_call | solution.py:216
  19.0 0.7 collective-permute-done.7.two_b
  19.8 0.1 add_convert_fusion
  19.8 0.1 collective-permute-start.11
  19.9 0.0 collective-permute-done.6.two_a
  19.9 0.1 add_convert_fusion.1
  20.0 1.3 %collective-permute-start.10 = (bf16[3,256,256]{2,1,0:T(8,128)(2,1)S(1)}, bf16[3,256,256]{2,1,0:T(8,128)(2,1)S(1)}, u32[]{:S(2)}, u32[]{:S(2)}) collective-permute-start(bf16[3,256,256]{2,1,0:T(8,128)(2,1)S(1)} %add_convert_fusion.1), channel_id=1, source_target_pairs={{0,6},{1,25},{2,4},{3,27},{4,2},{5,29},{6,0},{7,31},{8,14},{9,17},... | collective-permute-start | bytes 1179656 | tf_op jit(solution)/shard_map/ppermute | solution.py:43
  21.4 2.4 %collective-permute-done.4.upper = bf16[3,256,256]{2,1,0:T(8,128)(2,1)S(1)} collective-permute-done((bf16[3,256,256]{2,1,0:T(8,128)(2,1)S(1)}, bf16[3,256,256]{2,1,0:T(8,128)(2,1)S(1)}, u32[]{:S(2)}, u32[]{:S(2)}) %collective-permute-start.4) | collective-permute-done | bytes 393248 | tf_op jit(solution)/shard_map/ppermute | solution.py:43
  23.8 0.3 collective-permute-done.5.lower
  24.1 0.2 shard_map.66
  24.3 0.1 collective-permute-start.8
  24.4 1.9 %collective-permute-start.9 = (bf16[512,256]{1,0:T(8,128)(2,1)S(1)}, bf16[512,256]{1,0:T(8,128)(2,1)S(1)}, u32[]{:S(2)}, u32[]{:S(2)}) collective-permute-start(bf16[512,256]{1,0:T(8,128)(2,1)S(1)} %get-tuple-element.71), channel_id=1, source_target_pairs={{0,6},{1,25},{2,4},{3,27},{4,2},{5,29},{6,0},{7,31},{8,14},{9,17},... | collective-permute-start | bytes 786440 | tf_op jit(solution)/shard_map/ppermute | solution.py:43
  26.3 1.7 %collective-permute-done.11.lower = bf16[3,256,256]{2,1,0:T(8,128)(2,1)S(1)} collective-permute-done((bf16[3,256,256]{2,1,0:T(8,128)(2,1)S(1)}, bf16[3,256,256]{2,1,0:T(8,128)(2,1)S(1)}, u32[]{:S(2)}, u32[]{:S(2)}) %collective-permute-start.11) | collective-permute-done | bytes 393248 | tf_op jit(solution)/shard_map/ppermute | solution.py:43
  28.0 0.3 collective-permute-done.10.upper
  28.3 0.1 shard_map.68
  28.4 2.5 %collective-permute-start.12 = (bf16[512,256]{1,0:T(8,128)(2,1)S(1)}, bf16[512,256]{1,0:T(8,128)(2,1)S(1)}, u32[]{:S(2)}, u32[]{:S(2)}) collective-permute-start(bf16[512,256]{1,0:T(8,128)(2,1)S(1)} %get-tuple-element.75), channel_id=1, source_target_pairs={{0,16},{1,5},{2,18},{3,7},{4,20},{5,1},{6,22},{7,3},{8,24},{9,13},... | collective-permute-start | bytes 786440 | tf_op jit(solution)/shard_map/ppermute | solution.py:43
  30.9 0.6 collective-permute-start.13
  31.5 0.3 collective-permute-start.14
  31.8 0.0 collective-permute-done.8.one
  31.8 0.0 collective-permute-done.9.three
  31.8 0.1 shard_map.67
  31.9 4.8 %collective-permute-done.12 = bf16[512,256]{1,0:T(8,128)(2,1)S(1)} collective-permute-done((bf16[512,256]{1,0:T(8,128)(2,1)S(1)}, bf16[512,256]{1,0:T(8,128)(2,1)S(1)}, u32[]{:S(2)}, u32[]{:S(2)}) %collective-permute-start.12) | collective-permute-done | bytes 262176 | tf_op jit(solution)/shard_map/ppermute | solution.py:43
  36.6 1.8 %collective-permute-done.13 = bf16[512,256]{1,0:T(8,128)(2,1)S(1)} collective-permute-done((bf16[512,256]{1,0:T(8,128)(2,1)S(1)}, bf16[512,256]{1,0:T(8,128)(2,1)S(1)}, u32[]{:S(2)}, u32[]{:S(2)}) %collective-permute-start.13) | collective-permute-done | bytes 262176 | tf_op jit(solution)/shard_map/ppermute | solution.py:43
  38.4 1.0 %collective-permute-done.14 = bf16[512,256]{1,0:T(8,128)(2,1)S(1)} collective-permute-done((bf16[512,256]{1,0:T(8,128)(2,1)S(1)}, bf16[512,256]{1,0:T(8,128)(2,1)S(1)}, u32[]{:S(2)}, u32[]{:S(2)}) %collective-permute-start.14) | collective-permute-done | bytes 262176 | tf_op jit(solution)/shard_map/ppermute | solution.py:43
  39.4 0.1 add_convert_fusion.2
  39.5 17.2 %all_to_all.15 = bf16[8,64,256]{2,1,0:T(8,128)(2,1)S(1)} all-to-all(bf16[8,64,256]{2,1,0:T(8,128)(2,1)S(1)} %bitcast.3), channel_id=1, replica_groups=mesh['z'=8,'y'=4,'x'=4,'c'=2] {'z'}, dimensions={0} | all-to-all | bytes 524288 | tf_op jit(solution)/shard_map/all_to_all | solution.py:425
  56.9 11.9 %all_to_all.16 = bf16[8,64,256]{2,1,0:T(8,128)(2,1)S(1)} all-to-all(bf16[8,64,256]{2,1,0:T(8,128)(2,1)S(1)} %broadcast_in_dim.3), channel_id=1, replica_groups=mesh['z'=8,'y'=4,'x'=4,'c'=2] {'z'}, dimensions={0} | all-to-all | bytes 524288 | tf_op jit(solution)/shard_map/all_to_all | solution.py:427
  68.7 5.8 %shard_map.69 = bf16[32,2,16,256]{3,2,1,0:T(8,128)(2,1)S(1)} custom-call(bf16[512,256]{1,0:T(8,128)(2,1)S(1)} %bitcast.2), custom_call_target="tpu_custom_call" | custom-call | tf_op jit(solution)/shard_map/pallas_call | solution.py:322
  74.5 20.6 %all_to_all.17.returned = bf16[32,2,16,256]{3,2,1,0:T(8,128)(2,1)S(1)} all-to-all(bf16[32,2,16,256]{3,2,1,0:T(8,128)(2,1)S(1)} %shard_map.69), channel_id=1, replica_groups=mesh['z'=8,'y'=4,'x'=4,'c'=2] {'c','y','x'}, dimensions={0} | all-to-all | bytes 1048576 | tf_op jit(solution)/shard_map/all_to_all | solution.py:431
  95.1 0.9 shard_map.70
  (6 shorter events, 0.1 us)
Async XLA Ops:
  0.6 5.6 %copy-start = (f32[16,8192]{1,0:T(8,128)S(1)}, f32[16,8192]{1,0:T(8,128)}, u32[]{:S(2)}) copy-start(f32[16,8192]{1,0:T(8,128)} %momentum.1) | copy-start | bytes 1572868
  0.6 5.6 %copy-start.1 = (bf16[256,512]{1,0:T(8,128)(2,1)S(1)}, bf16[256,512]{1,0:T(8,128)(2,1)}, u32[]{:S(2)}) copy-start(bf16[256,512]{1,0:T(8,128)(2,1)} %latent.1) | copy-start | bytes 786436
  2.2 7.0 %collective-permute-start = (bf16[256,1024]{1,0:T(8,128)(2,1)S(1)}, bf16[256,1024]{1,0:T(8,128)(2,1)S(1)}, u32[]{:S(2)}, u32[]{:S(2)}) collective-permute-start(bf16[256,1024]{1,0:T(8,128)(2,1)S(1)} %get-tuple-element.44), channel_id=1, source_target_pairs={{0,1},{1,0},{2,3},{3,2},{4,5},{5,4},{6,7},{7,6},{8,9},{9,8},{10,11... | collective-permute-start | bytes 1572872 | tf_op jit(solution)/shard_map/ppermute | solution.py:47
  6.9 2.3 %collective-permute-start.2 = (bf16[32,4096]{1,0:T(8,128)(2,1)S(1)}, bf16[32,4096]{1,0:T(8,128)(2,1)S(1)}, u32[]{:S(2)}, u32[]{:S(2)}) collective-permute-start(bf16[32,4096]{1,0:T(8,128)(2,1)S(1)} %get-tuple-element.46), channel_id=1, source_target_pairs={{0,1},{1,0},{2,3},{3,2},{4,5},{5,4},{6,7},{7,6},{8,9},{9,8},{10,11... | collective-permute-start | bytes 786440 | tf_op jit(solution)/shard_map/ppermute | solution.py:47
  7.0 2.2 %collective-permute-start.1 = (bf16[512,256]{1,0:T(8,128)(2,1)S(1)}, bf16[512,256]{1,0:T(8,128)(2,1)S(1)}, u32[]{:S(2)}, u32[]{:S(2)}) collective-permute-start(bf16[512,256]{1,0:T(8,128)(2,1)S(1)} %get-tuple-element.55.lat), channel_id=1, source_target_pairs={{0,1},{1,0},{2,3},{3,2},{4,5},{5,4},{6,7},{7,6},{8,9},{9,8},{10,11... | collective-permute-start | bytes 786440 | tf_op jit(solution)/shard_map/ppermute | solution.py:47
  9.2 4.6 %collective-permute-start.3 = (bf16[256,3072]{1,0:T(8,128)(2,1)S(1)}, bf16[256,3072]{1,0:T(8,128)(2,1)S(1)}, u32[]{:S(2)}, u32[]{:S(2)}) collective-permute-start(bf16[256,3072]{1,0:T(8,128)(2,1)S(1)} %shard_map.61), channel_id=1, source_target_pairs={{0,1},{1,0},{2,3},{3,2},{4,5},{5,4},{6,7},{7,6},{8,9},{9,8},{10,11... | collective-permute-start | bytes 4718600 | tf_op jit(solution)/shard_map/ppermute | solution.py:47
  10.1 9.6 %collective-permute-start.7 = (bf16[4,256,256]{2,1,0:T(8,128)(2,1)S(1)}, bf16[4,256,256]{2,1,0:T(8,128)(2,1)S(1)}, u32[]{:S(2)}, u32[]{:S(2)}) collective-permute-start(bf16[4,256,256]{2,1,0:T(8,128)(2,1)S(1)} %get-tuple-element.69), channel_id=1, source_target_pairs={{0,6},{1,25},{2,4},{3,27},{4,2},{5,29},{6,0},{7,31},{8,14},{9,17},... | collective-permute-start | bytes 1572872 | tf_op jit(solution)/shard_map/ppermute | solution.py:43
  11.2 8.7 %collective-permute-start.6 = (bf16[4,256,256]{2,1,0:T(8,128)(2,1)S(1)}, bf16[4,256,256]{2,1,0:T(8,128)(2,1)S(1)}, u32[]{:S(2)}, u32[]{:S(2)}) collective-permute-start(bf16[4,256,256]{2,1,0:T(8,128)(2,1)S(1)} %get-tuple-element.68), channel_id=1, source_target_pairs={{0,2},{1,9},{2,0},{3,11},{4,6},{5,13},{6,4},{7,15},{8,10},{9,1},{1... | collective-permute-start | bytes 1572872 | tf_op jit(solution)/shard_map/ppermute | solution.py:43
  14.4 9.4 %collective-permute-start.4 = (bf16[3,256,256]{2,1,0:T(8,128)(2,1)S(1)}, bf16[3,256,256]{2,1,0:T(8,128)(2,1)S(1)}, u32[]{:S(2)}, u32[]{:S(2)}) collective-permute-start(bf16[3,256,256]{2,1,0:T(8,128)(2,1)S(1)} %get-tuple-element.64), channel_id=1, source_target_pairs={{0,2},{1,9},{2,0},{3,11},{4,6},{5,13},{6,4},{7,15},{8,10},{9,1},{1... | collective-permute-start | bytes 1179656 | tf_op jit(solution)/shard_map/ppermute | solution.py:43
  15.9 8.1 %collective-permute-start.5 = (bf16[3,256,256]{2,1,0:T(8,128)(2,1)S(1)}, bf16[3,256,256]{2,1,0:T(8,128)(2,1)S(1)}, u32[]{:S(2)}, u32[]{:S(2)}) collective-permute-start(bf16[3,256,256]{2,1,0:T(8,128)(2,1)S(1)} %get-tuple-element.65), channel_id=1, source_target_pairs={{0,6},{1,25},{2,4},{3,27},{4,2},{5,29},{6,0},{7,31},{8,14},{9,17},... | collective-permute-start | bytes 1179656 | tf_op jit(solution)/shard_map/ppermute | solution.py:43
  19.8 8.1 %collective-permute-start.11 = (bf16[3,256,256]{2,1,0:T(8,128)(2,1)S(1)}, bf16[3,256,256]{2,1,0:T(8,128)(2,1)S(1)}, u32[]{:S(2)}, u32[]{:S(2)}) collective-permute-start(bf16[3,256,256]{2,1,0:T(8,128)(2,1)S(1)} %add_convert_fusion), channel_id=1, source_target_pairs={{0,2},{1,9},{2,0},{3,11},{4,6},{5,13},{6,4},{7,15},{8,10},{9,1},{1... | collective-permute-start | bytes 1179656 | tf_op jit(solution)/shard_map/ppermute | solution.py:43
  20.0 8.2 %collective-permute-start.10 = (bf16[3,256,256]{2,1,0:T(8,128)(2,1)S(1)}, bf16[3,256,256]{2,1,0:T(8,128)(2,1)S(1)}, u32[]{:S(2)}, u32[]{:S(2)}) collective-permute-start(bf16[3,256,256]{2,1,0:T(8,128)(2,1)S(1)} %add_convert_fusion.1), channel_id=1, source_target_pairs={{0,6},{1,25},{2,4},{3,27},{4,2},{5,29},{6,0},{7,31},{8,14},{9,17},... | collective-permute-start | bytes 1179656 | tf_op jit(solution)/shard_map/ppermute | solution.py:43
  24.3 7.5 %collective-permute-start.8 = (bf16[512,256]{1,0:T(8,128)(2,1)S(1)}, bf16[512,256]{1,0:T(8,128)(2,1)S(1)}, u32[]{:S(2)}, u32[]{:S(2)}) collective-permute-start(bf16[512,256]{1,0:T(8,128)(2,1)S(1)} %get-tuple-element.70), channel_id=1, source_target_pairs={{0,2},{1,9},{2,0},{3,11},{4,6},{5,13},{6,4},{7,15},{8,10},{9,1},{1... | collective-permute-start | bytes 786440 | tf_op jit(solution)/shard_map/ppermute | solution.py:43
  24.4 7.4 %collective-permute-start.9 = (bf16[512,256]{1,0:T(8,128)(2,1)S(1)}, bf16[512,256]{1,0:T(8,128)(2,1)S(1)}, u32[]{:S(2)}, u32[]{:S(2)}) collective-permute-start(bf16[512,256]{1,0:T(8,128)(2,1)S(1)} %get-tuple-element.71), channel_id=1, source_target_pairs={{0,6},{1,25},{2,4},{3,27},{4,2},{5,29},{6,0},{7,31},{8,14},{9,17},... | collective-permute-start | bytes 786440 | tf_op jit(solution)/shard_map/ppermute | solution.py:43
  28.4 8.2 %collective-permute-start.12 = (bf16[512,256]{1,0:T(8,128)(2,1)S(1)}, bf16[512,256]{1,0:T(8,128)(2,1)S(1)}, u32[]{:S(2)}, u32[]{:S(2)}) collective-permute-start(bf16[512,256]{1,0:T(8,128)(2,1)S(1)} %get-tuple-element.75), channel_id=1, source_target_pairs={{0,16},{1,5},{2,18},{3,7},{4,20},{5,1},{6,22},{7,3},{8,24},{9,13},... | collective-permute-start | bytes 786440 | tf_op jit(solution)/shard_map/ppermute | solution.py:43
  30.9 7.5 %collective-permute-start.13 = (bf16[512,256]{1,0:T(8,128)(2,1)S(1)}, bf16[512,256]{1,0:T(8,128)(2,1)S(1)}, u32[]{:S(2)}, u32[]{:S(2)}) collective-permute-start(bf16[512,256]{1,0:T(8,128)(2,1)S(1)} %get-tuple-element.76), channel_id=1, source_target_pairs={{0,8},{1,3},{2,10},{3,1},{4,12},{5,7},{6,14},{7,5},{8,0},{9,11},{1... | collective-permute-start | bytes 786440 | tf_op jit(solution)/shard_map/ppermute | solution.py:43
  31.5 7.9 %collective-permute-start.14 = (bf16[512,256]{1,0:T(8,128)(2,1)S(1)}, bf16[512,256]{1,0:T(8,128)(2,1)S(1)}, u32[]{:S(2)}, u32[]{:S(2)}) collective-permute-start(bf16[512,256]{1,0:T(8,128)(2,1)S(1)} %get-tuple-element.77), channel_id=1, source_target_pairs={{0,24},{1,7},{2,26},{3,5},{4,28},{5,3},{6,30},{7,1},{8,16},{9,15},... | collective-permute-start | bytes 786440 | tf_op jit(solution)/shard_map/ppermute | solution.py:43
